TPU v7x, 256 devices: a whole 4x4x8 slice. The times are simulated.
256 devices in a mesh: lat: 16 (over z, y_lo), lon: 16 (over x, y_hi, core).
Axes of the slice: x: 4, y: 4 (y_hi: 2, y_lo: 2; y = y_hi * 2 + y_lo), z: 8, core: 2. Of those that a mesh axis runs over, the one named last changes fastest.
Arguments:
- fields: float32 [2, 192, 96, 512], P(None, 'lat', 'lon'), may hold values from -13 to 13, as said below
- grad_out: float32 [2, 192, 96, 512], P(None, 'lat', 'lon'), may hold values from -6 to 6
- region_ids: int32 [2, 192, 96], P(None, 'lat', 'lon'), may hold values from 0 to 2
- bias_index: int32 [144, 144], replicated, may hold values from 0 to 6335
- bias_table: float32 [6336, 16], replicated, may hold values from -4 to 4
- in_weight: float32 [512, 1536], replicated, may hold values from -5 to 5, as said below
- out_weight: float32 [512, 512], replicated, may hold values from -0.25 to 0.25
Outputs:
- grad_fields: float32 [2, 192, 96, 512], P(None, 'lat', 'lon')
- grad_in_weight: float32 [512, 1536], P('lon')
- grad_out_weight: float32 [512, 512], P('lon')
- grad_bias: float32 [6336, 16], P('lon')
Inputs may be any that keep to these rules, and one draw needn't show every extreme that they name: `fields`: rows of the tokens have scales that differ widely. `in_weight`: Fan-in scaled; the query and key columns of each head carry a gain of their own.
All inputs are finite; a program needn't handle non-finite values.
Results may differ from a plain program's by a relative error of at most 0.0003.
Values sent between devices are 32-bit elements; how exact they have to be, the bound alone decides.
No kernel may reach another device: no remote copies, remote signals or barrier semaphores. Data moves between devices by JAX's collectives and lax.ppermute only.
A program may use at most 128 MiB of HBM per device.

v0:
```python
import functools

import jax
import jax.numpy as jnp
import numpy as np
from jax import lax
from jax.experimental import pallas as pl
from jax.experimental.pallas import tpu as pltpu
from jax.sharding import PartitionSpec as P

WIDTH = 512
HEADS = 16
HEAD_DIM = 32
TOKENS = 144
QUAD = 36
BIAS_ROWS = 6336
HALF_SECTOR = 198
FACTOR = HEAD_DIM ** (-0.5)
F32 = jnp.float32
BF16 = jnp.bfloat16
MEGA = 1 << 20


def params(mib=48):
    return pltpu.CompilerParams(vmem_limit_bytes=mib * MEGA)


def whole(count):
    return [pl.BlockSpec(memory_space=pltpu.VMEM)] * count


def scalar():
    return pl.BlockSpec(memory_space=pltpu.SMEM)


def halves(x):
    high = x.astype(BF16)
    low = (x - high.astype(F32)).astype(BF16)
    return high, low


def dot(a, b, dims):
    return lax.dot_general(a, b, (dims, ((), ())), preferred_element_type=F32)


NN = ((1,), (0,))
NT = ((1,), (1,))
TN = ((0,), (0,))


def dot3(a, b, dims):
    ah, al = a
    bh, bl = b
    return dot(ah, bh, dims) + (dot(ah, bl, dims) + dot(al, bh, dims))


def token_order():
    grid = np.arange(TOKENS).reshape(2, 2, 6, 2, 3)
    return np.transpose(grid, (1, 3, 0, 2, 4)).reshape(-1)


def pack_kernel(last, fields, grads, ids, own, left, below, corner):
    lanes = lax.broadcasted_iota(jnp.int32, (6, WIDTH), 1)
    rows = lax.broadcasted_iota(jnp.int32, (6, WIDTH), 0)
    bump = last[0]
    plan = (
        (own, 0, 3, 2, None),
        (left, 0, 0, 3, None),
        (below, 6, 3, 0, bump),
        (corner, 6, 0, 1, bump),
    )
    for ref, row0, col0, quadrant, offset in plan:
        label = jnp.zeros((6, WIDTH), jnp.int32)
        for level in range(2):
            for row in range(6):
                spot = level * 18 + row * 3
                ref[spot : spot + 3, :] = fields[level, row0 + row, col0 : col0 + 3, :]
                ref[QUAD + spot : QUAD + spot + 3, :] = grads[
                    level, row0 + row, col0 : col0 + 3, :
                ]
            for col in range(3):
                column = ids[level, row0 : row0 + 6, col0 + col : col0 + col + 1] + 1
                if offset is not None:
                    column = column + offset
                place = quadrant * QUAD + level * 18 + col
                label = label + jnp.where(
                    lanes == rows * 3 + place, jnp.broadcast_to(column, (6, WIDTH)), 0
                )
        total = jnp.sum(label.astype(F32), axis=0, keepdims=True)
        ref[72:80, :] = jnp.broadcast_to(total, (8, WIDTH))


def pack(last, fields, grads, ids):
    shape = jax.ShapeDtypeStruct((80, WIDTH), F32)
    return pl.pallas_call(
        pack_kernel,
        out_shape=[shape] * 4,
        in_specs=[scalar()] + whole(3),
        out_specs=whole(4),
        compiler_params=params(),
        name="pack",
    )(last, fields, grads, ids)


def order_kernel(index, order, wide, narrow):
    value = index[...]
    high = (value >> 7).astype(F32).astype(BF16)
    low = (value & 127).astype(F32).astype(BF16)
    move = order[...]

    def moved(part):
        return dot(dot(move, part, NN).astype(BF16), move, NT)

    result = (moved(high) * 128.0 + moved(low)).astype(jnp.int32)
    wide[...] = result[:, :128]
    narrow[...] = result[:, 128:]


def ordered_index(bias_index):
    order = np.zeros((TOKENS, TOKENS), np.float32)
    order[np.arange(TOKENS), token_order()] = 1.0
    wide, narrow = pl.pallas_call(
        order_kernel,
        out_shape=[
            jax.ShapeDtypeStruct((TOKENS, 128), jnp.int32),
            jax.ShapeDtypeStruct((TOKENS, 16), jnp.int32),
        ],
        in_specs=whole(2),
        out_specs=whole(2),
        compiler_params=params(),
        name="order",
    )(bias_index, jnp.asarray(order, BF16))
    return wide, narrow.reshape(18, 128)


def lookup_kernel(wide, narrow, table, out_wide, out_narrow):
    spots = [(wide, out_wide, 8 * i, 8) for i in range(18)]
    spots += [(narrow, out_narrow, 8 * i, 8) for i in range(3)]
    groups = [spots[:7], spots[7:14], spots[14:]]

    def one_head(head, carry):
        for group in groups:
            lows = [src[at : at + size, :] & 127 for src, _, at, size in group]
            highs = [src[at : at + size, :] >> 7 for src, _, at, size in group]

            def step(block, found):
                row = jnp.broadcast_to(table[head, pl.ds(block, 1), :], (8, 128))
                new = []
                for low, high, value in zip(lows, highs, found):
                    pick = jnp.take_along_axis(row, low, axis=1, mode="promise_in_bounds")
                    new.append(jnp.where(high == block, pick, value))
                return tuple(new)

            found = lax.fori_loop(
                0, 50, step, tuple(jnp.zeros((8, 128), F32) for _ in group), unroll=5
            )
            for value, (_, dst, at, size) in zip(found, group):
                dst[head, at : at + size, :] = value
        return carry

    lax.fori_loop(0, HEADS, one_head, 0)


def lookup(wide, narrow, bias_table):
    table = jnp.pad(bias_table.T, ((0, 0), (0, 6400 - BIAS_ROWS))).reshape(HEADS, 50, 128)
    narrow = jnp.pad(narrow, ((0, 6), (0, 0)))
    out_wide, out_narrow = pl.pallas_call(
        lookup_kernel,
        out_shape=[
            jax.ShapeDtypeStruct((HEADS, TOKENS, 128), F32),
            jax.ShapeDtypeStruct((HEADS, 24, 128), F32),
        ],
        in_specs=whole(3),
        out_specs=whole(2),
        compiler_params=params(),
        name="lookup",
    )(wide, narrow, table)
    return out_wide, out_narrow[:, :18].reshape(HEADS, TOKENS, 16)


def main_kernel(
    core_ref,
    own,
    quad0,
    quad1,
    quad3,
    bias_wide,
    bias_narrow,
    in_weight,
    out_weight,
    keep,
    send,
    keep_wide,
    send_wide,
    keep_narrow,
    send_narrow,
    grad0,
    grad1,
    grad2,
    grad3,
    tokens,
    cotangent,
    proj,
    gatt,
    gproj,
    att,
    normed_t,
):
    core = core_ref[0]
    for slot, quad in enumerate((quad0, quad1, own, quad3)):
        at = slot * QUAD
        tokens[at : at + QUAD, :] = quad[0:QUAD, :]
        cotangent[at : at + QUAD, :] = quad[QUAD : 2 * QUAD, :]
    row = (quad0[72:73, :] + quad1[72:73, :] + own[72:73, :] + quad3[72:73, :])[:, :TOKENS]
    side = lax.broadcasted_iota(jnp.int32, (TOKENS, TOKENS), 0)
    along = lax.broadcasted_iota(jnp.int32, (TOKENS, TOKENS), 1)
    spread = jnp.broadcast_to(row, (TOKENS, TOKENS))
    column = jnp.sum(jnp.where(side == along, spread, 0.0), axis=1, keepdims=True)
    allowed = column == spread

    inputs = tokens[...]
    centered = inputs - jnp.mean(inputs, axis=1, keepdims=True)
    variance = jnp.mean(centered * centered, axis=1, keepdims=True)
    inv_std = lax.rsqrt(variance + 1e-05)
    normed = centered * inv_std
    tokens[...] = normed
    normed_t[...] = normed.T
    halves_normed = halves(normed)
    for part in range(3):
        at = part * WIDTH
        weight = halves(in_weight[:, at : at + WIDTH])
        proj[at : at + WIDTH, :] = dot3(halves_normed, weight, NN).T
    halves_cotangent = halves(cotangent[...])
    gatt[...] = dot3(halves(out_weight[...]), halves_cotangent, NT)

    def one_head(head):
        at = pl.multiple_of(head * HEAD_DIM, HEAD_DIM)
        qh, ql = halves(proj[pl.ds(at, HEAD_DIM), :] * FACTOR)
        kh, kl = halves(proj[pl.ds(at + WIDTH, HEAD_DIM), :])
        vh, vl = halves(proj[pl.ds(at + 2 * WIDTH, HEAD_DIM), :])
        gh, gl = halves(gatt[pl.ds(at, HEAD_DIM), :])
        bias = jnp.concatenate([bias_wide[head], bias_narrow[head]], axis=1)

        def stacked(*parts):
            return jnp.concatenate(parts, axis=0)

        scores = dot(stacked(qh, qh, ql), stacked(kh, kl, kh), TN) + bias
        scores = jnp.where(allowed, scores, -1000000000.0)
        peak = jnp.max(scores, axis=1, keepdims=True)
        exponent = jnp.exp(scores - peak)
        probs = exponent * (1.0 / jnp.sum(exponent, axis=1, keepdims=True))
        grad_probs = dot(stacked(gh, gh, gl), stacked(vh, vl, vh), TN)
        inner = jnp.sum(grad_probs * probs, axis=1, keepdims=True)
        grad_scores = probs * (grad_probs - inner)
        ph, plow = halves(probs)
        sh, sl = halves(grad_scores)

        def product(high, low, right_high, right_low, dims):
            both = dot(stacked(high, low), right_high, dims)
            return both[:HEAD_DIM] + (both[HEAD_DIM:] + dot(high, right_low, dims))

        att[pl.ds(at, HEAD_DIM), :] = product(vh, vl, ph, plow, NT)
        gproj[pl.ds(at + 2 * WIDTH, HEAD_DIM), :] = product(gh, gl, ph, plow, NN)
        gproj[pl.ds(at, HEAD_DIM), :] = product(kh, kl, sh, sl, NT) * FACTOR
        gproj[pl.ds(at + WIDTH, HEAD_DIM), :] = product(qh, ql, sh, sl, NN)
        return grad_scores

    for slot in range(8):
        grad_scores = one_head((1 - core) * 8 + slot)
        send_wide[:, slot, :] = grad_scores[:, :128]
        send_narrow[slot] = grad_scores[:, 128:]
        grad_scores = one_head(core * 8 + slot)
        keep_wide[:, slot, :] = grad_scores[:, :128]
        keep_narrow[slot] = grad_scores[:, 128:]

    for target, bit in ((send, 1 - core), (keep, core)):
        rows = [pl.ds(pl.multiple_of(64 * i + 32 * bit, 32), 32) for i in range(8)]
        left = halves(jnp.concatenate([normed_t[r, :] for r in rows], axis=0))
        for part in range(3):
            at = part * WIDTH
            target[:, at : at + WIDTH] = dot3(left, halves(gproj[at : at + WIDTH, :]), NT)
        left = halves(jnp.concatenate([att[r, :] for r in rows], axis=0))
        target[:, 3 * WIDTH :] = dot3(left, halves_cotangent, NN)

    grad_normed = jnp.zeros((WIDTH, TOKENS), F32)
    for part in range(3):
        at = part * WIDTH
        grad_normed = grad_normed + dot3(
            halves(in_weight[:, at : at + WIDTH]), halves(gproj[at : at + WIDTH, :]), NN
        )
    grad_normed = grad_normed.T
    normed = tokens[...]
    result = inv_std * (
        grad_normed
        - jnp.mean(grad_normed, axis=1, keepdims=True)
        - normed * jnp.mean(grad_normed * normed, axis=1, keepdims=True)
    )
    tokens[...] = result
    for slot, target in enumerate((grad0, grad1, grad2, grad3)):
        target[...] = tokens[slot * QUAD : slot * QUAD + QUAD, :]


def window(core, own, quad0, quad1, quad3, bias_wide, bias_narrow, in_weight, out_weight):
    def shape(*dims):
        return jax.ShapeDtypeStruct(dims, F32)

    grad = shape(QUAD, WIDTH)
    return pl.pallas_call(
        main_kernel,
        out_shape=[
            shape(256, 4 * WIDTH),
            shape(256, 4 * WIDTH),
            shape(TOKENS, 8, 128),
            shape(TOKENS, 8, 128),
            shape(8, TOKENS, 16),
            shape(8, TOKENS, 16),
            grad,
            grad,
            grad,
            grad,
        ],
        in_specs=[scalar()] + whole(8),
        out_specs=whole(10),
        scratch_shapes=[
            pltpu.VMEM((TOKENS, WIDTH), F32),
            pltpu.VMEM((TOKENS, WIDTH), F32),
            pltpu.VMEM((3 * WIDTH, TOKENS), F32),
            pltpu.VMEM((WIDTH, TOKENS), F32),
            pltpu.VMEM((3 * WIDTH, TOKENS), F32),
            pltpu.VMEM((WIDTH, TOKENS), F32),
            pltpu.VMEM((WIDTH, TOKENS), F32),
        ],
        compiler_params=params(56),
        name="window",
    )(core, own, quad0, quad1, quad3, bias_wide, bias_narrow, in_weight, out_weight)


def scatter_kernel(
    wide, narrow, keep_wide, came_wide, keep_narrow, came_narrow, out, total, wide_sum
):
    total[...] = jnp.zeros_like(total)
    wide_sum[...] = keep_wide[...] + came_wide[...]
    lines = lax.broadcasted_iota(jnp.int32, (256, 128), 0).astype(F32).astype(BF16)

    def sides(index, values):
        block = jnp.zeros_like(index)
        for edge in range(1, 32):
            block = block + jnp.where(index >= edge * HALF_SECTOR, 1, 0)
        inside = (index - block * HALF_SECTOR).astype(F32).astype(BF16)
        block = block.astype(F32).astype(BF16)
        high, low = halves(values)
        both = jnp.concatenate([high, low], axis=0)
        spread = jnp.broadcast_to(block, (16, 128))
        left = jnp.concatenate(
            [jnp.where(spread == float(b), both, jnp.zeros_like(both)) for b in range(32)], axis=0
        )
        hit = lines == jnp.broadcast_to(inside, (256, 128))
        right = jnp.where(hit, jnp.ones((256, 128), BF16), jnp.zeros((256, 128), BF16))
        return left, right

    def add(pieces):
        left = jnp.concatenate([p[0] for p in pieces], axis=1)
        right = jnp.concatenate([p[1] for p in pieces], axis=1)
        total[...] += dot(left, right, NT)

    def wide_step(step, carry):
        base = pl.multiple_of(step * 8, 8)
        index = wide[pl.ds(base, 8), :]
        for pair in range(4):
            add(
                [
                    sides(index[j : j + 1, :], wide_sum[base + j])
                    for j in (2 * pair, 2 * pair + 1)
                ]
            )
        return carry

    lax.fori_loop(0, 18, wide_step, 0)
    for pair in range(9):
        add(
            [
                sides(narrow[j : j + 1, :], keep_narrow[:, j, :] + came_narrow[:, j, :])
                for j in (2 * pair, 2 * pair + 1)
            ]
        )
    for block in range(32):
        chip, core, half = block // 4, block // 2 % 2, block % 2
        value = total[block * 16 : block * 16 + 8, :] + total[block * 16 + 8 : block * 16 + 16, :]
        out[chip, half * 16 + core * 8 : half * 16 + core * 8 + 8, :] = value


def scatter(wide, narrow, keep_wide, came_wide, keep_narrow, came_narrow):
    return pl.pallas_call(
        scatter_kernel,
        out_shape=jax.ShapeDtypeStruct((8, 32, 256), F32),
        in_specs=whole(6),
        out_specs=pl.BlockSpec(memory_space=pltpu.VMEM),
        scratch_shapes=[pltpu.VMEM((512, 256), F32), pltpu.VMEM((TOKENS, 8, 128), F32)],
        compiler_params=params(),
        name="scatter",
    )(
        wide,
        narrow,
        keep_wide,
        came_wide,
        keep_narrow.reshape(8, 18, 128),
        came_narrow.reshape(8, 18, 128),
    )


def join_kernel(keep, came, table, out):
    for i in range(8):
        out[i, :, : 4 * WIDTH] = keep[i * 32 : i * 32 + 32, :] + came[i * 32 : i * 32 + 32, :]
        out[i, :, 4 * WIDTH :] = table[i]


def join(keep, came, table):
    return pl.pallas_call(
        join_kernel,
        out_shape=jax.ShapeDtypeStruct((8, 32, 2304), F32),
        in_specs=whole(3),
        out_specs=pl.BlockSpec(memory_space=pltpu.VMEM),
        compiler_params=params(),
        name="join",
    )(keep, came, table)


def fold_lon_kernel(parts, out):
    def rows(at):
        total = parts[0, at : at + 8, :]
        for i in range(1, 8):
            total = total + parts[i, at : at + 8, :]
        return total

    for group in range(4):
        total = rows(group * 8)
        for col in range(4):
            if col < 3:
                out[group * 4 + col] = total[:, col * 640 : col * 640 + 640]
            else:
                out[group * 4 + col, :, :384] = total[:, 1920:2304]
                out[group * 4 + col, :, 384:] = jnp.zeros((8, 256), F32)


def fold_lon(parts):
    return pl.pallas_call(
        fold_lon_kernel,
        out_shape=jax.ShapeDtypeStruct((16, 8, 640), F32),
        in_specs=whole(1),
        out_specs=pl.BlockSpec(memory_space=pltpu.VMEM),
        compiler_params=params(),
        name="fold_lon",
    )(parts)


def fold_lat_kernel(parts, out):
    total = parts[0]
    for i in range(1, 16):
        total = total + parts[i]
    for i in range(16):
        out[i] = total


def fold_lat(parts):
    return pl.pallas_call(
        fold_lat_kernel,
        out_shape=jax.ShapeDtypeStruct((16, 8, 640), F32),
        in_specs=whole(1),
        out_specs=pl.BlockSpec(memory_space=pltpu.VMEM),
        compiler_params=params(),
        name="fold_lat",
    )(parts)


def unpack_kernel(core_ref, parts, grad_in, grad_out, keep, send):
    core = core_ref[0]
    for group in range(4):
        rows = slice(group * 8, group * 8 + 8)
        base = group * 4
        grad_in[rows, 0:640] = parts[base]
        grad_in[rows, 640:1280] = parts[base + 1]
        grad_in[rows, 1280:1536] = parts[base + 2, :, :256]
        grad_out[rows, 0:384] = parts[base + 2, :, 256:]
        grad_out[rows, 384:512] = parts[base + 3, :, :128]
    for half in range(2):
        keep[half] = parts[half * 8 + core * 4 + 3, :, 128:384]
        send[half] = parts[half * 8 + (1 - core) * 4 + 3, :, 128:384]


def unpack(core, parts):
    table = jax.ShapeDtypeStruct((2, 8, 256), F32)
    return pl.pallas_call(
        unpack_kernel,
        out_shape=[
            jax.ShapeDtypeStruct((32, 3 * WIDTH), F32),
            jax.ShapeDtypeStruct((32, WIDTH), F32),
            table,
            table,
        ],
        in_specs=[scalar()] + whole(1),
        out_specs=whole(4),
        compiler_params=params(),
        name="unpack",
    )(core, parts)


def place_kernel(grad_out, own, left, below, corner, out):
    for ref, row0, col0 in ((own, 0, 3), (left, 0, 0), (below, 6, 3), (corner, 6, 0)):
        for level in range(2):
            for row in range(6):
                spot = level * 18 + row * 3
                here = (level, row0 + row, slice(col0, col0 + 3), slice(None))
                out[here] = grad_out[here] + ref[spot : spot + 3, :]


def place(grad_out, own, left, below, corner):
    return pl.pallas_call(
        place_kernel,
        out_shape=jax.ShapeDtypeStruct(grad_out.shape, F32),
        in_specs=whole(5),
        out_specs=pl.BlockSpec(memory_space=pltpu.VMEM),
        compiler_params=params(),
        name="place",
    )(grad_out, own, left, below, corner)


def body(fields, grad_out, region_ids, bias_index, bias_table, in_weight, out_weight):
    lat_count = lax.axis_size("lat")
    lon_count = lax.axis_size("lon")
    both = ("lat", "lon")
    lat = lax.axis_index("lat")
    core = lax.rem(lax.axis_index("lon"), 2).reshape(1)

    def moves(down, right):
        return [
            (i * lon_count + j, (i + down) % lat_count * lon_count + (j + right) % lon_count)
            for i in range(lat_count)
            for j in range(lon_count)
        ]

    swap = [(j, j ^ 1) for j in range(lon_count)]
    last = jnp.where(lat == lat_count - 1, 3, 0).reshape(1)
    own, left, below, corner = pack(last, fields, grad_out, region_ids)
    quad3 = lax.ppermute(left, both, moves(0, -1))
    quad0 = lax.ppermute(below, both, moves(1, 0))
    quad1 = lax.ppermute(corner, both, moves(1, -1))
    wide, narrow = ordered_index(bias_index)
    bias_wide, bias_narrow = lookup(wide, narrow, bias_table)
    (
        keep,
        send,
        keep_wide,
        send_wide,
        keep_narrow,
        send_narrow,
        grad0,
        grad1,
        grad2,
        grad3,
    ) = window(core, own, quad0, quad1, quad3, bias_wide, bias_narrow, in_weight, out_weight)
    came_wide = lax.ppermute(send_wide, "lon", swap)
    came_narrow = lax.ppermute(send_narrow, "lon", swap)
    came = lax.ppermute(send, "lon", swap)
    back_left = lax.ppermute(grad3, both, moves(0, 1))
    back_below = lax.ppermute(grad0, both, moves(-1, 0))
    back_corner = lax.ppermute(grad1, both, moves(-1, 1))
    table = scatter(wide, narrow, keep_wide, came_wide, keep_narrow, came_narrow)
    joined = join(keep, came, table)
    chips = [[j for j in range(lon_count) if j % 2 == bit] for bit in range(2)]
    parts = lax.all_to_all(joined, "lon", 0, 0, axis_index_groups=chips)
    parts = lax.all_to_all(fold_lon(parts), "lat", 0, 0)
    parts = lax.all_to_all(fold_lat(parts), "lat", 0, 0)
    grad_in_weight, grad_out_weight, table_keep, table_send = unpack(core, parts)
    table_came = lax.ppermute(table_send, "lon", swap)
    first = jnp.where(core[0] == 0, table_keep, table_came)
    second = jnp.where(core[0] == 0, table_came, table_keep)
    table = jnp.concatenate([first, second], axis=1)[:, :, :HALF_SECTOR]
    grad_bias = jnp.transpose(table, (0, 2, 1)).reshape(2 * HALF_SECTOR, HEADS)
    grad_fields = place(grad_out, grad2, back_left, back_below, back_corner)
    return grad_fields, grad_in_weight, grad_out_weight, grad_bias


def solution(mesh):
    tokens = P(None, "lat", "lon", None)
    in_specs = (tokens, tokens, P(None, "lat", "lon"), P(), P(), P(), P())
    out_specs = (tokens, P("lon", None), P("lon", None), P("lon", None))
    return jax.shard_map(body, mesh=mesh, in_specs=in_specs, out_specs=out_specs, check_vma=False)
```

profile of v0, /device:TPU:8, one launch (start us, length us, event | category | flops | bytes accessed | tf_op | source)
XLA Modules:
  0.0 207.8 jit_solution(314887856207724066)
XLA Ops:
  0.6 0.0 copy-start.6
  0.7 1.1 copy.26.grads.grad_out
  1.8 1.0 copy.23.fields
  2.8 0.8 copy.25.ids
  3.6 0.2 pack.1
  3.8 0.0 copy-start.3
  3.9 0.7 copy-done.3
  4.5 1.8 collective-permute-start
  6.3 3.8 %collective-permute-start.1 = (f32[80,512]{1,0:T(8,128)S(1)}, f32[80,512]{1,0:T(8,128)S(1)}, u32[]{:S(2)}, u32[]{:S(2)}) collective-permute-start(f32[80,512]{1,0:T(8,128)S(1)} %get-tuple-element.28), channel_id=1, source_target_pairs={{0,31},{1,16},{2,17},{3,18},{4,19},{5,20},{6,21},{7,22},{8,23},{9,... | collective-permute-start | bytes 491528 | tf_op jit(solution)/shard_map/ppermute | solution.py:546
  10.1 2.0 collective-permute-start.2
  12.1 0.3 order.2
  12.4 0.1 reshape.34.narrow
  12.6 0.1 reshape.35.table
  12.7 79.1 %lookup.1 = (f32[16,144,128]{2,1,0:T(8,128)S(1)}, f32[16,24,128]{2,1,0:T(8,128)S(1)}) custom-call(s32[144,128]{1,0:T(8,128)S(1)} %get-tuple-element.30.wide, s32[24,128]{1,0:T(8,128)S(1)} %pad.8.narrow, f32[16,50,128]{2,1,0:T(8,128)S(1)} %reshape.35.table), custom_call_target="tpu_custom_call" | custom-call | tf_op jit(solution)/shard_map/lookup/pallas_call | solution.py:167
  91.8 1.1 copy-done.1
  92.9 1.5 reshape.36.bias_narrow
  94.3 0.0 collective-permute-done.1.quad1
  94.4 0.6 copy-done.8
  95.0 0.0 copy-done.9
  95.0 0.1 copy-done.10
  95.1 17.0 %window.1 = (f32[256,2048]{1,0:T(8,128)}, f32[256,2048]{1,0:T(8,128)}, f32[144,8,128]{2,1,0:T(8,128)}, f32[144,8,128]{2,1,0:T(8,128)}, f32[8,144,16]{2,1,0:T(8,1...) custom-call(s32[1]{0:T(128)} %bitcast.core_ref, ...), custom_call_target="tpu_custom_call" | custom-call | tf_op jit(solution)/shard_map/window/pallas_call | solution.py:308
  112.1 0.1 collective-permute-start.6
  112.2 0.5 collective-permute-start.7
  112.7 1.5 copy.27
  114.2 0.4 collective-permute-start.8
  114.6 1.3 reshape.37.keep_narrow
  115.9 0.8 collective-permute-done.8
  116.7 1.1 copy.28
  117.8 1.3 reshape.38.came_narrow
  119.1 0.0 collective-permute-done.7.came_wide
  119.1 11.4 %scatter.1.table = f32[8,32,256]{2,1,0:T(8,128)S(1)} custom-call(s32[144,128]{1,0:T(8,128)S(1)} %get-tuple-element.30.wide, s32[18,128]{1,0:T(8,128)S(1)} %reshape.34.narrow, f32[144,8,128]{2,1,0:T(8,128)S(1)} %copy-done.2, f32[144,8,128]{2,1,0:T(8,128)} %collective-permute-done.7.came_wide, f32[8,18,128]{2,1,0:T(8,128)S(1)} %reshape.37.keep_narrow, ...), custom_call_target="tpu_custom_call" | custom-call | tf_op jit(solution)/shard_map/scatter/pallas_call | solution.py:393
  130.5 0.0 collective-permute-done.6.came
  130.5 3.2 %join.1 = f32[8,32,2304]{2,1,0:T(8,128)} custom-call(f32[256,2048]{1,0:T(8,128)S(1)} %copy-done, f32[256,2048]{1,0:T(8,128)} %collective-permute-done.6.came, f32[8,32,256]{2,1,0:T(8,128)S(1)} %scatter.1.table), custom_call_target="tpu_custom_call" | custom-call | tf_op jit(solution)/shard_map/join/pallas_call | solution.py:418
  133.7 35.0 %all_to_all.15.parts = f32[8,32,2304]{2,1,0:T(8,128)S(1)} all-to-all(f32[8,32,2304]{2,1,0:T(8,128)} %join.1), channel_id=1, replica_groups={{0,2,4,6,8,10,12,14},{1,3,5,7,9,11,13,15},{16,18,20,22,24,26,28,30},{17..., dimensions={0} | all-to-all | bytes 4718592 | tf_op jit(solution)/shard_map/all_to_all | solution.py:570
  168.8 0.1 fold_lon.1
  168.9 20.2 %all_to_all.16.parts = f32[16,8,640]{2,1,0:T(8,128)S(1)} all-to-all(f32[16,8,640]{2,1,0:T(8,128)S(1)} %fold_lon.1), channel_id=1, replica_groups=mesh['lat'=16,'lon'=16] {'lat'}, dimensions={0} | all-to-all | bytes 655360 | tf_op jit(solution)/shard_map/all_to_all | solution.py:571
  189.1 0.7 fold_lat.1
  189.8 4.9 %all-to-all-start.2 = ((f32[16,8,640]{2,1,0:T(8,128)}), f32[16,8,640]{2,1,0:T(8,128)S(1)}, u32[]{:S(2)}, u32[]{:S(2)}) async-start(f32[16,8,640]{2,1,0:T(8,128)} %fold_lat.1), calls=%async_computation.2 | async-start | bytes 655360 | tf_op jit(solution)/shard_map/all_to_all | solution.py:572
  194.8 0.1 collective-permute-start.3
  194.9 0.3 collective-permute-start.4
  195.2 4.7 %collective-permute-start.5 = (f32[36,512]{1,0:T(8,128)S(1)}, f32[36,512]{1,0:T(8,128)S(1)}, u32[]{:S(2)}, u32[]{:S(2)}) collective-permute-start(f32[36,512]{1,0:T(8,128)S(1)} %copy-done.11), channel_id=1, source_target_pairs={{0,241},{1,242},{2,243},{3,244},{4,245},{5,246},{6,247},{7,248},{8... | collective-permute-start | bytes 221192 | tf_op jit(solution)/shard_map/ppermute | solution.py:566
  199.9 5.1 %all-to-all-done.2.parts = f32[16,8,640]{2,1,0:T(8,128)S(1)} async-done(((f32[16,8,640]{2,1,0:T(8,128)}), f32[16,8,640]{2,1,0:T(8,128)S(1)}, u32[]{:S(2)}, u32[]{:S(2)}) %all-to-all-start.2) | async-done | bytes 327712 | tf_op jit(solution)/shard_map/all_to_all | solution.py:572
  205.0 0.7 unpack.1
  205.7 0.0 collective-permute-done.4.below
  205.7 0.2 collective-permute-done.5.corner
  205.9 0.1 place.1
  206.1 0.9 copy.30
  207.1 0.7 reshape.39
  (31 shorter events, 0.1 us)
Async XLA Ops:
  0.6 11.5 %copy-start.6 = (bf16[144,144]{1,0:T(8,128)(2,1)S(1)}, bf16[144,144]{1,0:T(8,128)(2,1)}, u32[]{:S(2)}) copy-start(bf16[144,144]{1,0:T(8,128)(2,1)} %constant.21.clone.order) | copy-start | bytes 124420
  0.6 11.5 %copy-start.4 = (s32[144,144]{1,0:T(8,128)S(1)}, s32[144,144]{1,0:T(8,128)}, u32[]{:S(2)}) copy-start(s32[144,144]{1,0:T(8,128)} %index.1) | copy-start | bytes 248836
  0.7 11.9 %copy-start.7 = (f32[6336,16]{0,1:T(8,128)S(1)}, f32[6336,16]{0,1:T(8,128)}, u32[]{:S(2)}) copy-start(f32[6336,16]{0,1:T(8,128)} %param.12) | copy-start | bytes 1216516
  3.8 0.7 copy-start.3
  4.5 89.8 %collective-permute-start = (f32[80,512]{1,0:T(8,128)S(1)}, f32[80,512]{1,0:T(8,128)S(1)}, u32[]{:S(2)}, u32[]{:S(2)}) collective-permute-start(f32[80,512]{1,0:T(8,128)S(1)} %get-tuple-element.27), channel_id=1, source_target_pairs={{0,16},{1,17},{2,18},{3,19},{4,20},{5,21},{6,22},{7,23},{8,24},{9,... | collective-permute-start | bytes 491528 | tf_op jit(solution)/shard_map/ppermute | solution.py:545
  6.3 88.0 %collective-permute-start.1 = (f32[80,512]{1,0:T(8,128)S(1)}, f32[80,512]{1,0:T(8,128)S(1)}, u32[]{:S(2)}, u32[]{:S(2)}) collective-permute-start(f32[80,512]{1,0:T(8,128)S(1)} %get-tuple-element.28), channel_id=1, source_target_pairs={{0,31},{1,16},{2,17},{3,18},{4,19},{5,20},{6,21},{7,22},{8,23},{9,... | collective-permute-start | bytes 491528 | tf_op jit(solution)/shard_map/ppermute | solution.py:546
  10.1 84.3 %collective-permute-start.2 = (f32[80,512]{1,0:T(8,128)S(1)}, f32[80,512]{1,0:T(8,128)S(1)}, u32[]{:S(2)}, u32[]{:S(2)}) collective-permute-start(f32[80,512]{1,0:T(8,128)S(1)} %get-tuple-element.29), channel_id=1, source_target_pairs={{0,15},{1,0},{2,1},{3,2},{4,3},{5,4},{6,5},{7,6},{8,7},{9,8},{10,9... | collective-permute-start | bytes 491528 | tf_op jit(solution)/shard_map/ppermute | solution.py:544
  91.8 1.1 copy-start.1
  94.3 0.7 copy-start.8
  94.3 0.7 copy-start.9
  94.4 0.7 copy-start.10
  112.1 7.0 %copy-start.2 = (f32[144,8,128]{2,1,0:T(8,128)S(1)}, f32[144,8,128]{2,1,0:T(8,128)}, u32[]{:S(2)}) copy-start(f32[144,8,128]{2,1,0:T(8,128)} %get-tuple-element.40.keep_wide) | copy-start | bytes 1769476
  112.1 18.4 %collective-permute-start.6 = (f32[256,2048]{1,0:T(8,128)}, f32[256,2048]{1,0:T(8,128)}, u32[]{:S(2)}, u32[]{:S(2)}) collective-permute-start(f32[256,2048]{1,0:T(8,128)} %get-tuple-element.39), channel_id=1, source_target_pairs={{0,1},{1,0},{2,3},{3,2},{4,5},{5,4},{6,7},{7,6},{8,9},{9,8},{10,11... | collective-permute-start | bytes 6291464 | tf_op jit(solution)/shard_map/ppermute | solution.py:563
  112.2 6.9 %collective-permute-start.7 = (f32[144,8,128]{2,1,0:T(8,128)}, f32[144,8,128]{2,1,0:T(8,128)}, u32[]{:S(2)}, u32[]{:S(2)}) collective-permute-start(f32[144,8,128]{2,1,0:T(8,128)} %get-tuple-element.41), channel_id=1, source_target_pairs={{0,1},{1,0},{2,3},{3,2},{4,5},{5,4},{6,7},{7,6},{8,9},{9,8},{10,11... | collective-permute-start | bytes 1769480 | tf_op jit(solution)/shard_map/ppermute | solution.py:561
  112.7 17.8 %copy-start = (f32[256,2048]{1,0:T(8,128)S(1)}, f32[256,2048]{1,0:T(8,128)}, u32[]{:S(2)}) copy-start(f32[256,2048]{1,0:T(8,128)} %get-tuple-element.38.keep) | copy-start | bytes 6291460
  114.2 2.5 %collective-permute-start.8 = (f32[8,144,16]{1,2,0:T(8,128)S(1)}, f32[8,144,16]{1,2,0:T(8,128)S(1)}, u32[]{:S(2)}, u32[]{:S(2)}) collective-permute-start(f32[8,144,16]{1,2,0:T(8,128)S(1)} %copy.27), channel_id=1, source_target_pairs={{0,1},{1,0},{2,3},{3,2},{4,5},{5,4},{6,7},{7,6},{8,9},{9,8},{10,11... | collective-permute-start | bytes 221192 | tf_op jit(solution)/shard_map/ppermute | solution.py:562
  168.8 26.0 %copy-start.13 = (f32[36,512]{1,0:T(8,128)S(1)}, f32[36,512]{1,0:T(8,128)}, u32[]{:S(2)}) copy-start(f32[36,512]{1,0:T(8,128)} %get-tuple-element.35) | copy-start | bytes 221188
  168.8 26.1 %copy-start.12 = (f32[36,512]{1,0:T(8,128)S(1)}, f32[36,512]{1,0:T(8,128)}, u32[]{:S(2)}) copy-start(f32[36,512]{1,0:T(8,128)} %get-tuple-element.36) | copy-start | bytes 221188
  168.8 26.4 %copy-start.11 = (f32[36,512]{1,0:T(8,128)S(1)}, f32[36,512]{1,0:T(8,128)}, u32[]{:S(2)}) copy-start(f32[36,512]{1,0:T(8,128)} %get-tuple-element.37) | copy-start | bytes 221188
  168.8 37.1 %copy-start.5 = (f32[36,512]{1,0:T(8,128)S(1)}, f32[36,512]{1,0:T(8,128)}, u32[]{:S(2)}) copy-start(f32[36,512]{1,0:T(8,128)} %get-tuple-element.34.own) | copy-start | bytes 221188
  189.8 15.2 %all-to-all-start.2 = ((f32[16,8,640]{2,1,0:T(8,128)}), f32[16,8,640]{2,1,0:T(8,128)S(1)}, u32[]{:S(2)}, u32[]{:S(2)}) async-start(f32[16,8,640]{2,1,0:T(8,128)} %fold_lat.1), calls=%async_computation.2 | async-start | bytes 655360 | tf_op jit(solution)/shard_map/all_to_all | solution.py:572
  194.8 10.9 %collective-permute-start.3 = (f32[36,512]{1,0:T(8,128)S(1)}, f32[36,512]{1,0:T(8,128)S(1)}, u32[]{:S(2)}, u32[]{:S(2)}) collective-permute-start(f32[36,512]{1,0:T(8,128)S(1)} %copy-done.13), channel_id=1, source_target_pairs={{0,1},{1,2},{2,3},{3,4},{4,5},{5,6},{6,7},{7,8},{8,9},{9,10},{10,1... | collective-permute-start | bytes 221192 | tf_op jit(solution)/shard_map/ppermute | solution.py:564
  194.9 10.8 %collective-permute-start.4 = (f32[36,512]{1,0:T(8,128)S(1)}, f32[36,512]{1,0:T(8,128)S(1)}, u32[]{:S(2)}, u32[]{:S(2)}) collective-permute-start(f32[36,512]{1,0:T(8,128)S(1)} %copy-done.12), channel_id=1, source_target_pairs={{0,240},{1,241},{2,242},{3,243},{4,244},{5,245},{6,246},{7,247},{8... | collective-permute-start | bytes 221192 | tf_op jit(solution)/shard_map/ppermute | solution.py:565
  195.2 10.7 %collective-permute-start.5 = (f32[36,512]{1,0:T(8,128)S(1)}, f32[36,512]{1,0:T(8,128)S(1)}, u32[]{:S(2)}, u32[]{:S(2)}) collective-permute-start(f32[36,512]{1,0:T(8,128)S(1)} %copy-done.11), channel_id=1, source_target_pairs={{0,241},{1,242},{2,243},{3,244},{4,245},{5,246},{6,247},{7,248},{8... | collective-permute-start | bytes 221192 | tf_op jit(solution)/shard_map/ppermute | solution.py:566
  205.7 1.3 collective-permute-start.9
where the time goes:
time: 211 us; the launch traced here: 208 us
  Pallas kernels  113 us (54%)
  blocking collectives  55.2 us (26%)
  starting transfers between devices  18.6 us (9%)
  local copies, waits for them, and re-layouts  13.9 us (7%)
  waiting for transfers between devices  6.16 us (3%)
    pallas_call x1, Pallas kernels, lookup(): pl.pallas_call(lookup_kernel, out_shape=[jax.ShapeDtypeStruct((HEADS, TOK...  79.1 us
    all_to_all x1, blocking collectives, body(): parts = lax.all_to_all(joined, 'lon', 0, 0, axis_index_groups=chips)  35 us
    all_to_all x1, blocking collectives, body(): parts = lax.all_to_all(fold_lon(parts), 'lat', 0, 0)  20.2 us
    pallas_call x1, Pallas kernels, window(): pl.pallas_call(main_kernel, out_shape=[shape(256, 4 * WIDTH), shape(256,...  17 us
    pallas_call x1, Pallas kernels, scatter(): pl.pallas_call(scatter_kernel, out_shape=jax.ShapeDtypeStruct((8, 32, 256...  11.4 us
    unnamed x32, local copies, waits for them, and re-layouts  6.37 us
    all_to_all x1, waiting for transfers between devices, body(): parts = lax.all_to_all(fold_lat(parts), 'lat', 0, 0)  5.11 us
    all_to_all x1, starting transfers between devices, body(): parts = lax.all_to_all(fold_lat(parts), 'lat', 0, 0)  4.94 us
  transfers between devices with their start and end apart: 11, of which 3 were waited for; matrix products, arithmetic and copies ran while one was open for 4% of the time, Pallas kernels for 44%

commit v1 on v0

v1 whole, which is shorter than its diff:
```python
import functools

import jax
import jax.numpy as jnp
import numpy as np
from jax import lax
from jax.experimental import pallas as pl
from jax.experimental.pallas import tpu as pltpu
from jax.sharding import Mesh
from jax.sharding import PartitionSpec as P

WIDTH = 512
HEADS = 16
HEAD_DIM = 32
TOKENS = 144
QUAD = 36
BIAS_ROWS = 6336
HALF_SECTOR = 198
BLOCKS = 25
FACTOR = HEAD_DIM ** (-0.5)
F32 = jnp.float32
BF16 = jnp.bfloat16
MEGA = 1 << 20


def params(mib=16):
    return pltpu.CompilerParams(vmem_limit_bytes=mib * MEGA)


def whole(count):
    return [pl.BlockSpec(memory_space=pltpu.VMEM)] * count


def scalar():
    return pl.BlockSpec(memory_space=pltpu.SMEM)


def halves(x):
    high = x.astype(BF16)
    low = (x - high.astype(F32)).astype(BF16)
    return high, low


def dot(a, b, dims):
    return lax.dot_general(a, b, (dims, ((), ())), preferred_element_type=F32)


NN = ((1,), (0,))
NT = ((1,), (1,))
TN = ((0,), (0,))


def dot3(a, b, dims):
    ah, al = a
    bh, bl = b
    return dot(ah, bh, dims) + (dot(ah, bl, dims) + dot(al, bh, dims))


def token_order():
    grid = np.arange(TOKENS).reshape(2, 2, 6, 2, 3)
    return np.transpose(grid, (1, 3, 2, 4, 0)).reshape(-1)


def pack_kernel(last, fields, grads, ids, own, left, below, corner):
    lanes = lax.broadcasted_iota(jnp.int32, (2, WIDTH), 1)
    level = lax.broadcasted_iota(jnp.int32, (2, WIDTH), 0)
    bump = last[0]
    plan = (
        (own, 0, 3, 2, None),
        (left, 0, 0, 3, None),
        (below, 6, 3, 0, bump),
        (corner, 6, 0, 1, bump),
    )
    for ref, row0, col0, quadrant, offset in plan:
        label = jnp.zeros((2, WIDTH), jnp.int32)
        for row in range(6):
            for col in range(3):
                spot = row * 6 + col * 2
                ref[spot : spot + 2, :] = fields[row0 + row, col0 + col]
                ref[QUAD + spot : QUAD + spot + 2, :] = grads[row0 + row, col0 + col]
                value = ids[col0 + col, :, row0 + row : row0 + row + 1] + 1
                if offset is not None:
                    value = value + offset
                place = quadrant * QUAD + spot
                label = jnp.where(
                    lanes == level + place, jnp.broadcast_to(value, (2, WIDTH)), label
                )
        total = jnp.sum(label.astype(F32), axis=0, keepdims=True)
        ref[72:80, :] = jnp.broadcast_to(total, (8, WIDTH))


def pack(last, fields, grads, ids):
    shape = jax.ShapeDtypeStruct((80, WIDTH), F32)
    return pl.pallas_call(
        pack_kernel,
        out_shape=[shape] * 4,
        in_specs=[scalar()] + whole(3),
        out_specs=whole(4),
        compiler_params=params(),
        name="pack",
    )(last, fields, grads, ids)


def one_hot(row, lines):
    low = (row & 255).astype(F32).astype(BF16)
    hit = lines == jnp.broadcast_to(low, (256, 128))
    return jnp.where(hit, jnp.ones((256, 128), BF16), jnp.zeros((256, 128), BF16))


def line_numbers():
    return lax.broadcasted_iota(jnp.int32, (256, 128), 0).astype(F32).astype(BF16)


def lookup_kernel(core_ref, index, order, table, bias, wide, narrow, left):
    value = index[...]
    high = (value >> 7).astype(F32).astype(BF16)
    low = (value & 127).astype(F32).astype(BF16)
    move = order[...]

    def moved(part):
        return dot(dot(move, part, NN).astype(BF16), move, NT)

    result = moved(high) * 128.0 + moved(low)
    wide[...] = result[:, :128].astype(jnp.int32)
    tail = jnp.concatenate([result[:, 128:], jnp.zeros((TOKENS, 112), F32)], axis=1)
    for i in range(18):
        spread = pltpu.roll(tail[8 * i : 8 * i + 8, :], 0, 1, stride=16, stride_axis=0)
        narrow[i : i + 1, :] = jnp.sum(spread, axis=0, keepdims=True).astype(jnp.int32)

    first = core_ref[0] == 0
    for block in range(BLOCKS):
        count = min(256, BIAS_ROWS - block * 256)
        top = table[0:8, block * 256 : block * 256 + count]
        bottom = table[8:16, block * 256 : block * 256 + count]
        part = jnp.concatenate(
            [jnp.where(first, bottom, top), jnp.where(first, top, bottom)], axis=0
        )
        if count < 256:
            part = jnp.concatenate([part, jnp.zeros((16, 256 - count), F32)], axis=1)
        left[block * 32 : block * 32 + 16, :], left[block * 32 + 16 : block * 32 + 32, :] = halves(
            part
        )
    lines = line_numbers()
    matrix = left[...]

    def find(rows):
        right = jnp.concatenate([one_hot(row, lines) for row in rows], axis=1)
        found = dot(matrix, right, NN)
        block = jnp.concatenate([row >> 8 for row in rows], axis=1)
        block = jnp.broadcast_to(block, (32, 256))
        total = jnp.zeros((32, 256), F32)
        for b in range(BLOCKS):
            total = jnp.where(block == b, found[b * 32 : b * 32 + 32], total)
        return total[:16] + total[16:]

    def step(i, carry):
        base = pl.multiple_of(i * 8, 8)
        rows = wide[pl.ds(base, 8), :]
        for pair in range(4):
            found = find([rows[2 * pair + j : 2 * pair + j + 1, :] for j in range(2)])
            for j in range(2):
                bias[base + 2 * pair + j, :, 0:128] = found[:, j * 128 : j * 128 + 128]
        return carry

    lax.fori_loop(0, 18, step, 0)
    for pair in range(9):
        found = find([narrow[2 * pair + j : 2 * pair + j + 1, :] for j in range(2)])
        for j in range(16):
            bias[16 * pair + j, :, 128:144] = found[:, 16 * j : 16 * j + 16]


def lookup(core, bias_index, bias_table):
    order = np.zeros((TOKENS, TOKENS), np.float32)
    order[np.arange(TOKENS), token_order()] = 1.0
    return pl.pallas_call(
        lookup_kernel,
        out_shape=[
            jax.ShapeDtypeStruct((TOKENS, HEADS, TOKENS), F32),
            jax.ShapeDtypeStruct((TOKENS, 128), jnp.int32),
            jax.ShapeDtypeStruct((18, 128), jnp.int32),
        ],
        in_specs=[scalar()] + whole(3),
        out_specs=whole(3),
        scratch_shapes=[pltpu.VMEM((BLOCKS * 32, 256), BF16)],
        compiler_params=params(),
        name="lookup",
    )(core, bias_index, jnp.asarray(order, BF16), bias_table.T)


def main_kernel(
    core_ref,
    own,
    quad0,
    quad1,
    quad3,
    bias,
    in_weight,
    out_weight,
    keep,
    send,
    keep_wide,
    send_wide,
    keep_narrow,
    send_narrow,
    grad0,
    grad1,
    grad2,
    grad3,
    tokens,
    cotangent,
    proj,
    gatt,
    gproj,
    att,
    normed_t,
    tails,
):
    core = core_ref[0]
    for slot, quad in enumerate((quad0, quad1, own, quad3)):
        at = slot * QUAD
        tokens[at : at + QUAD, :] = quad[0:QUAD, :]
        cotangent[at : at + QUAD, :] = quad[QUAD : 2 * QUAD, :]
    row = (quad0[72:73, :] + quad1[72:73, :] + own[72:73, :] + quad3[72:73, :])[:, :TOKENS]
    side = lax.broadcasted_iota(jnp.int32, (TOKENS, TOKENS), 0)
    along = lax.broadcasted_iota(jnp.int32, (TOKENS, TOKENS), 1)
    spread = jnp.broadcast_to(row, (TOKENS, TOKENS))
    column = jnp.sum(jnp.where(side == along, spread, 0.0), axis=1, keepdims=True)
    allowed = column == spread

    inputs = tokens[...]
    centered = inputs - jnp.mean(inputs, axis=1, keepdims=True)
    variance = jnp.mean(centered * centered, axis=1, keepdims=True)
    inv_std = lax.rsqrt(variance + 1e-05)
    normed = centered * inv_std
    tokens[...] = normed
    normed_t[...] = normed.T
    halves_normed = halves(normed)
    for part in range(3):
        at = part * WIDTH
        weight = halves(in_weight[:, at : at + WIDTH])
        proj[at : at + WIDTH, :] = dot3(halves_normed, weight, NN).T
    halves_cotangent = halves(cotangent[...])
    gatt[...] = dot3(halves(out_weight[...]), halves_cotangent, NT)

    def one_head(head, slot):
        at = pl.multiple_of(head * HEAD_DIM, HEAD_DIM)
        qh, ql = halves(proj[pl.ds(at, HEAD_DIM), :] * FACTOR)
        kh, kl = halves(proj[pl.ds(at + WIDTH, HEAD_DIM), :])
        vh, vl = halves(proj[pl.ds(at + 2 * WIDTH, HEAD_DIM), :])
        gh, gl = halves(gatt[pl.ds(at, HEAD_DIM), :])

        def stacked(*parts):
            return jnp.concatenate(parts, axis=0)

        scores = dot(stacked(qh, qh, ql), stacked(kh, kl, kh), TN) + bias[:, slot, :]
        scores = jnp.where(allowed, scores, -1000000000.0)
        peak = jnp.max(scores, axis=1, keepdims=True)
        exponent = jnp.exp(scores - peak)
        probs = exponent * (1.0 / jnp.sum(exponent, axis=1, keepdims=True))
        grad_probs = dot(stacked(gh, gh, gl), stacked(vh, vl, vh), TN)
        inner = jnp.sum(grad_probs * probs, axis=1, keepdims=True)
        grad_scores = probs * (grad_probs - inner)
        ph, plow = halves(probs)
        sh, sl = halves(grad_scores)

        def product(high, low, right_high, right_low, dims):
            both = dot(stacked(high, low), right_high, dims)
            return both[:HEAD_DIM] + (both[HEAD_DIM:] + dot(high, right_low, dims))

        att[pl.ds(at, HEAD_DIM), :] = product(vh, vl, ph, plow, NT)
        gproj[pl.ds(at + 2 * WIDTH, HEAD_DIM), :] = product(gh, gl, ph, plow, NN)
        gproj[pl.ds(at, HEAD_DIM), :] = product(kh, kl, sh, sl, NT) * FACTOR
        gproj[pl.ds(at + WIDTH, HEAD_DIM), :] = product(qh, ql, sh, sl, NN)
        return grad_scores

    tails[...] = jnp.zeros_like(tails)
    for slot in range(8):
        grad_scores = one_head((1 - core) * 8 + slot, slot)
        send_wide[:, slot, :] = grad_scores[:, :128]
        tails[:, slot, 0:16] = grad_scores[:, 128:]
        grad_scores = one_head(core * 8 + slot, 8 + slot)
        keep_wide[:, slot, :] = grad_scores[:, :128]
        tails[:, 8 + slot, 0:16] = grad_scores[:, 128:]
    for i in range(18):
        total = tails[8 * i]
        for j in range(1, 8):
            total = total + pltpu.roll(tails[8 * i + j], 16 * j, 1)
        send_narrow[i] = total[0:8]
        keep_narrow[i] = total[8:16]

    for target, bit in ((send, 1 - core), (keep, core)):
        rows = [pl.ds(pl.multiple_of(64 * i + 32 * bit, 32), 32) for i in range(8)]
        left = halves(jnp.concatenate([normed_t[r, :] for r in rows], axis=0))
        for part in range(3):
            at = part * WIDTH
            target[:, at : at + WIDTH] = dot3(left, halves(gproj[at : at + WIDTH, :]), NT)
        left = halves(jnp.concatenate([att[r, :] for r in rows], axis=0))
        target[:, 3 * WIDTH :] = dot3(left, halves_cotangent, NN)

    grad_normed = jnp.zeros((WIDTH, TOKENS), F32)
    for part in range(3):
        at = part * WIDTH
        grad_normed = grad_normed + dot3(
            halves(in_weight[:, at : at + WIDTH]), halves(gproj[at : at + WIDTH, :]), NN
        )
    grad_normed = grad_normed.T
    normed = tokens[...]
    result = inv_std * (
        grad_normed
        - jnp.mean(grad_normed, axis=1, keepdims=True)
        - normed * jnp.mean(grad_normed * normed, axis=1, keepdims=True)
    )
    tokens[...] = result
    for slot, target in enumerate((grad0, grad1, grad2, grad3)):
        target[...] = tokens[slot * QUAD : slot * QUAD + QUAD, :]


def window(core, own, quad0, quad1, quad3, bias, in_weight, out_weight):
    def shape(*dims):
        return jax.ShapeDtypeStruct(dims, F32)

    grad = shape(QUAD, WIDTH)
    return pl.pallas_call(
        main_kernel,
        out_shape=[
            shape(256, 4 * WIDTH),
            shape(256, 4 * WIDTH),
            shape(TOKENS, 8, 128),
            shape(TOKENS, 8, 128),
            shape(18, 8, 128),
            shape(18, 8, 128),
            grad,
            grad,
            grad,
            grad,
        ],
        in_specs=[scalar()] + whole(7),
        out_specs=whole(10),
        scratch_shapes=[
            pltpu.VMEM((TOKENS, WIDTH), F32),
            pltpu.VMEM((TOKENS, WIDTH), F32),
            pltpu.VMEM((3 * WIDTH, TOKENS), F32),
            pltpu.VMEM((WIDTH, TOKENS), F32),
            pltpu.VMEM((3 * WIDTH, TOKENS), F32),
            pltpu.VMEM((WIDTH, TOKENS), F32),
            pltpu.VMEM((WIDTH, TOKENS), F32),
            pltpu.VMEM((TOKENS, HEADS, 128), F32),
        ],
        compiler_params=params(26),
        name="window",
    )(core, own, quad0, quad1, quad3, bias, in_weight, out_weight)


def scatter_kernel(
    wide, narrow, keep_wide, came_wide, keep_narrow, came_narrow, out, total, line
):
    total[...] = jnp.zeros_like(total)
    lines = line_numbers()

    def sides(row, values):
        block = (row >> 8).astype(F32).astype(BF16)
        both = jnp.concatenate(halves(values), axis=0)
        spread = jnp.broadcast_to(block, (16, 128))
        left = jnp.concatenate(
            [jnp.where(spread == float(b), both, jnp.zeros_like(both)) for b in range(BLOCKS)],
            axis=0,
        )
        return left, one_hot(row, lines)

    def add(pieces):
        left = jnp.concatenate([p[0] for p in pieces], axis=1)
        right = jnp.concatenate([p[1] for p in pieces], axis=1)
        total[...] += dot(left, right, NT)

    def step(i, carry):
        base = pl.multiple_of(i * 8, 8)
        rows = wide[pl.ds(base, 8), :]
        for pair in range(4):
            add(
                [
                    sides(rows[j : j + 1, :], keep_wide[base + j] + came_wide[base + j])
                    for j in (2 * pair, 2 * pair + 1)
                ]
            )
        return carry

    lax.fori_loop(0, 18, step, 0)
    for pair in range(9):
        add(
            [
                sides(narrow[j : j + 1, :], keep_narrow[j] + came_narrow[j])
                for j in (2 * pair, 2 * pair + 1)
            ]
        )
    for b in range(BLOCKS):
        line[:, b * 256 : b * 256 + 256] = (
            total[b * 16 : b * 16 + 8, :] + total[b * 16 + 8 : b * 16 + 16, :]
        )
    line[:, BLOCKS * 256 :] = jnp.zeros((8, 256), F32)
    for m in range(32):
        chip, core, half = m // 4, m // 2 % 2, m % 2
        start = m * HALF_SECTOR
        base, shift = start // 128 * 128, start % 128
        piece = line[:, base : base + 512]
        if shift:
            piece = pltpu.roll(piece, 512 - shift, 1)
        out[chip, half * 16 + core * 8 : half * 16 + core * 8 + 8, :] = piece[:, :256]


def scatter(wide, narrow, keep_wide, came_wide, keep_narrow, came_narrow):
    return pl.pallas_call(
        scatter_kernel,
        out_shape=jax.ShapeDtypeStruct((8, 32, 256), F32),
        in_specs=whole(6),
        out_specs=pl.BlockSpec(memory_space=pltpu.VMEM),
        scratch_shapes=[
            pltpu.VMEM((BLOCKS * 16, 256), F32),
            pltpu.VMEM((8, BLOCKS * 256 + 256), F32),
        ],
        compiler_params=params(),
        name="scatter",
    )(wide, narrow, keep_wide, came_wide, keep_narrow, came_narrow)


def join_kernel(keep, came, table, out):
    out[0, :, : 4 * WIDTH] = keep[...] + came[...]
    out[0, :, 4 * WIDTH :] = table[0]


def join(keep, came, table):
    block = pl.BlockSpec((32, 4 * WIDTH), lambda i: (i, 0))
    return pl.pallas_call(
        join_kernel,
        out_shape=jax.ShapeDtypeStruct((8, 32, 2304), F32),
        grid=(8,),
        in_specs=[block, block, pl.BlockSpec((1, 32, 256), lambda i: (i, 0, 0))],
        out_specs=pl.BlockSpec((1, 32, 2304), lambda i: (i, 0, 0)),
        compiler_params=params(),
        name="join",
    )(keep, came, table)


def fold_lon_kernel(parts, out):
    def rows(at):
        total = parts[0, at : at + 8, :]
        for i in range(1, 8):
            total = total + parts[i, at : at + 8, :]
        return total

    for group in range(4):
        total = rows(group * 8)
        for col in range(4):
            if col < 3:
                out[group * 4 + col] = total[:, col * 640 : col * 640 + 640]
            else:
                out[group * 4 + col, :, :384] = total[:, 1920:2304]
                out[group * 4 + col, :, 384:] = jnp.zeros((8, 256), F32)


def fold_lon(parts):
    return pl.pallas_call(
        fold_lon_kernel,
        out_shape=jax.ShapeDtypeStruct((16, 8, 640), F32),
        in_specs=whole(1),
        out_specs=pl.BlockSpec(memory_space=pltpu.VMEM),
        compiler_params=params(),
        name="fold_lon",
    )(parts)


def fold_lat_kernel(parts, out):
    total = parts[0]
    for i in range(1, 16):
        total = total + parts[i]
    for i in range(32):
        out[i] = total


def fold_lat(parts):
    return pl.pallas_call(
        fold_lat_kernel,
        out_shape=jax.ShapeDtypeStruct((32, 8, 640), F32),
        in_specs=whole(1),
        out_specs=pl.BlockSpec(memory_space=pltpu.VMEM),
        compiler_params=params(),
        name="fold_lat",
    )(parts)


def unpack_kernel(core_ref, parts, grad_in, grad_out, grad_bias):
    core = core_ref[0]
    for group in range(4):
        rows = slice(group * 8, group * 8 + 8)
        base = group * 8 + core
        grad_in[rows, 0:640] = parts[base]
        grad_in[rows, 640:1280] = parts[base + 2]
        grad_in[rows, 1280:1536] = parts[base + 4, :, :256]
        grad_out[rows, 0:384] = parts[base + 4, :, 256:]
        grad_out[rows, 384:512] = parts[base + 6, :, :128]
    for other in range(2):
        rows = slice(other * 8, other * 8 + 8)
        for half in range(2):
            piece = parts[(half * 2 + core) * 8 + 6 + other, :, 128:384]
            grad_bias[rows, half * HALF_SECTOR : half * HALF_SECTOR + HALF_SECTOR] = piece[
                :, :HALF_SECTOR
            ]


def unpack(core, parts):
    return pl.pallas_call(
        unpack_kernel,
        out_shape=[
            jax.ShapeDtypeStruct((32, 3 * WIDTH), F32),
            jax.ShapeDtypeStruct((32, WIDTH), F32),
            jax.ShapeDtypeStruct((HEADS, 2 * HALF_SECTOR), F32),
        ],
        in_specs=[scalar()] + whole(1),
        out_specs=whole(3),
        compiler_params=params(),
        name="unpack",
    )(core, parts)


def place_kernel(grad_out, own, left, below, corner, out):
    for ref, row0, col0 in ((own, 0, 3), (left, 0, 0), (below, 6, 3), (corner, 6, 0)):
        for row in range(6):
            for col in range(3):
                spot = row * 6 + col * 2
                out[row0 + row, col0 + col] = (
                    grad_out[row0 + row, col0 + col] + ref[spot : spot + 2, :]
                )


def place(grad_out, own, left, below, corner):
    return pl.pallas_call(
        place_kernel,
        out_shape=jax.ShapeDtypeStruct(grad_out.shape, F32),
        in_specs=whole(5),
        out_specs=pl.BlockSpec(memory_space=pltpu.VMEM),
        compiler_params=params(),
        name="place",
    )(grad_out, own, left, below, corner)


LAT = ("z", "y_lo")
LON = ("x", "y_hi", "core")


def body(fields, grad_out, region_ids, bias_index, bias_table, in_weight, out_weight):
    everything = LAT + LON
    lat = lax.axis_index(LAT)
    core = lax.axis_index("core").reshape(1)

    def moves(down, right):
        return [
            (i * 16 + j, (i + down) % 16 * 16 + (j + right) % 16)
            for i in range(16)
            for j in range(16)
        ]

    swap = [(0, 1), (1, 0)]
    last = jnp.where(lat == 15, 3, 0).reshape(1)
    grad_out = jnp.transpose(grad_out, (1, 2, 0, 3))
    own, left, below, corner = pack(
        last, jnp.transpose(fields, (1, 2, 0, 3)), grad_out, jnp.transpose(region_ids, (2, 0, 1))
    )
    quad3 = lax.ppermute(left, everything, moves(0, -1))
    quad0 = lax.ppermute(below, everything, moves(1, 0))
    quad1 = lax.ppermute(corner, everything, moves(1, -1))
    bias, wide, narrow = lookup(core, bias_index, bias_table)
    (
        keep,
        send,
        keep_wide,
        send_wide,
        keep_narrow,
        send_narrow,
        grad0,
        grad1,
        grad2,
        grad3,
    ) = window(core, own, quad0, quad1, quad3, bias, in_weight, out_weight)
    came_wide = lax.ppermute(send_wide, "core", swap)
    came_narrow = lax.ppermute(send_narrow, "core", swap)
    came = lax.ppermute(send, "core", swap)
    back_left = lax.ppermute(grad3, everything, moves(0, 1))
    back_below = lax.ppermute(grad0, everything, moves(-1, 0))
    back_corner = lax.ppermute(grad1, everything, moves(-1, 1))
    table = scatter(wide, narrow, keep_wide, came_wide, keep_narrow, came_narrow)
    grad_fields = place(grad_out, grad2, back_left, back_below, back_corner)
    joined = join(keep, came, table)
    joined, grad_fields = lax.optimization_barrier((joined, grad_fields))
    parts = lax.all_to_all(joined, ("x", "y_hi"), 0, 0)
    parts = lax.all_to_all(fold_lon(parts), LAT, 0, 0)
    parts = lax.all_to_all(fold_lat(parts), LAT + ("core",), 0, 0)
    grad_in_weight, grad_out_weight, grad_bias = unpack(core, parts)
    return jnp.transpose(grad_fields, (2, 0, 1, 3)), grad_in_weight, grad_out_weight, grad_bias.T


def solution(mesh):
    split = Mesh(mesh.devices.reshape(8, 2, 4, 2, 2), LAT + LON)
    tokens = P(None, LAT, LON, None)
    in_specs = (tokens, tokens, P(None, LAT, LON), P(), P(), P(), P())
    out_specs = (tokens, P(LON, None), P(LON, None), P(LON, None))
    return jax.shard_map(body, mesh=split, in_specs=in_specs, out_specs=out_specs, check_vma=False)
```

time: 211 us -> 146 us (0.69); the launches traced: 208 us -> 145 us
  Pallas kernels: 113 us -> 37.8 us
  blocking collectives: 55.2 us -> 79.3 us
  starting transfers between devices: 18.6 us -> 11.5 us
  local copies, waits for them, and re-layouts: 13.9 us -> 8.52 us
    pallas_call x3 -> x2, Pallas kernels: 80.2 us -> 12.7 us  [the longest x1 12.6 us: lookup(): pl.pallas_call(lookup_kernel, out_shape=[jax.ShapeDtypeStruct((TOKENS, HE...]
    all_to_all x2 -> x3, blocking collectives: 55.2 us -> 79.3 us  [the longest x1 33.5 us: body(): parts = lax.all_to_all(joined, ('x', 'y_hi'), 0, 0)]
    ppermute x10 -> x9, waiting for transfers between devices: 1.05 us -> 6.99 us  [the longest x1 4.26 us: body(): back_left = lax.ppermute(grad3, everything, moves(0, 1))]
    all_to_all x1 -> x0, waiting for transfers between devices: 5.11 us -> none  [body(): parts = lax.all_to_all(fold_lat(parts), 'lat', 0, 0)]
    all_to_all x1 -> x0, starting transfers between devices: 4.94 us -> none  [body(): parts = lax.all_to_all(fold_lat(parts), 'lat', 0, 0)]
    reshape x6 -> x0, local copies, waits for them, and re-layouts: 4.87 us -> none  [the longest x1 1.45 us: lookup(): return (out_wide, out_narrow[:, :18].reshape(HEADS, TOKENS, 16))]
    pallas_call x1, Pallas kernels: 11.4 us -> 8.5 us  [scatter(): pl.pallas_call(scatter_kernel, out_shape=jax.ShapeDtypeStruct((8, 32, 256...]
    pallas_call x1, Pallas kernels: 3.24 us -> 0.35 us  [join(): pl.pallas_call(join_kernel, out_shape=jax.ShapeDtypeStruct((8, 32, 2304),...]
  transfers between devices with their start and end apart: 11 -> 9, of which waited for: 3 -> 2; matrix products, arithmetic and copies ran while one was open for 4% -> 0% of each run, Pallas kernels for 44% -> 15%
where the time goes in v1:
time: 146 us; the launch traced here: 145 us
  blocking collectives  79.3 us (54%)
  Pallas kernels  37.8 us (26%)
  starting transfers between devices  11.5 us (8%)
  local copies, waits for them, and re-layouts  8.52 us (6%)
  waiting for transfers between devices  6.99 us (5%)
    all_to_all x1, blocking collectives, body(): parts = lax.all_to_all(joined, ('x', 'y_hi'), 0, 0)  33.5 us
    all_to_all x1, blocking collectives, body(): parts = lax.all_to_all(fold_lat(parts), LAT + ('core',), 0, 0)  24.9 us
    all_to_all x1, blocking collectives, body(): parts = lax.all_to_all(fold_lon(parts), LAT, 0, 0)  20.8 us
    pallas_call x1, Pallas kernels, window(): pl.pallas_call(main_kernel, out_shape=[shape(256, 4 * WIDTH), shape(256,...  14.5 us
    pallas_call x1, Pallas kernels, lookup(): pl.pallas_call(lookup_kernel, out_shape=[jax.ShapeDtypeStruct((TOKENS, HE...  12.6 us
    unnamed x18, local copies, waits for them, and re-layouts  8.52 us
    pallas_call x1, Pallas kernels, scatter(): pl.pallas_call(scatter_kernel, out_shape=jax.ShapeDtypeStruct((8, 32, 256...  8.5 us
    ppermute x1, waiting for transfers between devices, body(): back_left = lax.ppermute(grad3, everything, moves(0, 1))  4.26 us
  transfers between devices with their start and end apart: 9, of which 2 were waited for; matrix products, arithmetic and copies ran while one was open for 0% of the time, Pallas kernels for 15%

profile of v1, /device:TPU:8, one launch (start us, length us, event | category | flops | bytes accessed | tf_op | source)
XLA Modules:
  0.0 144.9 jit_solution(4000984470764810885)
XLA Ops:
  0.6 0.0 copy-start.1
  0.7 1.0 copy-done.1
  1.6 0.0 copy-start.5
  1.6 1.0 copy-done.5
  2.6 0.0 copy-start.8
  2.6 0.7 copy-done.8
  3.3 0.2 pack.1
  3.5 1.9 %collective-permute-start = (f32[80,512]{1,0:T(8,128)S(1)}, f32[80,512]{1,0:T(8,128)S(1)}, u32[]{:S(2)}, u32[]{:S(2)}) collective-permute-start(f32[80,512]{1,0:T(8,128)S(1)} %get-tuple-element.27), channel_id=1, source_target_pairs={{0,16},{1,17},{2,18},{3,19},{4,20},{5,21},{6,22},{7,23},{8,24},{9,... | collective-permute-start | bytes 491528 | tf_op jit(solution)/shard_map/ppermute | solution.py:568
  5.4 3.8 %collective-permute-start.1 = (f32[80,512]{1,0:T(8,128)S(1)}, f32[80,512]{1,0:T(8,128)S(1)}, u32[]{:S(2)}, u32[]{:S(2)}) collective-permute-start(f32[80,512]{1,0:T(8,128)S(1)} %get-tuple-element.28), channel_id=1, source_target_pairs={{0,31},{1,16},{2,17},{3,18},{4,19},{5,20},{6,21},{7,22},{8,23},{9,... | collective-permute-start | bytes 491528 | tf_op jit(solution)/shard_map/ppermute | solution.py:569
  9.1 2.0 %collective-permute-start.2 = (f32[80,512]{1,0:T(8,128)S(1)}, f32[80,512]{1,0:T(8,128)S(1)}, u32[]{:S(2)}, u32[]{:S(2)}) collective-permute-start(f32[80,512]{1,0:T(8,128)S(1)} %get-tuple-element.29), channel_id=1, source_target_pairs={{0,15},{1,0},{2,1},{3,2},{4,3},{5,4},{6,5},{7,6},{8,7},{9,8},{10,9... | collective-permute-start | bytes 491528 | tf_op jit(solution)/shard_map/ppermute | solution.py:567
  11.2 0.0 copy-start.4
  11.2 1.0 copy-done.4
  12.2 0.0 copy-start.6
  12.2 0.9 copy-done.6
  13.1 0.0 copy-start.7
  13.1 0.9 copy-done.7
  14.0 12.6 %lookup.1 = (f32[144,16,144]{2,1,0:T(8,128)S(1)}, s32[144,128]{1,0:T(8,128)S(1)}, s32[18,128]{1,0:T(8,128)S(1)}) custom-call(s32[1]{0:T(128)} %bitcast.core_ref, s32[144,144]{1,0:T(8,128)S(1)} %copy-done.6, bf16[144,144]{1,0:T(8,128)(2,1)S(1)} %copy-done.7, f32[16,6336]{1,0:T(8,128)S(1)} %bitcast.10), custom_call_target="tpu_custom_call" | custom-call | tf_op jit(solution)/shard_map/lookup/pallas_call | solution.py:175
  26.6 0.0 collective-permute-done.quad0
  26.6 0.0 collective-permute-done.1.quad1
  26.6 0.0 collective-permute-done.2.quad3
  26.6 0.0 copy-start
  26.6 1.9 %copy-done = f32[512,1536]{1,0:T(8,128)S(1)} copy-done((f32[512,1536]{1,0:T(8,128)S(1)}, f32[512,1536]{1,0:T(8,128)}, u32[]{:S(2)}) %copy-start) | copy-done | bytes 3145752
  28.5 0.0 copy-start.3
  28.5 1.2 copy-done.3
  29.7 0.0 copy-start.2
  29.7 14.5 %window.1 = (f32[256,2048]{1,0:T(8,128)S(1)}, f32[256,2048]{1,0:T(8,128)S(1)}, f32[144,8,128]{2,1,0:T(8,128)S(1)}, f32[144,8,128]{2,1,0:T(8,128)S(1)}, f32[18,8,...) custom-call(s32[1]{0:T(128)} %bitcast.core_ref, ...), custom_call_target="tpu_custom_call" | custom-call | tf_op jit(solution)/shard_map/window/pallas_call | solution.py:323
  44.2 0.1 collective-permute-start.3
  44.3 0.5 collective-permute-start.4
  44.8 0.1 collective-permute-start.6
  44.9 1.3 collective-permute-start.7
  46.3 1.8 %collective-permute-start.8 = (f32[36,512]{1,0:T(8,128)S(1)}, f32[36,512]{1,0:T(8,128)S(1)}, u32[]{:S(2)}, u32[]{:S(2)}) collective-permute-start(f32[36,512]{1,0:T(8,128)S(1)} %get-tuple-element.42), channel_id=1, source_target_pairs={{0,241},{1,242},{2,243},{3,244},{4,245},{5,246},{6,247},{7,248},{8... | collective-permute-start | bytes 221192 | tf_op jit(solution)/shard_map/ppermute | solution.py:588
  48.1 4.3 %collective-permute-done.6.left = f32[36,512]{1,0:T(8,128)S(1)} collective-permute-done((f32[36,512]{1,0:T(8,128)S(1)}, f32[36,512]{1,0:T(8,128)S(1)}, u32[]{:S(2)}, u32[]{:S(2)}) %collective-permute-start.6) | collective-permute-done | bytes 73760 | tf_op jit(solution)/shard_map/ppermute | solution.py:586
  52.3 0.0 collective-permute-start.5
  52.3 0.0 collective-permute-done.7.below
  52.4 2.7 %collective-permute-done.8.corner = f32[36,512]{1,0:T(8,128)S(1)} collective-permute-done((f32[36,512]{1,0:T(8,128)S(1)}, f32[36,512]{1,0:T(8,128)S(1)}, u32[]{:S(2)}, u32[]{:S(2)}) %collective-permute-start.8) | collective-permute-done | bytes 73760 | tf_op jit(solution)/shard_map/ppermute | solution.py:588
  55.1 0.0 copy-done.2
  55.1 0.8 place.1
  55.8 0.0 collective-permute-done.5.came_narrow
  55.9 0.0 collective-permute-done.4.came_wide
  55.9 8.5 %scatter.1.table = f32[8,32,256]{2,1,0:T(8,128)S(1)} custom-call(s32[144,128]{1,0:T(8,128)S(1)} %get-tuple-element.33.wide, s32[18,128]{1,0:T(8,128)S(1)} %get-tuple-element.34.narrow, f32[144,8,128]{2,1,0:T(8,128)S(1)} %get-tuple-element.35.keep_wide, f32[144,8,128]{2,1,0:T(8,128)S(1)} %collective-permute-done.4.came_wide, ...), custom_call_target="tpu_custom_call" | custom-call | tf_op jit(solution)/shard_map/scatter/pallas_call | solution.py:411
  64.4 0.0 collective-permute-done.3.came
  64.4 0.3 join.1
  64.7 33.5 %all_to_all.15.parts = f32[8,32,2304]{2,1,0:T(8,128)S(1)} all-to-all(f32[8,32,2304]{2,1,0:T(8,128)S(1)} %join.1), channel_id=1, replica_groups=mesh['z'=8,'y_lo'=2,'x'=4,'y_hi'=2,'core'=2] {'x','y_hi'}, dimensions={0} | all-to-all | bytes 4718592 | tf_op jit(solution)/shard_map/all_to_all | solution.py:593
  98.3 0.1 fold_lon.1
  98.4 20.8 %all_to_all.16.parts = f32[16,8,640]{2,1,0:T(8,128)S(1)} all-to-all(f32[16,8,640]{2,1,0:T(8,128)S(1)} %fold_lon.1), channel_id=1, replica_groups=mesh['z'=8,'y_lo'=2,'x'=4,'y_hi'=2,'core'=2] {'z','y_lo'}, dimensions={0} | all-to-all | bytes 655360 | tf_op jit(solution)/shard_map/all_to_all | solution.py:594
  119.2 0.1 fold_lat.1
  119.3 24.9 %all_to_all.17.parts = f32[32,8,640]{2,1,0:T(8,128)S(1)} all-to-all(f32[32,8,640]{2,1,0:T(8,128)S(1)} %fold_lat.1), channel_id=1, replica_groups=mesh['z'=8,'y_lo'=2,'x'=4,'y_hi'=2,'core'=2] {'z','y_lo','core'}, dimensions={0} | all-to-all | bytes 1310720 | tf_op jit(solution)/shard_map/all_to_all | solution.py:595
  144.2 0.7 unpack.1
Async XLA Ops:
  0.6 1.0 copy-start.1
  1.6 1.0 copy-start.5
  2.6 0.7 copy-start.8
  3.5 23.1 %collective-permute-start = (f32[80,512]{1,0:T(8,128)S(1)}, f32[80,512]{1,0:T(8,128)S(1)}, u32[]{:S(2)}, u32[]{:S(2)}) collective-permute-start(f32[80,512]{1,0:T(8,128)S(1)} %get-tuple-element.27), channel_id=1, source_target_pairs={{0,16},{1,17},{2,18},{3,19},{4,20},{5,21},{6,22},{7,23},{8,24},{9,... | collective-permute-start | bytes 491528 | tf_op jit(solution)/shard_map/ppermute | solution.py:568
  5.4 21.2 %collective-permute-start.1 = (f32[80,512]{1,0:T(8,128)S(1)}, f32[80,512]{1,0:T(8,128)S(1)}, u32[]{:S(2)}, u32[]{:S(2)}) collective-permute-start(f32[80,512]{1,0:T(8,128)S(1)} %get-tuple-element.28), channel_id=1, source_target_pairs={{0,31},{1,16},{2,17},{3,18},{4,19},{5,20},{6,21},{7,22},{8,23},{9,... | collective-permute-start | bytes 491528 | tf_op jit(solution)/shard_map/ppermute | solution.py:569
  9.1 17.5 %collective-permute-start.2 = (f32[80,512]{1,0:T(8,128)S(1)}, f32[80,512]{1,0:T(8,128)S(1)}, u32[]{:S(2)}, u32[]{:S(2)}) collective-permute-start(f32[80,512]{1,0:T(8,128)S(1)} %get-tuple-element.29), channel_id=1, source_target_pairs={{0,15},{1,0},{2,1},{3,2},{4,3},{5,4},{6,5},{7,6},{8,7},{9,8},{10,9... | collective-permute-start | bytes 491528 | tf_op jit(solution)/shard_map/ppermute | solution.py:567
  11.2 1.0 copy-start.4
  12.2 0.9 copy-start.6
  13.1 0.9 copy-start.7
  26.6 1.9 %copy-start = (f32[512,1536]{1,0:T(8,128)S(1)}, f32[512,1536]{1,0:T(8,128)}, u32[]{:S(2)}) copy-start(f32[512,1536]{1,0:T(8,128)} %in_weight.1) | copy-start | bytes 9437188
  28.5 1.2 copy-start.3
  29.7 25.3 %copy-start.2 = (f32[2,12,6,512]{3,0,2,1:T(2,128)S(1)}, f32[2,12,6,512]{3,0,2,1:T(2,128)}, u32[]{:S(2)}) copy-start(f32[2,12,6,512]{3,0,2,1:T(2,128)} %param.9) | copy-start | bytes 884740
  44.2 20.1 %collective-permute-start.3 = (f32[256,2048]{1,0:T(8,128)S(1)}, f32[256,2048]{1,0:T(8,128)S(1)}, u32[]{:S(2)}, u32[]{:S(2)}) collective-permute-start(f32[256,2048]{1,0:T(8,128)S(1)} %get-tuple-element.32), channel_id=1, source_target_pairs={{0,1},{1,0},{2,3},{3,2},{4,5},{5,4},{6,7},{7,6},{8,9},{9,8},{10,11... | collective-permute-start | bytes 6291464 | tf_op jit(solution)/shard_map/ppermute | solution.py:585
  44.3 11.5 %collective-permute-start.4 = (f32[144,8,128]{2,1,0:T(8,128)S(1)}, f32[144,8,128]{2,1,0:T(8,128)S(1)}, u32[]{:S(2)}, u32[]{:S(2)}) collective-permute-start(f32[144,8,128]{2,1,0:T(8,128)S(1)} %get-tuple-element.36), channel_id=1, source_target_pairs={{0,1},{1,0},{2,3},{3,2},{4,5},{5,4},{6,7},{7,6},{8,9},{9,8},{10,11... | collective-permute-start | bytes 1769480 | tf_op jit(solution)/shard_map/ppermute | solution.py:583
  44.8 7.5 %collective-permute-start.6 = (f32[36,512]{1,0:T(8,128)S(1)}, f32[36,512]{1,0:T(8,128)S(1)}, u32[]{:S(2)}, u32[]{:S(2)}) collective-permute-start(f32[36,512]{1,0:T(8,128)S(1)} %get-tuple-element.40), channel_id=1, source_target_pairs={{0,1},{1,2},{2,3},{3,4},{4,5},{5,6},{6,7},{7,8},{8,9},{9,10},{10,1... | collective-permute-start | bytes 221192 | tf_op jit(solution)/shard_map/ppermute | solution.py:586
  44.9 7.4 %collective-permute-start.7 = (f32[36,512]{1,0:T(8,128)S(1)}, f32[36,512]{1,0:T(8,128)S(1)}, u32[]{:S(2)}, u32[]{:S(2)}) collective-permute-start(f32[36,512]{1,0:T(8,128)S(1)} %get-tuple-element.41), channel_id=1, source_target_pairs={{0,240},{1,241},{2,242},{3,243},{4,244},{5,245},{6,246},{7,247},{8... | collective-permute-start | bytes 221192 | tf_op jit(solution)/shard_map/ppermute | solution.py:587
  46.3 8.8 %collective-permute-start.8 = (f32[36,512]{1,0:T(8,128)S(1)}, f32[36,512]{1,0:T(8,128)S(1)}, u32[]{:S(2)}, u32[]{:S(2)}) collective-permute-start(f32[36,512]{1,0:T(8,128)S(1)} %get-tuple-element.42), channel_id=1, source_target_pairs={{0,241},{1,242},{2,243},{3,244},{4,245},{5,246},{6,247},{7,248},{8... | collective-permute-start | bytes 221192 | tf_op jit(solution)/shard_map/ppermute | solution.py:588
  52.3 3.5 %collective-permute-start.5 = (f32[18,8,128]{2,1,0:T(8,128)S(1)}, f32[18,8,128]{2,1,0:T(8,128)S(1)}, u32[]{:S(2)}, u32[]{:S(2)}) collective-permute-start(f32[18,8,128]{2,1,0:T(8,128)S(1)} %get-tuple-element.38), channel_id=1, source_target_pairs={{0,1},{1,0},{2,3},{3,2},{4,5},{5,4},{6,7},{7,6},{8,9},{9,8},{10,11... | collective-permute-start | bytes 221192 | tf_op jit(solution)/shard_map/ppermute | solution.py:584

commit v2 on v1

--- a/solution.py
+++ b/solution.py
@@ -27,6 +27,14 @@
     return pltpu.CompilerParams(vmem_limit_bytes=mib * MEGA)
 
 
+def cost(micros):
+    return pl.CostEstimate(flops=int(micros * 1e9), bytes_accessed=0, transcendentals=0)
+
+
+def hbm(count):
+    return [pl.BlockSpec(memory_space=pltpu.HBM)] * count
+
+
 def whole(count):
     return [pl.BlockSpec(memory_space=pltpu.VMEM)] * count
 
@@ -61,7 +69,19 @@
     return np.transpose(grid, (1, 3, 2, 4, 0)).reshape(-1)
 
 
-def pack_kernel(last, fields, grads, ids, own, left, below, corner):
+def pack_kernel(
+    last, fields_in, grads_in, ids_in, own, left, below, corner, fields, grads, ids, arrived
+):
+    copies = [
+        pltpu.make_async_copy(source, target, arrived.at[i])
+        for i, (source, target) in enumerate(
+            ((fields_in, fields), (grads_in, grads), (ids_in, ids))
+        )
+    ]
+    for copy in copies:
+        copy.start()
+    for copy in copies:
+        copy.wait()
     lanes = lax.broadcasted_iota(jnp.int32, (2, WIDTH), 1)
     level = lax.broadcasted_iota(jnp.int32, (2, WIDTH), 0)
     bump = last[0]
@@ -94,9 +114,16 @@
     return pl.pallas_call(
         pack_kernel,
         out_shape=[shape] * 4,
-        in_specs=[scalar()] + whole(3),
+        in_specs=[scalar()] + hbm(3),
         out_specs=whole(4),
-        compiler_params=params(),
+        scratch_shapes=[
+            pltpu.VMEM(fields.shape, F32),
+            pltpu.VMEM(grads.shape, F32),
+            pltpu.VMEM(ids.shape, jnp.int32),
+            pltpu.SemaphoreType.DMA((3,)),
+        ],
+        compiler_params=params(8),
+        cost_estimate=cost(2),
         name="pack",
     )(last, fields, grads, ids)
 
@@ -111,7 +138,31 @@
     return lax.broadcasted_iota(jnp.int32, (256, 128), 0).astype(F32).astype(BF16)
 
 
-def lookup_kernel(core_ref, index, order, table, bias, wide, narrow, left):
+def lookup_kernel(
+    core_ref,
+    index,
+    order,
+    table,
+    in_hbm,
+    out_hbm,
+    bias,
+    wide,
+    narrow,
+    in_high,
+    in_low,
+    out_high,
+    out_low,
+    left,
+    in_weight,
+    out_weight,
+    arrived,
+):
+    copies = [
+        pltpu.make_async_copy(in_hbm, in_weight, arrived.at[0]),
+        pltpu.make_async_copy(out_hbm, out_weight, arrived.at[1]),
+    ]
+    for copy in copies:
+        copy.start()
     value = index[...]
     high = (value >> 7).astype(F32).astype(BF16)
     low = (value & 127).astype(F32).astype(BF16)
@@ -167,9 +218,15 @@
         found = find([narrow[2 * pair + j : 2 * pair + j + 1, :] for j in range(2)])
         for j in range(16):
             bias[16 * pair + j, :, 128:144] = found[:, 16 * j : 16 * j + 16]
-
-
-def lookup(core, bias_index, bias_table):
+    for copy in copies:
+        copy.wait()
+    for part in range(3):
+        cols = slice(part * WIDTH, part * WIDTH + WIDTH)
+        in_high[:, cols], in_low[:, cols] = halves(in_weight[:, cols])
+    out_high[...], out_low[...] = halves(out_weight[...])
+
+
+def lookup(core, bias_index, bias_table, in_weight, out_weight):
     order = np.zeros((TOKENS, TOKENS), np.float32)
     order[np.arange(TOKENS), token_order()] = 1.0
     return pl.pallas_call(
@@ -178,41 +235,52 @@
             jax.ShapeDtypeStruct((TOKENS, HEADS, TOKENS), F32),
             jax.ShapeDtypeStruct((TOKENS, 128), jnp.int32),
             jax.ShapeDtypeStruct((18, 128), jnp.int32),
+        ]
+        + [jax.ShapeDtypeStruct(in_weight.shape, BF16)] * 2
+        + [jax.ShapeDtypeStruct(out_weight.shape, BF16)] * 2,
+        in_specs=[scalar()] + whole(3) + hbm(2),
+        out_specs=whole(7),
+        scratch_shapes=[
+            pltpu.VMEM((BLOCKS * 32, 256), BF16),
+            pltpu.VMEM(in_weight.shape, F32),
+            pltpu.VMEM(out_weight.shape, F32),
+            pltpu.SemaphoreType.DMA((2,)),
         ],
-        in_specs=[scalar()] + whole(3),
-        out_specs=whole(3),
-        scratch_shapes=[pltpu.VMEM((BLOCKS * 32, 256), BF16)],
-        compiler_params=params(),
+        compiler_params=params(20),
+        cost_estimate=cost(13),
         name="lookup",
-    )(core, bias_index, jnp.asarray(order, BF16), bias_table.T)
-
-
-def main_kernel(
+    )(core, bias_index, jnp.asarray(order, BF16), bias_table.T, in_weight, out_weight)
+
+
+def attend_kernel(
     core_ref,
     own,
     quad0,
     quad1,
     quad3,
     bias,
-    in_weight,
-    out_weight,
-    keep,
-    send,
+    in_high,
+    in_low,
+    out_high,
+    out_low,
     keep_wide,
     send_wide,
     keep_narrow,
     send_narrow,
-    grad0,
-    grad1,
-    grad2,
-    grad3,
+    normed_high,
+    normed_low,
+    att_high,
+    att_low,
+    gproj_high,
+    gproj_low,
+    cot_high,
+    cot_low,
+    normed_out,
+    inv_std_out,
     tokens,
     cotangent,
     proj,
     gatt,
-    gproj,
-    att,
-    normed_t,
     tails,
 ):
     core = core_ref[0]
@@ -232,15 +300,16 @@
     variance = jnp.mean(centered * centered, axis=1, keepdims=True)
     inv_std = lax.rsqrt(variance + 1e-05)
     normed = centered * inv_std
-    tokens[...] = normed
-    normed_t[...] = normed.T
+    normed_out[...] = normed
+    inv_std_out[...] = jnp.broadcast_to(inv_std, (TOKENS, 128))
+    normed_high[...], normed_low[...] = halves(normed.T)
     halves_normed = halves(normed)
     for part in range(3):
-        at = part * WIDTH
-        weight = halves(in_weight[:, at : at + WIDTH])
-        proj[at : at + WIDTH, :] = dot3(halves_normed, weight, NN).T
+        cols = slice(part * WIDTH, part * WIDTH + WIDTH)
+        proj[cols, :] = dot3(halves_normed, (in_high[:, cols], in_low[:, cols]), NN).T
     halves_cotangent = halves(cotangent[...])
-    gatt[...] = dot3(halves(out_weight[...]), halves_cotangent, NT)
+    cot_high[...], cot_low[...] = halves_cotangent
+    gatt[...] = dot3((out_high[...], out_low[...]), halves_cotangent, NT)
 
     def one_head(head, slot):
         at = pl.multiple_of(head * HEAD_DIM, HEAD_DIM)
@@ -267,10 +336,14 @@
             both = dot(stacked(high, low), right_high, dims)
             return both[:HEAD_DIM] + (both[HEAD_DIM:] + dot(high, right_low, dims))
 
-        att[pl.ds(at, HEAD_DIM), :] = product(vh, vl, ph, plow, NT)
-        gproj[pl.ds(at + 2 * WIDTH, HEAD_DIM), :] = product(gh, gl, ph, plow, NN)
-        gproj[pl.ds(at, HEAD_DIM), :] = product(kh, kl, sh, sl, NT) * FACTOR
-        gproj[pl.ds(at + WIDTH, HEAD_DIM), :] = product(qh, ql, sh, sl, NN)
+        def store(high, low, offset, value):
+            rows = pl.ds(at + offset, HEAD_DIM)
+            high[rows, :], low[rows, :] = halves(value)
+
+        store(att_high, att_low, 0, product(vh, vl, ph, plow, NT))
+        store(gproj_high, gproj_low, 2 * WIDTH, product(gh, gl, ph, plow, NN))
+        store(gproj_high, gproj_low, 0, product(kh, kl, sh, sl, NT) * FACTOR)
+        store(gproj_high, gproj_low, WIDTH, product(qh, ql, sh, sl, NN))
         return grad_scores
 
     tails[...] = jnp.zeros_like(tails)
@@ -288,24 +361,104 @@
         send_narrow[i] = total[0:8]
         keep_narrow[i] = total[8:16]
 
+
+def shape(*dims, dtype=F32):
+    return jax.ShapeDtypeStruct(dims, dtype)
+
+
+def attend(core, own, quad0, quad1, quad3, bias, *weights):
+    thin = shape(WIDTH, TOKENS, dtype=BF16)
+    return pl.pallas_call(
+        attend_kernel,
+        out_shape=[
+            shape(TOKENS, 8, 128),
+            shape(TOKENS, 8, 128),
+            shape(18, 8, 128),
+            shape(18, 8, 128),
+            thin,
+            thin,
+            thin,
+            thin,
+            shape(3 * WIDTH, TOKENS, dtype=BF16),
+            shape(3 * WIDTH, TOKENS, dtype=BF16),
+            shape(TOKENS, WIDTH, dtype=BF16),
+            shape(TOKENS, WIDTH, dtype=BF16),
+            shape(TOKENS, WIDTH),
+            shape(TOKENS, 128),
+        ],
+        in_specs=[scalar()] + whole(9),
+        out_specs=whole(14),
+        scratch_shapes=[
+            pltpu.VMEM((TOKENS, WIDTH), F32),
+            pltpu.VMEM((TOKENS, WIDTH), F32),
+            pltpu.VMEM((3 * WIDTH, TOKENS), F32),
+            pltpu.VMEM((WIDTH, TOKENS), F32),
+            pltpu.VMEM((TOKENS, HEADS, 128), F32),
+        ],
+        compiler_params=params(24),
+        cost_estimate=cost(10),
+        name="attend",
+    )(core, own, quad0, quad1, quad3, bias, *weights)
+
+
+def weights_kernel(
+    core_ref,
+    normed_high,
+    normed_low,
+    att_high,
+    att_low,
+    gproj_high,
+    gproj_low,
+    cot_high,
+    cot_low,
+    keep,
+    send,
+):
+    core = core_ref[0]
     for target, bit in ((send, 1 - core), (keep, core)):
         rows = [pl.ds(pl.multiple_of(64 * i + 32 * bit, 32), 32) for i in range(8)]
-        left = halves(jnp.concatenate([normed_t[r, :] for r in rows], axis=0))
+
+        def gathered(ref):
+            return jnp.concatenate([ref[r, :] for r in rows], axis=0)
+
+        left = (gathered(normed_high), gathered(normed_low))
         for part in range(3):
-            at = part * WIDTH
-            target[:, at : at + WIDTH] = dot3(left, halves(gproj[at : at + WIDTH, :]), NT)
-        left = halves(jnp.concatenate([att[r, :] for r in rows], axis=0))
-        target[:, 3 * WIDTH :] = dot3(left, halves_cotangent, NN)
-
-    grad_normed = jnp.zeros((WIDTH, TOKENS), F32)
-    for part in range(3):
-        at = part * WIDTH
-        grad_normed = grad_normed + dot3(
-            halves(in_weight[:, at : at + WIDTH]), halves(gproj[at : at + WIDTH, :]), NN
-        )
-    grad_normed = grad_normed.T
-    normed = tokens[...]
-    result = inv_std * (
+            cols = slice(part * WIDTH, part * WIDTH + WIDTH)
+            target[:, cols] = dot3(left, (gproj_high[cols, :], gproj_low[cols, :]), NT)
+        left = (gathered(att_high), gathered(att_low))
+        target[:, 3 * WIDTH :] = dot3(left, (cot_high[...], cot_low[...]), NN)
+
+
+def weights(core, *parts):
+    return pl.pallas_call(
+        weights_kernel,
+        out_shape=[shape(256, 4 * WIDTH)] * 2,
+        in_specs=[scalar()] + whole(8),
+        out_specs=whole(2),
+        compiler_params=params(),
+        cost_estimate=cost(3),
+        name="weights",
+    )(core, *parts)
+
+
+def inputs_kernel(
+    gproj_high,
+    gproj_low,
+    in_high,
+    in_low,
+    normed_in,
+    inv_std_in,
+    grad0,
+    grad1,
+    grad2,
+    grad3,
+    tokens,
+):
+    grad_normed = dot3(
+        (in_high[...], in_low[...]), (gproj_high[...], gproj_low[...]), NN
+    ).T
+    normed = normed_in[...]
+    result = inv_std_in[:, 0:1] * (
         grad_normed
         - jnp.mean(grad_normed, axis=1, keepdims=True)
         - normed * jnp.mean(grad_normed * normed, axis=1, keepdims=True)
@@ -315,44 +468,32 @@
         target[...] = tokens[slot * QUAD : slot * QUAD + QUAD, :]
 
 
-def window(core, own, quad0, quad1, quad3, bias, in_weight, out_weight):
-    def shape(*dims):
-        return jax.ShapeDtypeStruct(dims, F32)
-
-    grad = shape(QUAD, WIDTH)
-    return pl.pallas_call(
-        main_kernel,
-        out_shape=[
-            shape(256, 4 * WIDTH),
-            shape(256, 4 * WIDTH),
-            shape(TOKENS, 8, 128),
-            shape(TOKENS, 8, 128),
-            shape(18, 8, 128),
-            shape(18, 8, 128),
-            grad,
-            grad,
-            grad,
-            grad,
-        ],
-        in_specs=[scalar()] + whole(7),
-        out_specs=whole(10),
-        scratch_shapes=[
-            pltpu.VMEM((TOKENS, WIDTH), F32),
-            pltpu.VMEM((TOKENS, WIDTH), F32),
-            pltpu.VMEM((3 * WIDTH, TOKENS), F32),
-            pltpu.VMEM((WIDTH, TOKENS), F32),
-            pltpu.VMEM((3 * WIDTH, TOKENS), F32),
-            pltpu.VMEM((WIDTH, TOKENS), F32),
-            pltpu.VMEM((WIDTH, TOKENS), F32),
-            pltpu.VMEM((TOKENS, HEADS, 128), F32),
-        ],
-        compiler_params=params(26),
-        name="window",
-    )(core, own, quad0, quad1, quad3, bias, in_weight, out_weight)
+def input_grads(*parts):
+    return pl.pallas_call(
+        inputs_kernel,
+        out_shape=[shape(QUAD, WIDTH)] * 4,
+        in_specs=whole(6),
+        out_specs=whole(4),
+        scratch_shapes=[pltpu.VMEM((TOKENS, WIDTH), F32)],
+        compiler_params=params(),
+        cost_estimate=cost(3),
+        name="input_grads",
+    )(*parts)
 
 
 def scatter_kernel(
-    wide, narrow, keep_wide, came_wide, keep_narrow, came_narrow, out, total, line
+    core_ref,
+    wide,
+    narrow,
+    keep_wide,
+    came_wide,
+    keep_narrow,
+    came_narrow,
+    keep,
+    send,
+    total,
+    line,
+    sectors,
 ):
     total[...] = jnp.zeros_like(total)
     lines = line_numbers()
@@ -404,121 +545,171 @@
         piece = line[:, base : base + 512]
         if shift:
             piece = pltpu.roll(piece, 512 - shift, 1)
-        out[chip, half * 16 + core * 8 : half * 16 + core * 8 + 8, :] = piece[:, :256]
-
-
-def scatter(wide, narrow, keep_wide, came_wide, keep_narrow, came_narrow):
+        sectors[core, chip, half * 8 : half * 8 + 8, :] = piece[:, :256]
+    keep[...] = sectors[core_ref[0]]
+    send[...] = sectors[1 - core_ref[0]]
+
+
+def scatter(core, wide, narrow, keep_wide, came_wide, keep_narrow, came_narrow):
     return pl.pallas_call(
         scatter_kernel,
-        out_shape=jax.ShapeDtypeStruct((8, 32, 256), F32),
-        in_specs=whole(6),
-        out_specs=pl.BlockSpec(memory_space=pltpu.VMEM),
+        out_shape=[shape(8, 16, 256)] * 2,
+        in_specs=[scalar()] + whole(6),
+        out_specs=whole(2),
         scratch_shapes=[
             pltpu.VMEM((BLOCKS * 16, 256), F32),
             pltpu.VMEM((8, BLOCKS * 256 + 256), F32),
+            pltpu.VMEM((2, 8, 16, 256), F32),
         ],
         compiler_params=params(),
+        cost_estimate=cost(9),
         name="scatter",
-    )(wide, narrow, keep_wide, came_wide, keep_narrow, came_narrow)
-
-
-def join_kernel(keep, came, table, out):
-    out[0, :, : 4 * WIDTH] = keep[...] + came[...]
-    out[0, :, 4 * WIDTH :] = table[0]
-
-
-def join(keep, came, table):
-    block = pl.BlockSpec((32, 4 * WIDTH), lambda i: (i, 0))
+    )(core, wide, narrow, keep_wide, came_wide, keep_narrow, came_narrow)
+
+
+SIZE_A, SIZE_C = 384, 256
+
+
+def split_kernel(bits, keep, came, own, send_a, send_b, send_c):
+    odd, low = bits[0], bits[1]
+
+    def columns(base, size, bit):
+        cols = pl.ds(pl.multiple_of(base + size * bit, 128), size)
+        return keep[:, cols] + came[:, cols]
+
+    own[:, 0:384] = columns(0, SIZE_A, odd)
+    own[:, 384:768] = columns(768, SIZE_A, 1 - odd)
+    own[:, 768:1024] = columns(1536, SIZE_C, low)
+    send_a[...] = columns(0, SIZE_A, 1 - odd)
+    send_b[...] = columns(768, SIZE_A, odd)
+    send_c[...] = columns(1536, SIZE_C, 1 - low)
+
+
+def split(bits, keep, came):
+    return pl.pallas_call(
+        split_kernel,
+        out_shape=[shape(256, 1024), shape(256, SIZE_A), shape(256, SIZE_A), shape(256, SIZE_C)],
+        in_specs=[scalar()] + whole(2),
+        out_specs=whole(4),
+        compiler_params=params(),
+        cost_estimate=cost(1),
+        name="split",
+    )(bits, keep, came)
+
+
+def join_kernel(core_ref, own, came_a, came_b, came_c, table_keep, table_came, out):
+    for i in range(8):
+        rows = slice(i * 32, i * 32 + 32)
+        out[i, :, 0:384] = own[rows, 0:384] + came_a[rows, :]
+        out[i, :, 384:768] = own[rows, 384:768] + came_b[rows, :]
+        out[i, :, 768:1024] = own[rows, 768:1024] + came_c[rows, :]
+    first = core_ref[0] == 0
+    mine, other = table_keep[...], table_came[...]
+    out[:, 0:16, 1024:] = jnp.where(first, mine, other)
+    out[:, 16:32, 1024:] = jnp.where(first, other, mine)
+
+
+def join(core, *parts):
     return pl.pallas_call(
         join_kernel,
-        out_shape=jax.ShapeDtypeStruct((8, 32, 2304), F32),
-        grid=(8,),
-        in_specs=[block, block, pl.BlockSpec((1, 32, 256), lambda i: (i, 0, 0))],
-        out_specs=pl.BlockSpec((1, 32, 2304), lambda i: (i, 0, 0)),
+        out_shape=shape(8, 32, 1280),
+        in_specs=[scalar()] + whole(6),
+        out_specs=pl.BlockSpec(memory_space=pltpu.VMEM),
         compiler_params=params(),
+        cost_estimate=cost(1),
         name="join",
-    )(keep, came, table)
-
-
-def fold_lon_kernel(parts, out):
-    def rows(at):
-        total = parts[0, at : at + 8, :]
-        for i in range(1, 8):
-            total = total + parts[i, at : at + 8, :]
-        return total
-
-    for group in range(4):
-        total = rows(group * 8)
-        for col in range(4):
-            if col < 3:
-                out[group * 4 + col] = total[:, col * 640 : col * 640 + 640]
-            else:
-                out[group * 4 + col, :, :384] = total[:, 1920:2304]
-                out[group * 4 + col, :, 384:] = jnp.zeros((8, 256), F32)
+    )(core, *parts)
+
+
+def fold_lon_kernel(parts, out, total):
+    value = parts[0]
+    for i in range(1, 8):
+        value = value + parts[i]
+    total[...] = value
+    for p in range(16):
+        z, y = p // 2, p % 2
+        rank = (z // 2) * 2 + y
+        out[p, :, 0:768] = total[4 * rank : 4 * rank + 4, 0:768]
+        out[p, :, 768:1024] = total[4 * z : 4 * z + 4, 768:1024]
+        out[p, :, 1024:1152] = total[4 * z : 4 * z + 4, 1024 + 128 * y : 1152 + 128 * y]
 
 
 def fold_lon(parts):
     return pl.pallas_call(
         fold_lon_kernel,
-        out_shape=jax.ShapeDtypeStruct((16, 8, 640), F32),
+        out_shape=shape(16, 4, 1152),
         in_specs=whole(1),
         out_specs=pl.BlockSpec(memory_space=pltpu.VMEM),
+        scratch_shapes=[pltpu.VMEM((32, 1280), F32)],
         compiler_params=params(),
         name="fold_lon",
     )(parts)
 
 
-def fold_lat_kernel(parts, out):
-    total = parts[0]
-    for i in range(1, 16):
-        total = total + parts[i]
-    for i in range(32):
+def fold_lat_kernel(bits, parts, out):
+    odd, low = bits[0], bits[1]
+
+    def summed(sources, cols):
+        total = parts[sources[0], :, cols]
+        for source in sources[1:]:
+            total = total + parts[source, :, cols]
+        return total
+
+    same_z = [(2 * k + odd) * 2 + y for k in range(4) for y in range(2)]
+    same_y = [2 * z + low for z in range(8)]
+    total = jnp.concatenate(
+        [
+            summed(same_z, slice(0, 768)),
+            summed(same_y, slice(768, 1024)),
+            summed(list(range(16)), slice(1024, 1152)),
+        ],
+        axis=1,
+    )
+    for i in range(16):
         out[i] = total
 
 
-def fold_lat(parts):
+def fold_lat(bits, parts):
     return pl.pallas_call(
         fold_lat_kernel,
-        out_shape=jax.ShapeDtypeStruct((32, 8, 640), F32),
-        in_specs=whole(1),
+        out_shape=shape(16, 4, 1152),
+        in_specs=[scalar()] + whole(1),
         out_specs=pl.BlockSpec(memory_space=pltpu.VMEM),
         compiler_params=params(),
         name="fold_lat",
-    )(parts)
-
-
-def unpack_kernel(core_ref, parts, grad_in, grad_out, grad_bias):
-    core = core_ref[0]
-    for group in range(4):
-        rows = slice(group * 8, group * 8 + 8)
-        base = group * 8 + core
-        grad_in[rows, 0:640] = parts[base]
-        grad_in[rows, 640:1280] = parts[base + 2]
-        grad_in[rows, 1280:1536] = parts[base + 4, :, :256]
-        grad_out[rows, 0:384] = parts[base + 4, :, 256:]
-        grad_out[rows, 384:512] = parts[base + 6, :, :128]
-    for other in range(2):
-        rows = slice(other * 8, other * 8 + 8)
+    )(bits, parts)
+
+
+def unpack_kernel(parts, grad_in, grad_out, grad_bias, table):
+    for p in range(16):
+        z, y = p // 2, p % 2
+        odd = z % 2
+        rank = (z // 2) * 2 + y
+        rows = slice(4 * rank, 4 * rank + 4)
+        grad_in[rows, 384 * odd : 384 * odd + 384] = parts[p, :, 0:384]
+        start = 768 + 384 * (1 - odd)
+        grad_in[rows, start : start + 384] = parts[p, :, 384:768]
+        rows = slice(4 * z, 4 * z + 4)
+        grad_out[rows, 256 * y : 256 * y + 256] = parts[p, :, 768:1024]
+        table[rows, 128 * y : 128 * y + 128] = parts[p, :, 1024:1152]
+    for core in range(2):
         for half in range(2):
-            piece = parts[(half * 2 + core) * 8 + 6 + other, :, 128:384]
-            grad_bias[rows, half * HALF_SECTOR : half * HALF_SECTOR + HALF_SECTOR] = piece[
-                :, :HALF_SECTOR
-            ]
-
-
-def unpack(core, parts):
+            base = core * 16 + half * 8
+            grad_bias[core * 8 : core * 8 + 8, half * HALF_SECTOR : (half + 1) * HALF_SECTOR] = (
+                table[base : base + 8, :HALF_SECTOR]
+            )
+
+
+def unpack(parts):
     return pl.pallas_call(
         unpack_kernel,
-        out_shape=[
-            jax.ShapeDtypeStruct((32, 3 * WIDTH), F32),
-            jax.ShapeDtypeStruct((32, WIDTH), F32),
-            jax.ShapeDtypeStruct((HEADS, 2 * HALF_SECTOR), F32),
-        ],
-        in_specs=[scalar()] + whole(1),
+        out_shape=[shape(32, 3 * WIDTH), shape(32, WIDTH), shape(HEADS, 2 * HALF_SECTOR)],
+        in_specs=whole(1),
         out_specs=whole(3),
+        scratch_shapes=[pltpu.VMEM((32, 256), F32)],
         compiler_params=params(),
         name="unpack",
-    )(core, parts)
+    )(parts)
 
 
 def place_kernel(grad_out, own, left, below, corner, out):
@@ -550,6 +741,7 @@
     everything = LAT + LON
     lat = lax.axis_index(LAT)
     core = lax.axis_index("core").reshape(1)
+    bits = jnp.stack([lax.rem(lax.axis_index("z"), 2), lax.axis_index("y_lo")])
 
     def moves(down, right):
         return [
@@ -567,33 +759,62 @@
     quad3 = lax.ppermute(left, everything, moves(0, -1))
     quad0 = lax.ppermute(below, everything, moves(1, 0))
     quad1 = lax.ppermute(corner, everything, moves(1, -1))
-    bias, wide, narrow = lookup(core, bias_index, bias_table)
+    bias, wide, narrow, *halved = lookup(core, bias_index, bias_table, in_weight, out_weight)
     (
-        keep,
-        send,
         keep_wide,
         send_wide,
         keep_narrow,
         send_narrow,
-        grad0,
-        grad1,
-        grad2,
-        grad3,
-    ) = window(core, own, quad0, quad1, quad3, bias, in_weight, out_weight)
+        normed_high,
+        normed_low,
+        att_high,
+        att_low,
+        gproj_high,
+        gproj_low,
+        cot_high,
+        cot_low,
+        normed,
+        inv_std,
+    ) = attend(core, own, quad0, quad1, quad3, bias, *halved)
     came_wide = lax.ppermute(send_wide, "core", swap)
     came_narrow = lax.ppermute(send_narrow, "core", swap)
+    keep, send = weights(
+        core,
+        normed_high,
+        normed_low,
+        att_high,
+        att_low,
+        gproj_high,
+        gproj_low,
+        cot_high,
+        cot_low,
+    )
     came = lax.ppermute(send, "core", swap)
+    normed, send = lax.optimization_barrier((normed, send))
+    grad0, grad1, grad2, grad3 = input_grads(
+        gproj_high, gproj_low, halved[0], halved[1], normed, inv_std
+    )
     back_left = lax.ppermute(grad3, everything, moves(0, 1))
     back_below = lax.ppermute(grad0, everything, moves(-1, 0))
     back_corner = lax.ppermute(grad1, everything, moves(-1, 1))
-    table = scatter(wide, narrow, keep_wide, came_wide, keep_narrow, came_narrow)
+    keep, grad2 = lax.optimization_barrier((keep, grad2))
+    part, send_a, send_b, send_c = split(bits, keep, came)
+    came_a = lax.ppermute(send_a, "z", [(i, i ^ 1) for i in range(8)])
+    came_b = lax.ppermute(send_b, "z", [(i, ((i + 1) % 8 ^ 1) + 7 & 7) for i in range(8)])
+    came_c = lax.ppermute(send_c, "y_lo", swap)
+    wide, part = lax.optimization_barrier((wide, part))
+    table_keep, table_send = scatter(
+        core, wide, narrow, keep_wide, came_wide, keep_narrow, came_narrow
+    )
+    table_came = lax.ppermute(table_send, "core", swap)
+    grad2, table_send = lax.optimization_barrier((grad2, table_send))
     grad_fields = place(grad_out, grad2, back_left, back_below, back_corner)
-    joined = join(keep, came, table)
-    joined, grad_fields = lax.optimization_barrier((joined, grad_fields))
+    part, grad_fields = lax.optimization_barrier((part, grad_fields))
+    joined = join(core, part, came_a, came_b, came_c, table_keep, table_came)
     parts = lax.all_to_all(joined, ("x", "y_hi"), 0, 0)
     parts = lax.all_to_all(fold_lon(parts), LAT, 0, 0)
-    parts = lax.all_to_all(fold_lat(parts), LAT + ("core",), 0, 0)
-    grad_in_weight, grad_out_weight, grad_bias = unpack(core, parts)
+    parts = lax.all_to_all(fold_lat(bits, parts), LAT, 0, 0)
+    grad_in_weight, grad_out_weight, grad_bias = unpack(parts)
     return jnp.transpose(grad_fields, (2, 0, 1, 3)), grad_in_weight, grad_out_weight, grad_bias.T
 
 

time: 146 us -> 137 us (0.938)
  blocking collectives: 79.3 us -> 52.5 us
  starting transfers between devices: 11.5 us -> 18.6 us
  Pallas kernels: 37.8 us -> 44.3 us
  local copies, waits for them, and re-layouts: 8.52 us -> 13.6 us
    all_to_all x1, blocking collectives: 24.9 us -> 13.2 us  [body(): parts = lax.all_to_all(fold_lat(bits, parts), LAT, 0, 0)]
    all_to_all x1, blocking collectives: 33.5 us -> 23 us  [body(): parts = lax.all_to_all(joined, ('x', 'y_hi'), 0, 0)]
    ppermute x0 -> x4, starting transfers between devices: none -> 7.26 us  [the longest x1 4.77 us: body(): lax.ppermute(send_b, 'z', [(i, ((i + 1) % 8 ^ 1) + 7 & 7) for i in range(...]
    unnamed x18 -> x54, local copies, waits for them, and re-layouts: 8.52 us -> 13.6 us
    pallas_call x6 -> x9, Pallas kernels: 24.2 us -> 28.9 us  [the longest x1 12.5 us: attend(): pl.pallas_call(attend_kernel, out_shape=[shape(TOKENS, 8, 128), shape(TOK...]
    all_to_all x1, blocking collectives: 20.8 us -> 16.3 us  [body(): parts = lax.all_to_all(fold_lon(parts), LAT, 0, 0)]
    ppermute x1, waiting for transfers between devices: 4.26 us -> 0.01 us  [body(): back_left = lax.ppermute(grad3, everything, moves(0, 1))]
    ppermute x1, waiting for transfers between devices: 2.72 us -> 5.96 us  [body(): back_corner = lax.ppermute(grad1, everything, moves(-1, 1))]
  transfers between devices with their start and end apart: 9 -> 13, of which waited for: 2 -> 1; matrix products, arithmetic and copies ran while one was open for 0% -> 0% of each run, Pallas kernels for 15% -> 19%
where the time goes in v2:
time: 137 us; the launch traced here: 136 us
  blocking collectives  52.5 us (38%)
  Pallas kernels  44.3 us (32%)
  starting transfers between devices  18.6 us (14%)
  local copies, waits for them, and re-layouts  13.6 us (10%)
  waiting for transfers between devices  5.99 us (4%)
    all_to_all x1, blocking collectives, body(): parts = lax.all_to_all(joined, ('x', 'y_hi'), 0, 0)  23 us
    all_to_all x1, blocking collectives, body(): parts = lax.all_to_all(fold_lon(parts), LAT, 0, 0)  16.3 us
    unnamed x54, local copies, waits for them, and re-layouts  13.6 us
    pallas_call x1, Pallas kernels, lookup(): pl.pallas_call(lookup_kernel, out_shape=[jax.ShapeDtypeStruct((TOKENS, HE...  13.5 us
    all_to_all x1, blocking collectives, body(): parts = lax.all_to_all(fold_lat(bits, parts), LAT, 0, 0)  13.2 us
    pallas_call x1, Pallas kernels, attend(): pl.pallas_call(attend_kernel, out_shape=[shape(TOKENS, 8, 128), shape(TOK...  12.5 us
    pallas_call x1, Pallas kernels, scatter(): pl.pallas_call(scatter_kernel, out_shape=[shape(8, 16, 256)] * 2, in_spec...  8.47 us
    ppermute x1, waiting for transfers between devices, body(): back_corner = lax.ppermute(grad1, everything, moves(-1, 1))  5.96 us
  transfers between devices with their start and end apart: 13, of which 1 were waited for; matrix products, arithmetic and copies ran while one was open for 0% of the time, Pallas kernels for 19%

profile of v2, /device:TPU:8, one launch (start us, length us, event | category | flops | bytes accessed | tf_op | source)
XLA Modules:
  0.0 136.0 jit_solution(5380542672825306685)
XLA Ops:
  0.6 0.0 copy-start
  0.7 1.0 copy-done
  1.6 1.0 copy-done.5
  2.6 0.7 copy-done.7
  3.3 1.2 pack.1
  4.5 0.7 copy-done.19
  5.1 1.8 %collective-permute-start = (f32[80,512]{1,0:T(8,128)}, f32[80,512]{1,0:T(8,128)}, u32[]{:S(2)}, u32[]{:S(2)}) collective-permute-start(f32[80,512]{1,0:T(8,128)} %get-tuple-element.54), channel_id=1, source_target_pairs={{0,16},{1,17},{2,18},{3,19},{4,20},{5,21},{6,22},{7,23},{8,24},{9,... | collective-permute-start | bytes 491528 | tf_op jit(solution)/shard_map/ppermute | solution.py:760
  6.9 3.8 %collective-permute-start.1 = (f32[80,512]{1,0:T(8,128)}, f32[80,512]{1,0:T(8,128)}, u32[]{:S(2)}, u32[]{:S(2)}) collective-permute-start(f32[80,512]{1,0:T(8,128)} %get-tuple-element.55), channel_id=1, source_target_pairs={{0,31},{1,16},{2,17},{3,18},{4,19},{5,20},{6,21},{7,22},{8,23},{9,... | collective-permute-start | bytes 491528 | tf_op jit(solution)/shard_map/ppermute | solution.py:761
  10.7 2.0 %collective-permute-start.2 = (f32[80,512]{1,0:T(8,128)}, f32[80,512]{1,0:T(8,128)}, u32[]{:S(2)}, u32[]{:S(2)}) collective-permute-start(f32[80,512]{1,0:T(8,128)} %get-tuple-element.56), channel_id=1, source_target_pairs={{0,15},{1,0},{2,1},{3,2},{4,3},{5,4},{6,5},{7,6},{8,7},{9,8},{10,9... | collective-permute-start | bytes 491528 | tf_op jit(solution)/shard_map/ppermute | solution.py:759
  12.7 1.2 copy-done.3
  13.9 0.9 copy-done.6
  14.9 0.9 copy-done.8
  15.7 13.5 %lookup.1 = (f32[144,16,144]{2,1,0:T(8,128)S(1)}, s32[144,128]{1,0:T(8,128)S(1)}, s32[18,128]{1,0:T(8,128)S(1)}, bf16[512,1536]{1,0:T(8,128)(2,1)S(1)}, bf16[512...) custom-call(s32[1]{0:T(128)} %bitcast.core_ref, s32[144,144]{1,0:T(8,128)S(1)} %copy-done.6, ...), custom_call_target="tpu_custom_call" | custom-call | flops 12999999488 | tf_op jit(solution)/shard_map/lookup/pallas_call | solution.py:232
  29.2 0.6 copy-done.23
  29.9 0.6 copy-done.25
  30.5 0.0 collective-permute-done.quad0
  30.5 0.0 collective-permute-done.1.quad1
  30.5 12.5 %attend.1 = (f32[144,8,128]{2,1,0:T(8,128)S(1)}, f32[144,8,128]{2,1,0:T(8,128)S(1)}, f32[18,8,128]{2,1,0:T(8,128)S(1)}, f32[18,8,128]{2,1,0:T(8,128)S(1)}, bf16[...) custom-call(s32[1]{0:T(128)} %bitcast.core_ref, ...), custom_call_target="tpu_custom_call" | custom-call | flops 10000000000 | tf_op jit(solution)/shard_map/attend/pallas_call | solution.py:371
  43.1 0.0 copy-start.17
  43.1 3.0 %weights.1 = (f32[256,2048]{1,0:T(8,128)S(1)}, f32[256,2048]{1,0:T(8,128)}) custom-call(s32[1]{0:T(128)} %bitcast.core_ref, bf16[512,144]{1,0:T(8,128)(2,1)S(1)} %get-tuple-element.62.normed_high, bf16[512,144]{1,0:T(8,128)(2,1)S(1)} %get-tuple-element.63.normed_low, bf16[512,144]{1,0:T(8,128)(2,1)S(1)} %get-tuple-element.64.att_high, ...), custom_call_target="tpu_custom_call" | custom-call | flops 3000000000 | tf_op jit(solution)/shard_map/weights/pallas_call | solution.py:433
  46.1 0.3 collective-permute-start.3
  46.4 0.5 collective-permute-start.4
  46.9 0.1 pad_add_fusion.bits
  47.0 0.1 collective-permute-start.5
  47.1 1.4 %copy-done.10 = bf16[512,1536]{1,0:T(8,128)(2,1)S(1)} copy-done((bf16[512,1536]{1,0:T(8,128)(2,1)S(1)}, bf16[512,1536]{1,0:T(8,128)(2,1)}, u32[]{:S(2)}) %copy-start.10) | copy-done | bytes 1572888
  48.5 1.4 %copy-done.12 = bf16[512,1536]{1,0:T(8,128)(2,1)S(1)} copy-done((bf16[512,1536]{1,0:T(8,128)(2,1)S(1)}, bf16[512,1536]{1,0:T(8,128)(2,1)}, u32[]{:S(2)}) %copy-start.12) | copy-done | bytes 1572888
  49.9 1.1 copy-done.14
  51.0 1.1 copy-done.16
  52.2 1.0 copy-done.18
  53.1 1.6 %input_grads.1 = (f32[36,512]{1,0:T(8,128)S(1)}, f32[36,512]{1,0:T(8,128)S(1)}, f32[36,512]{1,0:T(8,128)S(1)}, f32[36,512]{1,0:T(8,128)S(1)}) custom-call(bf16[1536,144]{1,0:T(8,128)(2,1)S(1)} %copy-done.14, bf16[1536,144]{1,0:T(8,128)(2,1)S(1)} %copy-done.16, bf16[512,1536]{1,0:T(8,128)(2,1)S(1)} %copy-done.10, bf16[512,1536]{1,0:T(8,128)(2,1)S(1)} %copy-done.12, ...), custom_call_target="tpu_custom_call" | custom-call | flops 3000000000 | tf_op jit(solution)/shard_map/input_grads/pallas_call | solution.py:472
  54.7 0.5 collective-permute-start.6
  55.2 1.3 collective-permute-start.7
  56.5 0.0 collective-permute-done.3.came
  56.6 1.8 %split.1 = (f32[256,1024]{1,0:T(8,128)S(1)}, f32[256,384]{1,0:T(8,128)S(1)}, f32[256,384]{1,0:T(8,128)S(1)}, f32[256,256]{1,0:T(8,128)S(1)}) custom-call(s32[2]{0:T(128)S(1)} %pad_add_fusion.bits, f32[256,2048]{1,0:T(8,128)S(1)} %get-tuple-element.76.keep, f32[256,2048]{1,0:T(8,128)} %collective-permute-done.3.came), custom_call_target="tpu_custom_call" | custom-call | flops 1000000000 | tf_op jit(solution)/shard_map/split/pallas_call | solution.py:589
  58.4 2.4 %collective-permute-start.11 = (f32[256,256]{1,0:T(8,128)S(1)}, f32[256,256]{1,0:T(8,128)S(1)}, u32[]{:S(2)}, u32[]{:S(2)}) collective-permute-start(f32[256,256]{1,0:T(8,128)S(1)} %get-tuple-element.95), channel_id=1, source_target_pairs={{0,16},{16,0},{1,17},{17,1},{2,18},{18,2},{3,19},{19,3},{4,20},{20... | collective-permute-start | bytes 786440 | tf_op jit(solution)/shard_map/ppermute | solution.py:804
  60.8 4.8 %collective-permute-start.10 = (f32[256,384]{1,0:T(8,128)S(1)}, f32[256,384]{1,0:T(8,128)S(1)}, u32[]{:S(2)}, u32[]{:S(2)}) collective-permute-start(f32[256,384]{1,0:T(8,128)S(1)} %get-tuple-element.94), channel_id=1, source_target_pairs={{0,224},{32,64},{64,32},{96,128},{128,96},{160,192},{192,160},{224... | collective-permute-start | bytes 1179656 | tf_op jit(solution)/shard_map/ppermute | solution.py:803
  65.6 8.5 %scatter.1 = (f32[8,16,256]{2,1,0:T(8,128)S(1)}, f32[8,16,256]{2,1,0:T(8,128)S(1)}) custom-call(s32[1]{0:T(128)} %bitcast.core_ref, s32[144,128]{1,0:T(8,128)S(1)} %copy-done.24, s32[18,128]{1,0:T(8,128)S(1)} %copy-done.26, f32[144,8,128]{2,1,0:T(8,128)S(1)} %copy-done.22, f32[144,8,128]{2,1,0:T(8,128)S(1)} %collective-permute-done.4.came_wide, ...), custom_call_target="tpu_custom_call" | custom-call | flops 8999999488 | tf_op jit(solution)/shard_map/scatter/pallas_call | solution.py:554
  74.1 0.1 collective-permute-start.12
  74.2 1.0 collective-permute-start.8
  75.2 6.0 %collective-permute-done.8.corner = f32[36,512]{1,0:T(8,128)S(1)} collective-permute-done((f32[36,512]{1,0:T(8,128)S(1)}, f32[36,512]{1,0:T(8,128)S(1)}, u32[]{:S(2)}, u32[]{:S(2)}) %collective-permute-start.8) | collective-permute-done | bytes 73760 | tf_op jit(solution)/shard_map/ppermute | solution.py:799
  81.2 0.8 place.1
  82.0 0.1 join.1
  82.1 23.0 %all_to_all.15.parts = f32[8,32,1280]{2,1,0:T(8,128)S(1)} all-to-all(f32[8,32,1280]{2,1,0:T(8,128)S(1)} %join.1), channel_id=1, replica_groups=mesh['z'=8,'y_lo'=2,'x'=4,'y_hi'=2,'core'=2] {'x','y_hi'}, dimensions={0} | all-to-all | bytes 2621440 | tf_op jit(solution)/shard_map/all_to_all | solution.py:814
  105.2 0.1 fold_lon.1
  105.3 16.3 %all_to_all.16.parts = f32[16,4,1152]{2,1,0:T(4,128)S(1)} all-to-all(f32[16,4,1152]{2,1,0:T(4,128)S(1)} %fold_lon.1), channel_id=1, replica_groups=mesh['z'=8,'y_lo'=2,'x'=4,'y_hi'=2,'core'=2] {'z','y_lo'}, dimensions={0} | all-to-all | bytes 589824 | tf_op jit(solution)/shard_map/all_to_all | solution.py:815
  121.5 0.6 fold_lat.1
  122.1 13.2 %all_to_all.17.parts = f32[16,4,1152]{2,1,0:T(4,128)S(1)} all-to-all(f32[16,4,1152]{2,1,0:T(4,128)S(1)} %fold_lat.1), channel_id=1, replica_groups=mesh['z'=8,'y_lo'=2,'x'=4,'y_hi'=2,'core'=2] {'z','y_lo'}, dimensions={0} | all-to-all | bytes 589824 | tf_op jit(solution)/shard_map/all_to_all | solution.py:816
  135.3 0.7 unpack.1
  (48 shorter events, 0.1 us)
Async XLA Ops:
  0.6 1.0 copy-start
  1.6 1.0 copy-start.5
  2.6 0.7 copy-start.7
  3.3 9.5 %copy-start.2 = (f32[512,1536]{1,0:T(8,128)S(1)}, f32[512,1536]{1,0:T(8,128)}, u32[]{:S(2)}) copy-start(f32[512,1536]{1,0:T(8,128)} %in_hbm.1) | copy-start | bytes 9437188
  3.3 9.5 %copy-start.4 = (f32[6336,16]{0,1:T(8,128)S(1)}, f32[6336,16]{0,1:T(8,128)}, u32[]{:S(2)}) copy-start(f32[6336,16]{0,1:T(8,128)} %param.12) | copy-start | bytes 1216516
  4.5 0.7 copy-start.19
  5.1 25.4 %collective-permute-start = (f32[80,512]{1,0:T(8,128)}, f32[80,512]{1,0:T(8,128)}, u32[]{:S(2)}, u32[]{:S(2)}) collective-permute-start(f32[80,512]{1,0:T(8,128)} %get-tuple-element.54), channel_id=1, source_target_pairs={{0,16},{1,17},{2,18},{3,19},{4,20},{5,21},{6,22},{7,23},{8,24},{9,... | collective-permute-start | bytes 491528 | tf_op jit(solution)/shard_map/ppermute | solution.py:760
  6.9 23.6 %collective-permute-start.1 = (f32[80,512]{1,0:T(8,128)}, f32[80,512]{1,0:T(8,128)}, u32[]{:S(2)}, u32[]{:S(2)}) collective-permute-start(f32[80,512]{1,0:T(8,128)} %get-tuple-element.55), channel_id=1, source_target_pairs={{0,31},{1,16},{2,17},{3,18},{4,19},{5,20},{6,21},{7,22},{8,23},{9,... | collective-permute-start | bytes 491528 | tf_op jit(solution)/shard_map/ppermute | solution.py:761
  10.7 19.8 %collective-permute-start.2 = (f32[80,512]{1,0:T(8,128)}, f32[80,512]{1,0:T(8,128)}, u32[]{:S(2)}, u32[]{:S(2)}) collective-permute-start(f32[80,512]{1,0:T(8,128)} %get-tuple-element.56), channel_id=1, source_target_pairs={{0,15},{1,0},{2,1},{3,2},{4,3},{5,4},{6,5},{7,6},{8,7},{9,8},{10,9... | collective-permute-start | bytes 491528 | tf_op jit(solution)/shard_map/ppermute | solution.py:759
  12.7 1.2 copy-start.3
  13.9 0.9 copy-start.6
  14.9 0.9 copy-start.8
  15.7 14.8 %copy-start.20 = (f32[80,512]{1,0:T(8,128)S(1)}, f32[80,512]{1,0:T(8,128)}, u32[]{:S(2)}) copy-start(f32[80,512]{1,0:T(8,128)} %copy-done.19) | copy-start | bytes 491524
  29.2 0.6 copy-start.23
  29.9 0.6 copy-start.25
  30.5 12.6 %copy-start.9 = (bf16[512,1536]{1,0:T(8,128)(2,1)}, bf16[512,1536]{1,0:T(8,128)(2,1)S(1)}, u32[]{:S(2)}) copy-start(bf16[512,1536]{1,0:T(8,128)(2,1)S(1)} %get-tuple-element.58.in_high) | copy-start | bytes 4718596
  30.5 12.6 %copy-start.11 = (bf16[512,1536]{1,0:T(8,128)(2,1)}, bf16[512,1536]{1,0:T(8,128)(2,1)S(1)}, u32[]{:S(2)}) copy-start(bf16[512,1536]{1,0:T(8,128)(2,1)S(1)} %get-tuple-element.59.in_low) | copy-start | bytes 4718596
  43.1 3.0 %copy-start.13 = (bf16[1536,144]{1,0:T(8,128)(2,1)}, bf16[1536,144]{1,0:T(8,128)(2,1)S(1)}, u32[]{:S(2)}) copy-start(bf16[1536,144]{1,0:T(8,128)(2,1)S(1)} %get-tuple-element.66.gproj_high) | copy-start | bytes 1327108
  43.1 3.0 %copy-start.15 = (bf16[1536,144]{1,0:T(8,128)(2,1)}, bf16[1536,144]{1,0:T(8,128)(2,1)S(1)}, u32[]{:S(2)}) copy-start(bf16[1536,144]{1,0:T(8,128)(2,1)S(1)} %get-tuple-element.67.gproj_low) | copy-start | bytes 1327108
  43.1 3.0 %copy-start.17 = (f32[144,512]{1,0:T(8,128)}, f32[144,512]{1,0:T(8,128)S(1)}, u32[]{:S(2)}) copy-start(f32[144,512]{1,0:T(8,128)S(1)} %get-tuple-element.73.normed_in) | copy-start | bytes 884740
  43.1 3.0 %copy-start.21 = (f32[144,8,128]{2,1,0:T(8,128)}, f32[144,8,128]{2,1,0:T(8,128)S(1)}, u32[]{:S(2)}) copy-start(f32[144,8,128]{2,1,0:T(8,128)S(1)} %get-tuple-element.82.keep_wide) | copy-start | bytes 1769476
  46.1 10.5 %collective-permute-start.3 = (f32[256,2048]{1,0:T(8,128)}, f32[256,2048]{1,0:T(8,128)}, u32[]{:S(2)}, u32[]{:S(2)}) collective-permute-start(f32[256,2048]{1,0:T(8,128)} %get-tuple-element.72), channel_id=1, source_target_pairs={{0,1},{1,0},{2,3},{3,2},{4,5},{5,4},{6,7},{7,6},{8,9},{9,8},{10,11... | collective-permute-start | bytes 6291464 | tf_op jit(solution)/shard_map/ppermute | solution.py:792
  46.4 14.4 %collective-permute-start.4 = (f32[144,8,128]{2,1,0:T(8,128)S(1)}, f32[144,8,128]{2,1,0:T(8,128)S(1)}, u32[]{:S(2)}, u32[]{:S(2)}) collective-permute-start(f32[144,8,128]{2,1,0:T(8,128)S(1)} %get-tuple-element.83), channel_id=1, source_target_pairs={{0,1},{1,0},{2,3},{3,2},{4,5},{5,4},{6,7},{7,6},{8,9},{9,8},{10,11... | collective-permute-start | bytes 1769480 | tf_op jit(solution)/shard_map/ppermute | solution.py:779
  47.0 13.8 %collective-permute-start.5 = (f32[18,8,128]{2,1,0:T(8,128)S(1)}, f32[18,8,128]{2,1,0:T(8,128)S(1)}, u32[]{:S(2)}, u32[]{:S(2)}) collective-permute-start(f32[18,8,128]{2,1,0:T(8,128)S(1)} %get-tuple-element.85), channel_id=1, source_target_pairs={{0,1},{1,0},{2,3},{3,2},{4,5},{5,4},{6,7},{7,6},{8,9},{9,8},{10,11... | collective-permute-start | bytes 221192 | tf_op jit(solution)/shard_map/ppermute | solution.py:780
  47.1 1.4 %copy-start.10 = (bf16[512,1536]{1,0:T(8,128)(2,1)S(1)}, bf16[512,1536]{1,0:T(8,128)(2,1)}, u32[]{:S(2)}) copy-start(bf16[512,1536]{1,0:T(8,128)(2,1)} %copy-done.9) | copy-start | bytes 4718596
  48.5 1.4 %copy-start.12 = (bf16[512,1536]{1,0:T(8,128)(2,1)S(1)}, bf16[512,1536]{1,0:T(8,128)(2,1)}, u32[]{:S(2)}) copy-start(bf16[512,1536]{1,0:T(8,128)(2,1)} %copy-done.11) | copy-start | bytes 4718596
  49.9 1.1 copy-start.14
  51.0 1.1 copy-start.16
  52.2 1.0 copy-start.18
  54.7 19.4 %collective-permute-start.6 = (f32[36,512]{1,0:T(8,128)S(1)}, f32[36,512]{1,0:T(8,128)S(1)}, u32[]{:S(2)}, u32[]{:S(2)}) collective-permute-start(f32[36,512]{1,0:T(8,128)S(1)} %get-tuple-element.88), channel_id=1, source_target_pairs={{0,1},{1,2},{2,3},{3,4},{4,5},{5,6},{6,7},{7,8},{8,9},{9,10},{10,1... | collective-permute-start | bytes 221192 | tf_op jit(solution)/shard_map/ppermute | solution.py:797
  55.2 10.4 %copy-start.22 = (f32[144,8,128]{2,1,0:T(8,128)S(1)}, f32[144,8,128]{2,1,0:T(8,128)}, u32[]{:S(2)}) copy-start(f32[144,8,128]{2,1,0:T(8,128)} %copy-done.21) | copy-start | bytes 1769476
  55.2 10.4 %copy-start.24 = (s32[144,128]{1,0:T(8,128)S(1)}, s32[144,128]{1,0:T(8,128)}, u32[]{:S(2)}) copy-start(s32[144,128]{1,0:T(8,128)} %copy-done.23) | copy-start | bytes 221188
  55.2 10.4 %copy-start.26 = (s32[18,128]{1,0:T(8,128)S(1)}, s32[18,128]{1,0:T(8,128)}, u32[]{:S(2)}) copy-start(s32[18,128]{1,0:T(8,128)} %copy-done.25) | copy-start | bytes 27652
  55.2 19.0 %collective-permute-start.7 = (f32[36,512]{1,0:T(8,128)S(1)}, f32[36,512]{1,0:T(8,128)S(1)}, u32[]{:S(2)}, u32[]{:S(2)}) collective-permute-start(f32[36,512]{1,0:T(8,128)S(1)} %get-tuple-element.89), channel_id=1, source_target_pairs={{0,240},{1,241},{2,242},{3,243},{4,244},{5,245},{6,246},{7,247},{8... | collective-permute-start | bytes 221192 | tf_op jit(solution)/shard_map/ppermute | solution.py:798
  58.4 23.6 %collective-permute-start.11 = (f32[256,256]{1,0:T(8,128)S(1)}, f32[256,256]{1,0:T(8,128)S(1)}, u32[]{:S(2)}, u32[]{:S(2)}) collective-permute-start(f32[256,256]{1,0:T(8,128)S(1)} %get-tuple-element.95), channel_id=1, source_target_pairs={{0,16},{16,0},{1,17},{17,1},{2,18},{18,2},{3,19},{19,3},{4,20},{20... | collective-permute-start | bytes 786440 | tf_op jit(solution)/shard_map/ppermute | solution.py:804
  60.8 21.2 %collective-permute-start.9 = (f32[256,384]{1,0:T(8,128)S(1)}, f32[256,384]{1,0:T(8,128)S(1)}, u32[]{:S(2)}, u32[]{:S(2)}) collective-permute-start(f32[256,384]{1,0:T(8,128)S(1)} %get-tuple-element.93), channel_id=1, source_target_pairs={{0,32},{32,0},{64,96},{96,64},{128,160},{160,128},{192,224},{224,1... | collective-permute-start | bytes 1179656 | tf_op jit(solution)/shard_map/ppermute | solution.py:802
  60.8 21.2 %collective-permute-start.10 = (f32[256,384]{1,0:T(8,128)S(1)}, f32[256,384]{1,0:T(8,128)S(1)}, u32[]{:S(2)}, u32[]{:S(2)}) collective-permute-start(f32[256,384]{1,0:T(8,128)S(1)} %get-tuple-element.94), channel_id=1, source_target_pairs={{0,224},{32,64},{64,32},{96,128},{128,96},{160,192},{192,160},{224... | collective-permute-start | bytes 1179656 | tf_op jit(solution)/shard_map/ppermute | solution.py:803
  65.6 15.6 %copy-start.1 = (f32[2,12,6,512]{3,0,2,1:T(2,128)S(1)}, f32[2,12,6,512]{3,0,2,1:T(2,128)}, u32[]{:S(2)}) copy-start(f32[2,12,6,512]{3,0,2,1:T(2,128)} %param.9) | copy-start | bytes 884740
  74.1 7.9 %collective-permute-start.12 = (f32[8,16,256]{2,1,0:T(8,128)S(1)}, f32[8,16,256]{2,1,0:T(8,128)S(1)}, u32[]{:S(2)}, u32[]{:S(2)}) collective-permute-start(f32[8,16,256]{2,1,0:T(8,128)S(1)} %get-tuple-element.86), channel_id=1, source_target_pairs={{0,1},{1,0},{2,3},{3,2},{4,5},{5,4},{6,7},{7,6},{8,9},{9,8},{10,11... | collective-permute-start | bytes 393224 | tf_op jit(solution)/shard_map/ppermute | solution.py:809
  74.2 7.0 %collective-permute-start.8 = (f32[36,512]{1,0:T(8,128)S(1)}, f32[36,512]{1,0:T(8,128)S(1)}, u32[]{:S(2)}, u32[]{:S(2)}) collective-permute-start(f32[36,512]{1,0:T(8,128)S(1)} %get-tuple-element.90), channel_id=1, source_target_pairs={{0,241},{1,242},{2,243},{3,244},{4,245},{5,246},{6,247},{7,248},{8... | collective-permute-start | bytes 221192 | tf_op jit(solution)/shard_map/ppermute | solution.py:799

commit v3 on v1

--- a/solution.py
+++ b/solution.py
@@ -1,8 +1,5 @@
-import functools
-
 import jax
 import jax.numpy as jnp
-import numpy as np
 from jax import lax
 from jax.experimental import pallas as pl
 from jax.experimental.pallas import tpu as pltpu
@@ -17,14 +14,20 @@
 BIAS_ROWS = 6336
 HALF_SECTOR = 198
 BLOCKS = 25
+PACK_MIB = 4
+ROWS = 162
 FACTOR = HEAD_DIM ** (-0.5)
 F32 = jnp.float32
 BF16 = jnp.bfloat16
 MEGA = 1 << 20
 
 
-def params(mib=16):
+def params(mib=8):
     return pltpu.CompilerParams(vmem_limit_bytes=mib * MEGA)
+
+
+def cost(micros):
+    return pl.CostEstimate(flops=int(micros * 1e9), bytes_accessed=0, transcendentals=0)
 
 
 def whole(count):
@@ -57,8 +60,25 @@
 
 
 def token_order():
-    grid = np.arange(TOKENS).reshape(2, 2, 6, 2, 3)
-    return np.transpose(grid, (1, 3, 2, 4, 0)).reshape(-1)
+    place = lax.broadcasted_iota(jnp.int32, (TOKENS, TOKENS), 0)
+    token = lax.broadcasted_iota(jnp.int32, (TOKENS, TOKENS), 1)
+
+    def steps(value, size, count):
+        total = jnp.zeros_like(value)
+        for i in range(1, count):
+            total = total + jnp.where(value >= i * size, 1, 0)
+        return total
+
+    quad = steps(place, QUAD, 4)
+    rest = place - QUAD * quad
+    row = steps(rest, 6, 6)
+    rest = rest - 6 * row
+    col = steps(rest, 2, 3)
+    level = rest - 2 * col
+    row_half = steps(quad, 2, 2)
+    col_half = quad - 2 * row_half
+    source = level * 72 + (6 * row_half + row) * 6 + 3 * col_half + col
+    return jnp.where(source == token, 1.0, 0.0).astype(BF16)
 
 
 def pack_kernel(last, fields, grads, ids, own, left, below, corner):
@@ -96,7 +116,8 @@
         out_shape=[shape] * 4,
         in_specs=[scalar()] + whole(3),
         out_specs=whole(4),
-        compiler_params=params(),
+        compiler_params=params(PACK_MIB),
+        cost_estimate=cost(1),
         name="pack",
     )(last, fields, grads, ids)
 
@@ -111,21 +132,21 @@
     return lax.broadcasted_iota(jnp.int32, (256, 128), 0).astype(F32).astype(BF16)
 
 
-def lookup_kernel(core_ref, index, order, table, bias, wide, narrow, left):
+def lookup_kernel(core_ref, index, table, bias, places, left):
     value = index[...]
     high = (value >> 7).astype(F32).astype(BF16)
     low = (value & 127).astype(F32).astype(BF16)
-    move = order[...]
+    move = token_order()
 
     def moved(part):
         return dot(dot(move, part, NN).astype(BF16), move, NT)
 
     result = moved(high) * 128.0 + moved(low)
-    wide[...] = result[:, :128].astype(jnp.int32)
+    places[0:TOKENS, :] = result[:, :128].astype(jnp.int32)
     tail = jnp.concatenate([result[:, 128:], jnp.zeros((TOKENS, 112), F32)], axis=1)
     for i in range(18):
         spread = pltpu.roll(tail[8 * i : 8 * i + 8, :], 0, 1, stride=16, stride_axis=0)
-        narrow[i : i + 1, :] = jnp.sum(spread, axis=0, keepdims=True).astype(jnp.int32)
+        places[TOKENS + i : TOKENS + i + 1, :] = jnp.sum(spread, axis=0, keepdims=True).astype(jnp.int32)
 
     first = core_ref[0] == 0
     for block in range(BLOCKS):
@@ -155,7 +176,7 @@
 
     def step(i, carry):
         base = pl.multiple_of(i * 8, 8)
-        rows = wide[pl.ds(base, 8), :]
+        rows = places[pl.ds(base, 8), :]
         for pair in range(4):
             found = find([rows[2 * pair + j : 2 * pair + j + 1, :] for j in range(2)])
             for j in range(2):
@@ -164,27 +185,26 @@
 
     lax.fori_loop(0, 18, step, 0)
     for pair in range(9):
-        found = find([narrow[2 * pair + j : 2 * pair + j + 1, :] for j in range(2)])
+        at = TOKENS + 2 * pair
+        found = find([places[at + j : at + j + 1, :] for j in range(2)])
         for j in range(16):
             bias[16 * pair + j, :, 128:144] = found[:, 16 * j : 16 * j + 16]
 
 
 def lookup(core, bias_index, bias_table):
-    order = np.zeros((TOKENS, TOKENS), np.float32)
-    order[np.arange(TOKENS), token_order()] = 1.0
     return pl.pallas_call(
         lookup_kernel,
         out_shape=[
             jax.ShapeDtypeStruct((TOKENS, HEADS, TOKENS), F32),
-            jax.ShapeDtypeStruct((TOKENS, 128), jnp.int32),
-            jax.ShapeDtypeStruct((18, 128), jnp.int32),
+            jax.ShapeDtypeStruct((ROWS, 128), jnp.int32),
         ],
-        in_specs=[scalar()] + whole(3),
-        out_specs=whole(3),
+        in_specs=[scalar()] + whole(2),
+        out_specs=whole(2),
         scratch_shapes=[pltpu.VMEM((BLOCKS * 32, 256), BF16)],
-        compiler_params=params(),
+        compiler_params=params(6),
+        cost_estimate=cost(13),
         name="lookup",
-    )(core, bias_index, jnp.asarray(order, BF16), bias_table.T)
+    )(core, bias_index, bias_table.T)
 
 
 def main_kernel(
@@ -198,10 +218,8 @@
     out_weight,
     keep,
     send,
-    keep_wide,
-    send_wide,
-    keep_narrow,
-    send_narrow,
+    keep_scores,
+    send_scores,
     grad0,
     grad1,
     grad2,
@@ -276,17 +294,17 @@
     tails[...] = jnp.zeros_like(tails)
     for slot in range(8):
         grad_scores = one_head((1 - core) * 8 + slot, slot)
-        send_wide[:, slot, :] = grad_scores[:, :128]
+        send_scores[0:TOKENS, slot, :] = grad_scores[:, :128]
         tails[:, slot, 0:16] = grad_scores[:, 128:]
         grad_scores = one_head(core * 8 + slot, 8 + slot)
-        keep_wide[:, slot, :] = grad_scores[:, :128]
+        keep_scores[0:TOKENS, slot, :] = grad_scores[:, :128]
         tails[:, 8 + slot, 0:16] = grad_scores[:, 128:]
     for i in range(18):
         total = tails[8 * i]
         for j in range(1, 8):
             total = total + pltpu.roll(tails[8 * i + j], 16 * j, 1)
-        send_narrow[i] = total[0:8]
-        keep_narrow[i] = total[8:16]
+        send_scores[TOKENS + i] = total[0:8]
+        keep_scores[TOKENS + i] = total[8:16]
 
     for target, bit in ((send, 1 - core), (keep, core)):
         rows = [pl.ds(pl.multiple_of(64 * i + 32 * bit, 32), 32) for i in range(8)]
@@ -315,27 +333,26 @@
         target[...] = tokens[slot * QUAD : slot * QUAD + QUAD, :]
 
 
+def shape(*dims):
+    return jax.ShapeDtypeStruct(dims, F32)
+
+
 def window(core, own, quad0, quad1, quad3, bias, in_weight, out_weight):
-    def shape(*dims):
-        return jax.ShapeDtypeStruct(dims, F32)
-
     grad = shape(QUAD, WIDTH)
     return pl.pallas_call(
         main_kernel,
         out_shape=[
             shape(256, 4 * WIDTH),
             shape(256, 4 * WIDTH),
-            shape(TOKENS, 8, 128),
-            shape(TOKENS, 8, 128),
-            shape(18, 8, 128),
-            shape(18, 8, 128),
+            shape(ROWS, 8, 128),
+            shape(ROWS, 8, 128),
             grad,
             grad,
             grad,
             grad,
         ],
         in_specs=[scalar()] + whole(7),
-        out_specs=whole(10),
+        out_specs=whole(8),
         scratch_shapes=[
             pltpu.VMEM((TOKENS, WIDTH), F32),
             pltpu.VMEM((TOKENS, WIDTH), F32),
@@ -346,15 +363,13 @@
             pltpu.VMEM((WIDTH, TOKENS), F32),
             pltpu.VMEM((TOKENS, HEADS, 128), F32),
         ],
-        compiler_params=params(26),
+        compiler_params=params(14),
+        cost_estimate=cost(14),
         name="window",
     )(core, own, quad0, quad1, quad3, bias, in_weight, out_weight)
 
 
-def scatter_kernel(
-    wide, narrow, keep_wide, came_wide, keep_narrow, came_narrow, out, total, line
-):
-    total[...] = jnp.zeros_like(total)
+def add_pairs(places, keep, came, total, first, last):
     lines = line_numbers()
 
     def sides(row, values):
@@ -367,31 +382,50 @@
         )
         return left, one_hot(row, lines)
 
-    def add(pieces):
+    def add(rows, base, pair):
+        pieces = [
+            sides(rows[j : j + 1, :], keep[base + j] + came[base + j])
+            for j in (2 * pair, 2 * pair + 1)
+        ]
         left = jnp.concatenate([p[0] for p in pieces], axis=1)
         right = jnp.concatenate([p[1] for p in pieces], axis=1)
         total[...] += dot(left, right, NT)
 
     def step(i, carry):
         base = pl.multiple_of(i * 8, 8)
-        rows = wide[pl.ds(base, 8), :]
+        rows = places[pl.ds(base, 8), :]
         for pair in range(4):
-            add(
-                [
-                    sides(rows[j : j + 1, :], keep_wide[base + j] + came_wide[base + j])
-                    for j in (2 * pair, 2 * pair + 1)
-                ]
-            )
+            add(rows, base, pair)
         return carry
 
-    lax.fori_loop(0, 18, step, 0)
-    for pair in range(9):
-        add(
-            [
-                sides(narrow[j : j + 1, :], keep_narrow[j] + came_narrow[j])
-                for j in (2 * pair, 2 * pair + 1)
-            ]
-        )
+    lax.fori_loop(first // 8, last // 8, step, 0)
+    if last % 8:
+        base = last // 8 * 8
+        rows = places[base:last, :]
+        for pair in range(last % 8 // 2):
+            add(rows, base, pair)
+
+
+def scatter_start_kernel(places, keep, came, total):
+    total[...] = jnp.zeros_like(total)
+    add_pairs(places, keep, came, total, 0, 80)
+
+
+def scatter_start(places, keep, came):
+    return pl.pallas_call(
+        scatter_start_kernel,
+        out_shape=shape(BLOCKS * 16, 256),
+        in_specs=whole(3),
+        out_specs=pl.BlockSpec(memory_space=pltpu.VMEM),
+        compiler_params=params(6),
+        cost_estimate=cost(4.2),
+        name="scatter_start",
+    )(places, keep, came)
+
+
+def scatter_end_kernel(core_ref, places, keep, came, start, mine, other, total, line, sectors):
+    total[...] = start[...]
+    add_pairs(places, keep, came, total, 80, ROWS)
     for b in range(BLOCKS):
         line[:, b * 256 : b * 256 + 256] = (
             total[b * 16 : b * 16 + 8, :] + total[b * 16 + 8 : b * 16 + 16, :]
@@ -399,126 +433,181 @@
     line[:, BLOCKS * 256 :] = jnp.zeros((8, 256), F32)
     for m in range(32):
         chip, core, half = m // 4, m // 2 % 2, m % 2
-        start = m * HALF_SECTOR
-        base, shift = start // 128 * 128, start % 128
+        start_at = m * HALF_SECTOR
+        base, shift = start_at // 128 * 128, start_at % 128
         piece = line[:, base : base + 512]
         if shift:
             piece = pltpu.roll(piece, 512 - shift, 1)
-        out[chip, half * 16 + core * 8 : half * 16 + core * 8 + 8, :] = piece[:, :256]
-
-
-def scatter(wide, narrow, keep_wide, came_wide, keep_narrow, came_narrow):
-    return pl.pallas_call(
-        scatter_kernel,
-        out_shape=jax.ShapeDtypeStruct((8, 32, 256), F32),
-        in_specs=whole(6),
-        out_specs=pl.BlockSpec(memory_space=pltpu.VMEM),
+        sectors[core, chip, half * 8 : half * 8 + 8, :] = piece[:, :256]
+    mine[...] = sectors[core_ref[0]]
+    other[...] = sectors[1 - core_ref[0]]
+
+
+def scatter_end(core, places, keep, came, start):
+    return pl.pallas_call(
+        scatter_end_kernel,
+        out_shape=[shape(8, 16, 256)] * 2,
+        in_specs=[scalar()] + whole(4),
+        out_specs=whole(2),
         scratch_shapes=[
             pltpu.VMEM((BLOCKS * 16, 256), F32),
             pltpu.VMEM((8, BLOCKS * 256 + 256), F32),
+            pltpu.VMEM((2, 8, 16, 256), F32),
         ],
+        compiler_params=params(6),
+        cost_estimate=cost(4.6),
+        name="scatter_end",
+    )(core, places, keep, came, start)
+
+
+SIZE_A, SIZE_C = 384, 256
+
+
+def split_kernel(bits, keep, came, own, send_a, send_b, send_c):
+    def columns(base, size, bit):
+        cols = slice(base + size * bit, base + size * bit + size)
+        return keep[:, cols] + came[:, cols]
+
+    for bit in range(2):
+
+        @pl.when(bits[0] == bit)
+        def _():
+            own[:, 0:384] = columns(0, SIZE_A, bit)
+            own[:, 384:768] = columns(768, SIZE_A, 1 - bit)
+            send_a[...] = columns(0, SIZE_A, 1 - bit)
+            send_b[...] = columns(768, SIZE_A, bit)
+
+        @pl.when(bits[1] == bit)
+        def _():
+            own[:, 768:1024] = columns(1536, SIZE_C, bit)
+            send_c[...] = columns(1536, SIZE_C, 1 - bit)
+
+
+def split(bits, keep, came):
+    return pl.pallas_call(
+        split_kernel,
+        out_shape=[shape(256, 1024), shape(256, SIZE_A), shape(256, SIZE_A), shape(256, SIZE_C)],
+        in_specs=[scalar()] + whole(2),
+        out_specs=whole(4),
         compiler_params=params(),
-        name="scatter",
-    )(wide, narrow, keep_wide, came_wide, keep_narrow, came_narrow)
-
-
-def join_kernel(keep, came, table, out):
-    out[0, :, : 4 * WIDTH] = keep[...] + came[...]
-    out[0, :, 4 * WIDTH :] = table[0]
-
-
-def join(keep, came, table):
-    block = pl.BlockSpec((32, 4 * WIDTH), lambda i: (i, 0))
+        cost_estimate=cost(1),
+        name="split",
+    )(bits, keep, came)
+
+
+def join_kernel(core_ref, own, came_a, came_b, came_c, table_keep, table_came, out):
+    for i in range(8):
+        rows = slice(i * 32, i * 32 + 32)
+        out[i, :, 0:384] = own[rows, 0:384] + came_a[rows, :]
+        out[i, :, 384:768] = own[rows, 384:768] + came_b[rows, :]
+        out[i, :, 768:1024] = own[rows, 768:1024] + came_c[rows, :]
+    first = core_ref[0] == 0
+    mine, other = table_keep[...], table_came[...]
+    out[:, 0:16, 1024:] = jnp.where(first, mine, other)
+    out[:, 16:32, 1024:] = jnp.where(first, other, mine)
+
+
+def join(core, *parts):
     return pl.pallas_call(
         join_kernel,
-        out_shape=jax.ShapeDtypeStruct((8, 32, 2304), F32),
-        grid=(8,),
-        in_specs=[block, block, pl.BlockSpec((1, 32, 256), lambda i: (i, 0, 0))],
-        out_specs=pl.BlockSpec((1, 32, 2304), lambda i: (i, 0, 0)),
+        out_shape=shape(8, 32, 1280),
+        in_specs=[scalar()] + whole(6),
+        out_specs=pl.BlockSpec(memory_space=pltpu.VMEM),
         compiler_params=params(),
+        cost_estimate=cost(1),
         name="join",
-    )(keep, came, table)
-
-
-def fold_lon_kernel(parts, out):
-    def rows(at):
-        total = parts[0, at : at + 8, :]
-        for i in range(1, 8):
-            total = total + parts[i, at : at + 8, :]
-        return total
-
-    for group in range(4):
-        total = rows(group * 8)
-        for col in range(4):
-            if col < 3:
-                out[group * 4 + col] = total[:, col * 640 : col * 640 + 640]
-            else:
-                out[group * 4 + col, :, :384] = total[:, 1920:2304]
-                out[group * 4 + col, :, 384:] = jnp.zeros((8, 256), F32)
+    )(core, *parts)
+
+
+def fold_lon_kernel(parts, out, total):
+    value = parts[0]
+    for i in range(1, 8):
+        value = value + parts[i]
+    total[...] = value
+    for p in range(16):
+        z, y = p // 2, p % 2
+        rank = (z // 2) * 2 + y
+        out[p, :, 0:768] = total[4 * rank : 4 * rank + 4, 0:768]
+        out[p, :, 768:1024] = total[4 * z : 4 * z + 4, 768:1024]
+        out[p, :, 1024:1152] = total[4 * z : 4 * z + 4, 1024 + 128 * y : 1152 + 128 * y]
 
 
 def fold_lon(parts):
     return pl.pallas_call(
         fold_lon_kernel,
-        out_shape=jax.ShapeDtypeStruct((16, 8, 640), F32),
+        out_shape=shape(16, 4, 1152),
         in_specs=whole(1),
         out_specs=pl.BlockSpec(memory_space=pltpu.VMEM),
+        scratch_shapes=[pltpu.VMEM((32, 1280), F32)],
         compiler_params=params(),
         name="fold_lon",
     )(parts)
 
 
-def fold_lat_kernel(parts, out):
-    total = parts[0]
-    for i in range(1, 16):
-        total = total + parts[i]
-    for i in range(32):
+def fold_lat_kernel(bits, parts, out):
+    odd, low = bits[0], bits[1]
+
+    def summed(sources, cols):
+        total = parts[sources[0], :, cols]
+        for source in sources[1:]:
+            total = total + parts[source, :, cols]
+        return total
+
+    same_z = [(2 * k + odd) * 2 + y for k in range(4) for y in range(2)]
+    same_y = [2 * z + low for z in range(8)]
+    total = jnp.concatenate(
+        [
+            summed(same_z, slice(0, 768)),
+            summed(same_y, slice(768, 1024)),
+            summed(list(range(16)), slice(1024, 1152)),
+        ],
+        axis=1,
+    )
+    for i in range(16):
         out[i] = total
 
 
-def fold_lat(parts):
+def fold_lat(bits, parts):
     return pl.pallas_call(
         fold_lat_kernel,
-        out_shape=jax.ShapeDtypeStruct((32, 8, 640), F32),
-        in_specs=whole(1),
+        out_shape=shape(16, 4, 1152),
+        in_specs=[scalar()] + whole(1),
         out_specs=pl.BlockSpec(memory_space=pltpu.VMEM),
         compiler_params=params(),
         name="fold_lat",
-    )(parts)
-
-
-def unpack_kernel(core_ref, parts, grad_in, grad_out, grad_bias):
-    core = core_ref[0]
-    for group in range(4):
-        rows = slice(group * 8, group * 8 + 8)
-        base = group * 8 + core
-        grad_in[rows, 0:640] = parts[base]
-        grad_in[rows, 640:1280] = parts[base + 2]
-        grad_in[rows, 1280:1536] = parts[base + 4, :, :256]
-        grad_out[rows, 0:384] = parts[base + 4, :, 256:]
-        grad_out[rows, 384:512] = parts[base + 6, :, :128]
-    for other in range(2):
-        rows = slice(other * 8, other * 8 + 8)
+    )(bits, parts)
+
+
+def unpack_kernel(parts, grad_in, grad_out, grad_bias, table):
+    for p in range(16):
+        z, y = p // 2, p % 2
+        odd = z % 2
+        rank = (z // 2) * 2 + y
+        rows = slice(4 * rank, 4 * rank + 4)
+        grad_in[rows, 384 * odd : 384 * odd + 384] = parts[p, :, 0:384]
+        start = 768 + 384 * (1 - odd)
+        grad_in[rows, start : start + 384] = parts[p, :, 384:768]
+        rows = slice(4 * z, 4 * z + 4)
+        grad_out[rows, 256 * y : 256 * y + 256] = parts[p, :, 768:1024]
+        table[rows, 128 * y : 128 * y + 128] = parts[p, :, 1024:1152]
+    for core in range(2):
         for half in range(2):
-            piece = parts[(half * 2 + core) * 8 + 6 + other, :, 128:384]
-            grad_bias[rows, half * HALF_SECTOR : half * HALF_SECTOR + HALF_SECTOR] = piece[
-                :, :HALF_SECTOR
-            ]
-
-
-def unpack(core, parts):
+            base = core * 16 + half * 8
+            grad_bias[core * 8 : core * 8 + 8, half * HALF_SECTOR : (half + 1) * HALF_SECTOR] = (
+                table[base : base + 8, :HALF_SECTOR]
+            )
+
+
+def unpack(parts):
     return pl.pallas_call(
         unpack_kernel,
-        out_shape=[
-            jax.ShapeDtypeStruct((32, 3 * WIDTH), F32),
-            jax.ShapeDtypeStruct((32, WIDTH), F32),
-            jax.ShapeDtypeStruct((HEADS, 2 * HALF_SECTOR), F32),
-        ],
-        in_specs=[scalar()] + whole(1),
+        out_shape=[shape(32, 3 * WIDTH), shape(32, WIDTH), shape(HEADS, 2 * HALF_SECTOR)],
+        in_specs=whole(1),
         out_specs=whole(3),
+        scratch_shapes=[pltpu.VMEM((32, 256), F32)],
         compiler_params=params(),
         name="unpack",
-    )(core, parts)
+    )(parts)
 
 
 def place_kernel(grad_out, own, left, below, corner, out):
@@ -550,6 +639,7 @@
     everything = LAT + LON
     lat = lax.axis_index(LAT)
     core = lax.axis_index("core").reshape(1)
+    bits = jnp.stack([lax.rem(lax.axis_index("z"), 2), lax.axis_index("y_lo")])
 
     def moves(down, right):
         return [
@@ -567,33 +657,31 @@
     quad3 = lax.ppermute(left, everything, moves(0, -1))
     quad0 = lax.ppermute(below, everything, moves(1, 0))
     quad1 = lax.ppermute(corner, everything, moves(1, -1))
-    bias, wide, narrow = lookup(core, bias_index, bias_table)
-    (
-        keep,
-        send,
-        keep_wide,
-        send_wide,
-        keep_narrow,
-        send_narrow,
-        grad0,
-        grad1,
-        grad2,
-        grad3,
-    ) = window(core, own, quad0, quad1, quad3, bias, in_weight, out_weight)
-    came_wide = lax.ppermute(send_wide, "core", swap)
-    came_narrow = lax.ppermute(send_narrow, "core", swap)
+    bias, places = lookup(core, bias_index, bias_table)
+    keep, send, keep_scores, send_scores, grad0, grad1, grad2, grad3 = window(
+        core, own, quad0, quad1, quad3, bias, in_weight, out_weight
+    )
+    came_scores = lax.ppermute(send_scores, "core", swap)
     came = lax.ppermute(send, "core", swap)
+    start = scatter_start(places, keep_scores, came_scores)
+    keep, start = lax.optimization_barrier((keep, start))
+    part, send_a, send_b, send_c = split(bits, keep, came)
+    came_a = lax.ppermute(send_a, "z", [(i, i ^ 1) for i in range(8)])
+    came_b = lax.ppermute(send_b, "z", [(i, ((i + 1) % 8 ^ 1) + 7 & 7) for i in range(8)])
+    came_c = lax.ppermute(send_c, "y_lo", swap)
+    part, start = lax.optimization_barrier((part, start))
+    mine, other = scatter_end(core, places, keep_scores, came_scores, start)
+    came_table = lax.ppermute(other, "core", swap)
     back_left = lax.ppermute(grad3, everything, moves(0, 1))
     back_below = lax.ppermute(grad0, everything, moves(-1, 0))
     back_corner = lax.ppermute(grad1, everything, moves(-1, 1))
-    table = scatter(wide, narrow, keep_wide, came_wide, keep_narrow, came_narrow)
+    joined = join(core, part, came_a, came_b, came_c, mine, came_table)
+    parts = lax.all_to_all(joined, ("x", "y_hi"), 0, 0)
+    parts, grad2 = lax.optimization_barrier((parts, grad2))
     grad_fields = place(grad_out, grad2, back_left, back_below, back_corner)
-    joined = join(keep, came, table)
-    joined, grad_fields = lax.optimization_barrier((joined, grad_fields))
-    parts = lax.all_to_all(joined, ("x", "y_hi"), 0, 0)
     parts = lax.all_to_all(fold_lon(parts), LAT, 0, 0)
-    parts = lax.all_to_all(fold_lat(parts), LAT + ("core",), 0, 0)
-    grad_in_weight, grad_out_weight, grad_bias = unpack(core, parts)
+    parts = lax.all_to_all(fold_lat(bits, parts), LAT, 0, 0)
+    grad_in_weight, grad_out_weight, grad_bias = unpack(parts)
     return jnp.transpose(grad_fields, (2, 0, 1, 3)), grad_in_weight, grad_out_weight, grad_bias.T
 
 

time: 146 us -> 129 us (0.88)
  blocking collectives: 79.3 us -> 38.1 us
  starting transfers between devices: 11.5 us -> 25.5 us
  waiting for transfers between devices: 6.99 us -> 14 us
  Pallas kernels: 37.8 us -> 42.1 us
    all_to_all x1 -> x0, blocking collectives: 24.9 us -> none  [body(): parts = lax.all_to_all(fold_lat(parts), LAT + ('core',), 0, 0)]
    all_to_all x1, blocking collectives: 33.5 us -> 21.8 us  [body(): parts = lax.all_to_all(joined, ('x', 'y_hi'), 0, 0)]
    ppermute x2 -> x5, waiting for transfers between devices: 0.01 us -> 8.47 us  [the longest x1 4.15 us: body(): came_scores = lax.ppermute(send_scores, 'core', swap)]
    ppermute x2 -> x5, starting transfers between devices: 0.5 us -> 8.01 us  [the longest x1 4.04 us: body(): lax.ppermute(send_b, 'z', [(i, ((i + 1) % 8 ^ 1) + 7 & 7) for i in range(...]
    all_to_all x0 -> x1, starting transfers between devices: none -> 4.98 us  [body(): parts = lax.all_to_all(fold_lat(bits, parts), LAT, 0, 0)]
    all_to_all x1, blocking collectives: 20.8 us -> 16.3 us  [body(): parts = lax.all_to_all(fold_lon(parts), LAT, 0, 0)]
    pallas_call x5 -> x7, Pallas kernels: 9.72 us -> 13 us  [the longest x1 4.63 us: scatter_end(): pl.pallas_call(scatter_end_kernel, out_shape=[shape(8, 16, 256)] * 2, in_...]
    ppermute x1, starting transfers between devices: 1.82 us -> 4.55 us  [body(): back_corner = lax.ppermute(grad1, everything, moves(-1, 1))]
  transfers between devices with their start and end apart: 9 -> 13, of which waited for: 2 -> 6; matrix products, arithmetic and copies ran while one was open for 0% -> 0% of each run, Pallas kernels for 15% -> 17%
where the time goes in v3:
time: 129 us
  Pallas kernels  42.1 us (33%)
  blocking collectives  38.1 us (30%)
  starting transfers between devices  25.5 us (20%)
  waiting for transfers between devices  14 us (11%)
  local copies, waits for them, and re-layouts  8.07 us (6%)
    all_to_all x1, blocking collectives, body(): parts = lax.all_to_all(joined, ('x', 'y_hi'), 0, 0)  21.8 us
    all_to_all x1, blocking collectives, body(): parts = lax.all_to_all(fold_lon(parts), LAT, 0, 0)  16.3 us
    pallas_call x1, Pallas kernels, window(): pl.pallas_call(main_kernel, out_shape=[shape(256, 4 * WIDTH), shape(256,...  15.3 us
    pallas_call x1, Pallas kernels, lookup(): pl.pallas_call(lookup_kernel, out_shape=[jax.ShapeDtypeStruct((TOKENS, HE...  12.7 us
    unnamed x44, local copies, waits for them, and re-layouts  8.07 us
    all_to_all x1, starting transfers between devices, body(): parts = lax.all_to_all(fold_lat(bits, parts), LAT, 0, 0)  4.98 us
    pallas_call x1, Pallas kernels, scatter_end(): pl.pallas_call(scatter_end_kernel, out_shape=[shape(8, 16, 256)] * 2, in_...  4.63 us
    ppermute x1, starting transfers between devices, body(): back_corner = lax.ppermute(grad1, everything, moves(-1, 1))  4.55 us
  transfers between devices with their start and end apart: 13, of which 6 were waited for; matrix products, arithmetic and copies ran while one was open for 0% of the time, Pallas kernels for 17%

profile of v3, /device:TPU:8, one launch (start us, length us, event | category | flops | bytes accessed | tf_op | source)
XLA Modules:
  0.0 128.7 jit_solution(16274960684751519649)
XLA Ops:
  0.6 0.0 copy-start
  0.7 1.0 copy-done
  1.6 1.0 copy-done.5
  2.6 0.7 copy-done.13
  3.3 0.2 pack.1
  3.5 0.0 copy-start.14
  3.5 0.7 copy-done.14
  4.2 1.8 %collective-permute-start = (f32[80,512]{1,0:T(8,128)S(1)}, f32[80,512]{1,0:T(8,128)S(1)}, u32[]{:S(2)}, u32[]{:S(2)}) collective-permute-start(f32[80,512]{1,0:T(8,128)S(1)} %get-tuple-element.34), channel_id=1, source_target_pairs={{0,16},{1,17},{2,18},{3,19},{4,20},{5,21},{6,22},{7,23},{8,24},{9,... | collective-permute-start | bytes 491528 | tf_op jit(solution)/shard_map/ppermute | solution.py:658
  6.0 3.8 %collective-permute-start.1 = (f32[80,512]{1,0:T(8,128)S(1)}, f32[80,512]{1,0:T(8,128)S(1)}, u32[]{:S(2)}, u32[]{:S(2)}) collective-permute-start(f32[80,512]{1,0:T(8,128)S(1)} %get-tuple-element.35), channel_id=1, source_target_pairs={{0,31},{1,16},{2,17},{3,18},{4,19},{5,20},{6,21},{7,22},{8,23},{9,... | collective-permute-start | bytes 491528 | tf_op jit(solution)/shard_map/ppermute | solution.py:659
  9.7 2.0 %collective-permute-start.2 = (f32[80,512]{1,0:T(8,128)S(1)}, f32[80,512]{1,0:T(8,128)S(1)}, u32[]{:S(2)}, u32[]{:S(2)}) collective-permute-start(f32[80,512]{1,0:T(8,128)S(1)} %get-tuple-element.36), channel_id=1, source_target_pairs={{0,15},{1,0},{2,1},{3,2},{4,3},{5,4},{6,5},{7,6},{8,7},{9,8},{10,9... | collective-permute-start | bytes 491528 | tf_op jit(solution)/shard_map/ppermute | solution.py:657
  11.8 0.0 copy-start.15
  11.8 12.7 %lookup.1 = (f32[144,16,144]{2,1,0:T(8,128)S(1)}, s32[162,128]{1,0:T(8,128)S(1)}) custom-call(s32[1]{0:T(128)} %bitcast.1.core_ref, s32[144,144]{1,0:T(8,128)S(1)} %copy-done.6, f32[16,6336]{1,0:T(8,128)S(1)} %bitcast.12), custom_call_target="tpu_custom_call" | custom-call | flops 12999999488 | tf_op jit(solution)/shard_map/lookup/pallas_call | solution.py:195
  24.5 0.0 copy-start.19
  24.5 0.0 collective-permute-done.quad0
  24.6 15.3 %window.1 = (f32[256,2048]{1,0:T(8,128)S(1)}, f32[256,2048]{1,0:T(8,128)}, f32[162,8,128]{2,1,0:T(8,128)S(1)}, f32[162,8,128]{2,1,0:T(8,128)S(1)}, f32[36,512]{1...) custom-call(s32[1]{0:T(128)} %bitcast.1.core_ref, f32[80,512]{1,0:T(8,128)S(1)} %copy-done.15, ...), custom_call_target="tpu_custom_call" | custom-call | flops 14000000000 | tf_op jit(solution)/shard_map/window/pallas_call | solution.py:342
  39.9 0.7 copy-done.7
  40.6 0.6 copy-done.9
  41.2 0.6 copy-done.11
  41.8 0.8 copy-done.16
  42.7 0.5 collective-permute-start.3
  43.2 0.1 pad_add_fusion.bits
  43.3 4.2 %collective-permute-done.3.came = f32[162,8,128]{2,1,0:T(8,128)S(1)} collective-permute-done((f32[162,8,128]{2,1,0:T(8,128)S(1)}, f32[162,8,128]{2,1,0:T(8,128)S(1)}, u32[]{:S(2)}, u32[]{:S(2)}) %collective-permute-start.3) | collective-permute-done | bytes 663584 | tf_op jit(solution)/shard_map/ppermute | solution.py:664
  47.4 1.1 copy-done.17
  48.5 0.9 copy-done.20
  49.4 4.3 %scatter_start.1.start = f32[400,256]{1,0:T(8,128)S(1)} custom-call(s32[162,128]{1,0:T(8,128)S(1)} %copy-done.20, f32[162,8,128]{2,1,0:T(8,128)S(1)} %copy-done.17, f32[162,8,128]{2,1,0:T(8,128)S(1)} %collective-permute-done.3.came), custom_call_target="tpu_custom_call" | custom-call | flops 4200000000 | tf_op jit(solution)/shard_map/scatter_start/pallas_call | solution.py:415
  53.7 0.0 copy-start.21
  53.7 1.9 %split.1 = (f32[256,1024]{1,0:T(8,128)S(1)}, f32[256,384]{1,0:T(8,128)S(1)}, f32[256,384]{1,0:T(8,128)S(1)}, f32[256,256]{1,0:T(8,128)S(1)}) custom-call(s32[2]{0:T(128)S(1)} %pad_add_fusion.bits, f32[256,2048]{1,0:T(8,128)S(1)} %get-tuple-element.42.keep, f32[256,2048]{1,0:T(8,128)} %collective-permute-done.4.came), custom_call_target="tpu_custom_call" | custom-call | flops 1000000000 | tf_op jit(solution)/shard_map/split/pallas_call | solution.py:487
  55.6 1.4 %collective-permute-start.7 = (f32[256,256]{1,0:T(8,128)S(1)}, f32[256,256]{1,0:T(8,128)S(1)}, u32[]{:S(2)}, u32[]{:S(2)}) collective-permute-start(f32[256,256]{1,0:T(8,128)S(1)} %get-tuple-element.49), channel_id=1, source_target_pairs={{0,16},{16,0},{1,17},{17,1},{2,18},{18,2},{3,19},{19,3},{4,20},{20... | collective-permute-start | bytes 786440 | tf_op jit(solution)/shard_map/ppermute | solution.py:671
  57.1 1.9 %collective-permute-start.5 = (f32[256,384]{1,0:T(8,128)S(1)}, f32[256,384]{1,0:T(8,128)S(1)}, u32[]{:S(2)}, u32[]{:S(2)}) collective-permute-start(f32[256,384]{1,0:T(8,128)S(1)} %get-tuple-element.47), channel_id=1, source_target_pairs={{0,32},{32,0},{64,96},{96,64},{128,160},{160,128},{192,224},{224,1... | collective-permute-start | bytes 1179656 | tf_op jit(solution)/shard_map/ppermute | solution.py:669
  59.0 4.0 %collective-permute-start.6 = (f32[256,384]{1,0:T(8,128)S(1)}, f32[256,384]{1,0:T(8,128)S(1)}, u32[]{:S(2)}, u32[]{:S(2)}) collective-permute-start(f32[256,384]{1,0:T(8,128)S(1)} %get-tuple-element.48), channel_id=1, source_target_pairs={{0,224},{32,64},{64,32},{96,128},{128,96},{160,192},{192,160},{224... | collective-permute-start | bytes 1179656 | tf_op jit(solution)/shard_map/ppermute | solution.py:670
  63.0 4.6 %scatter_end.1 = (f32[8,16,256]{2,1,0:T(8,128)S(1)}, f32[8,16,256]{2,1,0:T(8,128)S(1)}) custom-call(s32[1]{0:T(128)} %bitcast.1.core_ref, s32[162,128]{1,0:T(8,128)S(1)} %copy-done.21, f32[162,8,128]{2,1,0:T(8,128)S(1)} %copy-done.18, f32[162,8,128]{2,1,0:T(8,128)S(1)} %collective-permute-done.3.came, f32[400,256]{1,0:T(8,128)S(1)} %scatter_start.1.start), custom_call_target="tpu_custom_call" | custom-call | flops 4600000000 | tf_op jit(solution)/shard_map/scatter_end/pallas_call | solution.py:447
  67.7 0.1 collective-permute-start.8
  67.8 1.3 %collective-permute-done.8.table_came = f32[8,16,256]{2,1,0:T(8,128)S(1)} collective-permute-done((f32[8,16,256]{2,1,0:T(8,128)S(1)}, f32[8,16,256]{2,1,0:T(8,128)S(1)}, u32[]{:S(2)}, u32[]{:S(2)}) %collective-permute-start.8) | collective-permute-done | bytes 131104 | tf_op jit(solution)/shard_map/ppermute | solution.py:674
  69.1 3.0 %collective-permute-done.6.came_b = f32[256,384]{1,0:T(8,128)S(1)} collective-permute-done((f32[256,384]{1,0:T(8,128)S(1)}, f32[256,384]{1,0:T(8,128)S(1)}, u32[]{:S(2)}, u32[]{:S(2)}) %collective-permute-start.6) | collective-permute-done | bytes 393248 | tf_op jit(solution)/shard_map/ppermute | solution.py:670
  72.1 0.1 join.1
  72.2 21.8 %all_to_all.15.parts = f32[8,32,1280]{2,1,0:T(8,128)S(1)} all-to-all(f32[8,32,1280]{2,1,0:T(8,128)S(1)} %join.1), channel_id=1, replica_groups=mesh['z'=8,'y_lo'=2,'x'=4,'y_hi'=2,'core'=2] {'x','y_hi'}, dimensions={0} | all-to-all | bytes 2621440 | tf_op jit(solution)/shard_map/all_to_all | solution.py:679
  94.0 0.1 fold_lon.1
  94.1 16.3 %all_to_all.16.parts = f32[16,4,1152]{2,1,0:T(4,128)S(1)} all-to-all(f32[16,4,1152]{2,1,0:T(4,128)S(1)} %fold_lon.1), channel_id=1, replica_groups=mesh['z'=8,'y_lo'=2,'x'=4,'y_hi'=2,'core'=2] {'z','y_lo'}, dimensions={0} | all-to-all | bytes 589824 | tf_op jit(solution)/shard_map/all_to_all | solution.py:682
  110.4 1.3 fold_lat.1
  111.7 5.0 %all-to-all-start.2 = ((f32[16,4,1152]{2,1,0:T(4,128)}), f32[16,4,1152]{2,1,0:T(4,128)S(1)}, u32[]{:S(2)}, u32[]{:S(2)}) async-start(f32[16,4,1152]{2,1,0:T(4,128)} %fold_lat.1), calls=%async_computation.2 | async-start | bytes 589824 | tf_op jit(solution)/shard_map/all_to_all | solution.py:683
  116.7 0.1 collective-permute-start.9
  116.8 0.3 collective-permute-start.10
  117.1 4.5 %collective-permute-start.11 = (f32[36,512]{1,0:T(8,128)S(1)}, f32[36,512]{1,0:T(8,128)S(1)}, u32[]{:S(2)}, u32[]{:S(2)}) collective-permute-start(f32[36,512]{1,0:T(8,128)S(1)} %copy-done.8), channel_id=1, source_target_pairs={{0,241},{1,242},{2,243},{3,244},{4,245},{5,246},{6,247},{7,248},{8... | collective-permute-start | bytes 221192 | tf_op jit(solution)/shard_map/ppermute | solution.py:677
  121.7 3.1 %collective-permute-done.9.left = f32[36,512]{1,0:T(8,128)S(1)} collective-permute-done((f32[36,512]{1,0:T(8,128)S(1)}, f32[36,512]{1,0:T(8,128)S(1)}, u32[]{:S(2)}, u32[]{:S(2)}) %collective-permute-start.9) | collective-permute-done | bytes 73760 | tf_op jit(solution)/shard_map/ppermute | solution.py:675
  124.7 0.4 collective-permute-done.10.below
  125.1 2.1 %collective-permute-done.11.corner = f32[36,512]{1,0:T(8,128)S(1)} collective-permute-done((f32[36,512]{1,0:T(8,128)S(1)}, f32[36,512]{1,0:T(8,128)S(1)}, u32[]{:S(2)}, u32[]{:S(2)}) %collective-permute-start.11) | collective-permute-done | bytes 73760 | tf_op jit(solution)/shard_map/ppermute | solution.py:677
  127.2 0.8 place.1
  128.0 0.7 unpack.1
  (36 shorter events, 0.1 us)
Async XLA Ops:
  0.6 1.0 copy-start
  1.6 1.0 copy-start.5
  2.6 0.7 copy-start.13
  3.3 8.5 %copy-start.4 = (f32[6336,16]{0,1:T(8,128)S(1)}, f32[6336,16]{0,1:T(8,128)}, u32[]{:S(2)}) copy-start(f32[6336,16]{0,1:T(8,128)} %param.11) | copy-start | bytes 1216516
  3.3 8.5 %copy-start.6 = (s32[144,144]{1,0:T(8,128)S(1)}, s32[144,144]{1,0:T(8,128)}, u32[]{:S(2)}) copy-start(s32[144,144]{1,0:T(8,128)} %index.1) | copy-start | bytes 248836
  3.5 0.7 copy-start.14
  4.2 20.3 %collective-permute-start = (f32[80,512]{1,0:T(8,128)S(1)}, f32[80,512]{1,0:T(8,128)S(1)}, u32[]{:S(2)}, u32[]{:S(2)}) collective-permute-start(f32[80,512]{1,0:T(8,128)S(1)} %get-tuple-element.34), channel_id=1, source_target_pairs={{0,16},{1,17},{2,18},{3,19},{4,20},{5,21},{6,22},{7,23},{8,24},{9,... | collective-permute-start | bytes 491528 | tf_op jit(solution)/shard_map/ppermute | solution.py:658
  6.0 18.6 %collective-permute-start.1 = (f32[80,512]{1,0:T(8,128)S(1)}, f32[80,512]{1,0:T(8,128)S(1)}, u32[]{:S(2)}, u32[]{:S(2)}) collective-permute-start(f32[80,512]{1,0:T(8,128)S(1)} %get-tuple-element.35), channel_id=1, source_target_pairs={{0,31},{1,16},{2,17},{3,18},{4,19},{5,20},{6,21},{7,22},{8,23},{9,... | collective-permute-start | bytes 491528 | tf_op jit(solution)/shard_map/ppermute | solution.py:659
  9.7 14.8 %collective-permute-start.2 = (f32[80,512]{1,0:T(8,128)S(1)}, f32[80,512]{1,0:T(8,128)S(1)}, u32[]{:S(2)}, u32[]{:S(2)}) collective-permute-start(f32[80,512]{1,0:T(8,128)S(1)} %get-tuple-element.36), channel_id=1, source_target_pairs={{0,15},{1,0},{2,1},{3,2},{4,3},{5,4},{6,5},{7,6},{8,7},{9,8},{10,9... | collective-permute-start | bytes 491528 | tf_op jit(solution)/shard_map/ppermute | solution.py:657
  11.8 12.8 %copy-start.2 = (f32[512,1536]{1,0:T(8,128)S(1)}, f32[512,1536]{1,0:T(8,128)}, u32[]{:S(2)}) copy-start(f32[512,1536]{1,0:T(8,128)} %in_weight.1) | copy-start | bytes 9437188
  11.8 12.8 %copy-start.3 = (f32[512,512]{1,0:T(8,128)S(1)}, f32[512,512]{1,0:T(8,128)}, u32[]{:S(2)}) copy-start(f32[512,512]{1,0:T(8,128)} %out_weight.1) | copy-start | bytes 3145732
  11.8 12.8 %copy-start.15 = (f32[80,512]{1,0:T(8,128)S(1)}, f32[80,512]{1,0:T(8,128)}, u32[]{:S(2)}) copy-start(f32[80,512]{1,0:T(8,128)} %copy-done.14) | copy-start | bytes 491524
  24.5 15.4 %copy-start.19 = (s32[162,128]{1,0:T(8,128)}, s32[162,128]{1,0:T(8,128)S(1)}, u32[]{:S(2)}) copy-start(s32[162,128]{1,0:T(8,128)S(1)} %get-tuple-element.39.places) | copy-start | bytes 248836
  39.9 0.7 copy-start.7
  40.6 0.6 copy-start.9
  41.2 0.6 copy-start.11
  41.8 0.8 copy-start.16
  42.7 11.0 %collective-permute-start.4 = (f32[256,2048]{1,0:T(8,128)}, f32[256,2048]{1,0:T(8,128)}, u32[]{:S(2)}, u32[]{:S(2)}) collective-permute-start(f32[256,2048]{1,0:T(8,128)} %get-tuple-element.43), channel_id=1, source_target_pairs={{0,1},{1,0},{2,3},{3,2},{4,5},{5,4},{6,7},{7,6},{8,9},{9,8},{10,11... | collective-permute-start | bytes 6291464 | tf_op jit(solution)/shard_map/ppermute | solution.py:665
  42.7 4.7 %collective-permute-start.3 = (f32[162,8,128]{2,1,0:T(8,128)S(1)}, f32[162,8,128]{2,1,0:T(8,128)S(1)}, u32[]{:S(2)}, u32[]{:S(2)}) collective-permute-start(f32[162,8,128]{2,1,0:T(8,128)S(1)} %get-tuple-element.41), channel_id=1, source_target_pairs={{0,1},{1,0},{2,3},{3,2},{4,5},{5,4},{6,7},{7,6},{8,9},{9,8},{10,11... | collective-permute-start | bytes 1990664 | tf_op jit(solution)/shard_map/ppermute | solution.py:664
  47.4 1.1 copy-start.17
  48.5 0.9 copy-start.20
  53.7 9.4 %copy-start.18 = (f32[162,8,128]{2,1,0:T(8,128)S(1)}, f32[162,8,128]{2,1,0:T(8,128)}, u32[]{:S(2)}) copy-start(f32[162,8,128]{2,1,0:T(8,128)} %copy-done.16) | copy-start | bytes 1990660
  53.7 9.4 %copy-start.21 = (s32[162,128]{1,0:T(8,128)S(1)}, s32[162,128]{1,0:T(8,128)}, u32[]{:S(2)}) copy-start(s32[162,128]{1,0:T(8,128)} %copy-done.19) | copy-start | bytes 248836
  55.6 13.5 %collective-permute-start.7 = (f32[256,256]{1,0:T(8,128)S(1)}, f32[256,256]{1,0:T(8,128)S(1)}, u32[]{:S(2)}, u32[]{:S(2)}) collective-permute-start(f32[256,256]{1,0:T(8,128)S(1)} %get-tuple-element.49), channel_id=1, source_target_pairs={{0,16},{16,0},{1,17},{17,1},{2,18},{18,2},{3,19},{19,3},{4,20},{20... | collective-permute-start | bytes 786440 | tf_op jit(solution)/shard_map/ppermute | solution.py:671
  57.1 12.1 %collective-permute-start.5 = (f32[256,384]{1,0:T(8,128)S(1)}, f32[256,384]{1,0:T(8,128)S(1)}, u32[]{:S(2)}, u32[]{:S(2)}) collective-permute-start(f32[256,384]{1,0:T(8,128)S(1)} %get-tuple-element.47), channel_id=1, source_target_pairs={{0,32},{32,0},{64,96},{96,64},{128,160},{160,128},{192,224},{224,1... | collective-permute-start | bytes 1179656 | tf_op jit(solution)/shard_map/ppermute | solution.py:669
  59.0 13.1 %collective-permute-start.6 = (f32[256,384]{1,0:T(8,128)S(1)}, f32[256,384]{1,0:T(8,128)S(1)}, u32[]{:S(2)}, u32[]{:S(2)}) collective-permute-start(f32[256,384]{1,0:T(8,128)S(1)} %get-tuple-element.48), channel_id=1, source_target_pairs={{0,224},{32,64},{64,32},{96,128},{128,96},{160,192},{192,160},{224... | collective-permute-start | bytes 1179656 | tf_op jit(solution)/shard_map/ppermute | solution.py:670
  67.7 1.4 %collective-permute-start.8 = (f32[8,16,256]{2,1,0:T(8,128)S(1)}, f32[8,16,256]{2,1,0:T(8,128)S(1)}, u32[]{:S(2)}, u32[]{:S(2)}) collective-permute-start(f32[8,16,256]{2,1,0:T(8,128)S(1)} %get-tuple-element.52), channel_id=1, source_target_pairs={{0,1},{1,0},{2,3},{3,2},{4,5},{5,4},{6,7},{7,6},{8,9},{9,8},{10,11... | collective-permute-start | bytes 393224 | tf_op jit(solution)/shard_map/ppermute | solution.py:674
  94.0 22.7 %copy-start.12 = (f32[36,512]{1,0:T(8,128)S(1)}, f32[36,512]{1,0:T(8,128)}, u32[]{:S(2)}) copy-start(f32[36,512]{1,0:T(8,128)} %copy-done.11) | copy-start | bytes 221188
  94.0 22.8 %copy-start.10 = (f32[36,512]{1,0:T(8,128)S(1)}, f32[36,512]{1,0:T(8,128)}, u32[]{:S(2)}) copy-start(f32[36,512]{1,0:T(8,128)} %copy-done.9) | copy-start | bytes 221188
  94.0 23.1 %copy-start.8 = (f32[36,512]{1,0:T(8,128)S(1)}, f32[36,512]{1,0:T(8,128)}, u32[]{:S(2)}) copy-start(f32[36,512]{1,0:T(8,128)} %copy-done.7) | copy-start | bytes 221188
  94.0 33.2 %copy-start.1 = (f32[2,12,6,512]{3,0,2,1:T(2,128)S(1)}, f32[2,12,6,512]{3,0,2,1:T(2,128)}, u32[]{:S(2)}) copy-start(f32[2,12,6,512]{3,0,2,1:T(2,128)} %param.8) | copy-start | bytes 884740
  111.7 16.3 %all-to-all-start.2 = ((f32[16,4,1152]{2,1,0:T(4,128)}), f32[16,4,1152]{2,1,0:T(4,128)S(1)}, u32[]{:S(2)}, u32[]{:S(2)}) async-start(f32[16,4,1152]{2,1,0:T(4,128)} %fold_lat.1), calls=%async_computation.2 | async-start | bytes 589824 | tf_op jit(solution)/shard_map/all_to_all | solution.py:683
  116.7 8.0 %collective-permute-start.9 = (f32[36,512]{1,0:T(8,128)S(1)}, f32[36,512]{1,0:T(8,128)S(1)}, u32[]{:S(2)}, u32[]{:S(2)}) collective-permute-start(f32[36,512]{1,0:T(8,128)S(1)} %copy-done.12), channel_id=1, source_target_pairs={{0,1},{1,2},{2,3},{3,4},{4,5},{5,6},{6,7},{7,8},{8,9},{9,10},{10,1... | collective-permute-start | bytes 221192 | tf_op jit(solution)/shard_map/ppermute | solution.py:675
  116.8 8.3 %collective-permute-start.10 = (f32[36,512]{1,0:T(8,128)S(1)}, f32[36,512]{1,0:T(8,128)S(1)}, u32[]{:S(2)}, u32[]{:S(2)}) collective-permute-start(f32[36,512]{1,0:T(8,128)S(1)} %copy-done.10), channel_id=1, source_target_pairs={{0,240},{1,241},{2,242},{3,243},{4,244},{5,245},{6,246},{7,247},{8... | collective-permute-start | bytes 221192 | tf_op jit(solution)/shard_map/ppermute | solution.py:676
  117.1 10.1 %collective-permute-start.11 = (f32[36,512]{1,0:T(8,128)S(1)}, f32[36,512]{1,0:T(8,128)S(1)}, u32[]{:S(2)}, u32[]{:S(2)}) collective-permute-start(f32[36,512]{1,0:T(8,128)S(1)} %copy-done.8), channel_id=1, source_target_pairs={{0,241},{1,242},{2,243},{3,244},{4,245},{5,246},{6,247},{7,248},{8... | collective-permute-start | bytes 221192 | tf_op jit(solution)/shard_map/ppermute | solution.py:677

commit v4 on v3

--- a/solution.py
+++ b/solution.py
@@ -14,7 +14,7 @@
 BIAS_ROWS = 6336
 HALF_SECTOR = 198
 BLOCKS = 25
-PACK_MIB = 4
+PACK_MIB = 56
 ROWS = 162
 FACTOR = HEAD_DIM ** (-0.5)
 F32 = jnp.float32
@@ -22,7 +22,7 @@
 MEGA = 1 << 20
 
 
-def params(mib=8):
+def params(mib=16):
     return pltpu.CompilerParams(vmem_limit_bytes=mib * MEGA)
 
 
@@ -201,7 +201,7 @@
         in_specs=[scalar()] + whole(2),
         out_specs=whole(2),
         scratch_shapes=[pltpu.VMEM((BLOCKS * 32, 256), BF16)],
-        compiler_params=params(6),
+        compiler_params=params(),
         cost_estimate=cost(13),
         name="lookup",
     )(core, bias_index, bias_table.T)
@@ -260,45 +260,52 @@
     halves_cotangent = halves(cotangent[...])
     gatt[...] = dot3(halves(out_weight[...]), halves_cotangent, NT)
 
-    def one_head(head, slot):
-        at = pl.multiple_of(head * HEAD_DIM, HEAD_DIM)
-        qh, ql = halves(proj[pl.ds(at, HEAD_DIM), :] * FACTOR)
-        kh, kl = halves(proj[pl.ds(at + WIDTH, HEAD_DIM), :])
-        vh, vl = halves(proj[pl.ds(at + 2 * WIDTH, HEAD_DIM), :])
-        gh, gl = halves(gatt[pl.ds(at, HEAD_DIM), :])
-
-        def stacked(*parts):
-            return jnp.concatenate(parts, axis=0)
-
-        scores = dot(stacked(qh, qh, ql), stacked(kh, kl, kh), TN) + bias[:, slot, :]
-        scores = jnp.where(allowed, scores, -1000000000.0)
-        peak = jnp.max(scores, axis=1, keepdims=True)
-        exponent = jnp.exp(scores - peak)
-        probs = exponent * (1.0 / jnp.sum(exponent, axis=1, keepdims=True))
-        grad_probs = dot(stacked(gh, gh, gl), stacked(vh, vl, vh), TN)
-        inner = jnp.sum(grad_probs * probs, axis=1, keepdims=True)
-        grad_scores = probs * (grad_probs - inner)
-        ph, plow = halves(probs)
-        sh, sl = halves(grad_scores)
-
-        def product(high, low, right_high, right_low, dims):
-            both = dot(stacked(high, low), right_high, dims)
-            return both[:HEAD_DIM] + (both[HEAD_DIM:] + dot(high, right_low, dims))
-
-        att[pl.ds(at, HEAD_DIM), :] = product(vh, vl, ph, plow, NT)
-        gproj[pl.ds(at + 2 * WIDTH, HEAD_DIM), :] = product(gh, gl, ph, plow, NN)
-        gproj[pl.ds(at, HEAD_DIM), :] = product(kh, kl, sh, sl, NT) * FACTOR
-        gproj[pl.ds(at + WIDTH, HEAD_DIM), :] = product(qh, ql, sh, sl, NN)
-        return grad_scores
+    def stacked(*parts):
+        return jnp.concatenate(parts, axis=0)
+
+    def product(high, low, right_high, right_low, dims):
+        both = dot(stacked(high, low), right_high, dims)
+        return both[:HEAD_DIM] + (both[HEAD_DIM:] + dot(high, right_low, dims))
+
+    def some_heads(heads):
+        ats = [pl.multiple_of(head * HEAD_DIM, HEAD_DIM) for head, _ in heads]
+        q = [halves(proj[pl.ds(at, HEAD_DIM), :] * FACTOR) for at in ats]
+        k = [halves(proj[pl.ds(at + WIDTH, HEAD_DIM), :]) for at in ats]
+        v = [halves(proj[pl.ds(at + 2 * WIDTH, HEAD_DIM), :]) for at in ats]
+        g = [halves(gatt[pl.ds(at, HEAD_DIM), :]) for at in ats]
+
+        def outer(left, right):
+            return dot(
+                stacked(left[0], left[0], left[1]), stacked(right[0], right[1], right[0]), TN
+            )
+
+        scores = [outer(q[i], k[i]) + bias[:, slot, :] for i, (_, slot) in enumerate(heads)]
+        grad_probs = [outer(g[i], v[i]) for i in range(len(heads))]
+        scores = [jnp.where(allowed, x, -1000000000.0) for x in scores]
+        exponent = [jnp.exp(x - jnp.max(x, axis=1, keepdims=True)) for x in scores]
+        probs = [x * (1.0 / jnp.sum(x, axis=1, keepdims=True)) for x in exponent]
+        p = [halves(x) for x in probs]
+        for i, at in enumerate(ats):
+            att[pl.ds(at, HEAD_DIM), :] = product(*v[i], *p[i], NT)
+            gproj[pl.ds(at + 2 * WIDTH, HEAD_DIM), :] = product(*g[i], *p[i], NN)
+        grad_scores = [
+            x * (y - jnp.sum(x * y, axis=1, keepdims=True)) for x, y in zip(probs, grad_probs)
+        ]
+        s = [halves(x) for x in grad_scores]
+        for i, at in enumerate(ats):
+            gproj[pl.ds(at, HEAD_DIM), :] = product(*k[i], *s[i], NT) * FACTOR
+            gproj[pl.ds(at + WIDTH, HEAD_DIM), :] = product(*q[i], *s[i], NN)
+        for i, (_, slot) in enumerate(heads):
+            target = send_scores if slot < 8 else keep_scores
+            target[0:TOKENS, slot % 8, :] = grad_scores[i][:, :128]
+            tails[:, slot, 0:16] = grad_scores[i][:, 128:]
 
     tails[...] = jnp.zeros_like(tails)
-    for slot in range(8):
-        grad_scores = one_head((1 - core) * 8 + slot, slot)
-        send_scores[0:TOKENS, slot, :] = grad_scores[:, :128]
-        tails[:, slot, 0:16] = grad_scores[:, 128:]
-        grad_scores = one_head(core * 8 + slot, 8 + slot)
-        keep_scores[0:TOKENS, slot, :] = grad_scores[:, :128]
-        tails[:, 8 + slot, 0:16] = grad_scores[:, 128:]
+    order = [((1 - core) * 8 + slot, slot) for slot in range(8)]
+    order += [(core * 8 + slot, 8 + slot) for slot in range(8)]
+    for first in range(0, 16, 4):
+        some_heads(order[first : first + 4])
+
     for i in range(18):
         total = tails[8 * i]
         for j in range(1, 8):
@@ -363,7 +370,7 @@
             pltpu.VMEM((WIDTH, TOKENS), F32),
             pltpu.VMEM((TOKENS, HEADS, 128), F32),
         ],
-        compiler_params=params(14),
+        compiler_params=params(26),
         cost_estimate=cost(14),
         name="window",
     )(core, own, quad0, quad1, quad3, bias, in_weight, out_weight)
@@ -417,7 +424,7 @@
         out_shape=shape(BLOCKS * 16, 256),
         in_specs=whole(3),
         out_specs=pl.BlockSpec(memory_space=pltpu.VMEM),
-        compiler_params=params(6),
+        compiler_params=params(),
         cost_estimate=cost(4.2),
         name="scatter_start",
     )(places, keep, came)
@@ -454,7 +461,7 @@
             pltpu.VMEM((8, BLOCKS * 256 + 256), F32),
             pltpu.VMEM((2, 8, 16, 256), F32),
         ],
-        compiler_params=params(6),
+        compiler_params=params(),
         cost_estimate=cost(4.6),
         name="scatter_end",
     )(core, places, keep, came, start)
@@ -663,22 +670,25 @@
     )
     came_scores = lax.ppermute(send_scores, "core", swap)
     came = lax.ppermute(send, "core", swap)
+    back = (
+        lax.ppermute(grad3, everything, moves(0, 1)),
+        lax.ppermute(grad0, everything, moves(-1, 0)),
+        lax.ppermute(grad1, everything, moves(-1, 1)),
+    )
     start = scatter_start(places, keep_scores, came_scores)
     keep, start = lax.optimization_barrier((keep, start))
     part, send_a, send_b, send_c = split(bits, keep, came)
     came_a = lax.ppermute(send_a, "z", [(i, i ^ 1) for i in range(8)])
     came_b = lax.ppermute(send_b, "z", [(i, ((i + 1) % 8 ^ 1) + 7 & 7) for i in range(8)])
     came_c = lax.ppermute(send_c, "y_lo", swap)
-    part, start = lax.optimization_barrier((part, start))
+    part, start, back = lax.optimization_barrier((part, start, back))
     mine, other = scatter_end(core, places, keep_scores, came_scores, start)
     came_table = lax.ppermute(other, "core", swap)
-    back_left = lax.ppermute(grad3, everything, moves(0, 1))
-    back_below = lax.ppermute(grad0, everything, moves(-1, 0))
-    back_corner = lax.ppermute(grad1, everything, moves(-1, 1))
+    mine, grad2 = lax.optimization_barrier((mine, grad2))
+    grad_fields = place(grad_out, grad2, *back)
+    part, grad_fields = lax.optimization_barrier((part, grad_fields))
     joined = join(core, part, came_a, came_b, came_c, mine, came_table)
     parts = lax.all_to_all(joined, ("x", "y_hi"), 0, 0)
-    parts, grad2 = lax.optimization_barrier((parts, grad2))
-    grad_fields = place(grad_out, grad2, back_left, back_below, back_corner)
     parts = lax.all_to_all(fold_lon(parts), LAT, 0, 0)
     parts = lax.all_to_all(fold_lat(bits, parts), LAT, 0, 0)
     grad_in_weight, grad_out_weight, grad_bias = unpack(parts)

time: 129 us -> 121 us (0.938)
  blocking collectives: 38.1 us -> 52.4 us
  waiting for transfers between devices: 14 us -> 3.97 us
  starting transfers between devices: 25.5 us -> 18.8 us
  local copies, waits for them, and re-layouts: 8.07 us -> 3.54 us
    all_to_all x0 -> x1, blocking collectives: none -> 13 us  [body(): parts = lax.all_to_all(fold_lat(bits, parts), LAT, 0, 0)]
    ppermute x3, waiting for transfers between devices: 5.54 us -> 0.01 us  [the longest x1 0.01 us: body(): lax.ppermute(grad0, everything, moves(-1, 0))]
    all_to_all x1 -> x0, starting transfers between devices: 4.98 us -> none  [body(): parts = lax.all_to_all(fold_lat(bits, parts), LAT, 0, 0)]
    unnamed x44 -> x30, local copies, waits for them, and re-layouts: 8.07 us -> 3.54 us
    ppermute x1, waiting for transfers between devices: 4.15 us -> 0.66 us  [body(): came_scores = lax.ppermute(send_scores, 'core', swap)]
    pallas_call x1, Pallas kernels: 15.3 us -> 13.1 us  [window(): pl.pallas_call(main_kernel, out_shape=[shape(256, 4 * WIDTH), shape(256,...]
    pallas_call x1, Pallas kernels: 0.23 us -> 2.13 us  [pack(): pl.pallas_call(pack_kernel, out_shape=[shape] * 4, in_specs=[scalar()] +...]
    all_to_all x1, blocking collectives: 16.3 us -> 17.8 us  [body(): parts = lax.all_to_all(fold_lon(parts), LAT, 0, 0)]
  transfers between devices with their start and end apart: 13 -> 12, of which waited for: 6 -> 3; matrix products, arithmetic and copies ran while one was open for 0% -> 0% of each run, Pallas kernels for 17% -> 20%
where the time goes in v4:
time: 121 us
  blocking collectives  52.4 us (43%)
  Pallas kernels  41.1 us (34%)
  starting transfers between devices  18.8 us (16%)
  waiting for transfers between devices  3.97 us (3%)
  local copies, waits for them, and re-layouts  3.54 us (3%)
    all_to_all x1, blocking collectives, body(): parts = lax.all_to_all(joined, ('x', 'y_hi'), 0, 0)  21.6 us
    all_to_all x1, blocking collectives, body(): parts = lax.all_to_all(fold_lon(parts), LAT, 0, 0)  17.8 us
    pallas_call x1, Pallas kernels, window(): pl.pallas_call(main_kernel, out_shape=[shape(256, 4 * WIDTH), shape(256,...  13.1 us
    all_to_all x1, blocking collectives, body(): parts = lax.all_to_all(fold_lat(bits, parts), LAT, 0, 0)  13 us
    pallas_call x1, Pallas kernels, lookup(): pl.pallas_call(lookup_kernel, out_shape=[jax.ShapeDtypeStruct((TOKENS, HE...  12.7 us
    pallas_call x1, Pallas kernels, scatter_end(): pl.pallas_call(scatter_end_kernel, out_shape=[shape(8, 16, 256)] * 2, in_...  4.65 us
    pallas_call x1, Pallas kernels, scatter_start(): pl.pallas_call(scatter_start_kernel, out_shape=shape(BLOCKS * 16, 256), i...  4.26 us
    ppermute x1, starting transfers between devices, body(): lax.ppermute(send_b, 'z', [(i, ((i + 1) % 8 ^ 1) + 7 & 7) for i in range(...  4.04 us
  transfers between devices with their start and end apart: 12, of which 3 were waited for; matrix products, arithmetic and copies ran while one was open for 0% of the time, Pallas kernels for 20%

profile of v4, /device:TPU:8, one launch (start us, length us, event | category | flops | bytes accessed | tf_op | source)
XLA Modules:
  0.0 120.8 jit_solution(12618053776218211399)
XLA Ops:
  0.6 0.0 copy-start.3
  0.6 0.0 copy-start.4
  0.7 2.1 %pack.1 = (f32[80,512]{1,0:T(8,128)}, f32[80,512]{1,0:T(8,128)}, f32[80,512]{1,0:T(8,128)}, f32[80,512]{1,0:T(8,128)}) custom-call(s32[1]{0:T(128)} %bitcast.3.last, f32[12,6,2,512]{3,2,1,0:T(2,128)} %bitcast.14, f32[12,6,2,512]{3,2,1,0:T(2,128)} %bitcast.10, s32[6,2,12]{2,1,0:T(2,128)} %bitcast.16), custom_call_target="tpu_custom_call" | custom-call | flops 1000000000 | tf_op jit(solution)/shard_map/pack/pallas_call | solution.py:114
  2.8 1.8 %collective-permute-start = (f32[80,512]{1,0:T(8,128)}, f32[80,512]{1,0:T(8,128)S(1)}, u32[]{:S(2)}, u32[]{:S(2)}) collective-permute-start(f32[80,512]{1,0:T(8,128)} %get-tuple-element.39), channel_id=1, source_target_pairs={{0,16},{1,17},{2,18},{3,19},{4,20},{5,21},{6,22},{7,23},{8,24},{9,... | collective-permute-start | bytes 491528 | tf_op jit(solution)/shard_map/ppermute | solution.py:665
  4.6 3.8 %collective-permute-start.1 = (f32[80,512]{1,0:T(8,128)}, f32[80,512]{1,0:T(8,128)S(1)}, u32[]{:S(2)}, u32[]{:S(2)}) collective-permute-start(f32[80,512]{1,0:T(8,128)} %get-tuple-element.40), channel_id=1, source_target_pairs={{0,31},{1,16},{2,17},{3,18},{4,19},{5,20},{6,21},{7,22},{8,23},{9,... | collective-permute-start | bytes 491528 | tf_op jit(solution)/shard_map/ppermute | solution.py:666
  8.4 2.0 %collective-permute-start.2 = (f32[80,512]{1,0:T(8,128)}, f32[80,512]{1,0:T(8,128)S(1)}, u32[]{:S(2)}, u32[]{:S(2)}) collective-permute-start(f32[80,512]{1,0:T(8,128)} %get-tuple-element.41), channel_id=1, source_target_pairs={{0,15},{1,0},{2,1},{3,2},{4,3},{5,4},{6,5},{7,6},{8,7},{9,8},{10,9... | collective-permute-start | bytes 491528 | tf_op jit(solution)/shard_map/ppermute | solution.py:664
  10.4 0.0 copy-start.8
  10.4 12.7 %lookup.1 = (f32[144,16,144]{2,1,0:T(8,128)S(1)}, s32[162,128]{1,0:T(8,128)S(1)}) custom-call(s32[1]{0:T(128)} %bitcast.2.core_ref, s32[144,144]{1,0:T(8,128)S(1)} %copy-done.4, f32[16,6336]{1,0:T(8,128)S(1)} %bitcast.12), custom_call_target="tpu_custom_call" | custom-call | flops 12999999488 | tf_op jit(solution)/shard_map/lookup/pallas_call | solution.py:195
  23.1 0.0 collective-permute-done.quad0
  23.1 0.0 collective-permute-done.1.quad1
  23.1 0.0 collective-permute-done.2.quad3
  23.2 13.1 %window.1 = (f32[256,2048]{1,0:T(8,128)S(1)}, f32[256,2048]{1,0:T(8,128)}, f32[162,8,128]{2,1,0:T(8,128)S(1)}, f32[162,8,128]{2,1,0:T(8,128)S(1)}, f32[36,512]{1...) custom-call(s32[1]{0:T(128)} %bitcast.2.core_ref, f32[80,512]{1,0:T(8,128)S(1)} %copy-done.8, ...), custom_call_target="tpu_custom_call" | custom-call | flops 14000000000 | tf_op jit(solution)/shard_map/window/pallas_call | solution.py:349
  36.3 0.8 copy-done.9
  37.2 0.0 collective-permute-start.4
  37.2 0.6 copy-done.5
  37.8 0.0 copy-done.7
  37.8 0.0 copy-done.6
  37.8 0.0 collective-permute-start.3
  37.8 0.1 pad_add_fusion.bits
  37.9 0.5 collective-permute-start.5
  38.4 1.3 %collective-permute-start.6 = (f32[36,512]{1,0:T(8,128)}, f32[36,512]{1,0:T(8,128)S(1)}, u32[]{:S(2)}, u32[]{:S(2)}) collective-permute-start(f32[36,512]{1,0:T(8,128)} %copy-done.6), channel_id=1, source_target_pairs={{0,240},{1,241},{2,242},{3,243},{4,244},{5,245},{6,246},{7,247},{8... | collective-permute-start | bytes 221192 | tf_op jit(solution)/shard_map/ppermute | solution.py:675
  39.8 1.8 %collective-permute-start.7 = (f32[36,512]{1,0:T(8,128)}, f32[36,512]{1,0:T(8,128)S(1)}, u32[]{:S(2)}, u32[]{:S(2)}) collective-permute-start(f32[36,512]{1,0:T(8,128)} %copy-done.5), channel_id=1, source_target_pairs={{0,241},{1,242},{2,243},{3,244},{4,245},{5,246},{6,247},{7,248},{8... | collective-permute-start | bytes 221192 | tf_op jit(solution)/shard_map/ppermute | solution.py:676
  41.6 0.7 collective-permute-done.3.came
  42.3 1.1 copy-done.10
  43.4 0.9 copy-done.13
  44.2 4.3 %scatter_start.1.start = f32[400,256]{1,0:T(8,128)S(1)} custom-call(s32[162,128]{1,0:T(8,128)S(1)} %copy-done.13, f32[162,8,128]{2,1,0:T(8,128)S(1)} %copy-done.10, f32[162,8,128]{2,1,0:T(8,128)S(1)} %collective-permute-done.3.came), custom_call_target="tpu_custom_call" | custom-call | flops 4200000000 | tf_op jit(solution)/shard_map/scatter_start/pallas_call | solution.py:422
  48.5 0.0 collective-permute-done.4.came
  48.5 1.9 %split.1 = (f32[256,1024]{1,0:T(8,128)S(1)}, f32[256,384]{1,0:T(8,128)S(1)}, f32[256,384]{1,0:T(8,128)S(1)}, f32[256,256]{1,0:T(8,128)S(1)}) custom-call(s32[2]{0:T(128)S(1)} %pad_add_fusion.bits, f32[256,2048]{1,0:T(8,128)S(1)} %get-tuple-element.47.keep, f32[256,2048]{1,0:T(8,128)} %collective-permute-done.4.came), custom_call_target="tpu_custom_call" | custom-call | flops 1000000000 | tf_op jit(solution)/shard_map/split/pallas_call | solution.py:494
  50.5 0.0 collective-permute-done.5.left
  50.5 0.0 collective-permute-done.6.below
  50.5 0.0 collective-permute-done.7.corner
  50.5 2.3 %collective-permute-start.10 = (f32[256,256]{1,0:T(8,128)S(1)}, f32[256,256]{1,0:T(8,128)S(1)}, u32[]{:S(2)}, u32[]{:S(2)}) collective-permute-start(f32[256,256]{1,0:T(8,128)S(1)} %get-tuple-element.66), channel_id=1, source_target_pairs={{0,16},{16,0},{1,17},{17,1},{2,18},{18,2},{3,19},{19,3},{4,20},{20... | collective-permute-start | bytes 786440 | tf_op jit(solution)/shard_map/ppermute | solution.py:683
  52.8 1.1 collective-permute-start.8
  53.9 4.0 %collective-permute-start.9 = (f32[256,384]{1,0:T(8,128)S(1)}, f32[256,384]{1,0:T(8,128)S(1)}, u32[]{:S(2)}, u32[]{:S(2)}) collective-permute-start(f32[256,384]{1,0:T(8,128)S(1)} %get-tuple-element.65), channel_id=1, source_target_pairs={{0,224},{32,64},{64,32},{96,128},{128,96},{160,192},{192,160},{224... | collective-permute-start | bytes 1179656 | tf_op jit(solution)/shard_map/ppermute | solution.py:682
  57.9 4.6 %scatter_end.1 = (f32[8,16,256]{2,1,0:T(8,128)S(1)}, f32[8,16,256]{2,1,0:T(8,128)S(1)}) custom-call(s32[1]{0:T(128)} %bitcast.2.core_ref, s32[162,128]{1,0:T(8,128)S(1)} %copy-done.14, f32[162,8,128]{2,1,0:T(8,128)S(1)} %copy-done.11, f32[162,8,128]{2,1,0:T(8,128)S(1)} %collective-permute-done.3.came, f32[400,256]{1,0:T(8,128)S(1)} %scatter_start.1.start), custom_call_target="tpu_custom_call" | custom-call | flops 4600000000 | tf_op jit(solution)/shard_map/scatter_end/pallas_call | solution.py:454
  62.6 0.1 collective-permute-start.11
  62.7 0.8 place.1
  63.5 0.5 collective-permute-done.11.table_came
  64.0 0.0 collective-permute-done.10.came_c
  64.0 0.0 collective-permute-done.8.came_a
  64.0 2.8 %collective-permute-done.9.came_b = f32[256,384]{1,0:T(8,128)S(1)} collective-permute-done((f32[256,384]{1,0:T(8,128)S(1)}, f32[256,384]{1,0:T(8,128)S(1)}, u32[]{:S(2)}, u32[]{:S(2)}) %collective-permute-start.9) | collective-permute-done | bytes 393248 | tf_op jit(solution)/shard_map/ppermute | solution.py:682
  66.8 0.1 join.1
  66.9 21.6 %all_to_all.15.parts = f32[8,32,1280]{2,1,0:T(8,128)S(1)} all-to-all(f32[8,32,1280]{2,1,0:T(8,128)S(1)} %join.1), channel_id=1, replica_groups=mesh['z'=8,'y_lo'=2,'x'=4,'y_hi'=2,'core'=2] {'x','y_hi'}, dimensions={0} | all-to-all | bytes 2621440 | tf_op jit(solution)/shard_map/all_to_all | solution.py:691
  88.6 0.1 fold_lon.1
  88.6 17.8 %all_to_all.16.parts = f32[16,4,1152]{2,1,0:T(4,128)S(1)} all-to-all(f32[16,4,1152]{2,1,0:T(4,128)S(1)} %fold_lon.1), channel_id=1, replica_groups=mesh['z'=8,'y_lo'=2,'x'=4,'y_hi'=2,'core'=2] {'z','y_lo'}, dimensions={0} | all-to-all | bytes 589824 | tf_op jit(solution)/shard_map/all_to_all | solution.py:692
  106.4 0.6 fold_lat.1
  107.0 13.0 %all_to_all.17.parts = f32[16,4,1152]{2,1,0:T(4,128)S(1)} all-to-all(f32[16,4,1152]{2,1,0:T(4,128)S(1)} %fold_lat.1), channel_id=1, replica_groups=mesh['z'=8,'y_lo'=2,'x'=4,'y_hi'=2,'core'=2] {'z','y_lo'}, dimensions={0} | all-to-all | bytes 589824 | tf_op jit(solution)/shard_map/all_to_all | solution.py:693
  120.0 0.7 unpack.1
  (21 shorter events, 0.0 us)
Async XLA Ops:
  0.6 9.8 %copy-start.3 = (f32[6336,16]{0,1:T(8,128)S(1)}, f32[6336,16]{0,1:T(8,128)}, u32[]{:S(2)}) copy-start(f32[6336,16]{0,1:T(8,128)} %param.11) | copy-start | bytes 1216516
  0.6 9.7 %copy-start.4 = (s32[144,144]{1,0:T(8,128)S(1)}, s32[144,144]{1,0:T(8,128)}, u32[]{:S(2)}) copy-start(s32[144,144]{1,0:T(8,128)} %index.1) | copy-start | bytes 248836
  2.8 20.3 %collective-permute-start = (f32[80,512]{1,0:T(8,128)}, f32[80,512]{1,0:T(8,128)S(1)}, u32[]{:S(2)}, u32[]{:S(2)}) collective-permute-start(f32[80,512]{1,0:T(8,128)} %get-tuple-element.39), channel_id=1, source_target_pairs={{0,16},{1,17},{2,18},{3,19},{4,20},{5,21},{6,22},{7,23},{8,24},{9,... | collective-permute-start | bytes 491528 | tf_op jit(solution)/shard_map/ppermute | solution.py:665
  4.6 18.5 %collective-permute-start.1 = (f32[80,512]{1,0:T(8,128)}, f32[80,512]{1,0:T(8,128)S(1)}, u32[]{:S(2)}, u32[]{:S(2)}) collective-permute-start(f32[80,512]{1,0:T(8,128)} %get-tuple-element.40), channel_id=1, source_target_pairs={{0,31},{1,16},{2,17},{3,18},{4,19},{5,20},{6,21},{7,22},{8,23},{9,... | collective-permute-start | bytes 491528 | tf_op jit(solution)/shard_map/ppermute | solution.py:666
  8.4 14.8 %collective-permute-start.2 = (f32[80,512]{1,0:T(8,128)}, f32[80,512]{1,0:T(8,128)S(1)}, u32[]{:S(2)}, u32[]{:S(2)}) collective-permute-start(f32[80,512]{1,0:T(8,128)} %get-tuple-element.41), channel_id=1, source_target_pairs={{0,15},{1,0},{2,1},{3,2},{4,3},{5,4},{6,5},{7,6},{8,7},{9,8},{10,9... | collective-permute-start | bytes 491528 | tf_op jit(solution)/shard_map/ppermute | solution.py:664
  10.4 12.8 %copy-start.1 = (f32[512,1536]{1,0:T(8,128)S(1)}, f32[512,1536]{1,0:T(8,128)}, u32[]{:S(2)}) copy-start(f32[512,1536]{1,0:T(8,128)} %in_weight.1) | copy-start | bytes 9437188
  10.4 12.8 %copy-start.2 = (f32[512,512]{1,0:T(8,128)S(1)}, f32[512,512]{1,0:T(8,128)}, u32[]{:S(2)}) copy-start(f32[512,512]{1,0:T(8,128)} %out_weight.1) | copy-start | bytes 3145732
  10.4 12.8 %copy-start.8 = (f32[80,512]{1,0:T(8,128)S(1)}, f32[80,512]{1,0:T(8,128)}, u32[]{:S(2)}) copy-start(f32[80,512]{1,0:T(8,128)} %get-tuple-element.38.own) | copy-start | bytes 491524
  23.1 13.2 %copy-start.12 = (s32[162,128]{1,0:T(8,128)}, s32[162,128]{1,0:T(8,128)S(1)}, u32[]{:S(2)}) copy-start(s32[162,128]{1,0:T(8,128)S(1)} %get-tuple-element.44.places) | copy-start | bytes 248836
  36.3 0.8 copy-start.9
  37.2 0.6 copy-start.5
  37.2 0.7 copy-start.7
  37.2 0.7 copy-start.6
  37.2 11.4 %collective-permute-start.4 = (f32[256,2048]{1,0:T(8,128)}, f32[256,2048]{1,0:T(8,128)}, u32[]{:S(2)}, u32[]{:S(2)}) collective-permute-start(f32[256,2048]{1,0:T(8,128)} %get-tuple-element.48), channel_id=1, source_target_pairs={{0,1},{1,0},{2,3},{3,2},{4,5},{5,4},{6,7},{7,6},{8,9},{9,8},{10,11... | collective-permute-start | bytes 6291464 | tf_op jit(solution)/shard_map/ppermute | solution.py:672
  37.8 4.4 %collective-permute-start.3 = (f32[162,8,128]{2,1,0:T(8,128)S(1)}, f32[162,8,128]{2,1,0:T(8,128)S(1)}, u32[]{:S(2)}, u32[]{:S(2)}) collective-permute-start(f32[162,8,128]{2,1,0:T(8,128)S(1)} %get-tuple-element.46), channel_id=1, source_target_pairs={{0,1},{1,0},{2,3},{3,2},{4,5},{5,4},{6,7},{7,6},{8,9},{9,8},{10,11... | collective-permute-start | bytes 1990664 | tf_op jit(solution)/shard_map/ppermute | solution.py:671
  37.9 12.6 %collective-permute-start.5 = (f32[36,512]{1,0:T(8,128)}, f32[36,512]{1,0:T(8,128)S(1)}, u32[]{:S(2)}, u32[]{:S(2)}) collective-permute-start(f32[36,512]{1,0:T(8,128)} %copy-done.7), channel_id=1, source_target_pairs={{0,1},{1,2},{2,3},{3,4},{4,5},{5,6},{6,7},{7,8},{8,9},{9,10},{10,1... | collective-permute-start | bytes 221192 | tf_op jit(solution)/shard_map/ppermute | solution.py:674
  38.4 12.1 %collective-permute-start.6 = (f32[36,512]{1,0:T(8,128)}, f32[36,512]{1,0:T(8,128)S(1)}, u32[]{:S(2)}, u32[]{:S(2)}) collective-permute-start(f32[36,512]{1,0:T(8,128)} %copy-done.6), channel_id=1, source_target_pairs={{0,240},{1,241},{2,242},{3,243},{4,244},{5,245},{6,246},{7,247},{8... | collective-permute-start | bytes 221192 | tf_op jit(solution)/shard_map/ppermute | solution.py:675
  39.8 10.7 %collective-permute-start.7 = (f32[36,512]{1,0:T(8,128)}, f32[36,512]{1,0:T(8,128)S(1)}, u32[]{:S(2)}, u32[]{:S(2)}) collective-permute-start(f32[36,512]{1,0:T(8,128)} %copy-done.5), channel_id=1, source_target_pairs={{0,241},{1,242},{2,243},{3,244},{4,245},{5,246},{6,247},{7,248},{8... | collective-permute-start | bytes 221192 | tf_op jit(solution)/shard_map/ppermute | solution.py:676
  42.3 1.1 copy-start.10
  43.4 0.9 copy-start.13
  48.5 9.4 %copy-start.11 = (f32[162,8,128]{2,1,0:T(8,128)S(1)}, f32[162,8,128]{2,1,0:T(8,128)}, u32[]{:S(2)}) copy-start(f32[162,8,128]{2,1,0:T(8,128)} %copy-done.9) | copy-start | bytes 1990660
  48.5 9.4 %copy-start.14 = (s32[162,128]{1,0:T(8,128)S(1)}, s32[162,128]{1,0:T(8,128)}, u32[]{:S(2)}) copy-start(s32[162,128]{1,0:T(8,128)} %copy-done.12) | copy-start | bytes 248836
  50.5 13.5 %collective-permute-start.10 = (f32[256,256]{1,0:T(8,128)S(1)}, f32[256,256]{1,0:T(8,128)S(1)}, u32[]{:S(2)}, u32[]{:S(2)}) collective-permute-start(f32[256,256]{1,0:T(8,128)S(1)} %get-tuple-element.66), channel_id=1, source_target_pairs={{0,16},{16,0},{1,17},{17,1},{2,18},{18,2},{3,19},{19,3},{4,20},{20... | collective-permute-start | bytes 786440 | tf_op jit(solution)/shard_map/ppermute | solution.py:683
  52.8 11.3 %collective-permute-start.8 = (f32[256,384]{1,0:T(8,128)S(1)}, f32[256,384]{1,0:T(8,128)S(1)}, u32[]{:S(2)}, u32[]{:S(2)}) collective-permute-start(f32[256,384]{1,0:T(8,128)S(1)} %get-tuple-element.64), channel_id=1, source_target_pairs={{0,32},{32,0},{64,96},{96,64},{128,160},{160,128},{192,224},{224,1... | collective-permute-start | bytes 1179656 | tf_op jit(solution)/shard_map/ppermute | solution.py:681
  53.9 8.8 %copy-start = (f32[2,12,6,512]{3,0,2,1:T(2,128)S(1)}, f32[2,12,6,512]{3,0,2,1:T(2,128)}, u32[]{:S(2)}) copy-start(f32[2,12,6,512]{3,0,2,1:T(2,128)} %param.8) | copy-start | bytes 884740
  53.9 12.9 %collective-permute-start.9 = (f32[256,384]{1,0:T(8,128)S(1)}, f32[256,384]{1,0:T(8,128)S(1)}, u32[]{:S(2)}, u32[]{:S(2)}) collective-permute-start(f32[256,384]{1,0:T(8,128)S(1)} %get-tuple-element.65), channel_id=1, source_target_pairs={{0,224},{32,64},{64,32},{96,128},{128,96},{160,192},{192,160},{224... | collective-permute-start | bytes 1179656 | tf_op jit(solution)/shard_map/ppermute | solution.py:682
  62.6 1.4 %collective-permute-start.11 = (f32[8,16,256]{2,1,0:T(8,128)S(1)}, f32[8,16,256]{2,1,0:T(8,128)S(1)}, u32[]{:S(2)}, u32[]{:S(2)}) collective-permute-start(f32[8,16,256]{2,1,0:T(8,128)S(1)} %get-tuple-element.68), channel_id=1, source_target_pairs={{0,1},{1,0},{2,3},{3,2},{4,5},{5,4},{6,7},{7,6},{8,9},{9,8},{10,11... | collective-permute-start | bytes 393224 | tf_op jit(solution)/shard_map/ppermute | solution.py:686

commit v5 on v4

v5 whole, which is shorter than its diff:
```python
import functools

import jax
import jax.numpy as jnp
from jax import lax
from jax.experimental import pallas as pl
from jax.experimental.pallas import tpu as pltpu
from jax.sharding import Mesh
from jax.sharding import PartitionSpec as P

WIDTH = 512
HEADS = 16
HEAD_DIM = 32
TOKENS = 144
QUAD = 36
BIAS_ROWS = 6336
HALF_SECTOR = 198
BLOCKS = 25
PACK_MIB = 56
ROWS = 162
SPLIT = 64
LOOKUP_COST = 6
WINDOW_COST = 0
SCATTER_COST = 9
FACTOR = HEAD_DIM ** (-0.5)
F32 = jnp.float32
BF16 = jnp.bfloat16
MEGA = 1 << 20


def params(mib=16):
    return pltpu.CompilerParams(vmem_limit_bytes=mib * MEGA)


def cost(micros):
    return pl.CostEstimate(flops=int(micros * 1e9), bytes_accessed=0, transcendentals=0)


def whole(count):
    return [pl.BlockSpec(memory_space=pltpu.VMEM)] * count


def scalar():
    return pl.BlockSpec(memory_space=pltpu.SMEM)


def halves(x):
    high = x.astype(BF16)
    low = (x - high.astype(F32)).astype(BF16)
    return high, low


def dot(a, b, dims):
    return lax.dot_general(a, b, (dims, ((), ())), preferred_element_type=F32)


NN = ((1,), (0,))
NT = ((1,), (1,))
TN = ((0,), (0,))


def dot3(a, b, dims):
    ah, al = a
    bh, bl = b
    return dot(ah, bh, dims) + (dot(ah, bl, dims) + dot(al, bh, dims))


def token_order():
    place = lax.broadcasted_iota(jnp.int32, (TOKENS, TOKENS), 0)
    token = lax.broadcasted_iota(jnp.int32, (TOKENS, TOKENS), 1)

    def steps(value, size, count):
        total = jnp.zeros_like(value)
        for i in range(1, count):
            total = total + jnp.where(value >= i * size, 1, 0)
        return total

    quad = steps(place, QUAD, 4)
    rest = place - QUAD * quad
    row = steps(rest, 6, 6)
    rest = rest - 6 * row
    col = steps(rest, 2, 3)
    level = rest - 2 * col
    row_half = steps(quad, 2, 2)
    col_half = quad - 2 * row_half
    source = level * 72 + (6 * row_half + row) * 6 + 3 * col_half + col
    return jnp.where(source == token, 1.0, 0.0).astype(BF16)


def pack_kernel(last, fields, grads, ids, own, down, left):
    lanes = lax.broadcasted_iota(jnp.int32, (2, WIDTH), 1)
    level = lax.broadcasted_iota(jnp.int32, (2, WIDTH), 0)
    bump = last[0]
    plan = (
        (own, 0, 0, 3, 2, None),
        (left, 0, 0, 0, 3, None),
        (down, 0, 6, 3, 0, bump),
        (down, 80, 6, 0, 1, bump),
    )
    for ref, base, row0, col0, quadrant, offset in plan:
        label = jnp.zeros((2, WIDTH), jnp.int32)
        for row in range(6):
            for col in range(3):
                spot = row * 6 + col * 2
                at = base + spot
                ref[at : at + 2, :] = fields[row0 + row, col0 + col]
                ref[QUAD + at : QUAD + at + 2, :] = grads[row0 + row, col0 + col]
                value = ids[col0 + col, :, row0 + row : row0 + row + 1] + 1
                if offset is not None:
                    value = value + offset
                place = quadrant * QUAD + spot
                label = jnp.where(
                    lanes == level + place, jnp.broadcast_to(value, (2, WIDTH)), label
                )
        total = jnp.sum(label.astype(F32), axis=0, keepdims=True)
        ref[base + 72 : base + 80, :] = jnp.broadcast_to(total, (8, WIDTH))


def pack(last, fields, grads, ids):
    return pl.pallas_call(
        pack_kernel,
        out_shape=[
            jax.ShapeDtypeStruct((80, WIDTH), F32),
            jax.ShapeDtypeStruct((160, WIDTH), F32),
            jax.ShapeDtypeStruct((80, WIDTH), F32),
        ],
        in_specs=[scalar()] + whole(3),
        out_specs=whole(3),
        compiler_params=params(PACK_MIB),
        cost_estimate=cost(1),
        name="pack",
    )(last, fields, grads, ids)


def stack_kernel(spans, first, second, out):
    (start1, stop1), (start2, stop2) = spans
    out[0 : stop1 - start1, :] = first[start1:stop1, :]
    out[stop1 - start1 :, :] = second[start2:stop2, :]


def stack(first, span1, second, span2):
    rows = span1[1] - span1[0] + span2[1] - span2[0]
    return pl.pallas_call(
        functools.partial(stack_kernel, (span1, span2)),
        out_shape=jax.ShapeDtypeStruct((rows, WIDTH), F32),
        in_specs=whole(2),
        out_specs=pl.BlockSpec(memory_space=pltpu.VMEM),
        compiler_params=params(),
        name="stack",
    )(first, second)


def one_hot(row, lines):
    low = (row & 255).astype(F32).astype(BF16)
    hit = lines == jnp.broadcast_to(low, (256, 128))
    return jnp.where(hit, jnp.ones((256, 128), BF16), jnp.zeros((256, 128), BF16))


def line_numbers():
    return lax.broadcasted_iota(jnp.int32, (256, 128), 0).astype(F32).astype(BF16)


def find_pairs(matrix, places, bias, steps, pairs, first):
    lines = line_numbers()
    left = matrix[...]

    def find(rows):
        right = jnp.concatenate([one_hot(row, lines) for row in rows], axis=1)
        found = dot(left, right, NN)
        block = jnp.concatenate([row >> 8 for row in rows], axis=1)
        block = jnp.broadcast_to(block, (32, 256))
        total = jnp.zeros((32, 256), F32)
        for b in range(BLOCKS):
            total = jnp.where(block == b, found[b * 32 : b * 32 + 32], total)
        return total[:16] + total[16:]

    def step(i, carry):
        base = pl.multiple_of(i * 8, 8)
        rows = places[pl.ds(base + first, 8), :]
        for pair in range(4):
            found = find([rows[2 * pair + j : 2 * pair + j + 1, :] for j in range(2)])
            for j in range(2):
                bias[base + 2 * pair + j, :, 0:128] = found[:, j * 128 : j * 128 + 128]
        return carry

    lax.fori_loop(0, steps, step, 0)
    for pair in range(pairs):
        at = TOKENS + first // 8 + 2 * pair
        found = find([places[at + j : at + j + 1, :] for j in range(2)])
        for j in range(16):
            bias[16 * pair + j, :, 128:144] = found[:, 16 * j : 16 * j + 16]


def lookup_start_kernel(core_ref, index, table, bias, places, left):
    value = index[...]
    high = (value >> 7).astype(F32).astype(BF16)
    low = (value & 127).astype(F32).astype(BF16)
    move = token_order()

    def moved(part):
        return dot(dot(move, part, NN).astype(BF16), move, NT)

    result = moved(high) * 128.0 + moved(low)
    places[0:TOKENS, :] = result[:, :128].astype(jnp.int32)
    tail = jnp.concatenate([result[:, 128:], jnp.zeros((TOKENS, 112), F32)], axis=1)
    for i in range(18):
        spread = pltpu.roll(tail[8 * i : 8 * i + 8, :], 0, 1, stride=16, stride_axis=0)
        places[TOKENS + i : TOKENS + i + 1, :] = jnp.sum(spread, axis=0, keepdims=True).astype(
            jnp.int32
        )

    first = core_ref[0] == 0
    for block in range(BLOCKS):
        count = min(256, BIAS_ROWS - block * 256)
        top = table[0:8, block * 256 : block * 256 + count]
        bottom = table[8:16, block * 256 : block * 256 + count]
        part = jnp.concatenate(
            [jnp.where(first, bottom, top), jnp.where(first, top, bottom)], axis=0
        )
        if count < 256:
            part = jnp.concatenate([part, jnp.zeros((16, 256 - count), F32)], axis=1)
        left[block * 32 : block * 32 + 16, :], left[block * 32 + 16 : block * 32 + 32, :] = halves(
            part
        )
    find_pairs(left, places, bias, SPLIT // 8, SPLIT // 16, 0)


def lookup_start(core, bias_index, bias_table):
    return pl.pallas_call(
        lookup_start_kernel,
        out_shape=[
            jax.ShapeDtypeStruct((SPLIT, HEADS, TOKENS), F32),
            jax.ShapeDtypeStruct((ROWS, 128), jnp.int32),
            jax.ShapeDtypeStruct((BLOCKS * 32, 256), BF16),
        ],
        in_specs=[scalar()] + whole(2),
        out_specs=whole(3),
        compiler_params=params(),
        cost_estimate=cost(LOOKUP_COST),
        name="lookup_start",
    )(core, bias_index, bias_table.T)


def lookup_end_kernel(places, left, bias):
    find_pairs(left, places, bias, (TOKENS - SPLIT) // 8, (TOKENS - SPLIT) // 16, SPLIT)


def lookup_end(places, left):
    return pl.pallas_call(
        lookup_end_kernel,
        out_shape=jax.ShapeDtypeStruct((TOKENS - SPLIT, HEADS, TOKENS), F32),
        in_specs=whole(2),
        out_specs=pl.BlockSpec(memory_space=pltpu.VMEM),
        compiler_params=params(),
        cost_estimate=cost(LOOKUP_COST),
        name="lookup_end",
    )(places, left)


def main_kernel(
    core_ref,
    own,
    above,
    beside,
    bias_start,
    bias_end,
    in_weight,
    out_weight,
    keep,
    send,
    keep_scores,
    send_scores,
    grad_above,
    grad_own,
    grad_beside,
    tokens,
    cotangent,
    proj,
    gatt,
    gproj,
    att,
    normed_t,
    tails,
):
    core = core_ref[0]
    row = jnp.zeros((1, WIDTH), F32)
    for slot, (quad, start) in enumerate(((above, 0), (beside, 0), (own, 0), (beside, 80))):
        at = slot * QUAD
        tokens[at : at + QUAD, :] = quad[start : start + QUAD, :]
        cotangent[at : at + QUAD, :] = quad[start + QUAD : start + 2 * QUAD, :]
        row = row + quad[start + 72 : start + 73, :]
    row = row[:, :TOKENS]
    side = lax.broadcasted_iota(jnp.int32, (TOKENS, TOKENS), 0)
    along = lax.broadcasted_iota(jnp.int32, (TOKENS, TOKENS), 1)
    spread = jnp.broadcast_to(row, (TOKENS, TOKENS))
    column = jnp.sum(jnp.where(side == along, spread, 0.0), axis=1, keepdims=True)
    allowed = column == spread

    inputs = tokens[...]
    centered = inputs - jnp.mean(inputs, axis=1, keepdims=True)
    variance = jnp.mean(centered * centered, axis=1, keepdims=True)
    inv_std = lax.rsqrt(variance + 1e-05)
    normed = centered * inv_std
    tokens[...] = normed
    normed_t[...] = normed.T
    halves_normed = halves(normed)
    for part in range(3):
        at = part * WIDTH
        weight = halves(in_weight[:, at : at + WIDTH])
        proj[at : at + WIDTH, :] = dot3(halves_normed, weight, NN).T
    halves_cotangent = halves(cotangent[...])
    gatt[...] = dot3(halves(out_weight[...]), halves_cotangent, NT)

    def stacked(*parts):
        return jnp.concatenate(parts, axis=0)

    def product(high, low, right_high, right_low, dims):
        both = dot(stacked(high, low), right_high, dims)
        return both[:HEAD_DIM] + (both[HEAD_DIM:] + dot(high, right_low, dims))

    def some_heads(heads):
        ats = [pl.multiple_of(head * HEAD_DIM, HEAD_DIM) for head, _ in heads]
        q = [halves(proj[pl.ds(at, HEAD_DIM), :] * FACTOR) for at in ats]
        k = [halves(proj[pl.ds(at + WIDTH, HEAD_DIM), :]) for at in ats]
        v = [halves(proj[pl.ds(at + 2 * WIDTH, HEAD_DIM), :]) for at in ats]
        g = [halves(gatt[pl.ds(at, HEAD_DIM), :]) for at in ats]

        def outer(left, right):
            return dot(
                stacked(left[0], left[0], left[1]), stacked(right[0], right[1], right[0]), TN
            )

        scores = [
            outer(q[i], k[i])
            + jnp.concatenate([bias_start[:, slot, :], bias_end[:, slot, :]], axis=0)
            for i, (_, slot) in enumerate(heads)
        ]
        grad_probs = [outer(g[i], v[i]) for i in range(len(heads))]
        scores = [jnp.where(allowed, x, -1000000000.0) for x in scores]
        exponent = [jnp.exp(x - jnp.max(x, axis=1, keepdims=True)) for x in scores]
        probs = [x * (1.0 / jnp.sum(x, axis=1, keepdims=True)) for x in exponent]
        p = [halves(x) for x in probs]
        for i, at in enumerate(ats):
            att[pl.ds(at, HEAD_DIM), :] = product(*v[i], *p[i], NT)
            gproj[pl.ds(at + 2 * WIDTH, HEAD_DIM), :] = product(*g[i], *p[i], NN)
        grad_scores = [
            x * (y - jnp.sum(x * y, axis=1, keepdims=True)) for x, y in zip(probs, grad_probs)
        ]
        s = [halves(x) for x in grad_scores]
        for i, at in enumerate(ats):
            gproj[pl.ds(at, HEAD_DIM), :] = product(*k[i], *s[i], NT) * FACTOR
            gproj[pl.ds(at + WIDTH, HEAD_DIM), :] = product(*q[i], *s[i], NN)
        for i, (_, slot) in enumerate(heads):
            target = send_scores if slot < 8 else keep_scores
            target[0:TOKENS, slot % 8, :] = grad_scores[i][:, :128]
            tails[:, slot, 0:16] = grad_scores[i][:, 128:]

    tails[...] = jnp.zeros_like(tails)
    order = [((1 - core) * 8 + slot, slot) for slot in range(8)]
    order += [(core * 8 + slot, 8 + slot) for slot in range(8)]
    for first in range(0, 16, 4):
        some_heads(order[first : first + 4])

    for i in range(18):
        total = tails[8 * i]
        for j in range(1, 8):
            total = total + pltpu.roll(tails[8 * i + j], 16 * j, 1)
        send_scores[TOKENS + i] = total[0:8]
        keep_scores[TOKENS + i] = total[8:16]

    for target, bit in ((send, 1 - core), (keep, core)):
        rows = [pl.ds(pl.multiple_of(64 * i + 32 * bit, 32), 32) for i in range(8)]
        left = halves(jnp.concatenate([normed_t[r, :] for r in rows], axis=0))
        for part in range(3):
            at = part * WIDTH
            target[:, at : at + WIDTH] = dot3(left, halves(gproj[at : at + WIDTH, :]), NT)
        left = halves(jnp.concatenate([att[r, :] for r in rows], axis=0))
        target[:, 3 * WIDTH :] = dot3(left, halves_cotangent, NN)

    grad_normed = jnp.zeros((WIDTH, TOKENS), F32)
    for part in range(3):
        at = part * WIDTH
        grad_normed = grad_normed + dot3(
            halves(in_weight[:, at : at + WIDTH]), halves(gproj[at : at + WIDTH, :]), NN
        )
    grad_normed = grad_normed.T
    normed = tokens[...]
    result = inv_std * (
        grad_normed
        - jnp.mean(grad_normed, axis=1, keepdims=True)
        - normed * jnp.mean(grad_normed * normed, axis=1, keepdims=True)
    )
    tokens[...] = result
    grad_above[...] = tokens[0:QUAD, :]
    grad_beside[0:QUAD, :] = tokens[QUAD : 2 * QUAD, :]
    grad_own[...] = tokens[2 * QUAD : 3 * QUAD, :]
    grad_beside[QUAD:, :] = tokens[3 * QUAD :, :]


def shape(*dims):
    return jax.ShapeDtypeStruct(dims, F32)


def window(core, own, above, beside, bias_start, bias_end, in_weight, out_weight):
    grad = shape(QUAD, WIDTH)
    return pl.pallas_call(
        main_kernel,
        out_shape=[
            shape(256, 4 * WIDTH),
            shape(256, 4 * WIDTH),
            shape(ROWS, 8, 128),
            shape(ROWS, 8, 128),
            grad,
            grad,
            shape(2 * QUAD, WIDTH),
        ],
        in_specs=[scalar()] + whole(7),
        out_specs=whole(7),
        scratch_shapes=[
            pltpu.VMEM((TOKENS, WIDTH), F32),
            pltpu.VMEM((TOKENS, WIDTH), F32),
            pltpu.VMEM((3 * WIDTH, TOKENS), F32),
            pltpu.VMEM((WIDTH, TOKENS), F32),
            pltpu.VMEM((3 * WIDTH, TOKENS), F32),
            pltpu.VMEM((WIDTH, TOKENS), F32),
            pltpu.VMEM((WIDTH, TOKENS), F32),
            pltpu.VMEM((TOKENS, HEADS, 128), F32),
        ],
        compiler_params=params(26),
        cost_estimate=cost(WINDOW_COST),
        name="window",
    )(core, own, above, beside, bias_start, bias_end, in_weight, out_weight)


def add_pairs(places, keep, came, total):
    lines = line_numbers()

    def sides(row, values):
        block = (row >> 8).astype(F32).astype(BF16)
        both = jnp.concatenate(halves(values), axis=0)
        spread = jnp.broadcast_to(block, (16, 128))
        left = jnp.concatenate(
            [jnp.where(spread == float(b), both, jnp.zeros_like(both)) for b in range(BLOCKS)],
            axis=0,
        )
        return left, one_hot(row, lines)

    def add(rows, base, pair):
        pieces = [
            sides(rows[j : j + 1, :], keep[base + j] + came[base + j])
            for j in (2 * pair, 2 * pair + 1)
        ]
        left = jnp.concatenate([p[0] for p in pieces], axis=1)
        right = jnp.concatenate([p[1] for p in pieces], axis=1)
        total[...] += dot(left, right, NT)

    def step(i, carry):
        base = pl.multiple_of(i * 8, 8)
        rows = places[pl.ds(base, 8), :]
        for pair in range(4):
            add(rows, base, pair)
        return carry

    lax.fori_loop(0, ROWS // 8, step, 0)
    add(places[ROWS - 2 : ROWS, :], ROWS - 2, 0)


def scatter_kernel(core_ref, places, keep, came, mine, other, total, line, sectors):
    total[...] = jnp.zeros_like(total)
    add_pairs(places, keep, came, total)
    for b in range(BLOCKS):
        line[:, b * 256 : b * 256 + 256] = (
            total[b * 16 : b * 16 + 8, :] + total[b * 16 + 8 : b * 16 + 16, :]
        )
    line[:, BLOCKS * 256 :] = jnp.zeros((8, 256), F32)
    for m in range(32):
        chip, core, half = m // 4, m // 2 % 2, m % 2
        start_at = m * HALF_SECTOR
        base, shift = start_at // 128 * 128, start_at % 128
        piece = line[:, base : base + 512]
        if shift:
            piece = pltpu.roll(piece, 512 - shift, 1)
        sectors[core, chip, half * 8 : half * 8 + 8, :] = piece[:, :256]
    mine[...] = sectors[core_ref[0]]
    other[...] = sectors[1 - core_ref[0]]


def scatter(core, places, keep, came):
    return pl.pallas_call(
        scatter_kernel,
        out_shape=[shape(8, 16, 256)] * 2,
        in_specs=[scalar()] + whole(3),
        out_specs=whole(2),
        scratch_shapes=[
            pltpu.VMEM((BLOCKS * 16, 256), F32),
            pltpu.VMEM((8, BLOCKS * 256 + 256), F32),
            pltpu.VMEM((2, 8, 16, 256), F32),
        ],
        compiler_params=params(),
        cost_estimate=cost(SCATTER_COST),
        name="scatter",
    )(core, places, keep, came)


def split_kernel(odd, keep, came, own, send_a, send_b):
    def columns(bit):
        cols = slice(512 * bit, 512 * bit + 512)
        return keep[:, cols] + came[:, cols]

    for bit in range(2):

        @pl.when(odd[0] == bit)
        def _():
            send_a[...] = columns(1 - bit)
            send_b[...] = columns(2 + bit)
            own[:, 0:512] = columns(bit)
            own[:, 512:1024] = columns(3 - bit)


def split(odd, keep, came):
    return pl.pallas_call(
        split_kernel,
        out_shape=[shape(256, 1024), shape(256, 512), shape(256, 512)],
        in_specs=[scalar()] + whole(2),
        out_specs=whole(3),
        compiler_params=params(),
        name="split",
    )(odd, keep, came)


def join_kernel(core_ref, own, came_a, came_b, table_keep, table_came, out):
    for i in range(8):
        rows = slice(i * 32, i * 32 + 32)
        out[i, :, 0:512] = own[rows, 0:512] + came_a[rows, :]
        out[i, :, 512:1024] = own[rows, 512:1024] + came_b[rows, :]
    first = core_ref[0] == 0
    mine, other = table_keep[...], table_came[...]
    out[:, 0:16, 1024:] = jnp.where(first, mine, other)
    out[:, 16:32, 1024:] = jnp.where(first, other, mine)


def join(core, *parts):
    return pl.pallas_call(
        join_kernel,
        out_shape=shape(8, 32, 1280),
        in_specs=[scalar()] + whole(5),
        out_specs=pl.BlockSpec(memory_space=pltpu.VMEM),
        compiler_params=params(),
        name="join",
    )(core, *parts)


def fold_lon_kernel(parts, out, total):
    value = parts[0]
    for i in range(1, 8):
        value = value + parts[i]
    total[...] = value
    for i in range(8):
        out[i] = total[4 * i : 4 * i + 4, :]


def fold_lon(parts):
    return pl.pallas_call(
        fold_lon_kernel,
        out_shape=shape(8, 4, 1280),
        in_specs=whole(1),
        out_specs=pl.BlockSpec(memory_space=pltpu.VMEM),
        scratch_shapes=[pltpu.VMEM((32, 1280), F32)],
        compiler_params=params(),
        name="fold_lon",
    )(parts)


def fold_lat_kernel(parts, out):
    total = parts[0]
    for i in range(1, 8):
        total = total + parts[i]
    for i in range(16):
        out[i] = total


def fold_lat(parts):
    return pl.pallas_call(
        fold_lat_kernel,
        out_shape=shape(16, 4, 1280),
        in_specs=whole(1),
        out_specs=pl.BlockSpec(memory_space=pltpu.VMEM),
        compiler_params=params(),
        name="fold_lat",
    )(parts)


def unpack_kernel(parts, grad_in, grad_out, grad_bias, table):
    for rank in range(8):
        rows = slice(4 * rank, 4 * rank + 4)
        even = (rank // 2) * 4 + rank % 2
        odd = even + 2
        grad_in[rows, 0:512] = parts[even, :, 0:512]
        grad_in[rows, 512:1024] = parts[odd, :, 0:512]
        grad_in[rows, 1024:1536] = parts[odd, :, 512:1024]
        grad_out[rows, :] = parts[even, :, 512:1024]
        table[rows, :] = parts[even, :, 1024:] + parts[odd, :, 1024:]
    for core in range(2):
        for half in range(2):
            base = core * 16 + half * 8
            grad_bias[core * 8 : core * 8 + 8, half * HALF_SECTOR : (half + 1) * HALF_SECTOR] = (
                table[base : base + 8, :HALF_SECTOR]
            )


def unpack(parts):
    return pl.pallas_call(
        unpack_kernel,
        out_shape=[shape(32, 3 * WIDTH), shape(32, WIDTH), shape(HEADS, 2 * HALF_SECTOR)],
        in_specs=whole(1),
        out_specs=whole(3),
        scratch_shapes=[pltpu.VMEM((32, 256), F32)],
        compiler_params=params(),
        name="unpack",
    )(parts)


def place_kernel(grad_out, own, beside, below, out):
    plan = ((own, 0, 0, 3), (beside, QUAD, 0, 0), (below, 0, 6, 3), (below, QUAD, 6, 0))
    for ref, base, row0, col0 in plan:
        for row in range(6):
            for col in range(3):
                spot = base + row * 6 + col * 2
                out[row0 + row, col0 + col] = (
                    grad_out[row0 + row, col0 + col] + ref[spot : spot + 2, :]
                )


def place(grad_out, own, beside, below):
    return pl.pallas_call(
        place_kernel,
        out_shape=jax.ShapeDtypeStruct(grad_out.shape, F32),
        in_specs=whole(4),
        out_specs=pl.BlockSpec(memory_space=pltpu.VMEM),
        compiler_params=params(),
        name="place",
    )(grad_out, own, beside, below)


LAT = ("z", "y_lo")
LON = ("x", "y_hi", "core")


def body(fields, grad_out, region_ids, bias_index, bias_table, in_weight, out_weight):
    everything = LAT + LON
    lat = lax.axis_index(LAT)
    core = lax.axis_index("core").reshape(1)
    odd = lax.rem(lax.axis_index("z"), 2).reshape(1)

    def moves(down, right):
        return [
            (i * 16 + j, (i + down) % 16 * 16 + (j + right) % 16)
            for i in range(16)
            for j in range(16)
        ]

    swap = [(0, 1), (1, 0)]
    last = jnp.where(lat == 15, 3, 0).reshape(1)
    grad_out = jnp.transpose(grad_out, (1, 2, 0, 3))
    own, down, left = pack(
        last, jnp.transpose(fields, (1, 2, 0, 3)), grad_out, jnp.transpose(region_ids, (2, 0, 1))
    )
    above = lax.ppermute(down, everything, moves(1, 0))
    bias_start, places, matrix = lookup_start(core, bias_index, bias_table)
    above, places = lax.optimization_barrier((above, places))
    beside = lax.ppermute(stack(above, (80, 160), left, (0, 80)), everything, moves(0, -1))
    bias_end = lookup_end(places, matrix)
    beside, bias_end = lax.optimization_barrier((beside, bias_end))
    keep, send, keep_scores, send_scores, grad_above, grad_own, grad_beside = window(
        core, own, above, beside, bias_start, bias_end, in_weight, out_weight
    )
    came = lax.ppermute(send, "core", swap)
    came_scores = lax.ppermute(send_scores, "core", swap)
    back_beside = lax.ppermute(grad_beside, everything, moves(0, 1))
    part, send_a, send_b = split(odd, keep, came)
    came_a = lax.ppermute(send_a, "z", [(i, i ^ 1) for i in range(8)])
    came_b = lax.ppermute(send_b, "z", [(i, ((i + 1) % 8 ^ 1) + 7 & 7) for i in range(8)])
    back_beside, part = lax.optimization_barrier((back_beside, part))
    back_below = lax.ppermute(
        stack(grad_above, (0, QUAD), back_beside, (0, QUAD)), everything, moves(-1, 0)
    )
    part, places = lax.optimization_barrier((part, places))
    mine, other = scatter(core, places, keep_scores, came_scores)
    came_table = lax.ppermute(other, "core", swap)
    mine, grad_own = lax.optimization_barrier((mine, grad_own))
    grad_fields = place(grad_out, grad_own, back_beside, back_below)
    part, grad_fields = lax.optimization_barrier((part, grad_fields))
    joined = join(core, part, came_a, came_b, mine, came_table)
    parts = lax.all_to_all(joined, ("x", "y_hi"), 0, 0)
    parity = [[z * 2 + y for z in range(bit, 8, 2) for y in range(2)] for bit in range(2)]
    parts = lax.all_to_all(fold_lon(parts), LAT, 0, 0, axis_index_groups=parity)
    parts = lax.all_to_all(fold_lat(parts), LAT, 0, 0)
    grad_in_weight, grad_out_weight, grad_bias = unpack(parts)
    return jnp.transpose(grad_fields, (2, 0, 1, 3)), grad_in_weight, grad_out_weight, grad_bias.T


def solution(mesh):
    split = Mesh(mesh.devices.reshape(8, 2, 4, 2, 2), LAT + LON)
    tokens = P(None, LAT, LON, None)
    in_specs = (tokens, tokens, P(None, LAT, LON), P(), P(), P(), P())
    out_specs = (tokens, P(LON, None), P(LON, None), P(LON, None))
    return jax.shard_map(body, mesh=split, in_specs=in_specs, out_specs=out_specs, check_vma=False)
```

time: 121 us -> 118 us (0.975)
  waiting for transfers between devices: 3.97 us -> 8.73 us
  starting transfers between devices: 18.8 us -> 15.2 us
  local copies, waits for them, and re-layouts: 3.54 us -> 0.03 us
  blocking collectives: 52.4 us -> 51 us
    ppermute x7 -> x4, waiting for transfers between devices: 0.02 us -> 4.21 us  [the longest x1 2.38 us: body(): back_beside = lax.ppermute(grad_beside, everything, moves(0, 1))]
    ppermute x1, waiting for transfers between devices: 0.01 us -> 3.99 us  [body(): came = lax.ppermute(send, 'core', swap)]
    unnamed x30 -> x14, local copies, waits for them, and re-layouts: 3.54 us -> 0.03 us
    ppermute x1, waiting for transfers between devices: 2.76 us -> 0.01 us  [body(): lax.ppermute(send_b, 'z', [(i, ((i + 1) % 8 ^ 1) + 7 & 7) for i in range(...]
    all_to_all x2, blocking collectives: 30.8 us -> 28.3 us  [the longest x1 14.6 us: body(): parts = lax.all_to_all(fold_lon(parts), LAT, 0, 0, axis_index_groups=parity)]
    ppermute x1, starting transfers between devices: 4.04 us -> 2.35 us  [body(): lax.ppermute(send_b, 'z', [(i, ((i + 1) % 8 ^ 1) + 7 & 7) for i in range(...]
    ppermute x7 -> x4, starting transfers between devices: 13.5 us -> 12.2 us  [the longest x1 7.12 us: body(): lax.ppermute(stack(grad_above, (0, QUAD), back_beside, (0, QUAD)), everyt...]
    pallas_call x7 -> x9, Pallas kernels: 26.3 us -> 27.1 us  [the longest x1 10 us: scatter(): pl.pallas_call(scatter_kernel, out_shape=[shape(8, 16, 256)] * 2, in_spec...]
  transfers between devices with their start and end apart: 12 -> 9, of which waited for: 3 -> 4; matrix products, arithmetic and copies ran while one was open for 0% -> 0% of each run, Pallas kernels for 20% -> 22%
where the time goes in v5:
time: 118 us
  blocking collectives  51 us (43%)
  Pallas kernels  41.8 us (35%)
  starting transfers between devices  15.2 us (13%)
  waiting for transfers between devices  8.73 us (7%)
    all_to_all x1, blocking collectives, body(): parts = lax.all_to_all(joined, ('x', 'y_hi'), 0, 0)  22.7 us
    all_to_all x1, blocking collectives, body(): parts = lax.all_to_all(fold_lon(parts), LAT, 0, 0, axis_index_groups=parity)  14.6 us
    all_to_all x1, blocking collectives, body(): parts = lax.all_to_all(fold_lat(parts), LAT, 0, 0)  13.7 us
    pallas_call x1, Pallas kernels, window(): pl.pallas_call(main_kernel, out_shape=[shape(256, 4 * WIDTH), shape(256,...  13.1 us
    pallas_call x1, Pallas kernels, scatter(): pl.pallas_call(scatter_kernel, out_shape=[shape(8, 16, 256)] * 2, in_spec...  10 us
    ppermute x1, starting transfers between devices, body(): lax.ppermute(stack(grad_above, (0, QUAD), back_beside, (0, QUAD)), everyt...  7.12 us
    pallas_call x1, Pallas kernels, lookup_end(): pl.pallas_call(lookup_end_kernel, out_shape=jax.ShapeDtypeStruct((TOKENS...  6.93 us
    pallas_call x1, Pallas kernels, lookup_start(): pl.pallas_call(lookup_start_kernel, out_shape=[jax.ShapeDtypeStruct((SPLI...  6.01 us
  transfers between devices with their start and end apart: 9, of which 4 were waited for; matrix products, arithmetic and copies ran while one was open for 0% of the time, Pallas kernels for 22%

profile of v5, /device:TPU:8, one launch (start us, length us, event | category | flops | bytes accessed | tf_op | source)
XLA Modules:
  0.0 117.5 jit_solution(1883822691597346693)
XLA Ops:
  0.6 0.0 copy-start.5
  0.6 0.0 copy-start.6
  0.7 2.2 %pack.1 = (f32[80,512]{1,0:T(8,128)}, f32[160,512]{1,0:T(8,128)}, f32[80,512]{1,0:T(8,128)}) custom-call(s32[1]{0:T(128)} %bitcast.1.last, f32[12,6,2,512]{3,2,1,0:T(2,128)} %bitcast.13, f32[12,6,2,512]{3,2,1,0:T(2,128)} %bitcast.9, s32[6,2,12]{2,1,0:T(2,128)} %bitcast.15), custom_call_target="tpu_custom_call" | custom-call | flops 1000000000 | tf_op jit(solution)/shard_map/pack/pallas_call | solution.py:120
  2.8 1.8 %collective-permute-start = (f32[160,512]{1,0:T(8,128)}, f32[160,512]{1,0:T(8,128)S(1)}, u32[]{:S(2)}, u32[]{:S(2)}) collective-permute-start(f32[160,512]{1,0:T(8,128)} %get-tuple-element.38), channel_id=1, source_target_pairs={{0,16},{1,17},{2,18},{3,19},{4,20},{5,21},{6,22},{7,23},{8,24},{9,... | collective-permute-start | bytes 983048 | tf_op jit(solution)/shard_map/ppermute | solution.py:668
  4.7 0.0 copy-done.5
  4.7 0.0 copy-done.6
  4.7 0.0 copy-start.3
  4.7 6.0 %lookup_start.1 = (f32[64,16,144]{2,1,0:T(8,128)S(1)}, s32[162,128]{1,0:T(8,128)S(1)}, bf16[800,256]{1,0:T(8,128)(2,1)S(1)}) custom-call(s32[1]{0:T(128)} %bitcast.core_ref, s32[144,144]{1,0:T(8,128)S(1)} %copy-done.6, f32[16,6336]{1,0:T(8,128)S(1)} %bitcast.11), custom_call_target="tpu_custom_call" | custom-call | flops 6000000000 | tf_op jit(solution)/shard_map/lookup_start/pallas_call | solution.py:229
  10.7 1.8 %collective-permute-done.first.above = f32[160,512]{1,0:T(8,128)S(1)} collective-permute-done((f32[160,512]{1,0:T(8,128)}, f32[160,512]{1,0:T(8,128)S(1)}, u32[]{:S(2)}, u32[]{:S(2)}) %collective-permute-start) | collective-permute-done | bytes 327712 | tf_op jit(solution)/shard_map/ppermute | solution.py:668
  12.5 0.0 copy-done.3
  12.5 3.3 %collective-permute-start.1 = (f32[160,512]{1,0:T(8,128)S(1)}, f32[160,512]{1,0:T(8,128)S(1)}, u32[]{:S(2)}, u32[]{:S(2)}) collective-permute-start(f32[160,512]{1,0:T(8,128)S(1)} %stack.2), channel_id=1, source_target_pairs={{0,15},{1,0},{2,1},{3,2},{4,3},{5,4},{6,5},{7,6},{8,7},{9,8},{10,9... | collective-permute-start | bytes 983048 | tf_op jit(solution)/shard_map/ppermute | solution.py:671
  15.9 0.0 copy-start
  15.9 0.0 copy-start.1
  15.9 0.0 copy-start.4
  15.9 6.9 %lookup_end.1.bias_end = f32[80,16,144]{2,1,0:T(8,128)S(1)} custom-call(s32[162,128]{1,0:T(8,128)S(1)} %get-tuple-element.53.places, bf16[800,256]{1,0:T(8,128)(2,1)S(1)} %get-tuple-element.43.left), custom_call_target="tpu_custom_call" | custom-call | flops 6000000000 | tf_op jit(solution)/shard_map/lookup_end/pallas_call | solution.py:249
  22.8 0.0 collective-permute-done.1.beside
  22.8 0.0 copy-done
  22.8 0.0 copy-done.1
  22.8 0.0 copy-done.4
  22.8 13.1 %window.1 = (f32[256,2048]{1,0:T(8,128)S(1)}, f32[256,2048]{1,0:T(8,128)}, f32[162,8,128]{2,1,0:T(8,128)S(1)}, f32[162,8,128]{2,1,0:T(8,128)}, f32[36,512]{1,0:T...) custom-call(s32[1]{0:T(128)} %bitcast.core_ref, f32[80,512]{1,0:T(8,128)S(1)} %copy-done.4, ...), custom_call_target="tpu_custom_call" | custom-call | tf_op jit(solution)/shard_map/window/pallas_call | solution.py:406
  35.9 0.0 collective-permute-start.3
  35.9 0.5 collective-permute-start.4
  36.4 0.0 collective-permute-start.2
  36.4 4.0 %collective-permute-done.3.came = f32[256,2048]{1,0:T(8,128)} collective-permute-done((f32[256,2048]{1,0:T(8,128)}, f32[256,2048]{1,0:T(8,128)}, u32[]{:S(2)}, u32[]{:S(2)}) %collective-permute-start.3) | collective-permute-done | bytes 2097184 | tf_op jit(solution)/shard_map/ppermute | solution.py:677
  40.4 1.8 %split.1 = (f32[256,1024]{1,0:T(8,128)S(1)}, f32[256,512]{1,0:T(8,128)S(1)}, f32[256,512]{1,0:T(8,128)S(1)}) custom-call(s32[1]{0:T(128)} %bitcast.6.odd, f32[256,2048]{1,0:T(8,128)S(1)} %get-tuple-element.48.keep, f32[256,2048]{1,0:T(8,128)} %collective-permute-done.3.came), custom_call_target="tpu_custom_call" | custom-call | tf_op jit(solution)/shard_map/split/pallas_call | solution.py:521
  42.2 2.4 %collective-permute-done.2.second.beside = f32[72,512]{1,0:T(8,128)S(1)} collective-permute-done((f32[72,512]{1,0:T(8,128)S(1)}, f32[72,512]{1,0:T(8,128)S(1)}, u32[]{:S(2)}, u32[]{:S(2)}) %collective-permute-start.2) | collective-permute-done | bytes 147488 | tf_op jit(solution)/shard_map/ppermute | solution.py:679
  44.6 7.1 %collective-permute-start.5 = (f32[72,512]{1,0:T(8,128)S(1)}, f32[72,512]{1,0:T(8,128)S(1)}, u32[]{:S(2)}, u32[]{:S(2)}) collective-permute-start(f32[72,512]{1,0:T(8,128)S(1)} %stack.3), channel_id=1, source_target_pairs={{0,240},{1,241},{2,242},{3,243},{4,244},{5,245},{6,246},{7,247},{8... | collective-permute-start | bytes 442376 | tf_op jit(solution)/shard_map/ppermute | solution.py:684
  51.7 0.0 collective-permute-start.6
  51.7 2.3 %collective-permute-start.7 = (f32[256,512]{1,0:T(8,128)S(1)}, f32[256,512]{1,0:T(8,128)S(1)}, u32[]{:S(2)}, u32[]{:S(2)}) collective-permute-start(f32[256,512]{1,0:T(8,128)S(1)} %get-tuple-element.64), channel_id=1, source_target_pairs={{0,224},{32,64},{64,32},{96,128},{128,96},{160,192},{192,160},{224... | collective-permute-start | bytes 1572872 | tf_op jit(solution)/shard_map/ppermute | solution.py:682
  54.1 0.0 collective-permute-done.4.came
  54.1 0.0 copy-start.2
  54.1 10.0 %scatter.1 = (f32[8,16,256]{2,1,0:T(8,128)S(1)}, f32[8,16,256]{2,1,0:T(8,128)S(1)}) custom-call(s32[1]{0:T(128)} %bitcast.core_ref, s32[162,128]{1,0:T(8,128)S(1)} %get-tuple-element.53.places, f32[162,8,128]{2,1,0:T(8,128)S(1)} %get-tuple-element.54.keep, f32[162,8,128]{2,1,0:T(8,128)} %collective-permute-done.4.came), custom_call_target="tpu_custom_call" | custom-call | flops 8999999488 | tf_op jit(solution)/shard_map/scatter/pallas_call | solution.py:489
  64.1 0.1 collective-permute-start.8
  64.2 0.0 collective-permute-done.5.below
  64.2 0.0 copy-done.2
  64.2 0.8 place.1
  65.0 0.5 collective-permute-done.8.table_came
  65.6 0.0 collective-permute-done.6.came_a
  65.6 0.0 collective-permute-done.7.came_b
  65.6 0.1 join.1
  65.7 22.7 %all_to_all.15.parts = f32[8,32,1280]{2,1,0:T(8,128)S(1)} all-to-all(f32[8,32,1280]{2,1,0:T(8,128)S(1)} %join.1), channel_id=1, replica_groups=mesh['z'=8,'y_lo'=2,'x'=4,'y_hi'=2,'core'=2] {'x','y_hi'}, dimensions={0} | all-to-all | bytes 2621440 | tf_op jit(solution)/shard_map/all_to_all | solution.py:694
  88.4 0.1 fold_lon.1
  88.5 14.6 %all_to_all.16.parts = f32[8,4,1280]{2,1,0:T(4,128)S(1)} all-to-all(f32[8,4,1280]{2,1,0:T(4,128)S(1)} %fold_lon.1), channel_id=1, replica_groups={{0,16,64,80,128,144,192,208},{32,48,96,112,160,176,224,240},{1,17,65,81..., dimensions={0} | all-to-all | bytes 327680 | tf_op jit(solution)/shard_map/all_to_all | solution.py:696
  103.1 13.7 %all_to_all.17.parts = f32[16,4,1280]{2,1,0:T(4,128)S(1)} all-to-all(f32[16,4,1280]{2,1,0:T(4,128)S(1)} %fold_lat.1), channel_id=1, replica_groups=mesh['z'=8,'y_lo'=2,'x'=4,'y_hi'=2,'core'=2] {'z','y_lo'}, dimensions={0} | all-to-all | bytes 655360 | tf_op jit(solution)/shard_map/all_to_all | solution.py:697
  116.8 0.7 unpack.1
  (3 shorter events, 0.1 us)
Async XLA Ops:
  0.6 4.0 %copy-start.5 = (f32[6336,16]{0,1:T(8,128)S(1)}, f32[6336,16]{0,1:T(8,128)}, u32[]{:S(2)}) copy-start(f32[6336,16]{0,1:T(8,128)} %param.11) | copy-start | bytes 1216516
  0.6 4.0 %copy-start.6 = (s32[144,144]{1,0:T(8,128)S(1)}, s32[144,144]{1,0:T(8,128)}, u32[]{:S(2)}) copy-start(s32[144,144]{1,0:T(8,128)} %index.1) | copy-start | bytes 248836
  2.8 9.7 %collective-permute-start = (f32[160,512]{1,0:T(8,128)}, f32[160,512]{1,0:T(8,128)S(1)}, u32[]{:S(2)}, u32[]{:S(2)}) collective-permute-start(f32[160,512]{1,0:T(8,128)} %get-tuple-element.38), channel_id=1, source_target_pairs={{0,16},{1,17},{2,18},{3,19},{4,20},{5,21},{6,22},{7,23},{8,24},{9,... | collective-permute-start | bytes 983048 | tf_op jit(solution)/shard_map/ppermute | solution.py:668
  4.7 7.9 %copy-start.3 = (f32[80,512]{1,0:T(8,128)S(1)}, f32[80,512]{1,0:T(8,128)}, u32[]{:S(2)}) copy-start(f32[80,512]{1,0:T(8,128)} %get-tuple-element.41.second) | copy-start | bytes 491524
  12.5 10.3 %collective-permute-start.1 = (f32[160,512]{1,0:T(8,128)S(1)}, f32[160,512]{1,0:T(8,128)S(1)}, u32[]{:S(2)}, u32[]{:S(2)}) collective-permute-start(f32[160,512]{1,0:T(8,128)S(1)} %stack.2), channel_id=1, source_target_pairs={{0,15},{1,0},{2,1},{3,2},{4,3},{5,4},{6,5},{7,6},{8,7},{9,8},{10,9... | collective-permute-start | bytes 983048 | tf_op jit(solution)/shard_map/ppermute | solution.py:671
  15.9 7.0 %copy-start = (f32[512,1536]{1,0:T(8,128)S(1)}, f32[512,1536]{1,0:T(8,128)}, u32[]{:S(2)}) copy-start(f32[512,1536]{1,0:T(8,128)} %in_weight.1) | copy-start | bytes 9437188
  15.9 7.0 %copy-start.1 = (f32[512,512]{1,0:T(8,128)S(1)}, f32[512,512]{1,0:T(8,128)}, u32[]{:S(2)}) copy-start(f32[512,512]{1,0:T(8,128)} %out_weight.1) | copy-start | bytes 3145732
  15.9 7.0 %copy-start.4 = (f32[80,512]{1,0:T(8,128)S(1)}, f32[80,512]{1,0:T(8,128)}, u32[]{:S(2)}) copy-start(f32[80,512]{1,0:T(8,128)} %get-tuple-element.37.own) | copy-start | bytes 491524
  35.9 4.5 %collective-permute-start.3 = (f32[256,2048]{1,0:T(8,128)}, f32[256,2048]{1,0:T(8,128)}, u32[]{:S(2)}, u32[]{:S(2)}) collective-permute-start(f32[256,2048]{1,0:T(8,128)} %get-tuple-element.49), channel_id=1, source_target_pairs={{0,1},{1,0},{2,3},{3,2},{4,5},{5,4},{6,7},{7,6},{8,9},{9,8},{10,11... | collective-permute-start | bytes 6291464 | tf_op jit(solution)/shard_map/ppermute | solution.py:677
  35.9 18.2 %collective-permute-start.4 = (f32[162,8,128]{2,1,0:T(8,128)}, f32[162,8,128]{2,1,0:T(8,128)}, u32[]{:S(2)}, u32[]{:S(2)}) collective-permute-start(f32[162,8,128]{2,1,0:T(8,128)} %get-tuple-element.55), channel_id=1, source_target_pairs={{0,1},{1,0},{2,3},{3,2},{4,5},{5,4},{6,7},{7,6},{8,9},{9,8},{10,11... | collective-permute-start | bytes 1990664 | tf_op jit(solution)/shard_map/ppermute | solution.py:678
  36.4 8.2 %collective-permute-start.2 = (f32[72,512]{1,0:T(8,128)S(1)}, f32[72,512]{1,0:T(8,128)S(1)}, u32[]{:S(2)}, u32[]{:S(2)}) collective-permute-start(f32[72,512]{1,0:T(8,128)S(1)} %get-tuple-element.47), channel_id=1, source_target_pairs={{0,1},{1,2},{2,3},{3,4},{4,5},{5,6},{6,7},{7,8},{8,9},{9,10},{10,1... | collective-permute-start | bytes 442376 | tf_op jit(solution)/shard_map/ppermute | solution.py:679
  44.6 19.6 %collective-permute-start.5 = (f32[72,512]{1,0:T(8,128)S(1)}, f32[72,512]{1,0:T(8,128)S(1)}, u32[]{:S(2)}, u32[]{:S(2)}) collective-permute-start(f32[72,512]{1,0:T(8,128)S(1)} %stack.3), channel_id=1, source_target_pairs={{0,240},{1,241},{2,242},{3,243},{4,244},{5,245},{6,246},{7,247},{8... | collective-permute-start | bytes 442376 | tf_op jit(solution)/shard_map/ppermute | solution.py:684
  51.7 13.8 %collective-permute-start.6 = (f32[256,512]{1,0:T(8,128)S(1)}, f32[256,512]{1,0:T(8,128)S(1)}, u32[]{:S(2)}, u32[]{:S(2)}) collective-permute-start(f32[256,512]{1,0:T(8,128)S(1)} %get-tuple-element.63), channel_id=1, source_target_pairs={{0,32},{32,0},{64,96},{96,64},{128,160},{160,128},{192,224},{224,1... | collective-permute-start | bytes 1572872 | tf_op jit(solution)/shard_map/ppermute | solution.py:681
  51.7 13.8 %collective-permute-start.7 = (f32[256,512]{1,0:T(8,128)S(1)}, f32[256,512]{1,0:T(8,128)S(1)}, u32[]{:S(2)}, u32[]{:S(2)}) collective-permute-start(f32[256,512]{1,0:T(8,128)S(1)} %get-tuple-element.64), channel_id=1, source_target_pairs={{0,224},{32,64},{64,32},{96,128},{128,96},{160,192},{192,160},{224... | collective-permute-start | bytes 1572872 | tf_op jit(solution)/shard_map/ppermute | solution.py:682
  54.1 10.2 %copy-start.2 = (f32[2,12,6,512]{3,0,2,1:T(2,128)S(1)}, f32[2,12,6,512]{3,0,2,1:T(2,128)}, u32[]{:S(2)}) copy-start(f32[2,12,6,512]{3,0,2,1:T(2,128)} %param.8) | copy-start | bytes 884740
  64.1 1.4 %collective-permute-start.8 = (f32[8,16,256]{2,1,0:T(8,128)S(1)}, f32[8,16,256]{2,1,0:T(8,128)S(1)}, u32[]{:S(2)}, u32[]{:S(2)}) collective-permute-start(f32[8,16,256]{2,1,0:T(8,128)S(1)} %get-tuple-element.66), channel_id=1, source_target_pairs={{0,1},{1,0},{2,3},{3,2},{4,5},{5,4},{6,7},{7,6},{8,9},{9,8},{10,11... | collective-permute-start | bytes 393224 | tf_op jit(solution)/shard_map/ppermute | solution.py:689

commit v6 on v5

--- a/solution.py
+++ b/solution.py
@@ -18,8 +18,7 @@
 BLOCKS = 25
 PACK_MIB = 56
 ROWS = 162
-SPLIT = 64
-LOOKUP_COST = 6
+LOOKUP_COST = 13
 WINDOW_COST = 0
 SCATTER_COST = 9
 FACTOR = HEAD_DIM ** (-0.5)
@@ -87,24 +86,23 @@
     return jnp.where(source == token, 1.0, 0.0).astype(BF16)
 
 
-def pack_kernel(last, fields, grads, ids, own, down, left):
+def pack_kernel(last, fields, grads, ids, own, left, below, corner):
     lanes = lax.broadcasted_iota(jnp.int32, (2, WIDTH), 1)
     level = lax.broadcasted_iota(jnp.int32, (2, WIDTH), 0)
     bump = last[0]
     plan = (
-        (own, 0, 0, 3, 2, None),
-        (left, 0, 0, 0, 3, None),
-        (down, 0, 6, 3, 0, bump),
-        (down, 80, 6, 0, 1, bump),
+        (own, 0, 3, 2, None),
+        (left, 0, 0, 3, None),
+        (below, 6, 3, 0, bump),
+        (corner, 6, 0, 1, bump),
     )
-    for ref, base, row0, col0, quadrant, offset in plan:
+    for ref, row0, col0, quadrant, offset in plan:
         label = jnp.zeros((2, WIDTH), jnp.int32)
         for row in range(6):
             for col in range(3):
                 spot = row * 6 + col * 2
-                at = base + spot
-                ref[at : at + 2, :] = fields[row0 + row, col0 + col]
-                ref[QUAD + at : QUAD + at + 2, :] = grads[row0 + row, col0 + col]
+                ref[spot : spot + 2, :] = fields[row0 + row, col0 + col]
+                ref[QUAD + spot : QUAD + spot + 2, :] = grads[row0 + row, col0 + col]
                 value = ids[col0 + col, :, row0 + row : row0 + row + 1] + 1
                 if offset is not None:
                     value = value + offset
@@ -113,19 +111,16 @@
                     lanes == level + place, jnp.broadcast_to(value, (2, WIDTH)), label
                 )
         total = jnp.sum(label.astype(F32), axis=0, keepdims=True)
-        ref[base + 72 : base + 80, :] = jnp.broadcast_to(total, (8, WIDTH))
+        ref[72:80, :] = jnp.broadcast_to(total, (8, WIDTH))
 
 
 def pack(last, fields, grads, ids):
+    shape = jax.ShapeDtypeStruct((80, WIDTH), F32)
     return pl.pallas_call(
         pack_kernel,
-        out_shape=[
-            jax.ShapeDtypeStruct((80, WIDTH), F32),
-            jax.ShapeDtypeStruct((160, WIDTH), F32),
-            jax.ShapeDtypeStruct((80, WIDTH), F32),
-        ],
+        out_shape=[shape] * 4,
         in_specs=[scalar()] + whole(3),
-        out_specs=whole(3),
+        out_specs=whole(4),
         compiler_params=params(PACK_MIB),
         cost_estimate=cost(1),
         name="pack",
@@ -160,38 +155,7 @@
     return lax.broadcasted_iota(jnp.int32, (256, 128), 0).astype(F32).astype(BF16)
 
 
-def find_pairs(matrix, places, bias, steps, pairs, first):
-    lines = line_numbers()
-    left = matrix[...]
-
-    def find(rows):
-        right = jnp.concatenate([one_hot(row, lines) for row in rows], axis=1)
-        found = dot(left, right, NN)
-        block = jnp.concatenate([row >> 8 for row in rows], axis=1)
-        block = jnp.broadcast_to(block, (32, 256))
-        total = jnp.zeros((32, 256), F32)
-        for b in range(BLOCKS):
-            total = jnp.where(block == b, found[b * 32 : b * 32 + 32], total)
-        return total[:16] + total[16:]
-
-    def step(i, carry):
-        base = pl.multiple_of(i * 8, 8)
-        rows = places[pl.ds(base + first, 8), :]
-        for pair in range(4):
-            found = find([rows[2 * pair + j : 2 * pair + j + 1, :] for j in range(2)])
-            for j in range(2):
-                bias[base + 2 * pair + j, :, 0:128] = found[:, j * 128 : j * 128 + 128]
-        return carry
-
-    lax.fori_loop(0, steps, step, 0)
-    for pair in range(pairs):
-        at = TOKENS + first // 8 + 2 * pair
-        found = find([places[at + j : at + j + 1, :] for j in range(2)])
-        for j in range(16):
-            bias[16 * pair + j, :, 128:144] = found[:, 16 * j : 16 * j + 16]
-
-
-def lookup_start_kernel(core_ref, index, table, bias, places, left):
+def lookup_kernel(core_ref, index, table, bias, places, left):
     value = index[...]
     high = (value >> 7).astype(F32).astype(BF16)
     low = (value & 127).astype(F32).astype(BF16)
@@ -205,9 +169,7 @@
     tail = jnp.concatenate([result[:, 128:], jnp.zeros((TOKENS, 112), F32)], axis=1)
     for i in range(18):
         spread = pltpu.roll(tail[8 * i : 8 * i + 8, :], 0, 1, stride=16, stride_axis=0)
-        places[TOKENS + i : TOKENS + i + 1, :] = jnp.sum(spread, axis=0, keepdims=True).astype(
-            jnp.int32
-        )
+        places[TOKENS + i : TOKENS + i + 1, :] = jnp.sum(spread, axis=0, keepdims=True).astype(jnp.int32)
 
     first = core_ref[0] == 0
     for block in range(BLOCKS):
@@ -222,48 +184,59 @@
         left[block * 32 : block * 32 + 16, :], left[block * 32 + 16 : block * 32 + 32, :] = halves(
             part
         )
-    find_pairs(left, places, bias, SPLIT // 8, SPLIT // 16, 0)
-
-
-def lookup_start(core, bias_index, bias_table):
-    return pl.pallas_call(
-        lookup_start_kernel,
+    lines = line_numbers()
+    matrix = left[...]
+
+    def find(rows):
+        right = jnp.concatenate([one_hot(row, lines) for row in rows], axis=1)
+        found = dot(matrix, right, NN)
+        block = jnp.concatenate([row >> 8 for row in rows], axis=1)
+        block = jnp.broadcast_to(block, (32, 256))
+        total = jnp.zeros((32, 256), F32)
+        for b in range(BLOCKS):
+            total = jnp.where(block == b, found[b * 32 : b * 32 + 32], total)
+        return total[:16] + total[16:]
+
+    def step(i, carry):
+        base = pl.multiple_of(i * 8, 8)
+        rows = places[pl.ds(base, 8), :]
+        for pair in range(4):
+            found = find([rows[2 * pair + j : 2 * pair + j + 1, :] for j in range(2)])
+            for j in range(2):
+                bias[base + 2 * pair + j, :, 0:128] = found[:, j * 128 : j * 128 + 128]
+        return carry
+
+    lax.fori_loop(0, 18, step, 0)
+    for pair in range(9):
+        at = TOKENS + 2 * pair
+        found = find([places[at + j : at + j + 1, :] for j in range(2)])
+        for j in range(16):
+            bias[16 * pair + j, :, 128:144] = found[:, 16 * j : 16 * j + 16]
+
+
+def lookup(core, bias_index, bias_table):
+    return pl.pallas_call(
+        lookup_kernel,
         out_shape=[
-            jax.ShapeDtypeStruct((SPLIT, HEADS, TOKENS), F32),
+            jax.ShapeDtypeStruct((TOKENS, HEADS, TOKENS), F32),
             jax.ShapeDtypeStruct((ROWS, 128), jnp.int32),
-            jax.ShapeDtypeStruct((BLOCKS * 32, 256), BF16),
         ],
         in_specs=[scalar()] + whole(2),
-        out_specs=whole(3),
+        out_specs=whole(2),
+        scratch_shapes=[pltpu.VMEM((BLOCKS * 32, 256), BF16)],
         compiler_params=params(),
         cost_estimate=cost(LOOKUP_COST),
-        name="lookup_start",
+        name="lookup",
     )(core, bias_index, bias_table.T)
-
-
-def lookup_end_kernel(places, left, bias):
-    find_pairs(left, places, bias, (TOKENS - SPLIT) // 8, (TOKENS - SPLIT) // 16, SPLIT)
-
-
-def lookup_end(places, left):
-    return pl.pallas_call(
-        lookup_end_kernel,
-        out_shape=jax.ShapeDtypeStruct((TOKENS - SPLIT, HEADS, TOKENS), F32),
-        in_specs=whole(2),
-        out_specs=pl.BlockSpec(memory_space=pltpu.VMEM),
-        compiler_params=params(),
-        cost_estimate=cost(LOOKUP_COST),
-        name="lookup_end",
-    )(places, left)
 
 
 def main_kernel(
     core_ref,
     own,
-    above,
-    beside,
-    bias_start,
-    bias_end,
+    quad0,
+    quad1,
+    quad3,
+    bias,
     in_weight,
     out_weight,
     keep,
@@ -284,7 +257,7 @@
 ):
     core = core_ref[0]
     row = jnp.zeros((1, WIDTH), F32)
-    for slot, (quad, start) in enumerate(((above, 0), (beside, 0), (own, 0), (beside, 80))):
+    for slot, (quad, start) in enumerate(((quad0, 0), (quad1, 0), (own, 0), (quad3, 0))):
         at = slot * QUAD
         tokens[at : at + QUAD, :] = quad[start : start + QUAD, :]
         cotangent[at : at + QUAD, :] = quad[start + QUAD : start + 2 * QUAD, :]
@@ -331,8 +304,7 @@
             )
 
         scores = [
-            outer(q[i], k[i])
-            + jnp.concatenate([bias_start[:, slot, :], bias_end[:, slot, :]], axis=0)
+            outer(q[i], k[i]) + bias[:, slot, :]
             for i, (_, slot) in enumerate(heads)
         ]
         grad_probs = [outer(g[i], v[i]) for i in range(len(heads))]
@@ -401,7 +373,7 @@
     return jax.ShapeDtypeStruct(dims, F32)
 
 
-def window(core, own, above, beside, bias_start, bias_end, in_weight, out_weight):
+def window(core, own, quad0, quad1, quad3, bias, in_weight, out_weight):
     grad = shape(QUAD, WIDTH)
     return pl.pallas_call(
         main_kernel,
@@ -429,7 +401,7 @@
         compiler_params=params(26),
         cost_estimate=cost(WINDOW_COST),
         name="window",
-    )(core, own, above, beside, bias_start, bias_end, in_weight, out_weight)
+    )(core, own, quad0, quad1, quad3, bias, in_weight, out_weight)
 
 
 def add_pairs(places, keep, came, total):
@@ -662,39 +634,37 @@
     swap = [(0, 1), (1, 0)]
     last = jnp.where(lat == 15, 3, 0).reshape(1)
     grad_out = jnp.transpose(grad_out, (1, 2, 0, 3))
-    own, down, left = pack(
+    own, left, below, corner = pack(
         last, jnp.transpose(fields, (1, 2, 0, 3)), grad_out, jnp.transpose(region_ids, (2, 0, 1))
     )
-    above = lax.ppermute(down, everything, moves(1, 0))
-    bias_start, places, matrix = lookup_start(core, bias_index, bias_table)
-    above, places = lax.optimization_barrier((above, places))
-    beside = lax.ppermute(stack(above, (80, 160), left, (0, 80)), everything, moves(0, -1))
-    bias_end = lookup_end(places, matrix)
-    beside, bias_end = lax.optimization_barrier((beside, bias_end))
+    quad3 = lax.ppermute(left, everything, moves(0, -1))
+    quad0 = lax.ppermute(below, everything, moves(1, 0))
+    quad1 = lax.ppermute(corner, everything, moves(1, -1))
+    bias, places = lookup(core, bias_index, bias_table)
     keep, send, keep_scores, send_scores, grad_above, grad_own, grad_beside = window(
-        core, own, above, beside, bias_start, bias_end, in_weight, out_weight
+        core, own, quad0, quad1, quad3, bias, in_weight, out_weight
     )
     came = lax.ppermute(send, "core", swap)
     came_scores = lax.ppermute(send_scores, "core", swap)
-    back_beside = lax.ppermute(grad_beside, everything, moves(0, 1))
     part, send_a, send_b = split(odd, keep, came)
     came_a = lax.ppermute(send_a, "z", [(i, i ^ 1) for i in range(8)])
     came_b = lax.ppermute(send_b, "z", [(i, ((i + 1) % 8 ^ 1) + 7 & 7) for i in range(8)])
-    back_beside, part = lax.optimization_barrier((back_beside, part))
+    part, places = lax.optimization_barrier((part, places))
+    mine, other = scatter(core, places, keep_scores, came_scores)
+    came_table = lax.ppermute(other, "core", swap)
+    grad_beside, mine = lax.optimization_barrier((grad_beside, mine))
+    back_beside = lax.ppermute(grad_beside, everything, moves(0, 1))
+    joined = join(core, part, came_a, came_b, mine, came_table)
+    parts = lax.all_to_all(joined, ("x", "y_hi"), 0, 0)
+    parts, back_beside = lax.optimization_barrier((parts, back_beside))
     back_below = lax.ppermute(
         stack(grad_above, (0, QUAD), back_beside, (0, QUAD)), everything, moves(-1, 0)
     )
-    part, places = lax.optimization_barrier((part, places))
-    mine, other = scatter(core, places, keep_scores, came_scores)
-    came_table = lax.ppermute(other, "core", swap)
-    mine, grad_own = lax.optimization_barrier((mine, grad_own))
-    grad_fields = place(grad_out, grad_own, back_beside, back_below)
-    part, grad_fields = lax.optimization_barrier((part, grad_fields))
-    joined = join(core, part, came_a, came_b, mine, came_table)
-    parts = lax.all_to_all(joined, ("x", "y_hi"), 0, 0)
     parity = [[z * 2 + y for z in range(bit, 8, 2) for y in range(2)] for bit in range(2)]
     parts = lax.all_to_all(fold_lon(parts), LAT, 0, 0, axis_index_groups=parity)
     parts = lax.all_to_all(fold_lat(parts), LAT, 0, 0)
+    parts, back_below = lax.optimization_barrier((parts, back_below))
+    grad_fields = place(grad_out, grad_own, back_beside, back_below)
     grad_in_weight, grad_out_weight, grad_bias = unpack(parts)
     return jnp.transpose(grad_fields, (2, 0, 1, 3)), grad_in_weight, grad_out_weight, grad_bias.T
 

time: 118 us -> 119 us (level)
  blocking collectives: 51 us -> 13.8 us
  waiting for transfers between devices: 8.73 us -> 37 us
  starting transfers between devices: 15.2 us -> 22.3 us
  Pallas kernels: 41.8 us -> 43.2 us
    all_to_all x2 -> x0, blocking collectives: 36.4 us -> none  [the longest x1 22.7 us: body(): parts = lax.all_to_all(joined, ('x', 'y_hi'), 0, 0)]
    ppermute x1, waiting for transfers between devices: 2.38 us -> 21.1 us  [body(): back_beside = lax.ppermute(grad_beside, everything, moves(0, 1))]
    ppermute x1, waiting for transfers between devices: 0.01 us -> 8.46 us  [body(): lax.ppermute(stack(grad_above, (0, QUAD), back_beside, (0, QUAD)), everyt...]
    all_to_all x0 -> x2, starting transfers between devices: none -> 7.64 us  [the longest x1 3.94 us: body(): parts = lax.all_to_all(fold_lat(parts), LAT, 0, 0)]
    ppermute x1, starting transfers between devices: 7.12 us -> 0.3 us  [body(): lax.ppermute(stack(grad_above, (0, QUAD), back_beside, (0, QUAD)), everyt...]
    ppermute x2 -> x3, starting transfers between devices: 5.12 us -> 7.59 us  [the longest x1 3.76 us: body(): quad1 = lax.ppermute(corner, everything, moves(1, -1))]
    ppermute x1, starting transfers between devices: 0.01 us -> 2.02 us  [body(): came_a = lax.ppermute(send_a, 'z', [(i, i ^ 1) for i in range(8)])]
    ppermute x2 -> x3, waiting for transfers between devices: 1.83 us -> 0.01 us  [the longest x1 0.01 us: body(): quad0 = lax.ppermute(below, everything, moves(1, 0))]
  transfers between devices with their start and end apart: 9 -> 12, of which waited for: 4 -> 6; matrix products, arithmetic and copies ran while one was open for 0% -> 0% of each run, Pallas kernels for 22% -> 21%
where the time goes in v6:
time: 119 us; the launch traced here: 118 us
  Pallas kernels  43.2 us (36%)
  waiting for transfers between devices  37 us (31%)
  starting transfers between devices  22.3 us (19%)
  blocking collectives  13.8 us (12%)
    ppermute x1, waiting for transfers between devices, body(): back_beside = lax.ppermute(grad_beside, everything, moves(0, 1))  21.1 us
    all_to_all x1, blocking collectives, body(): parts = lax.all_to_all(fold_lon(parts), LAT, 0, 0, axis_index_groups=parity)  13.8 us
    pallas_call x1, Pallas kernels, window(): pl.pallas_call(main_kernel, out_shape=[shape(256, 4 * WIDTH), shape(256,...  13 us
    pallas_call x1, Pallas kernels, lookup(): pl.pallas_call(lookup_kernel, out_shape=[jax.ShapeDtypeStruct((TOKENS, HE...  12.7 us
    pallas_call x1, Pallas kernels, scatter(): pl.pallas_call(scatter_kernel, out_shape=[shape(8, 16, 256)] * 2, in_spec...  9.99 us
    ppermute x1, waiting for transfers between devices, body(): lax.ppermute(stack(grad_above, (0, QUAD), back_beside, (0, QUAD)), everyt...  8.46 us
    ppermute x1, starting transfers between devices, body(): lax.ppermute(send_b, 'z', [(i, ((i + 1) % 8 ^ 1) + 7 & 7) for i in range(...  4.07 us
    ppermute x1, waiting for transfers between devices, body(): came = lax.ppermute(send, 'core', swap)  3.99 us
  transfers between devices with their start and end apart: 12, of which 6 were waited for; matrix products, arithmetic and copies ran while one was open for 0% of the time, Pallas kernels for 21%

profile of v6, /device:TPU:8, one launch (start us, length us, event | category | flops | bytes accessed | tf_op | source)
XLA Modules:
  0.0 117.9 jit_solution(9002928634662018049)
XLA Ops:
  0.6 0.0 copy-start.4
  0.6 0.0 copy-start.5
  0.7 2.1 %pack.1 = (f32[80,512]{1,0:T(8,128)}, f32[80,512]{1,0:T(8,128)}, f32[80,512]{1,0:T(8,128)}, f32[80,512]{1,0:T(8,128)}) custom-call(s32[1]{0:T(128)} %bitcast.2.last, f32[12,6,2,512]{3,2,1,0:T(2,128)} %bitcast.13, f32[12,6,2,512]{3,2,1,0:T(2,128)} %bitcast.9, s32[6,2,12]{2,1,0:T(2,128)} %bitcast.15), custom_call_target="tpu_custom_call" | custom-call | flops 1000000000 | tf_op jit(solution)/shard_map/pack/pallas_call | solution.py:119
  2.8 1.8 %collective-permute-start = (f32[80,512]{1,0:T(8,128)}, f32[80,512]{1,0:T(8,128)S(1)}, u32[]{:S(2)}, u32[]{:S(2)}) collective-permute-start(f32[80,512]{1,0:T(8,128)} %get-tuple-element.34), channel_id=1, source_target_pairs={{0,16},{1,17},{2,18},{3,19},{4,20},{5,21},{6,22},{7,23},{8,24},{9,... | collective-permute-start | bytes 491528 | tf_op jit(solution)/shard_map/ppermute | solution.py:641
  4.6 3.8 %collective-permute-start.1 = (f32[80,512]{1,0:T(8,128)}, f32[80,512]{1,0:T(8,128)S(1)}, u32[]{:S(2)}, u32[]{:S(2)}) collective-permute-start(f32[80,512]{1,0:T(8,128)} %get-tuple-element.35), channel_id=1, source_target_pairs={{0,31},{1,16},{2,17},{3,18},{4,19},{5,20},{6,21},{7,22},{8,23},{9,... | collective-permute-start | bytes 491528 | tf_op jit(solution)/shard_map/ppermute | solution.py:642
  8.4 2.0 %collective-permute-start.2 = (f32[80,512]{1,0:T(8,128)}, f32[80,512]{1,0:T(8,128)S(1)}, u32[]{:S(2)}, u32[]{:S(2)}) collective-permute-start(f32[80,512]{1,0:T(8,128)} %get-tuple-element.36), channel_id=1, source_target_pairs={{0,15},{1,0},{2,1},{3,2},{4,3},{5,4},{6,5},{7,6},{8,7},{9,8},{10,9... | collective-permute-start | bytes 491528 | tf_op jit(solution)/shard_map/ppermute | solution.py:640
  10.4 0.0 copy-done.4
  10.4 0.0 copy-done.5
  10.4 0.0 copy-start
  10.4 0.0 copy-start.3
  10.4 12.7 %lookup.1 = (f32[144,16,144]{2,1,0:T(8,128)S(1)}, s32[162,128]{1,0:T(8,128)S(1)}) custom-call(s32[1]{0:T(128)} %bitcast.1.core_ref, s32[144,144]{1,0:T(8,128)S(1)} %copy-done.5, f32[16,6336]{1,0:T(8,128)S(1)} %bitcast.11), custom_call_target="tpu_custom_call" | custom-call | flops 12999999488 | tf_op jit(solution)/shard_map/lookup/pallas_call | solution.py:218
  23.1 0.0 collective-permute-done.quad0
  23.1 0.0 collective-permute-done.1.quad1
  23.1 0.0 collective-permute-done.2.quad3
  23.1 0.0 copy-done
  23.1 0.0 copy-done.1
  23.2 0.0 copy-done.3
  23.2 13.0 %window.1 = (f32[256,2048]{1,0:T(8,128)S(1)}, f32[256,2048]{1,0:T(8,128)}, f32[162,8,128]{2,1,0:T(8,128)S(1)}, f32[162,8,128]{2,1,0:T(8,128)}, f32[36,512]{1,0:T...) custom-call(s32[1]{0:T(128)} %bitcast.1.core_ref, f32[80,512]{1,0:T(8,128)S(1)} %copy-done.3, ...), custom_call_target="tpu_custom_call" | custom-call | tf_op jit(solution)/shard_map/window/pallas_call | solution.py:378
  36.2 0.7 copy-done.6
  36.9 0.0 collective-permute-start.3
  36.9 0.5 collective-permute-start.6
  37.4 4.0 %collective-permute-done.3.came = f32[256,2048]{1,0:T(8,128)} collective-permute-done((f32[256,2048]{1,0:T(8,128)}, f32[256,2048]{1,0:T(8,128)}, u32[]{:S(2)}, u32[]{:S(2)}) %collective-permute-start.3) | collective-permute-done | bytes 2097184 | tf_op jit(solution)/shard_map/ppermute | solution.py:647
  41.4 1.8 %split.1 = (f32[256,1024]{1,0:T(8,128)S(1)}, f32[256,512]{1,0:T(8,128)S(1)}, f32[256,512]{1,0:T(8,128)S(1)}) custom-call(s32[1]{0:T(128)} %bitcast.6.odd, f32[256,2048]{1,0:T(8,128)S(1)} %get-tuple-element.39.keep, f32[256,2048]{1,0:T(8,128)} %collective-permute-done.3.came), custom_call_target="tpu_custom_call" | custom-call | tf_op jit(solution)/shard_map/split/pallas_call | solution.py:493
  43.2 2.0 %collective-permute-start.4 = (f32[256,512]{1,0:T(8,128)S(1)}, f32[256,512]{1,0:T(8,128)S(1)}, u32[]{:S(2)}, u32[]{:S(2)}) collective-permute-start(f32[256,512]{1,0:T(8,128)S(1)} %get-tuple-element.44), channel_id=1, source_target_pairs={{0,32},{32,0},{64,96},{96,64},{128,160},{160,128},{192,224},{224,1... | collective-permute-start | bytes 1572872 | tf_op jit(solution)/shard_map/ppermute | solution.py:650
  45.2 4.1 %collective-permute-start.5 = (f32[256,512]{1,0:T(8,128)S(1)}, f32[256,512]{1,0:T(8,128)S(1)}, u32[]{:S(2)}, u32[]{:S(2)}) collective-permute-start(f32[256,512]{1,0:T(8,128)S(1)} %get-tuple-element.45), channel_id=1, source_target_pairs={{0,224},{32,64},{64,32},{96,128},{128,96},{160,192},{192,160},{224... | collective-permute-start | bytes 1572872 | tf_op jit(solution)/shard_map/ppermute | solution.py:651
  49.3 0.0 collective-permute-done.6.came
  49.3 10.0 %scatter.1 = (f32[8,16,256]{2,1,0:T(8,128)S(1)}, f32[8,16,256]{2,1,0:T(8,128)S(1)}) custom-call(s32[1]{0:T(128)} %bitcast.1.core_ref, s32[162,128]{1,0:T(8,128)S(1)} %get-tuple-element.47.places, f32[162,8,128]{2,1,0:T(8,128)S(1)} %get-tuple-element.48.keep, f32[162,8,128]{2,1,0:T(8,128)} %collective-permute-done.6.came), custom_call_target="tpu_custom_call" | custom-call | flops 8999999488 | tf_op jit(solution)/shard_map/scatter/pallas_call | solution.py:461
  59.3 0.1 collective-permute-start.7
  59.4 1.3 %collective-permute-done.7.table_came = f32[8,16,256]{2,1,0:T(8,128)S(1)} collective-permute-done((f32[8,16,256]{2,1,0:T(8,128)S(1)}, f32[8,16,256]{2,1,0:T(8,128)S(1)}, u32[]{:S(2)}, u32[]{:S(2)}) %collective-permute-start.7) | collective-permute-done | bytes 131104 | tf_op jit(solution)/shard_map/ppermute | solution.py:654
  60.7 0.0 collective-permute-done.4.came_a
  60.7 0.5 collective-permute-done.5.came_b
  61.2 1.2 %join.1 = f32[8,32,1280]{2,1,0:T(8,128)} custom-call(s32[1]{0:T(128)} %bitcast.1.core_ref, f32[256,1024]{1,0:T(8,128)S(1)} %get-tuple-element.43.own, f32[256,512]{1,0:T(8,128)S(1)} %collective-permute-done.4.came_a, f32[256,512]{1,0:T(8,128)S(1)} %collective-permute-done.5.came_b, f32[8,16,256]{2,1,0:T(8,128)S(1)} %get-tuple-element.51.table_keep, ...), custom_call_target="tpu_custom_call" | custom-call | tf_op jit(solution)/shard_map/join/pallas_call | solution.py:515
  62.4 3.7 %all-to-all-start = ((f32[8,32,1280]{2,1,0:T(8,128)}), f32[8,32,1280]{2,1,0:T(8,128)S(1)}, u32[]{:S(2)}, u32[]{:S(2)}) async-start(f32[8,32,1280]{2,1,0:T(8,128)} %join.1), calls=%async_computation | async-start | bytes 2621440 | tf_op jit(solution)/shard_map/all_to_all | solution.py:658
  66.1 0.0 copy-done.7
  66.1 0.0 copy-start.2
  66.1 0.1 collective-permute-start.8
  66.2 21.1 %collective-permute-done.8.second.beside = f32[72,512]{1,0:T(8,128)S(1)} collective-permute-done((f32[72,512]{1,0:T(8,128)S(1)}, f32[72,512]{1,0:T(8,128)S(1)}, u32[]{:S(2)}, u32[]{:S(2)}) %collective-permute-start.8) | collective-permute-done | bytes 147488 | tf_op jit(solution)/shard_map/ppermute | solution.py:656
  87.3 0.0 all-to-all-done.parts
  87.3 0.1 fold_lon.1
  87.4 13.8 %all_to_all.15.parts = f32[8,4,1280]{2,1,0:T(4,128)S(1)} all-to-all(f32[8,4,1280]{2,1,0:T(4,128)S(1)} %fold_lon.1), channel_id=1, replica_groups={{0,16,64,80,128,144,192,208},{32,48,96,112,160,176,224,240},{1,17,65,81..., dimensions={0} | all-to-all | bytes 327680 | tf_op jit(solution)/shard_map/all_to_all | solution.py:664
  101.2 0.8 fold_lat.1
  102.0 3.9 %all-to-all-start.2 = ((f32[16,4,1280]{2,1,0:T(4,128)}), f32[16,4,1280]{2,1,0:T(4,128)S(1)}, u32[]{:S(2)}, u32[]{:S(2)}) async-start(f32[16,4,1280]{2,1,0:T(4,128)} %fold_lat.1), calls=%async_computation.2 | async-start | bytes 655360 | tf_op jit(solution)/shard_map/all_to_all | solution.py:665
  106.0 0.3 collective-permute-start.9
  106.3 8.5 %collective-permute-done.9.below = f32[72,512]{1,0:T(8,128)S(1)} collective-permute-done((f32[72,512]{1,0:T(8,128)S(1)}, f32[72,512]{1,0:T(8,128)S(1)}, u32[]{:S(2)}, u32[]{:S(2)}) %collective-permute-start.9) | collective-permute-done | bytes 147488 | tf_op jit(solution)/shard_map/ppermute | solution.py:660
  114.7 1.7 %all-to-all-done.2.parts = f32[16,4,1280]{2,1,0:T(4,128)S(1)} async-done(((f32[16,4,1280]{2,1,0:T(4,128)}), f32[16,4,1280]{2,1,0:T(4,128)S(1)}, u32[]{:S(2)}, u32[]{:S(2)}) %all-to-all-start.2) | async-done | bytes 327712 | tf_op jit(solution)/shard_map/all_to_all | solution.py:665
  116.4 0.7 unpack.1
  117.1 0.0 copy-done.2
  117.1 0.8 place.1
  (4 shorter events, 0.0 us)
Async XLA Ops:
  0.6 9.7 %copy-start.4 = (f32[6336,16]{0,1:T(8,128)S(1)}, f32[6336,16]{0,1:T(8,128)}, u32[]{:S(2)}) copy-start(f32[6336,16]{0,1:T(8,128)} %param.11) | copy-start | bytes 1216516
  0.6 9.7 %copy-start.5 = (s32[144,144]{1,0:T(8,128)S(1)}, s32[144,144]{1,0:T(8,128)}, u32[]{:S(2)}) copy-start(s32[144,144]{1,0:T(8,128)} %index.1) | copy-start | bytes 248836
  2.8 20.3 %collective-permute-start = (f32[80,512]{1,0:T(8,128)}, f32[80,512]{1,0:T(8,128)S(1)}, u32[]{:S(2)}, u32[]{:S(2)}) collective-permute-start(f32[80,512]{1,0:T(8,128)} %get-tuple-element.34), channel_id=1, source_target_pairs={{0,16},{1,17},{2,18},{3,19},{4,20},{5,21},{6,22},{7,23},{8,24},{9,... | collective-permute-start | bytes 491528 | tf_op jit(solution)/shard_map/ppermute | solution.py:641
  4.6 18.5 %collective-permute-start.1 = (f32[80,512]{1,0:T(8,128)}, f32[80,512]{1,0:T(8,128)S(1)}, u32[]{:S(2)}, u32[]{:S(2)}) collective-permute-start(f32[80,512]{1,0:T(8,128)} %get-tuple-element.35), channel_id=1, source_target_pairs={{0,31},{1,16},{2,17},{3,18},{4,19},{5,20},{6,21},{7,22},{8,23},{9,... | collective-permute-start | bytes 491528 | tf_op jit(solution)/shard_map/ppermute | solution.py:642
  8.4 14.8 %collective-permute-start.2 = (f32[80,512]{1,0:T(8,128)}, f32[80,512]{1,0:T(8,128)S(1)}, u32[]{:S(2)}, u32[]{:S(2)}) collective-permute-start(f32[80,512]{1,0:T(8,128)} %get-tuple-element.36), channel_id=1, source_target_pairs={{0,15},{1,0},{2,1},{3,2},{4,3},{5,4},{6,5},{7,6},{8,7},{9,8},{10,9... | collective-permute-start | bytes 491528 | tf_op jit(solution)/shard_map/ppermute | solution.py:640
  10.4 12.8 %copy-start = (f32[512,1536]{1,0:T(8,128)S(1)}, f32[512,1536]{1,0:T(8,128)}, u32[]{:S(2)}) copy-start(f32[512,1536]{1,0:T(8,128)} %in_weight.1) | copy-start | bytes 9437188
  10.4 12.8 %copy-start.1 = (f32[512,512]{1,0:T(8,128)S(1)}, f32[512,512]{1,0:T(8,128)}, u32[]{:S(2)}) copy-start(f32[512,512]{1,0:T(8,128)} %out_weight.1) | copy-start | bytes 3145732
  10.4 12.8 %copy-start.3 = (f32[80,512]{1,0:T(8,128)S(1)}, f32[80,512]{1,0:T(8,128)}, u32[]{:S(2)}) copy-start(f32[80,512]{1,0:T(8,128)} %get-tuple-element.33.own) | copy-start | bytes 491524
  36.2 0.7 copy-start.6
  36.9 4.5 %collective-permute-start.3 = (f32[256,2048]{1,0:T(8,128)}, f32[256,2048]{1,0:T(8,128)}, u32[]{:S(2)}, u32[]{:S(2)}) collective-permute-start(f32[256,2048]{1,0:T(8,128)} %get-tuple-element.40), channel_id=1, source_target_pairs={{0,1},{1,0},{2,3},{3,2},{4,5},{5,4},{6,7},{7,6},{8,9},{9,8},{10,11... | collective-permute-start | bytes 6291464 | tf_op jit(solution)/shard_map/ppermute | solution.py:647
  36.9 12.4 %collective-permute-start.6 = (f32[162,8,128]{2,1,0:T(8,128)}, f32[162,8,128]{2,1,0:T(8,128)}, u32[]{:S(2)}, u32[]{:S(2)}) collective-permute-start(f32[162,8,128]{2,1,0:T(8,128)} %get-tuple-element.49), channel_id=1, source_target_pairs={{0,1},{1,0},{2,3},{3,2},{4,5},{5,4},{6,7},{7,6},{8,9},{9,8},{10,11... | collective-permute-start | bytes 1990664 | tf_op jit(solution)/shard_map/ppermute | solution.py:648
  43.2 17.5 %collective-permute-start.4 = (f32[256,512]{1,0:T(8,128)S(1)}, f32[256,512]{1,0:T(8,128)S(1)}, u32[]{:S(2)}, u32[]{:S(2)}) collective-permute-start(f32[256,512]{1,0:T(8,128)S(1)} %get-tuple-element.44), channel_id=1, source_target_pairs={{0,32},{32,0},{64,96},{96,64},{128,160},{160,128},{192,224},{224,1... | collective-permute-start | bytes 1572872 | tf_op jit(solution)/shard_map/ppermute | solution.py:650
  45.2 16.0 %collective-permute-start.5 = (f32[256,512]{1,0:T(8,128)S(1)}, f32[256,512]{1,0:T(8,128)S(1)}, u32[]{:S(2)}, u32[]{:S(2)}) collective-permute-start(f32[256,512]{1,0:T(8,128)S(1)} %get-tuple-element.45), channel_id=1, source_target_pairs={{0,224},{32,64},{64,32},{96,128},{128,96},{160,192},{192,160},{224... | collective-permute-start | bytes 1572872 | tf_op jit(solution)/shard_map/ppermute | solution.py:651
  59.3 1.4 %collective-permute-start.7 = (f32[8,16,256]{2,1,0:T(8,128)S(1)}, f32[8,16,256]{2,1,0:T(8,128)S(1)}, u32[]{:S(2)}, u32[]{:S(2)}) collective-permute-start(f32[8,16,256]{2,1,0:T(8,128)S(1)} %get-tuple-element.52), channel_id=1, source_target_pairs={{0,1},{1,0},{2,3},{3,2},{4,5},{5,4},{6,7},{7,6},{8,9},{9,8},{10,11... | collective-permute-start | bytes 393224 | tf_op jit(solution)/shard_map/ppermute | solution.py:654
  62.4 3.7 %copy-start.7 = (f32[72,512]{1,0:T(8,128)S(1)}, f32[72,512]{1,0:T(8,128)}, u32[]{:S(2)}) copy-start(f32[72,512]{1,0:T(8,128)} %copy-done.6) | copy-start | bytes 442372
  62.4 24.9 %all-to-all-start = ((f32[8,32,1280]{2,1,0:T(8,128)}), f32[8,32,1280]{2,1,0:T(8,128)S(1)}, u32[]{:S(2)}, u32[]{:S(2)}) async-start(f32[8,32,1280]{2,1,0:T(8,128)} %join.1), calls=%async_computation | async-start | bytes 2621440 | tf_op jit(solution)/shard_map/all_to_all | solution.py:658
  66.1 51.0 %copy-start.2 = (f32[2,12,6,512]{3,0,2,1:T(2,128)S(1)}, f32[2,12,6,512]{3,0,2,1:T(2,128)}, u32[]{:S(2)}) copy-start(f32[2,12,6,512]{3,0,2,1:T(2,128)} %param.8) | copy-start | bytes 884740
  66.1 21.2 %collective-permute-start.8 = (f32[72,512]{1,0:T(8,128)S(1)}, f32[72,512]{1,0:T(8,128)S(1)}, u32[]{:S(2)}, u32[]{:S(2)}) collective-permute-start(f32[72,512]{1,0:T(8,128)S(1)} %copy-done.7), channel_id=1, source_target_pairs={{0,1},{1,2},{2,3},{3,4},{4,5},{5,6},{6,7},{7,8},{8,9},{9,10},{10,1... | collective-permute-start | bytes 442376 | tf_op jit(solution)/shard_map/ppermute | solution.py:656
  102.0 14.4 %all-to-all-start.2 = ((f32[16,4,1280]{2,1,0:T(4,128)}), f32[16,4,1280]{2,1,0:T(4,128)S(1)}, u32[]{:S(2)}, u32[]{:S(2)}) async-start(f32[16,4,1280]{2,1,0:T(4,128)} %fold_lat.1), calls=%async_computation.2 | async-start | bytes 655360 | tf_op jit(solution)/shard_map/all_to_all | solution.py:665
  106.0 8.8 %collective-permute-start.9 = (f32[72,512]{1,0:T(8,128)S(1)}, f32[72,512]{1,0:T(8,128)S(1)}, u32[]{:S(2)}, u32[]{:S(2)}) collective-permute-start(f32[72,512]{1,0:T(8,128)S(1)} %stack.1), channel_id=1, source_target_pairs={{0,240},{1,241},{2,242},{3,243},{4,244},{5,245},{6,246},{7,247},{8... | collective-permute-start | bytes 442376 | tf_op jit(solution)/shard_map/ppermute | solution.py:660

commit v7 on v6

--- a/solution.py
+++ b/solution.py
@@ -1,5 +1,3 @@
-import functools
-
 import jax
 import jax.numpy as jnp
 from jax import lax
@@ -127,24 +125,6 @@
     )(last, fields, grads, ids)
 
 
-def stack_kernel(spans, first, second, out):
-    (start1, stop1), (start2, stop2) = spans
-    out[0 : stop1 - start1, :] = first[start1:stop1, :]
-    out[stop1 - start1 :, :] = second[start2:stop2, :]
-
-
-def stack(first, span1, second, span2):
-    rows = span1[1] - span1[0] + span2[1] - span2[0]
-    return pl.pallas_call(
-        functools.partial(stack_kernel, (span1, span2)),
-        out_shape=jax.ShapeDtypeStruct((rows, WIDTH), F32),
-        in_specs=whole(2),
-        out_specs=pl.BlockSpec(memory_space=pltpu.VMEM),
-        compiler_params=params(),
-        name="stack",
-    )(first, second)
-
-
 def one_hot(row, lines):
     low = (row & 255).astype(F32).astype(BF16)
     hit = lines == jnp.broadcast_to(low, (256, 128))
@@ -243,9 +223,10 @@
     send,
     keep_scores,
     send_scores,
-    grad_above,
-    grad_own,
-    grad_beside,
+    grad0,
+    grad1,
+    grad2,
+    grad3,
     tokens,
     cotangent,
     proj,
@@ -363,10 +344,8 @@
         - normed * jnp.mean(grad_normed * normed, axis=1, keepdims=True)
     )
     tokens[...] = result
-    grad_above[...] = tokens[0:QUAD, :]
-    grad_beside[0:QUAD, :] = tokens[QUAD : 2 * QUAD, :]
-    grad_own[...] = tokens[2 * QUAD : 3 * QUAD, :]
-    grad_beside[QUAD:, :] = tokens[3 * QUAD :, :]
+    for slot, target in enumerate((grad0, grad1, grad2, grad3)):
+        target[...] = tokens[slot * QUAD : slot * QUAD + QUAD, :]
 
 
 def shape(*dims):
@@ -384,10 +363,11 @@
             shape(ROWS, 8, 128),
             grad,
             grad,
-            shape(2 * QUAD, WIDTH),
+            grad,
+            grad,
         ],
         in_specs=[scalar()] + whole(7),
-        out_specs=whole(7),
+        out_specs=whole(8),
         scratch_shapes=[
             pltpu.VMEM((TOKENS, WIDTH), F32),
             pltpu.VMEM((TOKENS, WIDTH), F32),
@@ -490,11 +470,15 @@
 
 
 def split(odd, keep, came):
+    def rows(width):
+        return pl.BlockSpec((64, width), lambda i: (i, 0))
+
     return pl.pallas_call(
         split_kernel,
         out_shape=[shape(256, 1024), shape(256, 512), shape(256, 512)],
-        in_specs=[scalar()] + whole(2),
-        out_specs=whole(3),
+        grid=(4,),
+        in_specs=[scalar(), rows(2048), rows(2048)],
+        out_specs=[rows(1024), rows(512), rows(512)],
         compiler_params=params(),
         name="split",
     )(odd, keep, came)
@@ -592,26 +576,25 @@
     )(parts)
 
 
-def place_kernel(grad_out, own, beside, below, out):
-    plan = ((own, 0, 0, 3), (beside, QUAD, 0, 0), (below, 0, 6, 3), (below, QUAD, 6, 0))
-    for ref, base, row0, col0 in plan:
+def place_kernel(grad_out, own, left, below, corner, out):
+    for ref, row0, col0 in ((own, 0, 3), (left, 0, 0), (below, 6, 3), (corner, 6, 0)):
         for row in range(6):
             for col in range(3):
-                spot = base + row * 6 + col * 2
+                spot = row * 6 + col * 2
                 out[row0 + row, col0 + col] = (
                     grad_out[row0 + row, col0 + col] + ref[spot : spot + 2, :]
                 )
 
 
-def place(grad_out, own, beside, below):
+def place(grad_out, own, left, below, corner):
     return pl.pallas_call(
         place_kernel,
         out_shape=jax.ShapeDtypeStruct(grad_out.shape, F32),
-        in_specs=whole(4),
+        in_specs=whole(5),
         out_specs=pl.BlockSpec(memory_space=pltpu.VMEM),
         compiler_params=params(),
         name="place",
-    )(grad_out, own, beside, below)
+    )(grad_out, own, left, below, corner)
 
 
 LAT = ("z", "y_lo")
@@ -641,30 +624,30 @@
     quad0 = lax.ppermute(below, everything, moves(1, 0))
     quad1 = lax.ppermute(corner, everything, moves(1, -1))
     bias, places = lookup(core, bias_index, bias_table)
-    keep, send, keep_scores, send_scores, grad_above, grad_own, grad_beside = window(
+    keep, send, keep_scores, send_scores, grad0, grad1, grad2, grad3 = window(
         core, own, quad0, quad1, quad3, bias, in_weight, out_weight
     )
     came = lax.ppermute(send, "core", swap)
     came_scores = lax.ppermute(send_scores, "core", swap)
+    back = (
+        lax.ppermute(grad3, everything, moves(0, 1)),
+        lax.ppermute(grad0, everything, moves(-1, 0)),
+        lax.ppermute(grad1, everything, moves(-1, 1)),
+    )
     part, send_a, send_b = split(odd, keep, came)
     came_a = lax.ppermute(send_a, "z", [(i, i ^ 1) for i in range(8)])
     came_b = lax.ppermute(send_b, "z", [(i, ((i + 1) % 8 ^ 1) + 7 & 7) for i in range(8)])
-    part, places = lax.optimization_barrier((part, places))
+    part, places, back = lax.optimization_barrier((part, places, back))
     mine, other = scatter(core, places, keep_scores, came_scores)
     came_table = lax.ppermute(other, "core", swap)
-    grad_beside, mine = lax.optimization_barrier((grad_beside, mine))
-    back_beside = lax.ppermute(grad_beside, everything, moves(0, 1))
+    mine, grad2 = lax.optimization_barrier((mine, grad2))
+    grad_fields = place(grad_out, grad2, *back)
+    part, grad_fields = lax.optimization_barrier((part, grad_fields))
     joined = join(core, part, came_a, came_b, mine, came_table)
     parts = lax.all_to_all(joined, ("x", "y_hi"), 0, 0)
-    parts, back_beside = lax.optimization_barrier((parts, back_beside))
-    back_below = lax.ppermute(
-        stack(grad_above, (0, QUAD), back_beside, (0, QUAD)), everything, moves(-1, 0)
-    )
     parity = [[z * 2 + y for z in range(bit, 8, 2) for y in range(2)] for bit in range(2)]
     parts = lax.all_to_all(fold_lon(parts), LAT, 0, 0, axis_index_groups=parity)
     parts = lax.all_to_all(fold_lat(parts), LAT, 0, 0)
-    parts, back_below = lax.optimization_barrier((parts, back_below))
-    grad_fields = place(grad_out, grad_own, back_beside, back_below)
     grad_in_weight, grad_out_weight, grad_bias = unpack(parts)
     return jnp.transpose(grad_fields, (2, 0, 1, 3)), grad_in_weight, grad_out_weight, grad_bias.T
 

time: 119 us -> 117 us (0.983)
  blocking collectives: 13.8 us -> 51 us
  waiting for transfers between devices: 37 us -> 5.26 us
  starting transfers between devices: 22.3 us -> 17.2 us
    all_to_all x0 -> x2, blocking collectives: none -> 35.9 us  [the longest x1 22.7 us: body(): parts = lax.all_to_all(joined, ('x', 'y_hi'), 0, 0)]
    ppermute x2 -> x3, waiting for transfers between devices: 29.5 us -> 3.79 us  [the longest x1 2.48 us: body(): lax.ppermute(grad1, everything, moves(-1, 1))]
    all_to_all x2 -> x0, starting transfers between devices: 7.64 us -> none  [the longest x1 3.94 us: body(): parts = lax.all_to_all(fold_lat(parts), LAT, 0, 0)]
    ppermute x1, waiting for transfers between devices: 3.99 us -> 0.93 us  [body(): came = lax.ppermute(send, 'core', swap)]
    ppermute x2 -> x3, starting transfers between devices: 0.39 us -> 3.06 us  [the longest x1 1.7 us: body(): lax.ppermute(grad1, everything, moves(-1, 1))]
    all_to_all x2 -> x0, waiting for transfers between devices: 1.66 us -> none  [the longest x1 1.66 us: body(): parts = lax.all_to_all(fold_lat(parts), LAT, 0, 0)]
    all_to_all x1, blocking collectives: 13.8 us -> 15.1 us  [body(): parts = lax.all_to_all(fold_lon(parts), LAT, 0, 0, axis_index_groups=parity)]
  transfers between devices with their start and end apart: 12 -> 11, of which waited for: 6 -> 4; matrix products, arithmetic and copies ran while one was open for 0% -> 0% of each run, Pallas kernels for 21% -> 22%
where the time goes in v7:
time: 117 us
  blocking collectives  51 us (44%)
  Pallas kernels  42.2 us (36%)
  starting transfers between devices  17.2 us (15%)
  waiting for transfers between devices  5.26 us (4%)
    all_to_all x1, blocking collectives, body(): parts = lax.all_to_all(joined, ('x', 'y_hi'), 0, 0)  22.7 us
    all_to_all x1, blocking collectives, body(): parts = lax.all_to_all(fold_lon(parts), LAT, 0, 0, axis_index_groups=parity)  15.1 us
    all_to_all x1, blocking collectives, body(): parts = lax.all_to_all(fold_lat(parts), LAT, 0, 0)  13.2 us
    pallas_call x1, Pallas kernels, window(): pl.pallas_call(main_kernel, out_shape=[shape(256, 4 * WIDTH), shape(256,...  13.2 us
    pallas_call x1, Pallas kernels, lookup(): pl.pallas_call(lookup_kernel, out_shape=[jax.ShapeDtypeStruct((TOKENS, HE...  12.7 us
    pallas_call x1, Pallas kernels, scatter(): pl.pallas_call(scatter_kernel, out_shape=[shape(8, 16, 256)] * 2, in_spec...  10 us
    ppermute x1, starting transfers between devices, body(): lax.ppermute(send_b, 'z', [(i, ((i + 1) % 8 ^ 1) + 7 & 7) for i in range(...  4.04 us
    ppermute x1, starting transfers between devices, body(): quad1 = lax.ppermute(corner, everything, moves(1, -1))  3.76 us
  transfers between devices with their start and end apart: 11, of which 4 were waited for; matrix products, arithmetic and copies ran while one was open for 0% of the time, Pallas kernels for 22%

profile of v7, /device:TPU:8, one launch (start us, length us, event | category | flops | bytes accessed | tf_op | source)
XLA Modules:
  0.0 116.5 jit_solution(15511872637094068129)
XLA Ops:
  0.6 0.0 copy-start.4
  0.6 0.0 copy-start.5
  0.7 2.1 %pack.1 = (f32[80,512]{1,0:T(8,128)}, f32[80,512]{1,0:T(8,128)}, f32[80,512]{1,0:T(8,128)}, f32[80,512]{1,0:T(8,128)}) custom-call(s32[1]{0:T(128)} %bitcast.2.last, f32[12,6,2,512]{3,2,1,0:T(2,128)} %bitcast.13, f32[12,6,2,512]{3,2,1,0:T(2,128)} %bitcast.9, s32[6,2,12]{2,1,0:T(2,128)} %bitcast.15), custom_call_target="tpu_custom_call" | custom-call | flops 1000000000 | tf_op jit(solution)/shard_map/pack/pallas_call | solution.py:117
  2.8 1.8 %collective-permute-start = (f32[80,512]{1,0:T(8,128)}, f32[80,512]{1,0:T(8,128)S(1)}, u32[]{:S(2)}, u32[]{:S(2)}) collective-permute-start(f32[80,512]{1,0:T(8,128)} %get-tuple-element.36), channel_id=1, source_target_pairs={{0,16},{1,17},{2,18},{3,19},{4,20},{5,21},{6,22},{7,23},{8,24},{9,... | collective-permute-start | bytes 491528 | tf_op jit(solution)/shard_map/ppermute | solution.py:624
  4.6 3.8 %collective-permute-start.1 = (f32[80,512]{1,0:T(8,128)}, f32[80,512]{1,0:T(8,128)S(1)}, u32[]{:S(2)}, u32[]{:S(2)}) collective-permute-start(f32[80,512]{1,0:T(8,128)} %get-tuple-element.37), channel_id=1, source_target_pairs={{0,31},{1,16},{2,17},{3,18},{4,19},{5,20},{6,21},{7,22},{8,23},{9,... | collective-permute-start | bytes 491528 | tf_op jit(solution)/shard_map/ppermute | solution.py:625
  8.4 2.0 %collective-permute-start.2 = (f32[80,512]{1,0:T(8,128)}, f32[80,512]{1,0:T(8,128)S(1)}, u32[]{:S(2)}, u32[]{:S(2)}) collective-permute-start(f32[80,512]{1,0:T(8,128)} %get-tuple-element.38), channel_id=1, source_target_pairs={{0,15},{1,0},{2,1},{3,2},{4,3},{5,4},{6,5},{7,6},{8,7},{9,8},{10,9... | collective-permute-start | bytes 491528 | tf_op jit(solution)/shard_map/ppermute | solution.py:623
  10.4 0.0 copy-done.4
  10.4 0.0 copy-done.5
  10.4 0.0 copy-start
  10.4 0.0 copy-start.1
  10.4 0.0 copy-start.3
  10.4 12.7 %lookup.1 = (f32[144,16,144]{2,1,0:T(8,128)S(1)}, s32[162,128]{1,0:T(8,128)S(1)}) custom-call(s32[1]{0:T(128)} %bitcast.1.core_ref, s32[144,144]{1,0:T(8,128)S(1)} %copy-done.5, f32[16,6336]{1,0:T(8,128)S(1)} %bitcast.11), custom_call_target="tpu_custom_call" | custom-call | flops 12999999488 | tf_op jit(solution)/shard_map/lookup/pallas_call | solution.py:198
  23.1 0.0 copy-start.6
  23.1 0.0 collective-permute-done.quad0
  23.1 0.0 collective-permute-done.1.quad1
  23.2 0.0 collective-permute-done.2.quad3
  23.2 0.0 copy-done
  23.2 0.0 copy-done.1
  23.2 0.0 copy-done.3
  23.2 13.2 %window.1 = (f32[256,2048]{1,0:T(8,128)S(1)}, f32[256,2048]{1,0:T(8,128)}, f32[162,8,128]{2,1,0:T(8,128)S(1)}, f32[162,8,128]{2,1,0:T(8,128)}, f32[36,512]{1,0:T...) custom-call(s32[1]{0:T(128)} %bitcast.1.core_ref, f32[80,512]{1,0:T(8,128)S(1)} %copy-done.3, ...), custom_call_target="tpu_custom_call" | custom-call | tf_op jit(solution)/shard_map/window/pallas_call | solution.py:357
  36.3 0.0 copy-done.6
  36.3 0.0 collective-permute-start.3
  36.4 0.5 collective-permute-start.7
  36.9 0.0 collective-permute-start.4
  36.9 1.3 %collective-permute-start.5 = (f32[36,512]{1,0:T(8,128)S(1)}, f32[36,512]{1,0:T(8,128)S(1)}, u32[]{:S(2)}, u32[]{:S(2)}) collective-permute-start(f32[36,512]{1,0:T(8,128)S(1)} %get-tuple-element.45), channel_id=1, source_target_pairs={{0,240},{1,241},{2,242},{3,243},{4,244},{5,245},{6,246},{7,247},{8... | collective-permute-start | bytes 221192 | tf_op jit(solution)/shard_map/ppermute | solution.py:634
  38.2 1.7 %collective-permute-start.6 = (f32[36,512]{1,0:T(8,128)S(1)}, f32[36,512]{1,0:T(8,128)S(1)}, u32[]{:S(2)}, u32[]{:S(2)}) collective-permute-start(f32[36,512]{1,0:T(8,128)S(1)} %get-tuple-element.46), channel_id=1, source_target_pairs={{0,241},{1,242},{2,243},{3,244},{4,245},{5,246},{6,247},{7,248},{8... | collective-permute-start | bytes 221192 | tf_op jit(solution)/shard_map/ppermute | solution.py:635
  39.9 0.9 collective-permute-done.3.came
  40.9 2.5 %split.1 = (f32[256,1024]{1,0:T(8,128)S(1)}, f32[256,512]{1,0:T(8,128)S(1)}, f32[256,512]{1,0:T(8,128)S(1)}) custom-call(s32[1]{0:T(128)} %bitcast.odd, f32[256,2048]{1,0:T(8,128)S(1)} %get-tuple-element.40.keep, f32[256,2048]{1,0:T(8,128)} %collective-permute-done.3.came), custom_call_target="tpu_custom_call" | custom-call | tf_op jit(solution)/shard_map/split/pallas_call | solution.py:476
  43.3 1.3 %collective-permute-done.4.left = f32[36,512]{1,0:T(8,128)S(1)} collective-permute-done((f32[36,512]{1,0:T(8,128)}, f32[36,512]{1,0:T(8,128)S(1)}, u32[]{:S(2)}, u32[]{:S(2)}) %collective-permute-start.4) | collective-permute-done | bytes 73760 | tf_op jit(solution)/shard_map/ppermute | solution.py:633
  44.6 0.0 collective-permute-done.5.below
  44.6 2.5 %collective-permute-done.6.corner = f32[36,512]{1,0:T(8,128)S(1)} collective-permute-done((f32[36,512]{1,0:T(8,128)S(1)}, f32[36,512]{1,0:T(8,128)S(1)}, u32[]{:S(2)}, u32[]{:S(2)}) %collective-permute-start.6) | collective-permute-done | bytes 73760 | tf_op jit(solution)/shard_map/ppermute | solution.py:635
  47.1 1.9 %collective-permute-start.8 = (f32[256,512]{1,0:T(8,128)S(1)}, f32[256,512]{1,0:T(8,128)S(1)}, u32[]{:S(2)}, u32[]{:S(2)}) collective-permute-start(f32[256,512]{1,0:T(8,128)S(1)} %get-tuple-element.59), channel_id=1, source_target_pairs={{0,32},{32,0},{64,96},{96,64},{128,160},{160,128},{192,224},{224,1... | collective-permute-start | bytes 1572872 | tf_op jit(solution)/shard_map/ppermute | solution.py:638
  49.1 4.0 %collective-permute-start.9 = (f32[256,512]{1,0:T(8,128)S(1)}, f32[256,512]{1,0:T(8,128)S(1)}, u32[]{:S(2)}, u32[]{:S(2)}) collective-permute-start(f32[256,512]{1,0:T(8,128)S(1)} %get-tuple-element.60), channel_id=1, source_target_pairs={{0,224},{32,64},{64,32},{96,128},{128,96},{160,192},{192,160},{224... | collective-permute-start | bytes 1572872 | tf_op jit(solution)/shard_map/ppermute | solution.py:639
  53.1 0.0 collective-permute-done.7.came
  53.1 0.0 copy-done.7
  53.1 10.0 %scatter.1 = (f32[8,16,256]{2,1,0:T(8,128)S(1)}, f32[8,16,256]{2,1,0:T(8,128)S(1)}) custom-call(s32[1]{0:T(128)} %bitcast.1.core_ref, s32[162,128]{1,0:T(8,128)S(1)} %copy-done.7, f32[162,8,128]{2,1,0:T(8,128)S(1)} %get-tuple-element.49.keep, f32[162,8,128]{2,1,0:T(8,128)} %collective-permute-done.7.came), custom_call_target="tpu_custom_call" | custom-call | flops 8999999488 | tf_op jit(solution)/shard_map/scatter/pallas_call | solution.py:441
  63.1 0.1 collective-permute-start.10
  63.2 0.0 copy-done.2
  63.3 0.8 place.1
  64.1 0.5 collective-permute-done.10.table_came
  64.6 0.0 collective-permute-done.8.came_a
  64.6 0.0 collective-permute-done.9.came_b
  64.6 0.1 join.1
  64.7 22.7 %all_to_all.15.parts = f32[8,32,1280]{2,1,0:T(8,128)S(1)} all-to-all(f32[8,32,1280]{2,1,0:T(8,128)S(1)} %join.1), channel_id=1, replica_groups=mesh['z'=8,'y_lo'=2,'x'=4,'y_hi'=2,'core'=2] {'x','y_hi'}, dimensions={0} | all-to-all | bytes 2621440 | tf_op jit(solution)/shard_map/all_to_all | solution.py:647
  87.4 0.1 fold_lon.1
  87.5 15.1 %all_to_all.16.parts = f32[8,4,1280]{2,1,0:T(4,128)S(1)} all-to-all(f32[8,4,1280]{2,1,0:T(4,128)S(1)} %fold_lon.1), channel_id=1, replica_groups={{0,16,64,80,128,144,192,208},{32,48,96,112,160,176,224,240},{1,17,65,81..., dimensions={0} | all-to-all | bytes 327680 | tf_op jit(solution)/shard_map/all_to_all | solution.py:649
  102.6 13.2 %all_to_all.17.parts = f32[16,4,1280]{2,1,0:T(4,128)S(1)} all-to-all(f32[16,4,1280]{2,1,0:T(4,128)S(1)} %fold_lat.1), channel_id=1, replica_groups=mesh['z'=8,'y_lo'=2,'x'=4,'y_hi'=2,'core'=2] {'z','y_lo'}, dimensions={0} | all-to-all | bytes 655360 | tf_op jit(solution)/shard_map/all_to_all | solution.py:650
  115.8 0.7 unpack.1
  (3 shorter events, 0.0 us)
Async XLA Ops:
  0.6 9.8 %copy-start.4 = (f32[6336,16]{0,1:T(8,128)S(1)}, f32[6336,16]{0,1:T(8,128)}, u32[]{:S(2)}) copy-start(f32[6336,16]{0,1:T(8,128)} %param.11) | copy-start | bytes 1216516
  0.6 9.7 %copy-start.5 = (s32[144,144]{1,0:T(8,128)S(1)}, s32[144,144]{1,0:T(8,128)}, u32[]{:S(2)}) copy-start(s32[144,144]{1,0:T(8,128)} %index.1) | copy-start | bytes 248836
  2.8 20.3 %collective-permute-start = (f32[80,512]{1,0:T(8,128)}, f32[80,512]{1,0:T(8,128)S(1)}, u32[]{:S(2)}, u32[]{:S(2)}) collective-permute-start(f32[80,512]{1,0:T(8,128)} %get-tuple-element.36), channel_id=1, source_target_pairs={{0,16},{1,17},{2,18},{3,19},{4,20},{5,21},{6,22},{7,23},{8,24},{9,... | collective-permute-start | bytes 491528 | tf_op jit(solution)/shard_map/ppermute | solution.py:624
  4.6 18.6 %collective-permute-start.1 = (f32[80,512]{1,0:T(8,128)}, f32[80,512]{1,0:T(8,128)S(1)}, u32[]{:S(2)}, u32[]{:S(2)}) collective-permute-start(f32[80,512]{1,0:T(8,128)} %get-tuple-element.37), channel_id=1, source_target_pairs={{0,31},{1,16},{2,17},{3,18},{4,19},{5,20},{6,21},{7,22},{8,23},{9,... | collective-permute-start | bytes 491528 | tf_op jit(solution)/shard_map/ppermute | solution.py:625
  8.4 14.8 %collective-permute-start.2 = (f32[80,512]{1,0:T(8,128)}, f32[80,512]{1,0:T(8,128)S(1)}, u32[]{:S(2)}, u32[]{:S(2)}) collective-permute-start(f32[80,512]{1,0:T(8,128)} %get-tuple-element.38), channel_id=1, source_target_pairs={{0,15},{1,0},{2,1},{3,2},{4,3},{5,4},{6,5},{7,6},{8,7},{9,8},{10,9... | collective-permute-start | bytes 491528 | tf_op jit(solution)/shard_map/ppermute | solution.py:623
  10.4 12.8 %copy-start = (f32[512,1536]{1,0:T(8,128)S(1)}, f32[512,1536]{1,0:T(8,128)}, u32[]{:S(2)}) copy-start(f32[512,1536]{1,0:T(8,128)} %in_weight.1) | copy-start | bytes 9437188
  10.4 12.8 %copy-start.1 = (f32[512,512]{1,0:T(8,128)S(1)}, f32[512,512]{1,0:T(8,128)}, u32[]{:S(2)}) copy-start(f32[512,512]{1,0:T(8,128)} %out_weight.1) | copy-start | bytes 3145732
  10.4 12.8 %copy-start.3 = (f32[80,512]{1,0:T(8,128)S(1)}, f32[80,512]{1,0:T(8,128)}, u32[]{:S(2)}) copy-start(f32[80,512]{1,0:T(8,128)} %get-tuple-element.35.own) | copy-start | bytes 491524
  23.1 13.2 %copy-start.6 = (s32[162,128]{1,0:T(8,128)}, s32[162,128]{1,0:T(8,128)S(1)}, u32[]{:S(2)}) copy-start(s32[162,128]{1,0:T(8,128)S(1)} %get-tuple-element.48.places) | copy-start | bytes 248836
  36.3 4.5 %collective-permute-start.3 = (f32[256,2048]{1,0:T(8,128)}, f32[256,2048]{1,0:T(8,128)}, u32[]{:S(2)}, u32[]{:S(2)}) collective-permute-start(f32[256,2048]{1,0:T(8,128)} %get-tuple-element.41), channel_id=1, source_target_pairs={{0,1},{1,0},{2,3},{3,2},{4,5},{5,4},{6,7},{7,6},{8,9},{9,8},{10,11... | collective-permute-start | bytes 6291464 | tf_op jit(solution)/shard_map/ppermute | solution.py:630
  36.4 16.7 %collective-permute-start.7 = (f32[162,8,128]{2,1,0:T(8,128)}, f32[162,8,128]{2,1,0:T(8,128)}, u32[]{:S(2)}, u32[]{:S(2)}) collective-permute-start(f32[162,8,128]{2,1,0:T(8,128)} %get-tuple-element.50), channel_id=1, source_target_pairs={{0,1},{1,0},{2,3},{3,2},{4,5},{5,4},{6,7},{7,6},{8,9},{9,8},{10,11... | collective-permute-start | bytes 1990664 | tf_op jit(solution)/shard_map/ppermute | solution.py:631
  36.9 7.8 %collective-permute-start.4 = (f32[36,512]{1,0:T(8,128)}, f32[36,512]{1,0:T(8,128)S(1)}, u32[]{:S(2)}, u32[]{:S(2)}) collective-permute-start(f32[36,512]{1,0:T(8,128)} %get-tuple-element.44), channel_id=1, source_target_pairs={{0,1},{1,2},{2,3},{3,4},{4,5},{5,6},{6,7},{7,8},{8,9},{9,10},{10,1... | collective-permute-start | bytes 221192 | tf_op jit(solution)/shard_map/ppermute | solution.py:633
  36.9 7.8 %collective-permute-start.5 = (f32[36,512]{1,0:T(8,128)S(1)}, f32[36,512]{1,0:T(8,128)S(1)}, u32[]{:S(2)}, u32[]{:S(2)}) collective-permute-start(f32[36,512]{1,0:T(8,128)S(1)} %get-tuple-element.45), channel_id=1, source_target_pairs={{0,240},{1,241},{2,242},{3,243},{4,244},{5,245},{6,246},{7,247},{8... | collective-permute-start | bytes 221192 | tf_op jit(solution)/shard_map/ppermute | solution.py:634
  38.2 8.9 %collective-permute-start.6 = (f32[36,512]{1,0:T(8,128)S(1)}, f32[36,512]{1,0:T(8,128)S(1)}, u32[]{:S(2)}, u32[]{:S(2)}) collective-permute-start(f32[36,512]{1,0:T(8,128)S(1)} %get-tuple-element.46), channel_id=1, source_target_pairs={{0,241},{1,242},{2,243},{3,244},{4,245},{5,246},{6,247},{7,248},{8... | collective-permute-start | bytes 221192 | tf_op jit(solution)/shard_map/ppermute | solution.py:635
  40.9 12.3 %copy-start.7 = (s32[162,128]{1,0:T(8,128)S(1)}, s32[162,128]{1,0:T(8,128)}, u32[]{:S(2)}) copy-start(s32[162,128]{1,0:T(8,128)} %copy-done.6) | copy-start | bytes 248836
  47.1 17.5 %collective-permute-start.8 = (f32[256,512]{1,0:T(8,128)S(1)}, f32[256,512]{1,0:T(8,128)S(1)}, u32[]{:S(2)}, u32[]{:S(2)}) collective-permute-start(f32[256,512]{1,0:T(8,128)S(1)} %get-tuple-element.59), channel_id=1, source_target_pairs={{0,32},{32,0},{64,96},{96,64},{128,160},{160,128},{192,224},{224,1... | collective-permute-start | bytes 1572872 | tf_op jit(solution)/shard_map/ppermute | solution.py:638
  49.1 15.5 %collective-permute-start.9 = (f32[256,512]{1,0:T(8,128)S(1)}, f32[256,512]{1,0:T(8,128)S(1)}, u32[]{:S(2)}, u32[]{:S(2)}) collective-permute-start(f32[256,512]{1,0:T(8,128)S(1)} %get-tuple-element.60), channel_id=1, source_target_pairs={{0,224},{32,64},{64,32},{96,128},{128,96},{160,192},{192,160},{224... | collective-permute-start | bytes 1572872 | tf_op jit(solution)/shard_map/ppermute | solution.py:639
  53.1 10.1 %copy-start.2 = (f32[2,12,6,512]{3,0,2,1:T(2,128)S(1)}, f32[2,12,6,512]{3,0,2,1:T(2,128)}, u32[]{:S(2)}) copy-start(f32[2,12,6,512]{3,0,2,1:T(2,128)} %param.8) | copy-start | bytes 884740
  63.1 1.4 %collective-permute-start.10 = (f32[8,16,256]{2,1,0:T(8,128)S(1)}, f32[8,16,256]{2,1,0:T(8,128)S(1)}, u32[]{:S(2)}, u32[]{:S(2)}) collective-permute-start(f32[8,16,256]{2,1,0:T(8,128)S(1)} %get-tuple-element.62), channel_id=1, source_target_pairs={{0,1},{1,0},{2,3},{3,2},{4,5},{5,4},{6,7},{7,6},{8,9},{9,8},{10,11... | collective-permute-start | bytes 393224 | tf_op jit(solution)/shard_map/ppermute | solution.py:642

commit v8 on v7

--- a/solution.py
+++ b/solution.py
@@ -186,7 +186,7 @@
                 bias[base + 2 * pair + j, :, 0:128] = found[:, j * 128 : j * 128 + 128]
         return carry
 
-    lax.fori_loop(0, 18, step, 0)
+    lax.fori_loop(0, 18, step, 0, unroll=9)
     for pair in range(9):
         at = TOKENS + 2 * pair
         found = find([places[at + j : at + j + 1, :] for j in range(2)])
@@ -413,7 +413,7 @@
             add(rows, base, pair)
         return carry
 
-    lax.fori_loop(0, ROWS // 8, step, 0)
+    lax.fori_loop(0, ROWS // 8, step, 0, unroll=10)
     add(places[ROWS - 2 : ROWS, :], ROWS - 2, 0)
 
 
@@ -470,15 +470,11 @@
 
 
 def split(odd, keep, came):
-    def rows(width):
-        return pl.BlockSpec((64, width), lambda i: (i, 0))
-
     return pl.pallas_call(
         split_kernel,
         out_shape=[shape(256, 1024), shape(256, 512), shape(256, 512)],
-        grid=(4,),
-        in_specs=[scalar(), rows(2048), rows(2048)],
-        out_specs=[rows(1024), rows(512), rows(512)],
+        in_specs=[scalar()] + whole(2),
+        out_specs=whole(3),
         compiler_params=params(),
         name="split",
     )(odd, keep, came)

time: 117 us -> 114 us (0.974)
  Pallas kernels: 42.2 us -> 35 us
  blocking collectives: 51 us -> 54.2 us
  waiting for transfers between devices: 5.26 us -> 6.91 us
    pallas_call x1, Pallas kernels: 10 us -> 6.17 us  [scatter(): pl.pallas_call(scatter_kernel, out_shape=[shape(8, 16, 256)] * 2, in_spec...]
    pallas_call x1, Pallas kernels: 12.7 us -> 9.91 us  [lookup(): pl.pallas_call(lookup_kernel, out_shape=[jax.ShapeDtypeStruct((TOKENS, HE...]
    all_to_all x1, blocking collectives: 22.7 us -> 24.9 us  [body(): parts = lax.all_to_all(joined, ('x', 'y_hi'), 0, 0)]
  transfers between devices with their start and end apart: 11 -> 11, of which waited for: 4 -> 5; matrix products, arithmetic and copies ran while one was open for 0% -> 0% of each run, Pallas kernels for 22% -> 16%
where the time goes in v8:
time: 114 us
  blocking collectives  54.2 us (48%)
  Pallas kernels  35 us (31%)
  starting transfers between devices  17.2 us (15%)
  waiting for transfers between devices  6.91 us (6%)
    all_to_all x1, blocking collectives, body(): parts = lax.all_to_all(joined, ('x', 'y_hi'), 0, 0)  24.9 us
    all_to_all x1, blocking collectives, body(): parts = lax.all_to_all(fold_lon(parts), LAT, 0, 0, axis_index_groups=parity)  15.5 us
    all_to_all x1, blocking collectives, body(): parts = lax.all_to_all(fold_lat(parts), LAT, 0, 0)  13.8 us
    pallas_call x1, Pallas kernels, window(): pl.pallas_call(main_kernel, out_shape=[shape(256, 4 * WIDTH), shape(256,...  13.2 us
    pallas_call x1, Pallas kernels, lookup(): pl.pallas_call(lookup_kernel, out_shape=[jax.ShapeDtypeStruct((TOKENS, HE...  9.91 us
    pallas_call x1, Pallas kernels, scatter(): pl.pallas_call(scatter_kernel, out_shape=[shape(8, 16, 256)] * 2, in_spec...  6.17 us
    ppermute x1, starting transfers between devices, body(): lax.ppermute(send_b, 'z', [(i, ((i + 1) % 8 ^ 1) + 7 & 7) for i in range(...  4.03 us
    ppermute x1, starting transfers between devices, body(): quad1 = lax.ppermute(corner, everything, moves(1, -1))  3.76 us
  transfers between devices with their start and end apart: 11, of which 5 were waited for; matrix products, arithmetic and copies ran while one was open for 0% of the time, Pallas kernels for 16%

profile of v8, /device:TPU:8, one launch (start us, length us, event | category | flops | bytes accessed | tf_op | source)
XLA Modules:
  0.0 114.1 jit_solution(9410669830713961163)
XLA Ops:
  0.6 0.0 copy-start.4
  0.6 0.0 copy-start.5
  0.7 2.1 %pack.1 = (f32[80,512]{1,0:T(8,128)}, f32[80,512]{1,0:T(8,128)}, f32[80,512]{1,0:T(8,128)}, f32[80,512]{1,0:T(8,128)}) custom-call(s32[1]{0:T(128)} %bitcast.2.last, f32[12,6,2,512]{3,2,1,0:T(2,128)} %bitcast.13, f32[12,6,2,512]{3,2,1,0:T(2,128)} %bitcast.9, s32[6,2,12]{2,1,0:T(2,128)} %bitcast.15), custom_call_target="tpu_custom_call" | custom-call | flops 1000000000 | tf_op jit(solution)/shard_map/pack/pallas_call | solution.py:117
  2.8 1.8 %collective-permute-start = (f32[80,512]{1,0:T(8,128)}, f32[80,512]{1,0:T(8,128)S(1)}, u32[]{:S(2)}, u32[]{:S(2)}) collective-permute-start(f32[80,512]{1,0:T(8,128)} %get-tuple-element.36), channel_id=1, source_target_pairs={{0,16},{1,17},{2,18},{3,19},{4,20},{5,21},{6,22},{7,23},{8,24},{9,... | collective-permute-start | bytes 491528 | tf_op jit(solution)/shard_map/ppermute | solution.py:620
  4.6 3.8 %collective-permute-start.1 = (f32[80,512]{1,0:T(8,128)}, f32[80,512]{1,0:T(8,128)S(1)}, u32[]{:S(2)}, u32[]{:S(2)}) collective-permute-start(f32[80,512]{1,0:T(8,128)} %get-tuple-element.37), channel_id=1, source_target_pairs={{0,31},{1,16},{2,17},{3,18},{4,19},{5,20},{6,21},{7,22},{8,23},{9,... | collective-permute-start | bytes 491528 | tf_op jit(solution)/shard_map/ppermute | solution.py:621
  8.4 2.0 %collective-permute-start.2 = (f32[80,512]{1,0:T(8,128)}, f32[80,512]{1,0:T(8,128)S(1)}, u32[]{:S(2)}, u32[]{:S(2)}) collective-permute-start(f32[80,512]{1,0:T(8,128)} %get-tuple-element.38), channel_id=1, source_target_pairs={{0,15},{1,0},{2,1},{3,2},{4,3},{5,4},{6,5},{7,6},{8,7},{9,8},{10,9... | collective-permute-start | bytes 491528 | tf_op jit(solution)/shard_map/ppermute | solution.py:619
  10.4 0.0 copy-done.4
  10.4 0.0 copy-done.5
  10.4 0.0 copy-start
  10.4 0.0 copy-start.3
  10.4 9.9 %lookup.1 = (f32[144,16,144]{2,1,0:T(8,128)S(1)}, s32[162,128]{1,0:T(8,128)S(1)}) custom-call(s32[1]{0:T(128)} %bitcast.1.core_ref, s32[144,144]{1,0:T(8,128)S(1)} %copy-done.5, f32[16,6336]{1,0:T(8,128)S(1)} %bitcast.11), custom_call_target="tpu_custom_call" | custom-call | flops 12999999488 | tf_op jit(solution)/shard_map/lookup/pallas_call | solution.py:198
  20.3 0.0 copy-start.6
  20.3 0.0 collective-permute-done.quad0
  20.3 0.0 collective-permute-done.1.quad1
  20.4 0.0 collective-permute-done.2.quad3
  20.4 0.0 copy-done
  20.4 0.0 copy-done.1
  20.4 0.0 copy-done.3
  20.4 13.2 %window.1 = (f32[256,2048]{1,0:T(8,128)S(1)}, f32[256,2048]{1,0:T(8,128)}, f32[162,8,128]{2,1,0:T(8,128)S(1)}, f32[162,8,128]{2,1,0:T(8,128)}, f32[36,512]{1,0:T...) custom-call(s32[1]{0:T(128)} %bitcast.1.core_ref, f32[80,512]{1,0:T(8,128)S(1)} %copy-done.3, ...), custom_call_target="tpu_custom_call" | custom-call | tf_op jit(solution)/shard_map/window/pallas_call | solution.py:357
  33.5 0.0 copy-done.6
  33.6 0.0 collective-permute-start.3
  33.6 0.5 collective-permute-start.7
  34.1 0.0 collective-permute-start.4
  34.1 1.3 %collective-permute-start.5 = (f32[36,512]{1,0:T(8,128)S(1)}, f32[36,512]{1,0:T(8,128)S(1)}, u32[]{:S(2)}, u32[]{:S(2)}) collective-permute-start(f32[36,512]{1,0:T(8,128)S(1)} %get-tuple-element.45), channel_id=1, source_target_pairs={{0,240},{1,241},{2,242},{3,243},{4,244},{5,245},{6,246},{7,247},{8... | collective-permute-start | bytes 221192 | tf_op jit(solution)/shard_map/ppermute | solution.py:630
  35.4 1.7 %collective-permute-start.6 = (f32[36,512]{1,0:T(8,128)S(1)}, f32[36,512]{1,0:T(8,128)S(1)}, u32[]{:S(2)}, u32[]{:S(2)}) collective-permute-start(f32[36,512]{1,0:T(8,128)S(1)} %get-tuple-element.46), channel_id=1, source_target_pairs={{0,241},{1,242},{2,243},{3,244},{4,245},{5,246},{6,247},{7,248},{8... | collective-permute-start | bytes 221192 | tf_op jit(solution)/shard_map/ppermute | solution.py:631
  37.1 0.9 collective-permute-done.3.came
  38.1 0.0 copy-start.7
  38.1 1.8 %split.1 = (f32[256,1024]{1,0:T(8,128)S(1)}, f32[256,512]{1,0:T(8,128)S(1)}, f32[256,512]{1,0:T(8,128)S(1)}) custom-call(s32[1]{0:T(128)} %bitcast.odd, f32[256,2048]{1,0:T(8,128)S(1)} %get-tuple-element.40.keep, f32[256,2048]{1,0:T(8,128)} %collective-permute-done.3.came), custom_call_target="tpu_custom_call" | custom-call | tf_op jit(solution)/shard_map/split/pallas_call | solution.py:473
  39.9 1.9 %collective-permute-done.4.left = f32[36,512]{1,0:T(8,128)S(1)} collective-permute-done((f32[36,512]{1,0:T(8,128)}, f32[36,512]{1,0:T(8,128)S(1)}, u32[]{:S(2)}, u32[]{:S(2)}) %collective-permute-start.4) | collective-permute-done | bytes 73760 | tf_op jit(solution)/shard_map/ppermute | solution.py:629
  41.8 0.0 collective-permute-done.5.below
  41.8 2.5 %collective-permute-done.6.corner = f32[36,512]{1,0:T(8,128)S(1)} collective-permute-done((f32[36,512]{1,0:T(8,128)S(1)}, f32[36,512]{1,0:T(8,128)S(1)}, u32[]{:S(2)}, u32[]{:S(2)}) %collective-permute-start.6) | collective-permute-done | bytes 73760 | tf_op jit(solution)/shard_map/ppermute | solution.py:631
  44.3 1.9 %collective-permute-start.8 = (f32[256,512]{1,0:T(8,128)S(1)}, f32[256,512]{1,0:T(8,128)S(1)}, u32[]{:S(2)}, u32[]{:S(2)}) collective-permute-start(f32[256,512]{1,0:T(8,128)S(1)} %get-tuple-element.59), channel_id=1, source_target_pairs={{0,32},{32,0},{64,96},{96,64},{128,160},{160,128},{192,224},{224,1... | collective-permute-start | bytes 1572872 | tf_op jit(solution)/shard_map/ppermute | solution.py:634
  46.3 4.0 %collective-permute-start.9 = (f32[256,512]{1,0:T(8,128)S(1)}, f32[256,512]{1,0:T(8,128)S(1)}, u32[]{:S(2)}, u32[]{:S(2)}) collective-permute-start(f32[256,512]{1,0:T(8,128)S(1)} %get-tuple-element.60), channel_id=1, source_target_pairs={{0,224},{32,64},{64,32},{96,128},{128,96},{160,192},{192,160},{224... | collective-permute-start | bytes 1572872 | tf_op jit(solution)/shard_map/ppermute | solution.py:635
  50.3 0.0 collective-permute-done.7.came
  50.3 0.0 copy-done.7
  50.3 6.2 %scatter.1 = (f32[8,16,256]{2,1,0:T(8,128)S(1)}, f32[8,16,256]{2,1,0:T(8,128)S(1)}) custom-call(s32[1]{0:T(128)} %bitcast.1.core_ref, s32[162,128]{1,0:T(8,128)S(1)} %copy-done.7, f32[162,8,128]{2,1,0:T(8,128)S(1)} %get-tuple-element.49.keep, f32[162,8,128]{2,1,0:T(8,128)} %collective-permute-done.7.came), custom_call_target="tpu_custom_call" | custom-call | flops 8999999488 | tf_op jit(solution)/shard_map/scatter/pallas_call | solution.py:441
  56.5 0.1 collective-permute-start.10
  56.6 0.0 copy-done.2
  56.6 0.8 place.1
  57.4 0.5 collective-permute-done.10.table_came
  57.9 0.0 collective-permute-done.8.came_a
  57.9 1.1 collective-permute-done.9.came_b
  59.0 0.1 join.1
  59.1 24.9 %all_to_all.15.parts = f32[8,32,1280]{2,1,0:T(8,128)S(1)} all-to-all(f32[8,32,1280]{2,1,0:T(8,128)S(1)} %join.1), channel_id=1, replica_groups=mesh['z'=8,'y_lo'=2,'x'=4,'y_hi'=2,'core'=2] {'x','y_hi'}, dimensions={0} | all-to-all | bytes 2621440 | tf_op jit(solution)/shard_map/all_to_all | solution.py:643
  84.0 0.1 fold_lon.1
  84.1 15.5 %all_to_all.16.parts = f32[8,4,1280]{2,1,0:T(4,128)S(1)} all-to-all(f32[8,4,1280]{2,1,0:T(4,128)S(1)} %fold_lon.1), channel_id=1, replica_groups={{0,16,64,80,128,144,192,208},{32,48,96,112,160,176,224,240},{1,17,65,81..., dimensions={0} | all-to-all | bytes 327680 | tf_op jit(solution)/shard_map/all_to_all | solution.py:645
  99.6 13.8 %all_to_all.17.parts = f32[16,4,1280]{2,1,0:T(4,128)S(1)} all-to-all(f32[16,4,1280]{2,1,0:T(4,128)S(1)} %fold_lat.1), channel_id=1, replica_groups=mesh['z'=8,'y_lo'=2,'x'=4,'y_hi'=2,'core'=2] {'z','y_lo'}, dimensions={0} | all-to-all | bytes 655360 | tf_op jit(solution)/shard_map/all_to_all | solution.py:646
  113.4 0.7 unpack.1
  (3 shorter events, 0.0 us)
Async XLA Ops:
  0.6 9.8 %copy-start.4 = (f32[6336,16]{0,1:T(8,128)S(1)}, f32[6336,16]{0,1:T(8,128)}, u32[]{:S(2)}) copy-start(f32[6336,16]{0,1:T(8,128)} %param.11) | copy-start | bytes 1216516
  0.6 9.7 %copy-start.5 = (s32[144,144]{1,0:T(8,128)S(1)}, s32[144,144]{1,0:T(8,128)}, u32[]{:S(2)}) copy-start(s32[144,144]{1,0:T(8,128)} %index.1) | copy-start | bytes 248836
  2.8 17.6 %collective-permute-start = (f32[80,512]{1,0:T(8,128)}, f32[80,512]{1,0:T(8,128)S(1)}, u32[]{:S(2)}, u32[]{:S(2)}) collective-permute-start(f32[80,512]{1,0:T(8,128)} %get-tuple-element.36), channel_id=1, source_target_pairs={{0,16},{1,17},{2,18},{3,19},{4,20},{5,21},{6,22},{7,23},{8,24},{9,... | collective-permute-start | bytes 491528 | tf_op jit(solution)/shard_map/ppermute | solution.py:620
  4.6 15.8 %collective-permute-start.1 = (f32[80,512]{1,0:T(8,128)}, f32[80,512]{1,0:T(8,128)S(1)}, u32[]{:S(2)}, u32[]{:S(2)}) collective-permute-start(f32[80,512]{1,0:T(8,128)} %get-tuple-element.37), channel_id=1, source_target_pairs={{0,31},{1,16},{2,17},{3,18},{4,19},{5,20},{6,21},{7,22},{8,23},{9,... | collective-permute-start | bytes 491528 | tf_op jit(solution)/shard_map/ppermute | solution.py:621
  8.4 12.0 %collective-permute-start.2 = (f32[80,512]{1,0:T(8,128)}, f32[80,512]{1,0:T(8,128)S(1)}, u32[]{:S(2)}, u32[]{:S(2)}) collective-permute-start(f32[80,512]{1,0:T(8,128)} %get-tuple-element.38), channel_id=1, source_target_pairs={{0,15},{1,0},{2,1},{3,2},{4,3},{5,4},{6,5},{7,6},{8,7},{9,8},{10,9... | collective-permute-start | bytes 491528 | tf_op jit(solution)/shard_map/ppermute | solution.py:619
  10.4 10.0 %copy-start = (f32[512,1536]{1,0:T(8,128)S(1)}, f32[512,1536]{1,0:T(8,128)}, u32[]{:S(2)}) copy-start(f32[512,1536]{1,0:T(8,128)} %in_weight.1) | copy-start | bytes 9437188
  10.4 10.0 %copy-start.1 = (f32[512,512]{1,0:T(8,128)S(1)}, f32[512,512]{1,0:T(8,128)}, u32[]{:S(2)}) copy-start(f32[512,512]{1,0:T(8,128)} %out_weight.1) | copy-start | bytes 3145732
  10.4 10.0 %copy-start.3 = (f32[80,512]{1,0:T(8,128)S(1)}, f32[80,512]{1,0:T(8,128)}, u32[]{:S(2)}) copy-start(f32[80,512]{1,0:T(8,128)} %get-tuple-element.35.own) | copy-start | bytes 491524
  20.3 13.2 %copy-start.6 = (s32[162,128]{1,0:T(8,128)}, s32[162,128]{1,0:T(8,128)S(1)}, u32[]{:S(2)}) copy-start(s32[162,128]{1,0:T(8,128)S(1)} %get-tuple-element.48.places) | copy-start | bytes 248836
  33.6 4.5 %collective-permute-start.3 = (f32[256,2048]{1,0:T(8,128)}, f32[256,2048]{1,0:T(8,128)}, u32[]{:S(2)}, u32[]{:S(2)}) collective-permute-start(f32[256,2048]{1,0:T(8,128)} %get-tuple-element.41), channel_id=1, source_target_pairs={{0,1},{1,0},{2,3},{3,2},{4,5},{5,4},{6,7},{7,6},{8,9},{9,8},{10,11... | collective-permute-start | bytes 6291464 | tf_op jit(solution)/shard_map/ppermute | solution.py:626
  33.6 16.7 %collective-permute-start.7 = (f32[162,8,128]{2,1,0:T(8,128)}, f32[162,8,128]{2,1,0:T(8,128)}, u32[]{:S(2)}, u32[]{:S(2)}) collective-permute-start(f32[162,8,128]{2,1,0:T(8,128)} %get-tuple-element.50), channel_id=1, source_target_pairs={{0,1},{1,0},{2,3},{3,2},{4,5},{5,4},{6,7},{7,6},{8,9},{9,8},{10,11... | collective-permute-start | bytes 1990664 | tf_op jit(solution)/shard_map/ppermute | solution.py:627
  34.1 7.8 %collective-permute-start.4 = (f32[36,512]{1,0:T(8,128)}, f32[36,512]{1,0:T(8,128)S(1)}, u32[]{:S(2)}, u32[]{:S(2)}) collective-permute-start(f32[36,512]{1,0:T(8,128)} %get-tuple-element.44), channel_id=1, source_target_pairs={{0,1},{1,2},{2,3},{3,4},{4,5},{5,6},{6,7},{7,8},{8,9},{9,10},{10,1... | collective-permute-start | bytes 221192 | tf_op jit(solution)/shard_map/ppermute | solution.py:629
  34.1 7.8 %collective-permute-start.5 = (f32[36,512]{1,0:T(8,128)S(1)}, f32[36,512]{1,0:T(8,128)S(1)}, u32[]{:S(2)}, u32[]{:S(2)}) collective-permute-start(f32[36,512]{1,0:T(8,128)S(1)} %get-tuple-element.45), channel_id=1, source_target_pairs={{0,240},{1,241},{2,242},{3,243},{4,244},{5,245},{6,246},{7,247},{8... | collective-permute-start | bytes 221192 | tf_op jit(solution)/shard_map/ppermute | solution.py:630
  35.4 8.9 %collective-permute-start.6 = (f32[36,512]{1,0:T(8,128)S(1)}, f32[36,512]{1,0:T(8,128)S(1)}, u32[]{:S(2)}, u32[]{:S(2)}) collective-permute-start(f32[36,512]{1,0:T(8,128)S(1)} %get-tuple-element.46), channel_id=1, source_target_pairs={{0,241},{1,242},{2,243},{3,244},{4,245},{5,246},{6,247},{7,248},{8... | collective-permute-start | bytes 221192 | tf_op jit(solution)/shard_map/ppermute | solution.py:631
  38.1 12.2 %copy-start.7 = (s32[162,128]{1,0:T(8,128)S(1)}, s32[162,128]{1,0:T(8,128)}, u32[]{:S(2)}) copy-start(s32[162,128]{1,0:T(8,128)} %copy-done.6) | copy-start | bytes 248836
  44.3 13.6 %collective-permute-start.8 = (f32[256,512]{1,0:T(8,128)S(1)}, f32[256,512]{1,0:T(8,128)S(1)}, u32[]{:S(2)}, u32[]{:S(2)}) collective-permute-start(f32[256,512]{1,0:T(8,128)S(1)} %get-tuple-element.59), channel_id=1, source_target_pairs={{0,32},{32,0},{64,96},{96,64},{128,160},{160,128},{192,224},{224,1... | collective-permute-start | bytes 1572872 | tf_op jit(solution)/shard_map/ppermute | solution.py:634
  46.3 12.7 %collective-permute-start.9 = (f32[256,512]{1,0:T(8,128)S(1)}, f32[256,512]{1,0:T(8,128)S(1)}, u32[]{:S(2)}, u32[]{:S(2)}) collective-permute-start(f32[256,512]{1,0:T(8,128)S(1)} %get-tuple-element.60), channel_id=1, source_target_pairs={{0,224},{32,64},{64,32},{96,128},{128,96},{160,192},{192,160},{224... | collective-permute-start | bytes 1572872 | tf_op jit(solution)/shard_map/ppermute | solution.py:635
  50.3 6.3 %copy-start.2 = (f32[2,12,6,512]{3,0,2,1:T(2,128)S(1)}, f32[2,12,6,512]{3,0,2,1:T(2,128)}, u32[]{:S(2)}) copy-start(f32[2,12,6,512]{3,0,2,1:T(2,128)} %param.8) | copy-start | bytes 884740
  56.5 1.4 %collective-permute-start.10 = (f32[8,16,256]{2,1,0:T(8,128)S(1)}, f32[8,16,256]{2,1,0:T(8,128)S(1)}, u32[]{:S(2)}, u32[]{:S(2)}) collective-permute-start(f32[8,16,256]{2,1,0:T(8,128)S(1)} %get-tuple-element.62), channel_id=1, source_target_pairs={{0,1},{1,0},{2,3},{3,2},{4,5},{5,4},{6,7},{7,6},{8,9},{9,8},{10,11... | collective-permute-start | bytes 393224 | tf_op jit(solution)/shard_map/ppermute | solution.py:638

commit v9 on v8

--- a/solution.py
+++ b/solution.py
@@ -186,7 +186,7 @@
                 bias[base + 2 * pair + j, :, 0:128] = found[:, j * 128 : j * 128 + 128]
         return carry
 
-    lax.fori_loop(0, 18, step, 0, unroll=9)
+    lax.fori_loop(0, 18, step, 0, unroll=18)
     for pair in range(9):
         at = TOKENS + 2 * pair
         found = find([places[at + j : at + j + 1, :] for j in range(2)])
@@ -311,8 +311,8 @@
     tails[...] = jnp.zeros_like(tails)
     order = [((1 - core) * 8 + slot, slot) for slot in range(8)]
     order += [(core * 8 + slot, 8 + slot) for slot in range(8)]
-    for first in range(0, 16, 4):
-        some_heads(order[first : first + 4])
+    for first in range(0, 16, 8):
+        some_heads(order[first : first + 8])
 
     for i in range(18):
         total = tails[8 * i]

time: 114 us -> 113 us (level)
  Pallas kernels: 35 us -> 33.4 us
where the time goes in v9:
time: 113 us
  blocking collectives  54.2 us (48%)
  Pallas kernels  33.4 us (30%)
  starting transfers between devices  17.4 us (15%)
  waiting for transfers between devices  6.74 us (6%)
    all_to_all x1, blocking collectives, body(): parts = lax.all_to_all(joined, ('x', 'y_hi'), 0, 0)  24.9 us
    all_to_all x1, blocking collectives, body(): parts = lax.all_to_all(fold_lon(parts), LAT, 0, 0, axis_index_groups=parity)  15.5 us
    all_to_all x1, blocking collectives, body(): parts = lax.all_to_all(fold_lat(parts), LAT, 0, 0)  13.9 us
    pallas_call x1, Pallas kernels, window(): pl.pallas_call(main_kernel, out_shape=[shape(256, 4 * WIDTH), shape(256,...  12.2 us
    pallas_call x1, Pallas kernels, lookup(): pl.pallas_call(lookup_kernel, out_shape=[jax.ShapeDtypeStruct((TOKENS, HE...  9.3 us
    pallas_call x1, Pallas kernels, scatter(): pl.pallas_call(scatter_kernel, out_shape=[shape(8, 16, 256)] * 2, in_spec...  6.19 us
    ppermute x1, starting transfers between devices, body(): lax.ppermute(send_b, 'z', [(i, ((i + 1) % 8 ^ 1) + 7 & 7) for i in range(...  4.04 us
    ppermute x1, starting transfers between devices, body(): quad1 = lax.ppermute(corner, everything, moves(1, -1))  3.76 us
  transfers between devices with their start and end apart: 11, of which 5 were waited for; matrix products, arithmetic and copies ran while one was open for 0% of the time, Pallas kernels for 16%

profile of v9, /device:TPU:8, one launch (start us, length us, event | category | flops | bytes accessed | tf_op | source)
XLA Modules:
  0.0 112.6 jit_solution(16604709640979066023)
XLA Ops:
  0.6 0.0 copy-start.4
  0.6 0.0 copy-start.5
  0.7 2.1 %pack.1 = (f32[80,512]{1,0:T(8,128)}, f32[80,512]{1,0:T(8,128)}, f32[80,512]{1,0:T(8,128)}, f32[80,512]{1,0:T(8,128)}) custom-call(s32[1]{0:T(128)} %bitcast.2.last, f32[12,6,2,512]{3,2,1,0:T(2,128)} %bitcast.13, f32[12,6,2,512]{3,2,1,0:T(2,128)} %bitcast.9, s32[6,2,12]{2,1,0:T(2,128)} %bitcast.15), custom_call_target="tpu_custom_call" | custom-call | flops 1000000000 | tf_op jit(solution)/shard_map/pack/pallas_call | solution.py:117
  2.8 1.8 %collective-permute-start = (f32[80,512]{1,0:T(8,128)}, f32[80,512]{1,0:T(8,128)S(1)}, u32[]{:S(2)}, u32[]{:S(2)}) collective-permute-start(f32[80,512]{1,0:T(8,128)} %get-tuple-element.36), channel_id=1, source_target_pairs={{0,16},{1,17},{2,18},{3,19},{4,20},{5,21},{6,22},{7,23},{8,24},{9,... | collective-permute-start | bytes 491528 | tf_op jit(solution)/shard_map/ppermute | solution.py:620
  4.6 3.8 %collective-permute-start.1 = (f32[80,512]{1,0:T(8,128)}, f32[80,512]{1,0:T(8,128)S(1)}, u32[]{:S(2)}, u32[]{:S(2)}) collective-permute-start(f32[80,512]{1,0:T(8,128)} %get-tuple-element.37), channel_id=1, source_target_pairs={{0,31},{1,16},{2,17},{3,18},{4,19},{5,20},{6,21},{7,22},{8,23},{9,... | collective-permute-start | bytes 491528 | tf_op jit(solution)/shard_map/ppermute | solution.py:621
  8.4 2.0 %collective-permute-start.2 = (f32[80,512]{1,0:T(8,128)}, f32[80,512]{1,0:T(8,128)S(1)}, u32[]{:S(2)}, u32[]{:S(2)}) collective-permute-start(f32[80,512]{1,0:T(8,128)} %get-tuple-element.38), channel_id=1, source_target_pairs={{0,15},{1,0},{2,1},{3,2},{4,3},{5,4},{6,5},{7,6},{8,7},{9,8},{10,9... | collective-permute-start | bytes 491528 | tf_op jit(solution)/shard_map/ppermute | solution.py:619
  10.4 0.0 copy-done.4
  10.4 0.0 copy-done.5
  10.4 0.0 copy-start.1
  10.4 0.0 copy-start.3
  10.4 9.3 %lookup.1 = (f32[144,16,144]{2,1,0:T(8,128)S(1)}, s32[162,128]{1,0:T(8,128)S(1)}) custom-call(s32[1]{0:T(128)} %bitcast.1.core_ref, s32[144,144]{1,0:T(8,128)S(1)} %copy-done.5, f32[16,6336]{1,0:T(8,128)S(1)} %bitcast.11), custom_call_target="tpu_custom_call" | custom-call | flops 12999999488 | tf_op jit(solution)/shard_map/lookup/pallas_call | solution.py:198
  19.7 0.0 copy-start.6
  19.7 0.0 collective-permute-done.quad0
  19.7 0.0 collective-permute-done.1.quad1
  19.7 0.0 collective-permute-done.2.quad3
  19.8 0.0 copy-done
  19.8 0.0 copy-done.1
  19.8 0.0 copy-done.3
  19.8 12.2 %window.1 = (f32[256,2048]{1,0:T(8,128)S(1)}, f32[256,2048]{1,0:T(8,128)}, f32[162,8,128]{2,1,0:T(8,128)S(1)}, f32[162,8,128]{2,1,0:T(8,128)}, f32[36,512]{1,0:T...) custom-call(s32[1]{0:T(128)} %bitcast.1.core_ref, f32[80,512]{1,0:T(8,128)S(1)} %copy-done.3, ...), custom_call_target="tpu_custom_call" | custom-call | tf_op jit(solution)/shard_map/window/pallas_call | solution.py:357
  32.0 0.0 copy-done.6
  32.0 0.0 collective-permute-start.3
  32.0 0.5 collective-permute-start.7
  32.5 0.0 collective-permute-start.4
  32.5 1.3 %collective-permute-start.5 = (f32[36,512]{1,0:T(8,128)S(1)}, f32[36,512]{1,0:T(8,128)S(1)}, u32[]{:S(2)}, u32[]{:S(2)}) collective-permute-start(f32[36,512]{1,0:T(8,128)S(1)} %get-tuple-element.45), channel_id=1, source_target_pairs={{0,240},{1,241},{2,242},{3,243},{4,244},{5,245},{6,246},{7,247},{8... | collective-permute-start | bytes 221192 | tf_op jit(solution)/shard_map/ppermute | solution.py:630
  33.8 1.9 %collective-permute-start.6 = (f32[36,512]{1,0:T(8,128)S(1)}, f32[36,512]{1,0:T(8,128)S(1)}, u32[]{:S(2)}, u32[]{:S(2)}) collective-permute-start(f32[36,512]{1,0:T(8,128)S(1)} %get-tuple-element.46), channel_id=1, source_target_pairs={{0,241},{1,242},{2,243},{3,244},{4,245},{5,246},{6,247},{7,248},{8... | collective-permute-start | bytes 221192 | tf_op jit(solution)/shard_map/ppermute | solution.py:631
  35.7 0.7 collective-permute-done.3.came
  36.5 0.0 copy-start.7
  36.5 1.8 %split.1 = (f32[256,1024]{1,0:T(8,128)S(1)}, f32[256,512]{1,0:T(8,128)S(1)}, f32[256,512]{1,0:T(8,128)S(1)}) custom-call(s32[1]{0:T(128)} %bitcast.odd, f32[256,2048]{1,0:T(8,128)S(1)} %get-tuple-element.40.keep, f32[256,2048]{1,0:T(8,128)} %collective-permute-done.3.came), custom_call_target="tpu_custom_call" | custom-call | tf_op jit(solution)/shard_map/split/pallas_call | solution.py:473
  38.3 1.9 %collective-permute-done.4.left = f32[36,512]{1,0:T(8,128)S(1)} collective-permute-done((f32[36,512]{1,0:T(8,128)}, f32[36,512]{1,0:T(8,128)S(1)}, u32[]{:S(2)}, u32[]{:S(2)}) %collective-permute-start.4) | collective-permute-done | bytes 73760 | tf_op jit(solution)/shard_map/ppermute | solution.py:629
  40.3 0.0 collective-permute-done.5.below
  40.3 2.5 %collective-permute-done.6.corner = f32[36,512]{1,0:T(8,128)S(1)} collective-permute-done((f32[36,512]{1,0:T(8,128)S(1)}, f32[36,512]{1,0:T(8,128)S(1)}, u32[]{:S(2)}, u32[]{:S(2)}) %collective-permute-start.6) | collective-permute-done | bytes 73760 | tf_op jit(solution)/shard_map/ppermute | solution.py:631
  42.8 1.9 %collective-permute-start.8 = (f32[256,512]{1,0:T(8,128)S(1)}, f32[256,512]{1,0:T(8,128)S(1)}, u32[]{:S(2)}, u32[]{:S(2)}) collective-permute-start(f32[256,512]{1,0:T(8,128)S(1)} %get-tuple-element.59), channel_id=1, source_target_pairs={{0,32},{32,0},{64,96},{96,64},{128,160},{160,128},{192,224},{224,1... | collective-permute-start | bytes 1572872 | tf_op jit(solution)/shard_map/ppermute | solution.py:634
  44.7 4.0 %collective-permute-start.9 = (f32[256,512]{1,0:T(8,128)S(1)}, f32[256,512]{1,0:T(8,128)S(1)}, u32[]{:S(2)}, u32[]{:S(2)}) collective-permute-start(f32[256,512]{1,0:T(8,128)S(1)} %get-tuple-element.60), channel_id=1, source_target_pairs={{0,224},{32,64},{64,32},{96,128},{128,96},{160,192},{192,160},{224... | collective-permute-start | bytes 1572872 | tf_op jit(solution)/shard_map/ppermute | solution.py:635
  48.7 0.0 collective-permute-done.7.came
  48.7 0.0 copy-done.7
  48.7 6.2 %scatter.1 = (f32[8,16,256]{2,1,0:T(8,128)S(1)}, f32[8,16,256]{2,1,0:T(8,128)S(1)}) custom-call(s32[1]{0:T(128)} %bitcast.1.core_ref, s32[162,128]{1,0:T(8,128)S(1)} %copy-done.7, f32[162,8,128]{2,1,0:T(8,128)S(1)} %get-tuple-element.49.keep, f32[162,8,128]{2,1,0:T(8,128)} %collective-permute-done.7.came), custom_call_target="tpu_custom_call" | custom-call | flops 8999999488 | tf_op jit(solution)/shard_map/scatter/pallas_call | solution.py:441
  54.9 0.1 collective-permute-start.10
  55.0 0.0 copy-done.2
  55.0 0.8 place.1
  55.8 0.5 collective-permute-done.10.table_came
  56.4 0.0 collective-permute-done.8.came_a
  56.4 1.0 collective-permute-done.9.came_b
  57.4 0.1 join.1
  57.5 24.9 %all_to_all.15.parts = f32[8,32,1280]{2,1,0:T(8,128)S(1)} all-to-all(f32[8,32,1280]{2,1,0:T(8,128)S(1)} %join.1), channel_id=1, replica_groups=mesh['z'=8,'y_lo'=2,'x'=4,'y_hi'=2,'core'=2] {'x','y_hi'}, dimensions={0} | all-to-all | bytes 2621440 | tf_op jit(solution)/shard_map/all_to_all | solution.py:643
  82.4 0.1 fold_lon.1
  82.5 15.5 %all_to_all.16.parts = f32[8,4,1280]{2,1,0:T(4,128)S(1)} all-to-all(f32[8,4,1280]{2,1,0:T(4,128)S(1)} %fold_lon.1), channel_id=1, replica_groups={{0,16,64,80,128,144,192,208},{32,48,96,112,160,176,224,240},{1,17,65,81..., dimensions={0} | all-to-all | bytes 327680 | tf_op jit(solution)/shard_map/all_to_all | solution.py:645
  98.0 13.9 %all_to_all.17.parts = f32[16,4,1280]{2,1,0:T(4,128)S(1)} all-to-all(f32[16,4,1280]{2,1,0:T(4,128)S(1)} %fold_lat.1), channel_id=1, replica_groups=mesh['z'=8,'y_lo'=2,'x'=4,'y_hi'=2,'core'=2] {'z','y_lo'}, dimensions={0} | all-to-all | bytes 655360 | tf_op jit(solution)/shard_map/all_to_all | solution.py:646
  111.8 0.7 unpack.1
  (3 shorter events, 0.0 us)
Async XLA Ops:
  0.6 9.8 %copy-start.4 = (f32[6336,16]{0,1:T(8,128)S(1)}, f32[6336,16]{0,1:T(8,128)}, u32[]{:S(2)}) copy-start(f32[6336,16]{0,1:T(8,128)} %param.11) | copy-start | bytes 1216516
  0.6 9.7 %copy-start.5 = (s32[144,144]{1,0:T(8,128)S(1)}, s32[144,144]{1,0:T(8,128)}, u32[]{:S(2)}) copy-start(s32[144,144]{1,0:T(8,128)} %index.1) | copy-start | bytes 248836
  2.8 16.9 %collective-permute-start = (f32[80,512]{1,0:T(8,128)}, f32[80,512]{1,0:T(8,128)S(1)}, u32[]{:S(2)}, u32[]{:S(2)}) collective-permute-start(f32[80,512]{1,0:T(8,128)} %get-tuple-element.36), channel_id=1, source_target_pairs={{0,16},{1,17},{2,18},{3,19},{4,20},{5,21},{6,22},{7,23},{8,24},{9,... | collective-permute-start | bytes 491528 | tf_op jit(solution)/shard_map/ppermute | solution.py:620
  4.6 15.1 %collective-permute-start.1 = (f32[80,512]{1,0:T(8,128)}, f32[80,512]{1,0:T(8,128)S(1)}, u32[]{:S(2)}, u32[]{:S(2)}) collective-permute-start(f32[80,512]{1,0:T(8,128)} %get-tuple-element.37), channel_id=1, source_target_pairs={{0,31},{1,16},{2,17},{3,18},{4,19},{5,20},{6,21},{7,22},{8,23},{9,... | collective-permute-start | bytes 491528 | tf_op jit(solution)/shard_map/ppermute | solution.py:621
  8.4 11.4 %collective-permute-start.2 = (f32[80,512]{1,0:T(8,128)}, f32[80,512]{1,0:T(8,128)S(1)}, u32[]{:S(2)}, u32[]{:S(2)}) collective-permute-start(f32[80,512]{1,0:T(8,128)} %get-tuple-element.38), channel_id=1, source_target_pairs={{0,15},{1,0},{2,1},{3,2},{4,3},{5,4},{6,5},{7,6},{8,7},{9,8},{10,9... | collective-permute-start | bytes 491528 | tf_op jit(solution)/shard_map/ppermute | solution.py:619
  10.4 9.4 %copy-start = (f32[512,1536]{1,0:T(8,128)S(1)}, f32[512,1536]{1,0:T(8,128)}, u32[]{:S(2)}) copy-start(f32[512,1536]{1,0:T(8,128)} %in_weight.1) | copy-start | bytes 9437188
  10.4 9.4 %copy-start.1 = (f32[512,512]{1,0:T(8,128)S(1)}, f32[512,512]{1,0:T(8,128)}, u32[]{:S(2)}) copy-start(f32[512,512]{1,0:T(8,128)} %out_weight.1) | copy-start | bytes 3145732
  10.4 9.4 %copy-start.3 = (f32[80,512]{1,0:T(8,128)S(1)}, f32[80,512]{1,0:T(8,128)}, u32[]{:S(2)}) copy-start(f32[80,512]{1,0:T(8,128)} %get-tuple-element.35.own) | copy-start | bytes 491524
  19.7 12.3 %copy-start.6 = (s32[162,128]{1,0:T(8,128)}, s32[162,128]{1,0:T(8,128)S(1)}, u32[]{:S(2)}) copy-start(s32[162,128]{1,0:T(8,128)S(1)} %get-tuple-element.48.places) | copy-start | bytes 248836
  32.0 4.5 %collective-permute-start.3 = (f32[256,2048]{1,0:T(8,128)}, f32[256,2048]{1,0:T(8,128)}, u32[]{:S(2)}, u32[]{:S(2)}) collective-permute-start(f32[256,2048]{1,0:T(8,128)} %get-tuple-element.41), channel_id=1, source_target_pairs={{0,1},{1,0},{2,3},{3,2},{4,5},{5,4},{6,7},{7,6},{8,9},{9,8},{10,11... | collective-permute-start | bytes 6291464 | tf_op jit(solution)/shard_map/ppermute | solution.py:626
  32.0 16.7 %collective-permute-start.7 = (f32[162,8,128]{2,1,0:T(8,128)}, f32[162,8,128]{2,1,0:T(8,128)}, u32[]{:S(2)}, u32[]{:S(2)}) collective-permute-start(f32[162,8,128]{2,1,0:T(8,128)} %get-tuple-element.50), channel_id=1, source_target_pairs={{0,1},{1,0},{2,3},{3,2},{4,5},{5,4},{6,7},{7,6},{8,9},{9,8},{10,11... | collective-permute-start | bytes 1990664 | tf_op jit(solution)/shard_map/ppermute | solution.py:627
  32.5 7.8 %collective-permute-start.4 = (f32[36,512]{1,0:T(8,128)}, f32[36,512]{1,0:T(8,128)S(1)}, u32[]{:S(2)}, u32[]{:S(2)}) collective-permute-start(f32[36,512]{1,0:T(8,128)} %get-tuple-element.44), channel_id=1, source_target_pairs={{0,1},{1,2},{2,3},{3,4},{4,5},{5,6},{6,7},{7,8},{8,9},{9,10},{10,1... | collective-permute-start | bytes 221192 | tf_op jit(solution)/shard_map/ppermute | solution.py:629
  32.5 7.8 %collective-permute-start.5 = (f32[36,512]{1,0:T(8,128)S(1)}, f32[36,512]{1,0:T(8,128)S(1)}, u32[]{:S(2)}, u32[]{:S(2)}) collective-permute-start(f32[36,512]{1,0:T(8,128)S(1)} %get-tuple-element.45), channel_id=1, source_target_pairs={{0,240},{1,241},{2,242},{3,243},{4,244},{5,245},{6,246},{7,247},{8... | collective-permute-start | bytes 221192 | tf_op jit(solution)/shard_map/ppermute | solution.py:630
  33.8 8.9 %collective-permute-start.6 = (f32[36,512]{1,0:T(8,128)S(1)}, f32[36,512]{1,0:T(8,128)S(1)}, u32[]{:S(2)}, u32[]{:S(2)}) collective-permute-start(f32[36,512]{1,0:T(8,128)S(1)} %get-tuple-element.46), channel_id=1, source_target_pairs={{0,241},{1,242},{2,243},{3,244},{4,245},{5,246},{6,247},{7,248},{8... | collective-permute-start | bytes 221192 | tf_op jit(solution)/shard_map/ppermute | solution.py:631
  36.5 12.2 %copy-start.7 = (s32[162,128]{1,0:T(8,128)S(1)}, s32[162,128]{1,0:T(8,128)}, u32[]{:S(2)}) copy-start(s32[162,128]{1,0:T(8,128)} %copy-done.6) | copy-start | bytes 248836
  42.8 13.6 %collective-permute-start.8 = (f32[256,512]{1,0:T(8,128)S(1)}, f32[256,512]{1,0:T(8,128)S(1)}, u32[]{:S(2)}, u32[]{:S(2)}) collective-permute-start(f32[256,512]{1,0:T(8,128)S(1)} %get-tuple-element.59), channel_id=1, source_target_pairs={{0,32},{32,0},{64,96},{96,64},{128,160},{160,128},{192,224},{224,1... | collective-permute-start | bytes 1572872 | tf_op jit(solution)/shard_map/ppermute | solution.py:634
  44.7 12.7 %collective-permute-start.9 = (f32[256,512]{1,0:T(8,128)S(1)}, f32[256,512]{1,0:T(8,128)S(1)}, u32[]{:S(2)}, u32[]{:S(2)}) collective-permute-start(f32[256,512]{1,0:T(8,128)S(1)} %get-tuple-element.60), channel_id=1, source_target_pairs={{0,224},{32,64},{64,32},{96,128},{128,96},{160,192},{192,160},{224... | collective-permute-start | bytes 1572872 | tf_op jit(solution)/shard_map/ppermute | solution.py:635
  48.7 6.3 %copy-start.2 = (f32[2,12,6,512]{3,0,2,1:T(2,128)S(1)}, f32[2,12,6,512]{3,0,2,1:T(2,128)}, u32[]{:S(2)}) copy-start(f32[2,12,6,512]{3,0,2,1:T(2,128)} %param.8) | copy-start | bytes 884740
  54.9 1.4 %collective-permute-start.10 = (f32[8,16,256]{2,1,0:T(8,128)S(1)}, f32[8,16,256]{2,1,0:T(8,128)S(1)}, u32[]{:S(2)}, u32[]{:S(2)}) collective-permute-start(f32[8,16,256]{2,1,0:T(8,128)S(1)} %get-tuple-element.62), channel_id=1, source_target_pairs={{0,1},{1,0},{2,3},{3,2},{4,5},{5,4},{6,7},{7,6},{8,9},{9,8},{10,11... | collective-permute-start | bytes 393224 | tf_op jit(solution)/shard_map/ppermute | solution.py:638

commit v10 on v9

--- a/solution.py
+++ b/solution.py
@@ -291,7 +291,7 @@
         grad_probs = [outer(g[i], v[i]) for i in range(len(heads))]
         scores = [jnp.where(allowed, x, -1000000000.0) for x in scores]
         exponent = [jnp.exp(x - jnp.max(x, axis=1, keepdims=True)) for x in scores]
-        probs = [x * (1.0 / jnp.sum(x, axis=1, keepdims=True)) for x in exponent]
+        probs = [x * pl.reciprocal(jnp.sum(x, axis=1, keepdims=True)) for x in exponent]
         p = [halves(x) for x in probs]
         for i, at in enumerate(ats):
             att[pl.ds(at, HEAD_DIM), :] = product(*v[i], *p[i], NT)
@@ -311,8 +311,7 @@
     tails[...] = jnp.zeros_like(tails)
     order = [((1 - core) * 8 + slot, slot) for slot in range(8)]
     order += [(core * 8 + slot, 8 + slot) for slot in range(8)]
-    for first in range(0, 16, 8):
-        some_heads(order[first : first + 8])
+    some_heads(order)
 
     for i in range(18):
         total = tails[8 * i]
@@ -413,7 +412,7 @@
             add(rows, base, pair)
         return carry
 
-    lax.fori_loop(0, ROWS // 8, step, 0, unroll=10)
+    lax.fori_loop(0, ROWS // 8, step, 0, unroll=20)
     add(places[ROWS - 2 : ROWS, :], ROWS - 2, 0)
 
 

time: 113 us -> 113 us (level)
  no operation moved by 1% of the time
where the time goes in v10:
time: 113 us; the launch traced here: 112 us
  blocking collectives  54.2 us (48%)
  Pallas kernels  32.7 us (29%)
  starting transfers between devices  17.4 us (15%)
  waiting for transfers between devices  7.19 us (6%)
    all_to_all x1, blocking collectives, body(): parts = lax.all_to_all(joined, ('x', 'y_hi'), 0, 0)  24.9 us
    all_to_all x1, blocking collectives, body(): parts = lax.all_to_all(fold_lon(parts), LAT, 0, 0, axis_index_groups=parity)  15.5 us
    all_to_all x1, blocking collectives, body(): parts = lax.all_to_all(fold_lat(parts), LAT, 0, 0)  13.9 us
    pallas_call x1, Pallas kernels, window(): pl.pallas_call(main_kernel, out_shape=[shape(256, 4 * WIDTH), shape(256,...  12 us
    pallas_call x1, Pallas kernels, lookup(): pl.pallas_call(lookup_kernel, out_shape=[jax.ShapeDtypeStruct((TOKENS, HE...  9.3 us
    pallas_call x1, Pallas kernels, scatter(): pl.pallas_call(scatter_kernel, out_shape=[shape(8, 16, 256)] * 2, in_spec...  5.74 us
    ppermute x1, starting transfers between devices, body(): lax.ppermute(send_b, 'z', [(i, ((i + 1) % 8 ^ 1) + 7 & 7) for i in range(...  4.04 us
    ppermute x1, starting transfers between devices, body(): quad1 = lax.ppermute(corner, everything, moves(1, -1))  3.76 us
  transfers between devices with their start and end apart: 11, of which 5 were waited for; matrix products, arithmetic and copies ran while one was open for 0% of the time, Pallas kernels for 16%

profile of v10, /device:TPU:8, one launch (start us, length us, event | category | flops | bytes accessed | tf_op | source)
XLA Modules:
  0.0 112.3 jit_solution(13343326621208461221)
XLA Ops:
  0.6 0.0 copy-start.4
  0.6 0.0 copy-start.5
  0.7 2.1 %pack.1 = (f32[80,512]{1,0:T(8,128)}, f32[80,512]{1,0:T(8,128)}, f32[80,512]{1,0:T(8,128)}, f32[80,512]{1,0:T(8,128)}) custom-call(s32[1]{0:T(128)} %bitcast.2.last, f32[12,6,2,512]{3,2,1,0:T(2,128)} %bitcast.13, f32[12,6,2,512]{3,2,1,0:T(2,128)} %bitcast.9, s32[6,2,12]{2,1,0:T(2,128)} %bitcast.15), custom_call_target="tpu_custom_call" | custom-call | flops 1000000000 | tf_op jit(solution)/shard_map/pack/pallas_call | solution.py:117
  2.8 1.8 %collective-permute-start = (f32[80,512]{1,0:T(8,128)}, f32[80,512]{1,0:T(8,128)S(1)}, u32[]{:S(2)}, u32[]{:S(2)}) collective-permute-start(f32[80,512]{1,0:T(8,128)} %get-tuple-element.36), channel_id=1, source_target_pairs={{0,16},{1,17},{2,18},{3,19},{4,20},{5,21},{6,22},{7,23},{8,24},{9,... | collective-permute-start | bytes 491528 | tf_op jit(solution)/shard_map/ppermute | solution.py:619
  4.6 3.8 %collective-permute-start.1 = (f32[80,512]{1,0:T(8,128)}, f32[80,512]{1,0:T(8,128)S(1)}, u32[]{:S(2)}, u32[]{:S(2)}) collective-permute-start(f32[80,512]{1,0:T(8,128)} %get-tuple-element.37), channel_id=1, source_target_pairs={{0,31},{1,16},{2,17},{3,18},{4,19},{5,20},{6,21},{7,22},{8,23},{9,... | collective-permute-start | bytes 491528 | tf_op jit(solution)/shard_map/ppermute | solution.py:620
  8.4 2.0 %collective-permute-start.2 = (f32[80,512]{1,0:T(8,128)}, f32[80,512]{1,0:T(8,128)S(1)}, u32[]{:S(2)}, u32[]{:S(2)}) collective-permute-start(f32[80,512]{1,0:T(8,128)} %get-tuple-element.38), channel_id=1, source_target_pairs={{0,15},{1,0},{2,1},{3,2},{4,3},{5,4},{6,5},{7,6},{8,7},{9,8},{10,9... | collective-permute-start | bytes 491528 | tf_op jit(solution)/shard_map/ppermute | solution.py:618
  10.4 0.0 copy-done.4
  10.4 0.0 copy-done.5
  10.4 0.0 copy-start.1
  10.4 0.0 copy-start.3
  10.4 9.3 %lookup.1 = (f32[144,16,144]{2,1,0:T(8,128)S(1)}, s32[162,128]{1,0:T(8,128)S(1)}) custom-call(s32[1]{0:T(128)} %bitcast.1.core_ref, s32[144,144]{1,0:T(8,128)S(1)} %copy-done.5, f32[16,6336]{1,0:T(8,128)S(1)} %bitcast.11), custom_call_target="tpu_custom_call" | custom-call | flops 12999999488 | tf_op jit(solution)/shard_map/lookup/pallas_call | solution.py:198
  19.7 0.0 copy-start.6
  19.7 0.0 collective-permute-done.quad0
  19.7 0.0 collective-permute-done.1.quad1
  19.7 0.0 collective-permute-done.2.quad3
  19.8 0.0 copy-done
  19.8 0.0 copy-done.1
  19.8 0.0 copy-done.3
  19.8 12.0 %window.1 = (f32[256,2048]{1,0:T(8,128)S(1)}, f32[256,2048]{1,0:T(8,128)}, f32[162,8,128]{2,1,0:T(8,128)S(1)}, f32[162,8,128]{2,1,0:T(8,128)}, f32[36,512]{1,0:T...) custom-call(s32[1]{0:T(128)} %bitcast.1.core_ref, f32[80,512]{1,0:T(8,128)S(1)} %copy-done.3, ...), custom_call_target="tpu_custom_call" | custom-call | tf_op jit(solution)/shard_map/window/pallas_call | solution.py:356
  31.7 0.0 copy-done.6
  31.8 0.0 collective-permute-start.3
  31.8 0.5 collective-permute-start.7
  32.3 0.0 collective-permute-start.4
  32.3 1.3 %collective-permute-start.5 = (f32[36,512]{1,0:T(8,128)S(1)}, f32[36,512]{1,0:T(8,128)S(1)}, u32[]{:S(2)}, u32[]{:S(2)}) collective-permute-start(f32[36,512]{1,0:T(8,128)S(1)} %get-tuple-element.45), channel_id=1, source_target_pairs={{0,240},{1,241},{2,242},{3,243},{4,244},{5,245},{6,246},{7,247},{8... | collective-permute-start | bytes 221192 | tf_op jit(solution)/shard_map/ppermute | solution.py:629
  33.6 1.9 %collective-permute-start.6 = (f32[36,512]{1,0:T(8,128)S(1)}, f32[36,512]{1,0:T(8,128)S(1)}, u32[]{:S(2)}, u32[]{:S(2)}) collective-permute-start(f32[36,512]{1,0:T(8,128)S(1)} %get-tuple-element.46), channel_id=1, source_target_pairs={{0,241},{1,242},{2,243},{3,244},{4,245},{5,246},{6,247},{7,248},{8... | collective-permute-start | bytes 221192 | tf_op jit(solution)/shard_map/ppermute | solution.py:630
  35.5 0.7 collective-permute-done.3.came
  36.3 0.0 copy-start.7
  36.3 1.8 %split.1 = (f32[256,1024]{1,0:T(8,128)S(1)}, f32[256,512]{1,0:T(8,128)S(1)}, f32[256,512]{1,0:T(8,128)S(1)}) custom-call(s32[1]{0:T(128)} %bitcast.odd, f32[256,2048]{1,0:T(8,128)S(1)} %get-tuple-element.40.keep, f32[256,2048]{1,0:T(8,128)} %collective-permute-done.3.came), custom_call_target="tpu_custom_call" | custom-call | tf_op jit(solution)/shard_map/split/pallas_call | solution.py:472
  38.1 1.9 %collective-permute-done.4.left = f32[36,512]{1,0:T(8,128)S(1)} collective-permute-done((f32[36,512]{1,0:T(8,128)}, f32[36,512]{1,0:T(8,128)S(1)}, u32[]{:S(2)}, u32[]{:S(2)}) %collective-permute-start.4) | collective-permute-done | bytes 73760 | tf_op jit(solution)/shard_map/ppermute | solution.py:628
  40.0 0.0 collective-permute-done.5.below
  40.0 2.5 %collective-permute-done.6.corner = f32[36,512]{1,0:T(8,128)S(1)} collective-permute-done((f32[36,512]{1,0:T(8,128)S(1)}, f32[36,512]{1,0:T(8,128)S(1)}, u32[]{:S(2)}, u32[]{:S(2)}) %collective-permute-start.6) | collective-permute-done | bytes 73760 | tf_op jit(solution)/shard_map/ppermute | solution.py:630
  42.5 1.9 %collective-permute-start.8 = (f32[256,512]{1,0:T(8,128)S(1)}, f32[256,512]{1,0:T(8,128)S(1)}, u32[]{:S(2)}, u32[]{:S(2)}) collective-permute-start(f32[256,512]{1,0:T(8,128)S(1)} %get-tuple-element.59), channel_id=1, source_target_pairs={{0,32},{32,0},{64,96},{96,64},{128,160},{160,128},{192,224},{224,1... | collective-permute-start | bytes 1572872 | tf_op jit(solution)/shard_map/ppermute | solution.py:633
  44.4 4.0 %collective-permute-start.9 = (f32[256,512]{1,0:T(8,128)S(1)}, f32[256,512]{1,0:T(8,128)S(1)}, u32[]{:S(2)}, u32[]{:S(2)}) collective-permute-start(f32[256,512]{1,0:T(8,128)S(1)} %get-tuple-element.60), channel_id=1, source_target_pairs={{0,224},{32,64},{64,32},{96,128},{128,96},{160,192},{192,160},{224... | collective-permute-start | bytes 1572872 | tf_op jit(solution)/shard_map/ppermute | solution.py:634
  48.5 0.0 collective-permute-done.7.came
  48.5 0.0 copy-done.7
  48.5 5.7 %scatter.1 = (f32[8,16,256]{2,1,0:T(8,128)S(1)}, f32[8,16,256]{2,1,0:T(8,128)S(1)}) custom-call(s32[1]{0:T(128)} %bitcast.1.core_ref, s32[162,128]{1,0:T(8,128)S(1)} %copy-done.7, f32[162,8,128]{2,1,0:T(8,128)S(1)} %get-tuple-element.49.keep, f32[162,8,128]{2,1,0:T(8,128)} %collective-permute-done.7.came), custom_call_target="tpu_custom_call" | custom-call | flops 8999999488 | tf_op jit(solution)/shard_map/scatter/pallas_call | solution.py:440
  54.2 0.1 collective-permute-start.10
  54.3 0.0 copy-done.2
  54.3 0.8 place.1
  55.1 0.5 collective-permute-done.10.table_came
  55.7 0.0 collective-permute-done.8.came_a
  55.7 1.5 %collective-permute-done.9.came_b = f32[256,512]{1,0:T(8,128)S(1)} collective-permute-done((f32[256,512]{1,0:T(8,128)S(1)}, f32[256,512]{1,0:T(8,128)S(1)}, u32[]{:S(2)}, u32[]{:S(2)}) %collective-permute-start.9) | collective-permute-done | bytes 524320 | tf_op jit(solution)/shard_map/ppermute | solution.py:634
  57.2 0.1 join.1
  57.3 24.9 %all_to_all.15.parts = f32[8,32,1280]{2,1,0:T(8,128)S(1)} all-to-all(f32[8,32,1280]{2,1,0:T(8,128)S(1)} %join.1), channel_id=1, replica_groups=mesh['z'=8,'y_lo'=2,'x'=4,'y_hi'=2,'core'=2] {'x','y_hi'}, dimensions={0} | all-to-all | bytes 2621440 | tf_op jit(solution)/shard_map/all_to_all | solution.py:642
  82.2 0.1 fold_lon.1
  82.2 15.5 %all_to_all.16.parts = f32[8,4,1280]{2,1,0:T(4,128)S(1)} all-to-all(f32[8,4,1280]{2,1,0:T(4,128)S(1)} %fold_lon.1), channel_id=1, replica_groups={{0,16,64,80,128,144,192,208},{32,48,96,112,160,176,224,240},{1,17,65,81..., dimensions={0} | all-to-all | bytes 327680 | tf_op jit(solution)/shard_map/all_to_all | solution.py:644
  97.8 13.9 %all_to_all.17.parts = f32[16,4,1280]{2,1,0:T(4,128)S(1)} all-to-all(f32[16,4,1280]{2,1,0:T(4,128)S(1)} %fold_lat.1), channel_id=1, replica_groups=mesh['z'=8,'y_lo'=2,'x'=4,'y_hi'=2,'core'=2] {'z','y_lo'}, dimensions={0} | all-to-all | bytes 655360 | tf_op jit(solution)/shard_map/all_to_all | solution.py:645
  111.6 0.7 unpack.1
  (3 shorter events, 0.0 us)
Async XLA Ops:
  0.6 9.8 %copy-start.4 = (f32[6336,16]{0,1:T(8,128)S(1)}, f32[6336,16]{0,1:T(8,128)}, u32[]{:S(2)}) copy-start(f32[6336,16]{0,1:T(8,128)} %param.11) | copy-start | bytes 1216516
  0.6 9.7 %copy-start.5 = (s32[144,144]{1,0:T(8,128)S(1)}, s32[144,144]{1,0:T(8,128)}, u32[]{:S(2)}) copy-start(s32[144,144]{1,0:T(8,128)} %index.1) | copy-start | bytes 248836
  2.8 16.9 %collective-permute-start = (f32[80,512]{1,0:T(8,128)}, f32[80,512]{1,0:T(8,128)S(1)}, u32[]{:S(2)}, u32[]{:S(2)}) collective-permute-start(f32[80,512]{1,0:T(8,128)} %get-tuple-element.36), channel_id=1, source_target_pairs={{0,16},{1,17},{2,18},{3,19},{4,20},{5,21},{6,22},{7,23},{8,24},{9,... | collective-permute-start | bytes 491528 | tf_op jit(solution)/shard_map/ppermute | solution.py:619
  4.6 15.1 %collective-permute-start.1 = (f32[80,512]{1,0:T(8,128)}, f32[80,512]{1,0:T(8,128)S(1)}, u32[]{:S(2)}, u32[]{:S(2)}) collective-permute-start(f32[80,512]{1,0:T(8,128)} %get-tuple-element.37), channel_id=1, source_target_pairs={{0,31},{1,16},{2,17},{3,18},{4,19},{5,20},{6,21},{7,22},{8,23},{9,... | collective-permute-start | bytes 491528 | tf_op jit(solution)/shard_map/ppermute | solution.py:620
  8.4 11.4 %collective-permute-start.2 = (f32[80,512]{1,0:T(8,128)}, f32[80,512]{1,0:T(8,128)S(1)}, u32[]{:S(2)}, u32[]{:S(2)}) collective-permute-start(f32[80,512]{1,0:T(8,128)} %get-tuple-element.38), channel_id=1, source_target_pairs={{0,15},{1,0},{2,1},{3,2},{4,3},{5,4},{6,5},{7,6},{8,7},{9,8},{10,9... | collective-permute-start | bytes 491528 | tf_op jit(solution)/shard_map/ppermute | solution.py:618
  10.4 9.4 %copy-start = (f32[512,1536]{1,0:T(8,128)S(1)}, f32[512,1536]{1,0:T(8,128)}, u32[]{:S(2)}) copy-start(f32[512,1536]{1,0:T(8,128)} %in_weight.1) | copy-start | bytes 9437188
  10.4 9.4 %copy-start.1 = (f32[512,512]{1,0:T(8,128)S(1)}, f32[512,512]{1,0:T(8,128)}, u32[]{:S(2)}) copy-start(f32[512,512]{1,0:T(8,128)} %out_weight.1) | copy-start | bytes 3145732
  10.4 9.4 %copy-start.3 = (f32[80,512]{1,0:T(8,128)S(1)}, f32[80,512]{1,0:T(8,128)}, u32[]{:S(2)}) copy-start(f32[80,512]{1,0:T(8,128)} %get-tuple-element.35.own) | copy-start | bytes 491524
  19.7 12.0 %copy-start.6 = (s32[162,128]{1,0:T(8,128)}, s32[162,128]{1,0:T(8,128)S(1)}, u32[]{:S(2)}) copy-start(s32[162,128]{1,0:T(8,128)S(1)} %get-tuple-element.48.places) | copy-start | bytes 248836
  31.8 4.5 %collective-permute-start.3 = (f32[256,2048]{1,0:T(8,128)}, f32[256,2048]{1,0:T(8,128)}, u32[]{:S(2)}, u32[]{:S(2)}) collective-permute-start(f32[256,2048]{1,0:T(8,128)} %get-tuple-element.41), channel_id=1, source_target_pairs={{0,1},{1,0},{2,3},{3,2},{4,5},{5,4},{6,7},{7,6},{8,9},{9,8},{10,11... | collective-permute-start | bytes 6291464 | tf_op jit(solution)/shard_map/ppermute | solution.py:625
  31.8 16.7 %collective-permute-start.7 = (f32[162,8,128]{2,1,0:T(8,128)}, f32[162,8,128]{2,1,0:T(8,128)}, u32[]{:S(2)}, u32[]{:S(2)}) collective-permute-start(f32[162,8,128]{2,1,0:T(8,128)} %get-tuple-element.50), channel_id=1, source_target_pairs={{0,1},{1,0},{2,3},{3,2},{4,5},{5,4},{6,7},{7,6},{8,9},{9,8},{10,11... | collective-permute-start | bytes 1990664 | tf_op jit(solution)/shard_map/ppermute | solution.py:626
  32.3 7.8 %collective-permute-start.4 = (f32[36,512]{1,0:T(8,128)}, f32[36,512]{1,0:T(8,128)S(1)}, u32[]{:S(2)}, u32[]{:S(2)}) collective-permute-start(f32[36,512]{1,0:T(8,128)} %get-tuple-element.44), channel_id=1, source_target_pairs={{0,1},{1,2},{2,3},{3,4},{4,5},{5,6},{6,7},{7,8},{8,9},{9,10},{10,1... | collective-permute-start | bytes 221192 | tf_op jit(solution)/shard_map/ppermute | solution.py:628
  32.3 7.8 %collective-permute-start.5 = (f32[36,512]{1,0:T(8,128)S(1)}, f32[36,512]{1,0:T(8,128)S(1)}, u32[]{:S(2)}, u32[]{:S(2)}) collective-permute-start(f32[36,512]{1,0:T(8,128)S(1)} %get-tuple-element.45), channel_id=1, source_target_pairs={{0,240},{1,241},{2,242},{3,243},{4,244},{5,245},{6,246},{7,247},{8... | collective-permute-start | bytes 221192 | tf_op jit(solution)/shard_map/ppermute | solution.py:629
  33.6 8.9 %collective-permute-start.6 = (f32[36,512]{1,0:T(8,128)S(1)}, f32[36,512]{1,0:T(8,128)S(1)}, u32[]{:S(2)}, u32[]{:S(2)}) collective-permute-start(f32[36,512]{1,0:T(8,128)S(1)} %get-tuple-element.46), channel_id=1, source_target_pairs={{0,241},{1,242},{2,243},{3,244},{4,245},{5,246},{6,247},{7,248},{8... | collective-permute-start | bytes 221192 | tf_op jit(solution)/shard_map/ppermute | solution.py:630
  36.3 12.2 %copy-start.7 = (s32[162,128]{1,0:T(8,128)S(1)}, s32[162,128]{1,0:T(8,128)}, u32[]{:S(2)}) copy-start(s32[162,128]{1,0:T(8,128)} %copy-done.6) | copy-start | bytes 248836
  42.5 13.1 %collective-permute-start.8 = (f32[256,512]{1,0:T(8,128)S(1)}, f32[256,512]{1,0:T(8,128)S(1)}, u32[]{:S(2)}, u32[]{:S(2)}) collective-permute-start(f32[256,512]{1,0:T(8,128)S(1)} %get-tuple-element.59), channel_id=1, source_target_pairs={{0,32},{32,0},{64,96},{96,64},{128,160},{160,128},{192,224},{224,1... | collective-permute-start | bytes 1572872 | tf_op jit(solution)/shard_map/ppermute | solution.py:633
  44.4 12.7 %collective-permute-start.9 = (f32[256,512]{1,0:T(8,128)S(1)}, f32[256,512]{1,0:T(8,128)S(1)}, u32[]{:S(2)}, u32[]{:S(2)}) collective-permute-start(f32[256,512]{1,0:T(8,128)S(1)} %get-tuple-element.60), channel_id=1, source_target_pairs={{0,224},{32,64},{64,32},{96,128},{128,96},{160,192},{192,160},{224... | collective-permute-start | bytes 1572872 | tf_op jit(solution)/shard_map/ppermute | solution.py:634
  48.5 5.8 %copy-start.2 = (f32[2,12,6,512]{3,0,2,1:T(2,128)S(1)}, f32[2,12,6,512]{3,0,2,1:T(2,128)}, u32[]{:S(2)}) copy-start(f32[2,12,6,512]{3,0,2,1:T(2,128)} %param.8) | copy-start | bytes 884740
  54.2 1.4 %collective-permute-start.10 = (f32[8,16,256]{2,1,0:T(8,128)S(1)}, f32[8,16,256]{2,1,0:T(8,128)S(1)}, u32[]{:S(2)}, u32[]{:S(2)}) collective-permute-start(f32[8,16,256]{2,1,0:T(8,128)S(1)} %get-tuple-element.62), channel_id=1, source_target_pairs={{0,1},{1,0},{2,3},{3,2},{4,5},{5,4},{6,7},{7,6},{8,9},{9,8},{10,11... | collective-permute-start | bytes 393224 | tf_op jit(solution)/shard_map/ppermute | solution.py:637
